TPU v7x, 128 devices: a whole 4x4x4 slice. The times are simulated.
128 devices in a mesh: shot: 16 (over x_hi, y, core), sub: 8 (over x_lo, z).
Axes of the slice: x: 4 (x_hi: 2, x_lo: 2; x = x_hi * 2 + x_lo), y: 4, z: 4, core: 2. Of those that a mesh axis runs over, the one named last changes fastest.
Arguments:
- courant_squared: float32 [2, 16, 8, 256, 128], P(None, 'shot', None, 'sub'), may hold values from 0.04 to 0.18
- wave_now: float32 [16, 64, 256, 128], P('shot', 'sub'), may hold values from -1.75 to 1.75
- wave_prev: float32 [16, 64, 256, 128], P('shot', 'sub'), may hold values from -1.75 to 1.75
- adj_late: float32 [16, 64, 256, 128], P('shot', 'sub'), may hold values from -1.75 to 1.75
- adj_later: float32 [16, 64, 256, 128], P('shot', 'sub'), may hold values from -1.75 to 1.75
- wavelet: float32 [16, 4], P('shot'), may hold values from -6 to 6
- sources: int32 [16], P('shot'), may hold values from 0 to 2097151
- receivers: int32 [16, 256], P('shot'), may hold values from 0 to 2097151
- observed: float32 [16, 4, 256], P('shot'), may hold values from -6 to 6
- apertures: int32 [16, 8], replicated, may hold values from 0 to 31, as said below
Outputs:
- gradient: float32 [2, 16, 8, 256, 128], P(None, 'shot', None, 'sub')
Inputs may be any that keep to these rules, and one draw needn't show every extreme that they name: `apertures`: row s holds 8 consecutive block numbers in ascending order.
All inputs are finite; a program needn't handle non-finite values.
Results may differ from a plain program's by a relative error of at most 0.0003.
Values sent between devices are 32-bit elements; how exact they have to be, the bound alone decides.
No kernel may reach another device: no remote copies, remote signals or barrier semaphores. Data moves between devices by JAX's collectives and lax.ppermute only.
A program may use at most 64 MiB of HBM per device.

v0:
```python
import jax
import jax.numpy as jnp
from jax import lax
from jax.sharding import PartitionSpec as P

STEPS = 4


STENCIL = (-205.0 / 72.0, 8.0 / 5.0, -1.0 / 5.0, 8.0 / 315.0, -1.0 / 560.0)


def extended(x, sides, width):
    for axis, dim in sides:
        size, length = (lax.axis_size(axis), x.shape[dim])
        up = [(i, (i + 1) % size) for i in range(size - 1)]
        down = [(j, i) for i, j in up]
        last = lax.slice_in_dim(x, length - width, length, axis=dim)
        first = lax.slice_in_dim(x, 0, width, axis=dim)
        before = lax.ppermute(last, axis, up)
        after = lax.ppermute(first, axis, down)
        x = jnp.concatenate([before, x, after], axis=dim)
    return x


def laplace(wavefield):
    padded_x = extended(wavefield, (("sub", 0),), 4)
    padded = jnp.pad(padded_x, ((0, 0), (4, 4), (4, 4)))
    size_x, size_y, size_z = wavefield.shape
    summed = 3.0 * STENCIL[0] * wavefield
    for shift_by in range(1, 5):
        beside = (
            padded[4 + shift_by : 4 + shift_by + size_x, 4 : 4 + size_y, 4 : 4 + size_z]
            + padded[4 - shift_by : 4 - shift_by + size_x, 4 : 4 + size_y, 4 : 4 + size_z]
        )
        beside = (
            beside
            + padded[4 : 4 + size_x, 4 + shift_by : 4 + shift_by + size_y, 4 : 4 + size_z]
            + padded[4 : 4 + size_x, 4 - shift_by : 4 - shift_by + size_y, 4 : 4 + size_z]
        )
        beside = (
            beside
            + padded[4 : 4 + size_x, 4 : 4 + size_y, 4 + shift_by : 4 + shift_by + size_z]
            + padded[4 : 4 + size_x, 4 : 4 + size_y, 4 - shift_by : 4 - shift_by + size_z]
        )
        summed = summed + STENCIL[shift_by] * beside
    return summed


def per_device(
    courant_squared,
    wave_now,
    wave_prev,
    adj_late,
    adj_later,
    wavelet,
    sources,
    receivers,
    observed,
    apertures,
):
    shot_count = lax.axis_size("shot")
    sub_count = lax.axis_size("sub")
    my_group = lax.axis_index("shot")
    my_part = lax.axis_index("sub")
    owned = courant_squared.shape[0]
    starts = apertures[:, 0]
    first_block = starts[my_group]
    block_ids = first_block + jnp.arange(sub_count)
    owner_ids = block_ids % shot_count
    row_ids = block_ids // shot_count
    piece = lax.all_gather(courant_squared, "shot", axis=1, tiled=True)
    first_row = jnp.int32(0)
    count_here = piece.shape[1]
    flat_rows = piece.reshape((owned * count_here,) + piece.shape[2:])
    inside = (owner_ids >= first_row) & (owner_ids < first_row + count_here)
    take_at = jnp.clip(row_ids * count_here + owner_ids, 0, owned * count_here - 1)
    picked = jnp.take(flat_rows, take_at, axis=0)
    slices = jnp.where(inside[:, None, None, None], picked, 0.0)
    assembled = lax.all_to_all(slices, "sub", split_axis=0, concat_axis=2, tiled=True)
    courant = assembled[0]
    shape = courant.shape
    cells = shape[0] * shape[1] * shape[2]
    source_cell = sources[0]
    source_mine = source_cell // cells == my_part
    source_local = source_cell % cells
    recv_cells = receivers[0]
    recv_mine = recv_cells // cells == my_part
    recv_local = recv_cells % cells
    current = wave_now[0]
    earlier = wave_prev[0]
    lap_terms = []
    samples = []
    for step in range(STEPS):
        lap_now = laplace(current)
        lap_terms.append(lap_now)
        next_wave = 2.0 * current - earlier + courant * lap_now
        amount = jnp.where(source_mine, wavelet[0, step], 0.0)
        next_wave = next_wave.reshape(-1).at[source_local].add(amount).reshape(shape)
        samples.append(next_wave.reshape(-1)[recv_local])
        earlier, current = (current, next_wave)
    adj_older = adj_later[0]
    adj_newer = adj_late[0]
    gradient_sum = jnp.zeros(shape, jnp.float32)
    for step in range(STEPS, 0, -1):
        adjoint = 2.0 * adj_newer + laplace(courant * adj_newer) - adj_older
        misfit = jnp.where(recv_mine, samples[step - 1] - observed[0, step - 1], 0.0)
        adjoint = adjoint.reshape(-1).at[recv_local].add(misfit).reshape(shape)
        gradient_sum = gradient_sum + adjoint * lap_terms[step - 1]
        adj_older, adj_newer = (adj_newer, adjoint)
    pieces = lax.all_to_all(gradient_sum[None], "sub", split_axis=2, concat_axis=0, tiled=True)
    zero_index = jnp.zeros((), jnp.int32)
    base = jnp.zeros((owned * shot_count,) + pieces.shape[1:], jnp.float32)
    full_model = lax.dynamic_update_slice(
        base, pieces, (first_block, zero_index, zero_index, zero_index)
    )
    full_model = full_model.reshape((owned, shot_count) + pieces.shape[1:])
    result = lax.psum_scatter(full_model, "shot", scatter_dimension=1, tiled=True)
    return result


def solution(mesh):
    in_specs = (
        P(None, "shot", None, "sub", None),
        P("shot", "sub", None, None),
        P("shot", "sub", None, None),
        P("shot", "sub", None, None),
        P("shot", "sub", None, None),
        P("shot", None),
        P("shot"),
        P("shot", None),
        P("shot", None, None),
        P(),
    )
    out_specs = P(None, "shot", None, "sub", None)
    return jax.shard_map(
        per_device, mesh=mesh, in_specs=in_specs, out_specs=out_specs, check_vma=False
    )
```

profile of v0, /device:TPU:1, one launch (start us, length us, event | category | flops | bytes accessed | tf_op | source)
XLA Modules:
  0.0 520.0 jit_solution(5761972227868849043)
XLA Ops:
  7.3 2.4 slice_bitcast_fusion
  9.6 1.3 collective-permute-start.2
  10.9 5.8 %collective-permute-start.3 = (f32[4,256,128]{2,1,0:T(8,128)}, f32[4,256,128]{2,1,0:T(8,128)}, u32[]{:S(2)}, u32[]{:S(2)}) collective-permute-start(f32[4,256,128]{2,1,0:T(8,128)} %get-tuple-element.75), channel_id=1, source_target_pairs={{0,1},{1,2},{2,3},{3,4},{4,5},{5,6},{6,7},{8,9},{9,10},{10,11},{11... | collective-permute-start | bytes 1572872 | tf_op jit(solution)/shard_map/ppermute | solution.py:19
  18.1 1.5 fusion.273
  24.7 45.9 %all-gather.2.cloned.1.call-done = f32[2,16,8,32,128]{4,3,2,1,0:T(8,128)} async-done(((f32[2,1,8,32,128]{4,3,2,1,0:T(8,128)}), f32[2,16,8,32,128]{4,3,2,1,0:T(8,128)}) %all-gather.2.cloned.1.call-update) | async-done | bytes 4194320 | tf_op jit(solution)/shard_map/all_gather | solution.py:71
  70.7 2.8 gather_fusion
  74.7 4.2 all-to-all-start
  78.9 4.5 select_maximum_fusion.12
  83.5 10.4 %all-to-all-done = f32[8,8,32,128]{3,2,1,0:T(8,128)S(1)} async-done(((f32[8,8,32,128]{3,2,1,0:T(8,128)}), f32[8,8,32,128]{3,2,1,0:T(8,128)S(1)}, u32[]{:S(2)}, u32[]{:S(2)}) %all-to-all-start) | async-done | bytes 1048608 | tf_op jit(solution)/shard_map/all_to_all | solution.py:79
  93.9 17.7 %fusion.251 = (f32[8,256,128]{2,1,0:T(8,128)S(1)}, f32[8,256,128]{2,1,0:T(8,128)}) fusion(f32[1,8,256,128]{3,2,1,0:T(8,128)} %param.20, f32[8,256,128]{2,1,0:T(8,128)S(1)} %bitcast.85, f32[1,8,256,128]{3,2,1,0:T(8,128)S(1)} %copy-done.3, f32[16,264,136]{2,1,0:T(8,128)} %select_maximum_fusion.12, f32[8,256,128]{2,1,0:T(8,128)S(1)} %bitcast.115, ...), kind=kLoop, calls=%fused_computation.425 | loop fusion | flops 10747904 | bytes 24117248 | tf_op jit(solution)/shard_map/add | solution.py:96
  114.3 4.8 collective-permute-start.5
  119.1 1.3 bitcast_multiply_fusion
  120.4 1.7 gather_fusion.4
  124.6 4.8 collective-permute-start.1
  129.4 3.4 select_maximum_fusion.10
  132.8 8.7 %multiply_add_fusion.2 = (f32[8,256,128]{2,1,0:T(8,128)}, f32[8,256,128]{2,1,0:T(8,128)}) fusion(f32[8,256,128]{2,1,0:T(8,128)} %bitcast.87, f32[8,256,128]{2,1,0:T(8,128)} %bitcast.95, f32[1,8,256,128]{3,2,1,0:T(8,128)} %param.19, f32[16,264,136]{2,1,0:T(8,128)S(1)} %select_maximum_fusion.10, f32[4,256,128]{2,1,0:T(8,128)} %collective-permute-done.5, ...), kind=kLoop, calls=%fused_computation.432 | loop fusion | flops 10747904 | bytes 23068672 | tf_op jit(solution)/shard_map/add | solution.py:96
  141.5 1.5 fusion.256
  143.0 1.4 fusion.269
  144.4 1.3 collective-permute-start.6
  145.7 4.6 collective-permute-start.7
  150.3 3.4 select_maximum_fusion.14
  153.7 3.4 collective-permute-done.6
  158.8 4.4 select_maximum_fusion.8
  163.2 19.8 %multiply_add_fusion.1 = (f32[8,256,128]{2,1,0:T(8,128)}, f32[8,256,128]{2,1,0:T(8,128)}) fusion(f32[8,256,128]{2,1,0:T(8,128)} %bitcast.88, f32[8,256,128]{2,1,0:T(8,128)} %bitcast.96, f32[8,256,128]{2,1,0:T(8,128)} %bitcast.98, f32[16,264,136]{2,1,0:T(8,128)} %select_maximum_fusion.8, f32[4,256,128]{2,1,0:T(8,128)} %copy-done.8, ...), kind=kLoop, calls=%fused_computation.431 | loop fusion | flops 10747904 | bytes 23068672 | tf_op jit(solution)/shard_map/add | solution.py:96
  183.1 1.5 fusion.257
  184.6 2.2 fusion.268
  188.1 5.7 %collective-permute-start.9 = (f32[4,256,128]{2,1,0:T(8,128)}, f32[4,256,128]{2,1,0:T(8,128)}, u32[]{:S(2)}, u32[]{:S(2)}) collective-permute-start(f32[4,256,128]{2,1,0:T(8,128)} %bitcast.41), channel_id=1, source_target_pairs={{0,1},{1,2},{2,3},{3,4},{4,5},{5,6},{6,7},{8,9},{9,10},{10,11},{11... | collective-permute-start | bytes 1572872 | tf_op jit(solution)/shard_map/ppermute | solution.py:19
  193.8 8.3 %fusion.215 = f32[8,256,128]{2,1,0:T(8,128)} fusion(f32[8,256,128]{2,1,0:T(8,128)} %copy-done.4, f32[4,256,128]{2,1,0:T(8,128)} %collective-permute-done.1, f32[4,256,128]{2,1,0:T(8,128)} %collective-permute-done, f32[16,264,136]{2,1,0:T(8,128)S(1)} %select_maximum_fusion.14, f32[1,8,256,128]{3,2,1,0:T(8,128)} %param.22, f32[1,8,256,128]{3,2,1,0:T(8,128)} %param.21), kind=kLoop, calls=%fused_computation.340 | loop fusion | flops 10485760 | bytes 22020096 | tf_op jit(solution)/shard_map/sub | solution.py:105
  202.1 3.2 gather_fusion.3
  205.4 3.2 gather_fusion.2
  208.6 3.3 select_maximum_fusion.6
  211.9 8.6 %multiply_add_fusion = (f32[8,256,128]{2,1,0:T(8,128)}, f32[8,256,128]{2,1,0:T(8,128)}) fusion(f32[8,256,128]{2,1,0:T(8,128)} %bitcast.89, f32[8,256,128]{2,1,0:T(8,128)} %bitcast.99, f32[8,256,128]{2,1,0:T(8,128)} %bitcast.113, f32[16,264,136]{2,1,0:T(8,128)S(1)} %select_maximum_fusion.6, f32[4,256,128]{2,1,0:T(8,128)} %collective-permute-done.9, ...), kind=kLoop, calls=%fused_computation.430 | loop fusion | flops 10747904 | bytes 23068672 | tf_op jit(solution)/shard_map/add | solution.py:96
  220.5 1.5 fusion.258
  222.0 3.3 gather_fusion.1
  225.3 4.1 scatter_fusion
  229.4 1.6 mul.233
  231.1 1.3 collective-permute-start.10
  232.4 4.2 collective-permute-start.11
  236.7 5.7 %collective-permute-done.10 = f32[4,256,128]{2,1,0:T(8,128)S(1)} collective-permute-done((f32[4,256,128]{2,1,0:T(8,128)S(1)}, f32[4,256,128]{2,1,0:T(8,128)S(1)}, u32[]{:S(2)}, u32[]{:S(2)}) %collective-permute-start.10) | collective-permute-done | bytes 524320 | tf_op jit(solution)/shard_map/ppermute | solution.py:20
  244.0 3.1 select_maximum_fusion.4
  247.1 8.2 %fusion.73 = f32[8,256,128]{2,1,0:T(8,128)} fusion(f32[8,256,128]{2,1,0:T(8,128)} %copy-done.6, f32[4,256,128]{2,1,0:T(8,128)} %copy-done.9, f32[4,256,128]{2,1,0:T(8,128)S(1)} %collective-permute-done.10, f32[16,264,136]{2,1,0:T(8,128)S(1)} %select_maximum_fusion.4, f32[1,8,256,128]{3,2,1,0:T(8,128)} %param.21, f32[8,256,128]{2,1,0:T(8,128)} %bitcast.103), kind=kLoop, calls=%fused_computation.198 | loop fusion | flops 10485760 | bytes 22020096 | tf_op jit(solution)/shard_map/sub | solution.py:105
  255.3 4.1 scatter_fusion.1
  259.5 1.6 mul.241
  261.2 1.3 collective-permute-start.12
  262.5 5.0 collective-permute-start.13
  267.5 5.2 %collective-permute-done.12 = f32[4,256,128]{2,1,0:T(8,128)S(1)} collective-permute-done((f32[4,256,128]{2,1,0:T(8,128)S(1)}, f32[4,256,128]{2,1,0:T(8,128)S(1)}, u32[]{:S(2)}, u32[]{:S(2)}) %collective-permute-start.12) | collective-permute-done | bytes 524320 | tf_op jit(solution)/shard_map/ppermute | solution.py:20
  274.4 3.1 select_maximum_fusion.2
  277.5 8.3 %fusion.43 = f32[8,256,128]{2,1,0:T(8,128)} fusion(f32[8,256,128]{2,1,0:T(8,128)} %bitcast.104, f32[8,256,128]{2,1,0:T(8,128)} %copy-done.7, f32[4,256,128]{2,1,0:T(8,128)} %copy-done.10, f32[4,256,128]{2,1,0:T(8,128)S(1)} %collective-permute-done.12, f32[16,264,136]{2,1,0:T(8,128)S(1)} %select_maximum_fusion.2, f32[8,256,128]{2,1,0:T(8,128)} %bitcast.108), kind=kLoop, calls=%fused_computation.168 | loop fusion | flops 10485760 | bytes 22020096 | tf_op jit(solution)/shard_map/sub | solution.py:105
  285.8 4.1 scatter_fusion.2
  289.9 1.6 mul.249
  291.7 1.3 collective-permute-start.14
  293.0 7.1 %collective-permute-start.15 = (f32[4,256,128]{2,1,0:T(8,128)S(1)}, f32[4,256,128]{2,1,0:T(8,128)S(1)}, u32[]{:S(2)}, u32[]{:S(2)}) collective-permute-start(f32[4,256,128]{2,1,0:T(8,128)S(1)} %get-tuple-element.64), channel_id=1, source_target_pairs={{0,1},{1,2},{2,3},{3,4},{4,5},{5,6},{6,7},{8,9},{9,10},{10,11},{11... | collective-permute-start | bytes 1572872 | tf_op jit(solution)/shard_map/ppermute | solution.py:19
  300.1 4.3 collective-permute-done.14
  304.5 1.5 collective-permute-done.15
  306.7 3.1 select_maximum_fusion
  309.8 8.3 %fusion.13 = f32[8,256,128]{2,1,0:T(8,128)} fusion(f32[8,256,128]{2,1,0:T(8,128)} %bitcast.109, f32[8,256,128]{2,1,0:T(8,128)} %copy-done.5, f32[4,256,128]{2,1,0:T(8,128)} %copy-done.11, f32[4,256,128]{2,1,0:T(8,128)S(1)} %collective-permute-done.14, f32[16,264,136]{2,1,0:T(8,128)S(1)} %select_maximum_fusion, f32[8,256,128]{2,1,0:T(8,128)} %bitcast.118), kind=kLoop, calls=%fused_computation.138 | loop fusion | flops 10485760 | bytes 22020096 | tf_op jit(solution)/shard_map/sub | solution.py:105
  318.1 4.1 scatter_fusion.3
  322.3 4.0 add_bitcast_fusion
  326.2 1.6 copy.16
  327.8 13.6 %all-to-all-start.1 = ((f32[1,8,256,128]{3,1,0,2:T(8,128)}), f32[1,8,256,128]{3,1,0,2:T(8,128)S(1)}, u32[]{:S(2)}, u32[]{:S(2)}) async-start(f32[1,8,256,128]{3,1,0,2:T(8,128)} %copy.16), calls=%async_computation.1 | async-start | bytes 2097152 | tf_op jit(solution)/shard_map/all_to_all | solution.py:110
  343.5 7.5 %all-to-all-done.1 = f32[1,8,256,128]{3,1,0,2:T(8,128)S(1)} async-done(((f32[1,8,256,128]{3,1,0,2:T(8,128)}), f32[1,8,256,128]{3,1,0,2:T(8,128)S(1)}, u32[]{:S(2)}, u32[]{:S(2)}) %all-to-all-start.1) | async-done | bytes 1048608 | tf_op jit(solution)/shard_map/all_to_all | solution.py:110
  350.9 2.6 broadcast_in_dim.48
  355.4 155.0 %all-reduce.11.cloned.1.call-done = f32[2,16,8,32,128]{4,3,2,1,0:T(8,128)} async-done(((f32[2,16,8,32,128]{4,3,2,1,0:T(8,128)}), f32[2,16,8,32,128]{4,3,2,1,0:T(8,128)}) %all-reduce.11.cloned.1.call-update) | async-done | bytes 4194320
  510.4 2.4 constant_dynamic-slice_fusion
  (68 shorter events, 19.7 us)
Async XLA Ops:
  6.5 64.1 %all-gather.2.cloned.1.call-start = ((), (), s32[]{:S(2)}) async-start(), calls=%async_computation.2 | async-start | bytes 4456448 | tf_op jit(solution)/shard_map/all_gather | solution.py:71
  7.3 71.6 %copy-start.13 = (f32[1,4,256]{2,1,0:T(4,128)S(1)}, f32[1,4,256]{2,1,0:T(4,128)}, u32[]{:S(2)}) copy-start(f32[1,4,256]{2,1,0:T(4,128)} %param.26) | copy-start | bytes 12292
  7.3 71.7 %copy-start.3 = (f32[1,8,256,128]{3,2,1,0:T(8,128)S(1)}, f32[1,8,256,128]{3,2,1,0:T(8,128)}, u32[]{:S(2)}) copy-start(f32[1,8,256,128]{3,2,1,0:T(8,128)} %param.19) | copy-start | bytes 3145732
  9.6 69.3 %collective-permute-start.2 = (f32[4,256,128]{2,1,0:T(8,128)}, f32[4,256,128]{2,1,0:T(8,128)}, u32[]{:S(2)}, u32[]{:S(2)}) collective-permute-start(f32[4,256,128]{2,1,0:T(8,128)} %get-tuple-element.76), channel_id=1, source_target_pairs={{1,0},{2,1},{3,2},{4,3},{5,4},{6,5},{7,6},{9,8},{10,9},{11,10},{12... | collective-permute-start | bytes 1572872 | tf_op jit(solution)/shard_map/ppermute | solution.py:20
  10.9 68.0 %collective-permute-start.3 = (f32[4,256,128]{2,1,0:T(8,128)}, f32[4,256,128]{2,1,0:T(8,128)}, u32[]{:S(2)}, u32[]{:S(2)}) collective-permute-start(f32[4,256,128]{2,1,0:T(8,128)} %get-tuple-element.75), channel_id=1, source_target_pairs={{0,1},{1,2},{2,3},{3,4},{4,5},{5,6},{6,7},{8,9},{9,10},{10,11},{11... | collective-permute-start | bytes 1572872 | tf_op jit(solution)/shard_map/ppermute | solution.py:19
  74.7 19.1 %all-to-all-start = ((f32[8,8,32,128]{3,2,1,0:T(8,128)}), f32[8,8,32,128]{3,2,1,0:T(8,128)S(1)}, u32[]{:S(2)}, u32[]{:S(2)}) async-start(f32[8,8,32,128]{3,2,1,0:T(8,128)} %select_select_fusion), calls=%async_computation | async-start | bytes 2097152 | tf_op jit(solution)/shard_map/all_to_all | solution.py:79
  93.9 25.2 %copy-start = (f32[1,8,8,32,128]{4,3,2,1,0:T(8,128)}, f32[1,8,8,32,128]{4,3,2,1,0:T(8,128)S(1)}, u32[]{:S(2)}) copy-start(f32[1,8,8,32,128]{4,3,2,1,0:T(8,128)S(1)} %copy.15) | copy-start | bytes 3145732
  111.7 17.7 %copy-start.12 = (s32[1,256]{1,0:T(1,128)S(1)}, s32[1,256]{1,0:T(1,128)}, u32[]{:S(2)}) copy-start(s32[1,256]{1,0:T(1,128)} %param.25) | copy-start | bytes 3076
  111.9 17.5 %copy-start.1 = (f32[262144]{0:T(1024)}, f32[262144]{0:T(1024)S(1)}, u32[]{:S(2)}) copy-start(f32[262144]{0:T(1024)S(1)} %fusion.255) | copy-start | bytes 3145732
  113.0 16.4 %collective-permute-start.4 = (f32[4,256,128]{2,1,0:T(8,128)}, f32[4,256,128]{2,1,0:T(8,128)}, u32[]{:S(2)}, u32[]{:S(2)}) collective-permute-start(f32[4,256,128]{2,1,0:T(8,128)} %bitcast.28), channel_id=1, source_target_pairs={{1,0},{2,1},{3,2},{4,3},{5,4},{6,5},{7,6},{9,8},{10,9},{11,10},{12... | collective-permute-start | bytes 1572872 | tf_op jit(solution)/shard_map/ppermute | solution.py:20
  114.3 15.1 %collective-permute-start.5 = (f32[4,256,128]{2,1,0:T(8,128)}, f32[4,256,128]{2,1,0:T(8,128)}, u32[]{:S(2)}, u32[]{:S(2)}) collective-permute-start(f32[4,256,128]{2,1,0:T(8,128)} %bitcast.29), channel_id=1, source_target_pairs={{0,1},{1,2},{2,3},{3,4},{4,5},{5,6},{6,7},{8,9},{9,10},{10,11},{11... | collective-permute-start | bytes 1572872 | tf_op jit(solution)/shard_map/ppermute | solution.py:19
  120.4 9.0 %copy-start.4 = (f32[8,256,128]{2,1,0:T(8,128)}, f32[8,256,128]{2,1,0:T(8,128)S(1)}, u32[]{:S(2)}) copy-start(f32[8,256,128]{2,1,0:T(8,128)S(1)} %bitcast_multiply_fusion) | copy-start | bytes 3145732
  123.3 27.0 %collective-permute-start = (f32[4,256,128]{2,1,0:T(8,128)}, f32[4,256,128]{2,1,0:T(8,128)}, u32[]{:S(2)}, u32[]{:S(2)}) collective-permute-start(f32[4,256,128]{2,1,0:T(8,128)} %get-tuple-element.77), channel_id=1, source_target_pairs={{1,0},{2,1},{3,2},{4,3},{5,4},{6,5},{7,6},{9,8},{10,9},{11,10},{12... | collective-permute-start | bytes 1572872 | tf_op jit(solution)/shard_map/ppermute | solution.py:20
  124.6 25.7 %collective-permute-start.1 = (f32[4,256,128]{2,1,0:T(8,128)}, f32[4,256,128]{2,1,0:T(8,128)}, u32[]{:S(2)}, u32[]{:S(2)}) collective-permute-start(f32[4,256,128]{2,1,0:T(8,128)} %get-tuple-element.78), channel_id=1, source_target_pairs={{0,1},{1,2},{2,3},{3,4},{4,5},{5,6},{6,7},{8,9},{9,10},{10,11},{11... | collective-permute-start | bytes 1572872 | tf_op jit(solution)/shard_map/ppermute | solution.py:19
  143.0 15.8 %copy-start.2 = (f32[262144]{0:T(1024)S(1)}, f32[262144]{0:T(1024)}, u32[]{:S(2)}) copy-start(f32[262144]{0:T(1024)} %fusion.256) | copy-start | bytes 3145732
  144.4 12.7 %collective-permute-start.6 = (f32[4,256,128]{2,1,0:T(8,128)S(1)}, f32[4,256,128]{2,1,0:T(8,128)S(1)}, u32[]{:S(2)}, u32[]{:S(2)}) collective-permute-start(f32[4,256,128]{2,1,0:T(8,128)S(1)} %bitcast.126), channel_id=1, source_target_pairs={{1,0},{2,1},{3,2},{4,3},{5,4},{6,5},{7,6},{9,8},{10,9},{11,10},{12... | collective-permute-start | bytes 1572872 | tf_op jit(solution)/shard_map/ppermute | solution.py:20
  145.7 12.3 %collective-permute-start.7 = (f32[4,256,128]{2,1,0:T(8,128)S(1)}, f32[4,256,128]{2,1,0:T(8,128)S(1)}, u32[]{:S(2)}, u32[]{:S(2)}) collective-permute-start(f32[4,256,128]{2,1,0:T(8,128)S(1)} %bitcast.125), channel_id=1, source_target_pairs={{0,1},{1,2},{2,3},{3,4},{4,5},{5,6},{6,7},{8,9},{9,10},{10,11},{11... | collective-permute-start | bytes 1572872 | tf_op jit(solution)/shard_map/ppermute | solution.py:19
  158.0 0.8 copy-start.8
  186.8 21.8 %collective-permute-start.8 = (f32[4,256,128]{2,1,0:T(8,128)}, f32[4,256,128]{2,1,0:T(8,128)S(1)}, u32[]{:S(2)}, u32[]{:S(2)}) collective-permute-start(f32[4,256,128]{2,1,0:T(8,128)} %bitcast.40), channel_id=1, source_target_pairs={{1,0},{2,1},{3,2},{4,3},{5,4},{6,5},{7,6},{9,8},{10,9},{11,10},{12... | collective-permute-start | bytes 1572872 | tf_op jit(solution)/shard_map/ppermute | solution.py:20
  188.1 20.6 %collective-permute-start.9 = (f32[4,256,128]{2,1,0:T(8,128)}, f32[4,256,128]{2,1,0:T(8,128)}, u32[]{:S(2)}, u32[]{:S(2)}) collective-permute-start(f32[4,256,128]{2,1,0:T(8,128)} %bitcast.41), channel_id=1, source_target_pairs={{0,1},{1,2},{2,3},{3,4},{4,5},{5,6},{6,7},{8,9},{9,10},{10,11},{11... | collective-permute-start | bytes 1572872 | tf_op jit(solution)/shard_map/ppermute | solution.py:19
  231.0 12.2 %copy-start.6 = (f32[8,256,128]{2,1,0:T(8,128)}, f32[8,256,128]{2,1,0:T(8,128)S(1)}, u32[]{:S(2)}) copy-start(f32[8,256,128]{2,1,0:T(8,128)S(1)} %mul.233) | copy-start | bytes 3145732
  231.1 11.2 %collective-permute-start.10 = (f32[4,256,128]{2,1,0:T(8,128)S(1)}, f32[4,256,128]{2,1,0:T(8,128)S(1)}, u32[]{:S(2)}, u32[]{:S(2)}) collective-permute-start(f32[4,256,128]{2,1,0:T(8,128)S(1)} %get-tuple-element.67), channel_id=1, source_target_pairs={{1,0},{2,1},{3,2},{4,3},{5,4},{6,5},{7,6},{9,8},{10,9},{11,10},{12... | collective-permute-start | bytes 1572872 | tf_op jit(solution)/shard_map/ppermute | solution.py:20
  232.4 10.8 %collective-permute-start.11 = (f32[4,256,128]{2,1,0:T(8,128)S(1)}, f32[4,256,128]{2,1,0:T(8,128)S(1)}, u32[]{:S(2)}, u32[]{:S(2)}) collective-permute-start(f32[4,256,128]{2,1,0:T(8,128)S(1)} %get-tuple-element.68), channel_id=1, source_target_pairs={{0,1},{1,2},{2,3},{3,4},{4,5},{5,6},{6,7},{8,9},{9,10},{10,11},{11... | collective-permute-start | bytes 1572872 | tf_op jit(solution)/shard_map/ppermute | solution.py:19
  243.2 0.8 copy-start.9
  261.1 12.5 %copy-start.7 = (f32[8,256,128]{2,1,0:T(8,128)}, f32[8,256,128]{2,1,0:T(8,128)S(1)}, u32[]{:S(2)}) copy-start(f32[8,256,128]{2,1,0:T(8,128)S(1)} %mul.241) | copy-start | bytes 3145732
  261.2 11.5 %collective-permute-start.12 = (f32[4,256,128]{2,1,0:T(8,128)S(1)}, f32[4,256,128]{2,1,0:T(8,128)S(1)}, u32[]{:S(2)}, u32[]{:S(2)}) collective-permute-start(f32[4,256,128]{2,1,0:T(8,128)S(1)} %get-tuple-element.65), channel_id=1, source_target_pairs={{1,0},{2,1},{3,2},{4,3},{5,4},{6,5},{7,6},{9,8},{10,9},{11,10},{12... | collective-permute-start | bytes 1572872 | tf_op jit(solution)/shard_map/ppermute | solution.py:20
  262.5 11.1 %collective-permute-start.13 = (f32[4,256,128]{2,1,0:T(8,128)S(1)}, f32[4,256,128]{2,1,0:T(8,128)S(1)}, u32[]{:S(2)}, u32[]{:S(2)}) collective-permute-start(f32[4,256,128]{2,1,0:T(8,128)S(1)} %get-tuple-element.66), channel_id=1, source_target_pairs={{0,1},{1,2},{2,3},{3,4},{4,5},{5,6},{6,7},{8,9},{9,10},{10,11},{11... | collective-permute-start | bytes 1572872 | tf_op jit(solution)/shard_map/ppermute | solution.py:19
  273.6 0.8 copy-start.10
  291.6 14.3 %copy-start.5 = (f32[8,256,128]{2,1,0:T(8,128)}, f32[8,256,128]{2,1,0:T(8,128)S(1)}, u32[]{:S(2)}) copy-start(f32[8,256,128]{2,1,0:T(8,128)S(1)} %mul.249) | copy-start | bytes 3145732
  291.7 12.8 %collective-permute-start.14 = (f32[4,256,128]{2,1,0:T(8,128)S(1)}, f32[4,256,128]{2,1,0:T(8,128)S(1)}, u32[]{:S(2)}, u32[]{:S(2)}) collective-permute-start(f32[4,256,128]{2,1,0:T(8,128)S(1)} %get-tuple-element.63), channel_id=1, source_target_pairs={{1,0},{2,1},{3,2},{4,3},{5,4},{6,5},{7,6},{9,8},{10,9},{11,10},{12... | collective-permute-start | bytes 1572872 | tf_op jit(solution)/shard_map/ppermute | solution.py:20
  293.0 13.0 %collective-permute-start.15 = (f32[4,256,128]{2,1,0:T(8,128)S(1)}, f32[4,256,128]{2,1,0:T(8,128)S(1)}, u32[]{:S(2)}, u32[]{:S(2)}) collective-permute-start(f32[4,256,128]{2,1,0:T(8,128)S(1)} %get-tuple-element.64), channel_id=1, source_target_pairs={{0,1},{1,2},{2,3},{3,4},{4,5},{5,6},{6,7},{8,9},{9,10},{10,11},{11... | collective-permute-start | bytes 1572872 | tf_op jit(solution)/shard_map/ppermute | solution.py:19
  305.9 0.8 copy-start.11
  327.8 23.1 %all-to-all-start.1 = ((f32[1,8,256,128]{3,1,0,2:T(8,128)}), f32[1,8,256,128]{3,1,0,2:T(8,128)S(1)}, u32[]{:S(2)}, u32[]{:S(2)}) async-start(f32[1,8,256,128]{3,1,0,2:T(8,128)} %copy.16), calls=%async_computation.1 | async-start | bytes 2097152 | tf_op jit(solution)/shard_map/all_to_all | solution.py:110
  341.5 168.9 %all-reduce.11.cloned.1.call-start = ((), (), s32[]{:S(2)}) async-start(), calls=%async_computation.3 | async-start | bytes 8388608
  350.9 3.8 copy-start.14
Sparse Core Ops, SparseCore 0:
  9.9 60.7 all-gather.1
  354.8 155.5 all-reduce.10
where the time goes:
time: 529 us; the launch traced here: 520 us
  waiting for transfers between devices  242 us (46%)
  other arithmetic  151 us (29%)
  starting transfers between devices  70.2 us (13%)
  local copies, waits for them, and re-layouts  37.2 us (7%)
  between operations  19.5 us (4%)
    unnamed x3, waiting for transfers between devices  156 us
    add x4, other arithmetic, per_device(): next_wave = 2.0 * current - earlier + courant * lap_now  54.8 us
    all_gather x1, waiting for transfers between devices, per_device(): piece = lax.all_gather(courant_squared, 'shot', axis=1, tiled=True)  45.9 us
    ppermute x8, starting transfers between devices, extended(): before = lax.ppermute(last, axis, up)  42.1 us
    sub x4, other arithmetic, per_device(): adjoint = 2.0 * adj_newer + laplace(courant * adj_newer) - adj_older  33.2 us
    concatenate x8, other arithmetic, extended(): x = jnp.concatenate([before, x, after], axis=dim)  28.2 us
    ppermute x8, waiting for transfers between devices, extended(): after = lax.ppermute(first, axis, down)  18.6 us
    scatter-add x4, other arithmetic, per_device(): adjoint = adjoint.reshape(-1).at[recv_local].add(misfit).reshape(shape)  16.5 us
  transfers between devices with their start and end apart: 20, of which 12 were waited for; matrix products, arithmetic and copies ran while one was open for 10% of the time, Pallas kernels for 0%

commit v1 on v0

v1 whole, which is shorter than its diff:
```python
import functools

import jax
import jax.numpy as jnp
import ml_dtypes
import numpy as np
from jax import lax
from jax.experimental import pallas as pl
from jax.experimental.pallas import tpu as pltpu
from jax.sharding import PartitionSpec as P

STEPS = 4
STENCIL = (-205.0 / 72.0, 8.0 / 5.0, -1.0 / 5.0, 8.0 / 315.0, -1.0 / 560.0)
F32 = jnp.float32
BF16 = jnp.bfloat16
SMEM = pl.BlockSpec(memory_space=pltpu.SMEM)
VMEM = pl.BlockSpec(memory_space=pltpu.VMEM)
NX, NYL, NZ = 64, 32, 128
GROUP = 8
PAD = 4
ROW0 = 8
ROWS = 48


def depth_operator():
    band = np.zeros((NZ, NZ), np.float32)
    for i in range(NZ):
        band[i, i] = np.float32(3.0 * STENCIL[0])
        for k in range(1, 5):
            for j in (i - k, i + k):
                if 0 <= j < NZ:
                    band[j, i] = np.float32(STENCIL[k])
    high = band.astype(ml_dtypes.bfloat16)
    low = (band - high.astype(np.float32)).astype(ml_dtypes.bfloat16)
    zero = np.zeros_like(high)
    return np.block([[high, low], [high, zero]])


def fill_edges(ext, halo_lo, halo_hi):
    zeros = jnp.zeros((PAD, ROWS, NZ), F32)
    ext[0:PAD] = zeros
    ext[PAD + NX : 2 * PAD + NX] = zeros

    def body(t, carry):
        lo = halo_lo[t]
        hi = halo_hi[t]
        for half in range(2):
            x = PAD + 2 * t + half
            ext[x, ROW0 - 4 : ROW0, :] = lo[4 * half : 4 * half + 4]
            ext[x, ROW0 + NYL : ROW0 + NYL + 4, :] = hi[4 * half : 4 * half + 4]
        return carry

    lax.fori_loop(0, NX // 2, body, 0, unroll=4)


def laplace_group(ext, oper, g, emit):
    base = PAD + g * GROUP
    own = ext[pl.ds(base, GROUP), ROW0 : ROW0 + NYL, :].reshape(GROUP * NYL, NZ)
    high = own.astype(BF16)
    low = (own - high.astype(F32)).astype(BF16)
    prod = jnp.dot(jnp.concatenate([high, low], axis=1), oper[...], preferred_element_type=F32)
    depth = prod[:, :NZ] + prod[:, NZ:]
    depth = depth.reshape(GROUP, NYL, NZ)
    for j in range(NYL // 8):
        r0 = ROW0 + 8 * j
        col = [ext[base - PAD + i, r0 : r0 + 8, :] for i in range(GROUP + 2 * PAD)]
        for xi in range(GROUP):
            acc = depth[xi, 8 * j : 8 * j + 8, :]
            for k in range(1, 5):
                beside = (
                    col[xi + PAD + k]
                    + col[xi + PAD - k]
                    + (
                        ext[base + xi, r0 + k : r0 + k + 8, :]
                        + ext[base + xi, r0 - k : r0 - k + 8, :]
                    )
                )
                acc = acc + STENCIL[k] * beside
            emit(xi, j, acc)


def send_rows(send_lo, send_hi, read):
    def body(t, carry):
        for half in range(2):
            send_lo[t, 4 * half : 4 * half + 4, :] = read(2 * t + half, 0)
            send_hi[t, 4 * half : 4 * half + 4, :] = read(2 * t + half, NYL - 4)
        return carry

    lax.fori_loop(0, NX // 2, body, 0, unroll=4)


def forward_kernel(packed, spots, amount, now, prev, r2, halo_lo, halo_hi, oper, lap, new, send_lo, send_hi, ext):
    first = spots[0]

    def plane(ref, which, g, xi):
        return ref[g, which, xi] if packed else ref[g * GROUP + xi]

    def copy(g, carry):
        for xi in range(GROUP):
            ext[PAD + g * GROUP + xi, ROW0 : ROW0 + NYL, :] = plane(now, 0, g, xi)
        return carry

    lax.fori_loop(0, NX // GROUP, copy, 0)
    fill_edges(ext, halo_lo, halo_hi)

    def body(g, carry):
        slot = lax.rem(first + g, GROUP)

        def emit(xi, j, value):
            rows = slice(8 * j, 8 * j + 8)
            x = g * GROUP + xi
            lap[x, rows, :] = value
            here = ext[PAD + x, ROW0 + 8 * j : ROW0 + 8 * j + 8, :]
            old = prev[g, 1, xi, rows, :] if packed else prev[x, rows, :]
            new[x, rows, :] = 2.0 * here - old + r2[slot, xi, rows, :] * value

        laplace_group(ext, oper, g, emit)
        return carry

    lax.fori_loop(0, NX // GROUP, body, 0)

    @pl.when(spots[1] == 1)
    def _():
        x, y, z = spots[2], spots[3], spots[4]
        lanes = lax.broadcasted_iota(jnp.int32, (1, NZ), 1)
        row = new[x, pl.ds(y, 1), :]
        new[x, pl.ds(y, 1), :] = row + jnp.where(lanes == z, amount[0], 0.0)

    send_rows(send_lo, send_hi, lambda x, r: new[x, r : r + 4, :])


def edge_kernel(packed, weighted, spots, now, r2, send_lo, send_hi):
    first = spots[0]

    def read(x, r):
        g, xi = x // GROUP, lax.rem(x, GROUP)
        value = now[g, 0, xi, r : r + 4, :]
        if weighted:
            value = value * r2[lax.rem(first + g, GROUP), xi, r : r + 4, :]
        return value

    send_rows(send_lo, send_hi, read)


def adjoint_kernel(
    packed, begin, last, spots, late, later, r2, halo_lo, halo_hi, oper, count, data, wave, lap, *rest
):
    rest = list(rest)
    total_in = None if begin else rest.pop(0)
    if last:
        total, ext = rest
        new = send_lo = send_hi = None
    else:
        total, new, send_lo, send_hi, ext = rest
    first = spots[0]

    def load(ref, which, g, xi, rows):
        return ref[g, which, xi, rows, :] if packed == 2 or (packed == 1 and which == 1) else ref[g * GROUP + xi, rows, :]

    every = slice(0, NYL)

    def copy(g, carry):
        slot = lax.rem(first + g, GROUP)
        for xi in range(GROUP):
            ext[PAD + g * GROUP + xi, ROW0 : ROW0 + NYL, :] = load(late, 0, g, xi, every) * r2[slot, xi]
        return carry

    lax.fori_loop(0, NX // GROUP, copy, 0)
    fill_edges(ext, halo_lo, halo_hi)

    def body(g, carry):
        slot = lax.rem(first + g, GROUP)

        def emit(xi, j, value):
            rows = slice(8 * j, 8 * j + 8)
            x = g * GROUP + xi
            mu = 2.0 * load(late, 0, g, xi, rows) + value - load(later, 1, g, xi, rows)
            mu = mu + (count[x, rows, :] * wave[x, rows, :] - data[x, rows, :])
            part = mu * lap[x, rows, :]
            if total_in is not None:
                part = part + total_in[x, rows, :]
            if last:
                total[slot, xi, rows, :] = part
            else:
                total[x, rows, :] = part
                new[x, rows, :] = mu

        laplace_group(ext, oper, g, emit)
        return carry

    lax.fori_loop(0, NX // GROUP, body, 0)
    if not last:

        def read(x, r):
            g, xi = x // GROUP, lax.rem(x, GROUP)
            return new[x, r : r + 4, :] * r2[lax.rem(first + g, GROUP), xi, r : r + 4, :]

        send_rows(send_lo, send_hi, read)


def receivers_kernel(cells, mine, observed, count, *datas):
    zeros = jnp.zeros((NYL, NZ), F32)

    def clear(x, carry):
        count[x] = zeros
        for d in datas:
            d[x] = zeros
        return carry

    lax.fori_loop(0, NX, clear, 0)
    lanes = lax.broadcasted_iota(jnp.int32, (1, NZ), 1)

    def body(r, carry):
        @pl.when(mine[r] == 1)
        def _():
            cell = cells[r]
            x = cell // (256 * NZ)
            y = lax.rem(cell // NZ, NYL)
            hit = lanes == lax.rem(cell, NZ)
            count[x, pl.ds(y, 1), :] = count[x, pl.ds(y, 1), :] + jnp.where(hit, 1.0, 0.0)
            for n, d in enumerate(datas):
                d[x, pl.ds(y, 1), :] = d[x, pl.ds(y, 1), :] + jnp.where(hit, observed[n, r], 0.0)

        return carry

    lax.fori_loop(0, cells.shape[0], body, 0)


def bins_kernel(slots, half, recv, keep, give):
    zeros = jnp.zeros((GROUP, NYL, NZ), F32)
    for i in range(2):
        keep[i] = zeros
        give[i] = zeros
    mine = half[0]
    for t in range(GROUP):
        m = slots[t]
        i = m // 2

        @pl.when(lax.rem(m, 2) == mine)
        def _():
            keep[i] = keep[i] + recv[t]

        @pl.when(lax.rem(m, 2) != mine)
        def _():
            give[i] = give[i] + recv[t]


FIELD = jax.ShapeDtypeStruct((NX, NYL, NZ), F32)
EDGE = jax.ShapeDtypeStruct((NX // 2, 8, NZ), F32)
EXT = pltpu.VMEM((NX + 2 * PAD, ROWS, NZ), F32)
PARAMS = pltpu.CompilerParams(vmem_limit_bytes=48 * 1024 * 1024)


def call(kernel, specs, outs, scratch=(), flops=0, moved=0):
    return pl.pallas_call(
        kernel,
        in_specs=specs,
        out_specs=[VMEM] * len(outs),
        out_shape=outs,
        scratch_shapes=list(scratch),
        compiler_params=PARAMS,
        cost_estimate=pl.CostEstimate(flops=flops, bytes_accessed=moved, transcendentals=0),
    )


def per_device(
    courant_squared,
    wave_now,
    wave_prev,
    adj_late,
    adj_later,
    wavelet,
    sources,
    receivers,
    observed,
    apertures,
):
    me = lax.axis_index("shot")
    part = lax.axis_index("sub")
    half, clas = me // 8, me % 8
    starts = apertures[:, 0]
    first = starts[me]
    oper = jnp.asarray(depth_operator())
    up = [(i, i + 1) for i in range(7)]
    down = [(i + 1, i) for i in range(7)]
    across = [(i, (i + 8) % 16) for i in range(16)]
    halves = [list(range(8)), list(range(8, 16))]

    def edges(lo, hi):
        return lax.ppermute(hi, "sub", up), lax.ppermute(lo, "sub", down)

    def turn(a, b):
        both = jnp.stack([f[0].reshape(GROUP, 8, NYL, NZ).transpose(1, 0, 2, 3) for f in (a, b)], axis=1)
        return lax.all_to_all(both, "sub", 0, 0, tiled=True)

    piece = courant_squared[:, 0]
    other = lax.ppermute(piece, "shot", across)
    mine_first = half == 0
    cand = jnp.stack(
        [
            jnp.where(mine_first, piece[0], other[0]),
            jnp.where(mine_first, other[0], piece[0]),
            jnp.where(mine_first, piece[1], other[1]),
            jnp.where(mine_first, other[1], piece[1]),
        ]
    )
    group_starts = lax.dynamic_slice(starts, (half * 8,), (8,))
    slots = (group_starts + (clas - group_starts) % 8) // 8
    r2 = lax.all_to_all(jnp.take(cand, slots, axis=0), "shot", 0, 0, axis_index_groups=halves, tiled=True)

    waves = turn(wave_now, wave_prev)
    adjs = turn(adj_late, adj_later)

    cell = sources[0]
    row = (cell // NZ) % 256
    spots = jnp.stack([first % 8, (row // NYL == part).astype(jnp.int32), cell // (256 * NZ), row % NYL, cell % NZ])
    cells = receivers[0]
    mine = ((cells // NZ) % 256 // NYL == part).astype(jnp.int32)
    count, *datas = call(receivers_kernel, [SMEM] * 3, [FIELD] * 5, moved=6 << 20)(cells, mine, observed[0])

    send = call(functools.partial(edge_kernel, True, False), [SMEM, VMEM, VMEM], [EDGE] * 2, moved=1 << 20)(spots, waves, r2)
    laps, fields = [], []
    now, prev = waves, waves
    for step in range(STEPS):
        halo = edges(*send)
        if step == 1:
            prev = waves[:, 0].reshape(NX, NYL, NZ)
        lap, new, *send = call(
            functools.partial(forward_kernel, step == 0),
            [SMEM, SMEM] + [VMEM] * 6,
            [FIELD, FIELD, EDGE, EDGE],
            [EXT],
            flops=10 << 20,
            moved=6 << 20,
        )(spots, wavelet[0, step : step + 1], now, prev, r2, *halo, oper)
        laps.append(lap)
        fields.append(new)
        now, prev = new, now

    send = call(functools.partial(edge_kernel, True, True), [SMEM, VMEM, VMEM], [EDGE] * 2, moved=1 << 20)(spots, adjs, r2)
    late, later = adjs, adjs
    total = None
    for step in range(STEPS, 0, -1):
        halo = edges(*send)
        begin, last = step == STEPS, step == 1
        if step == STEPS - 1:
            later = adjs[:, 0].reshape(NX, NYL, NZ)
        outs = [jax.ShapeDtypeStruct((8, GROUP, NYL, NZ), F32)] if last else [FIELD, FIELD, EDGE, EDGE]
        args = [spots, late, later, r2, *halo, oper, count, datas[step - 1], fields[step - 1], laps[step - 1]]
        if not begin:
            args.append(total)
        total, *more = call(
            functools.partial(adjoint_kernel, 2 if begin else 0, begin, last),
            [SMEM] + [VMEM] * (len(args) - 1),
            outs,
            [EXT],
            flops=10 << 20,
            moved=8 << 20,
        )(*args)
        if not last:
            late, later = more[0], late
            send = more[1:]

    recv = lax.all_to_all(total, "shot", 0, 0, axis_index_groups=halves, tiled=True)
    owned = jax.ShapeDtypeStruct((2, GROUP, NYL, NZ), F32)
    keep, give = call(bins_kernel, [SMEM, SMEM, VMEM], [owned, owned], moved=2 << 20)(slots, half[None], recv)
    result = keep + lax.ppermute(give, "shot", across)
    return result[:, None]


def solution(mesh):
    in_specs = (
        P(None, "shot", None, "sub", None),
        P("shot", "sub", None, None),
        P("shot", "sub", None, None),
        P("shot", "sub", None, None),
        P("shot", "sub", None, None),
        P("shot", None),
        P("shot"),
        P("shot", None),
        P("shot", None, None),
        P(),
    )
    out_specs = P(None, "shot", None, "sub", None)
    return jax.shard_map(
        per_device, mesh=mesh, in_specs=in_specs, out_specs=out_specs, check_vma=False
    )
```

time: 529 us -> 253 us (0.48); the launches traced: 520 us -> 250 us
  other arithmetic: 151 us -> 6.37 us
  waiting for transfers between devices: 242 us -> 98.6 us
  Pallas kernels: 0 us -> 45.2 us
  local copies, waits for them, and re-layouts: 37.2 us -> 17.7 us
  between operations: 19.5 us -> 3.2 us
  starting transfers between devices: 70.2 us -> 79.4 us
    unnamed x3 -> x0, waiting for transfers between devices: 156 us -> none
    add x4 -> x0, other arithmetic: 54.8 us -> none  [per_device(): next_wave = 2.0 * current - earlier + courant * lap_now]
    all_gather x1 -> x0, waiting for transfers between devices: 45.9 us -> none  [per_device(): piece = lax.all_gather(courant_squared, 'shot', axis=1, tiled=True)]
    pallas_call x0 -> x12, Pallas kernels: none -> 45.2 us  [the longest x4 22.3 us: per_device(): call(functools.partial(adjoint_kernel, 2 if begin else 0, begin, last), [...]
    all_to_all x2 -> x4, waiting for transfers between devices: 17.8 us -> 51.1 us  [the longest x2 22.8 us: turn(): return lax.all_to_all(both, 'sub', 0, 0, tiled=True)]
    sub x4 -> x0, other arithmetic: 33.2 us -> none  [per_device(): adjoint = 2.0 * adj_newer + laplace(courant * adj_newer) - adj_older]
    concatenate x8 -> x0, other arithmetic: 28.2 us -> none  [extended(): x = jnp.concatenate([before, x, after], axis=dim)]
    ppermute x16 -> x18, waiting for transfers between devices: 22.8 us -> 47.5 us  [the longest x16 36.6 us: edges(): return (lax.ppermute(hi, 'sub', up), lax.ppermute(lo, 'sub', down))]
  transfers between devices with their start and end apart: 20 -> 22, of which waited for: 12 -> 15; matrix products, arithmetic and copies ran while one was open for 10% -> 3% of each run, Pallas kernels for 0% -> 9%
where the time goes in v1:
time: 253 us; the launch traced here: 250 us
  waiting for transfers between devices  98.6 us (39%)
  starting transfers between devices  79.4 us (31%)
  Pallas kernels  45.2 us (18%)
  local copies, waits for them, and re-layouts  17.7 us (7%)
  other arithmetic  6.37 us (3%)
  between operations  3.2 us (1%)
    ppermute x16, starting transfers between devices, edges(): return (lax.ppermute(hi, 'sub', up), lax.ppermute(lo, 'sub', down))  45.5 us
    ppermute x16, waiting for transfers between devices, edges(): return (lax.ppermute(hi, 'sub', up), lax.ppermute(lo, 'sub', down))  36.6 us
    all_to_all x2, waiting for transfers between devices, turn(): return lax.all_to_all(both, 'sub', 0, 0, tiled=True)  22.8 us
    pallas_call x4, Pallas kernels, per_device(): call(functools.partial(adjoint_kernel, 2 if begin else 0, begin, last), [...  22.3 us
    all_to_all x1, waiting for transfers between devices, per_device(): lax.all_to_all(total, 'shot', 0, 0, axis_index_groups=halves, tiled=True)  15 us
    pallas_call x4, Pallas kernels, per_device(): call(functools.partial(forward_kernel, step == 0), [SMEM, SMEM] + [VMEM]...  14.9 us
    all_to_all x1, waiting for transfers between devices, per_device(): lax.all_to_all(jnp.take(cand, slots, axis=0), 'shot', 0, 0, axis_index_gr...  13.3 us
    unnamed x56, local copies, waits for them, and re-layouts  13 us
  transfers between devices with their start and end apart: 22, of which 15 were waited for; matrix products, arithmetic and copies ran while one was open for 3% of the time, Pallas kernels for 9%

profile of v1, /device:TPU:1, one launch (start us, length us, event | category | flops | bytes accessed | tf_op | source)
XLA Modules:
  0.0 250.4 jit_solution(7810252571445923467)
XLA Ops:
  0.0 3.6 %collective-permute-start = (f32[2,8,32,128]{3,2,1,0:T(8,128)}, f32[2,8,32,128]{3,2,1,0:T(8,128)S(1)}, u32[]{:S(2)}, u32[]{:S(2)}) collective-permute-start(f32[2,8,32,128]{3,2,1,0:T(8,128)} %bitcast.70), channel_id=1, source_target_pairs={{0,64},{8,72},{16,80},{24,88},{32,96},{40,104},{48,112},{56,120},{... | collective-permute-start | bytes 786440 | tf_op jit(solution)/shard_map/ppermute | solution.py:297
  3.6 0.7 slice.39
  4.4 5.0 %collective-permute-done = f32[2,8,32,128]{3,2,1,0:T(8,128)S(1)} collective-permute-done((f32[2,8,32,128]{3,2,1,0:T(8,128)}, f32[2,8,32,128]{3,2,1,0:T(8,128)S(1)}, u32[]{:S(2)}, u32[]{:S(2)}) %collective-permute-start) | collective-permute-done | bytes 262176 | tf_op jit(solution)/shard_map/ppermute | solution.py:297
  9.3 1.0 bitcast_select_fusion.3
  11.0 1.2 broadcast_select_fusion
  12.3 6.5 %all-to-all-start.1 = ((f32[8,8,32,128]{3,2,1,0:T(8,128)}), f32[8,8,32,128]{3,2,1,0:T(8,128)S(1)}, u32[]{:S(2)}, u32[]{:S(2)}) async-start(f32[8,8,32,128]{3,2,1,0:T(8,128)} %broadcast_select_fusion), calls=%async_computation.1 | async-start | bytes 2097152 | tf_op jit(solution)/shard_map/all_to_all | solution.py:309
  19.0 1.6 pad_maximum_fusion.1
  20.6 13.3 %all-to-all-done.1.r2 = f32[8,8,32,128]{3,2,1,0:T(8,128)S(1)} async-done(((f32[8,8,32,128]{3,2,1,0:T(8,128)}), f32[8,8,32,128]{3,2,1,0:T(8,128)S(1)}, u32[]{:S(2)}, u32[]{:S(2)}) %all-to-all-start.1) | async-done | bytes 1048608 | tf_op jit(solution)/shard_map/all_to_all | solution.py:309
  33.9 6.0 %all-to-all-start.2 = ((f32[8,2,8,32,128]{4,3,2,1,0:T(8,128)}), f32[8,2,8,32,128]{4,3,2,1,0:T(8,128)S(1)}, u32[]{:S(2)}, u32[]{:S(2)}) async-start(f32[8,2,8,32,128]{4,3,2,1,0:T(8,128)} %pad_maximum_fusion.1), calls=%async_computation.2 | async-start | bytes 4194304 | tf_op jit(solution)/shard_map/all_to_all | solution.py:294
  39.9 1.7 copy_bitcast_fusion.2
  41.6 1.6 pad_maximum_fusion
  43.2 22.8 %all-to-all-done.2.now.prev = f32[8,2,8,32,128]{4,3,2,1,0:T(8,128)S(1)} async-done(((f32[8,2,8,32,128]{4,3,2,1,0:T(8,128)}), f32[8,2,8,32,128]{4,3,2,1,0:T(8,128)S(1)}, u32[]{:S(2)}, u32[]{:S(2)}) %all-to-all-start.2) | async-done | bytes 2097184 | tf_op jit(solution)/shard_map/all_to_all | solution.py:294
  66.0 1.3 copy-done.2
  67.3 3.7 %all-to-all-start = ((f32[8,2,8,32,128]{4,3,2,1,0:T(8,128)}), f32[8,2,8,32,128]{4,3,2,1,0:T(8,128)S(1)}, u32[]{:S(2)}, u32[]{:S(2)}) async-start(f32[8,2,8,32,128]{4,3,2,1,0:T(8,128)} %pad_maximum_fusion), calls=%async_computation | async-start | bytes 4194304 | tf_op jit(solution)/shard_map/all_to_all | solution.py:294
  74.4 1.6 copy-done.3
  76.0 0.9 shard_map.111
  77.0 3.4 %collective-permute-start.3 = (f32[32,8,128]{2,1,0:T(8,128)S(1)}, f32[32,8,128]{2,1,0:T(8,128)S(1)}, u32[]{:S(2)}, u32[]{:S(2)}) collective-permute-start(f32[32,8,128]{2,1,0:T(8,128)S(1)} %get-tuple-element.46), channel_id=1, source_target_pairs={{0,1},{1,2},{2,3},{3,4},{4,5},{5,6},{6,7},{8,9},{9,10},{10,11},{11... | collective-permute-start | bytes 393224 | tf_op jit(solution)/shard_map/ppermute | solution.py:290
  80.3 1.3 collective-permute-start.4
  82.3 13.9 %collective-permute-done.3.halo_lo = f32[32,8,128]{2,1,0:T(8,128)S(1)} collective-permute-done((f32[32,8,128]{2,1,0:T(8,128)S(1)}, f32[32,8,128]{2,1,0:T(8,128)S(1)}, u32[]{:S(2)}, u32[]{:S(2)}) %collective-permute-start.3) | collective-permute-done | bytes 131104 | tf_op jit(solution)/shard_map/ppermute | solution.py:290
  96.1 2.1 collective-permute-done.4.halo_hi
  98.2 3.4 %shard_map.112 = (f32[64,32,128]{2,1,0:T(8,128)S(1)}, f32[64,32,128]{2,1,0:T(8,128)S(1)}, f32[32,8,128]{2,1,0:T(8,128)S(1)}, f32[32,8,128]{2,1,0:T(8,128)S(1)}) custom-call(s32[5]{0:T(128)S(1)} %stack.52.spots, f32[1]{0:T(128)} %bitcast.25.amount, f32[8,2,8,32,128]{4,3,2,1,0:T(8,128)S(1)} %copy-done.3, f32[8,2,8,32,128]{4,3,2,1,0:T(8,128)S(1)} %copy-done.3, ...), custom_call_target="tpu_custom_call" | custom-call | flops 10485760 | bytes 6291456 | tf_op jit(solution)/shard_map/pallas_call | solution.py:328
  101.6 1.0 copy-done.12
  102.6 3.1 %collective-permute-start.5 = (f32[32,8,128]{2,1,0:T(8,128)S(1)}, f32[32,8,128]{2,1,0:T(8,128)S(1)}, u32[]{:S(2)}, u32[]{:S(2)}) collective-permute-start(f32[32,8,128]{2,1,0:T(8,128)S(1)} %get-tuple-element.49), channel_id=1, source_target_pairs={{0,1},{1,2},{2,3},{3,4},{4,5},{5,6},{6,7},{8,9},{9,10},{10,11},{11... | collective-permute-start | bytes 393224 | tf_op jit(solution)/shard_map/ppermute | solution.py:290
  105.7 1.3 collective-permute-start.6
  107.6 3.8 %collective-permute-done.6.halo_hi = f32[32,8,128]{2,1,0:T(8,128)S(1)} collective-permute-done((f32[32,8,128]{2,1,0:T(8,128)S(1)}, f32[32,8,128]{2,1,0:T(8,128)S(1)}, u32[]{:S(2)}, u32[]{:S(2)}) %collective-permute-start.6) | collective-permute-done | bytes 131104 | tf_op jit(solution)/shard_map/ppermute | solution.py:290
  111.4 4.0 %shard_map.113 = (f32[64,32,128]{2,1,0:T(8,128)S(1)}, f32[64,32,128]{2,1,0:T(8,128)S(1)}, f32[32,8,128]{2,1,0:T(8,128)}, f32[32,8,128]{2,1,0:T(8,128)}) custom-call(s32[5]{0:T(128)S(1)} %stack.52.spots, f32[1]{0:T(128)} %bitcast.24.amount, f32[64,32,128]{2,1,0:T(8,128)S(1)} %get-tuple-element.48.now.prev.wave, f32[64,32,128]{2,1,0:T(8,128)S(1)} %bitcast.62, ...), custom_call_target="tpu_custom_call" | custom-call | flops 10485760 | bytes 6291456 | tf_op jit(solution)/shard_map/pallas_call | solution.py:328
  115.4 1.0 copy-done.8
  116.4 1.0 copy-done.13
  117.4 2.8 %collective-permute-start.7 = (f32[32,8,128]{2,1,0:T(8,128)}, f32[32,8,128]{2,1,0:T(8,128)S(1)}, u32[]{:S(2)}, u32[]{:S(2)}) collective-permute-start(f32[32,8,128]{2,1,0:T(8,128)} %get-tuple-element.52), channel_id=1, source_target_pairs={{0,1},{1,2},{2,3},{3,4},{4,5},{5,6},{6,7},{8,9},{9,10},{10,11},{11... | collective-permute-start | bytes 393224 | tf_op jit(solution)/shard_map/ppermute | solution.py:290
  120.3 1.3 collective-permute-start.8
  121.6 1.1 shard_map.109
  122.8 4.9 %collective-permute-start.1 = (f32[32,8,128]{2,1,0:T(8,128)S(1)}, f32[32,8,128]{2,1,0:T(8,128)S(1)}, u32[]{:S(2)}, u32[]{:S(2)}) collective-permute-start(f32[32,8,128]{2,1,0:T(8,128)S(1)} %get-tuple-element.42), channel_id=1, source_target_pairs={{0,1},{1,2},{2,3},{3,4},{4,5},{5,6},{6,7},{8,9},{9,10},{10,11},{11... | collective-permute-start | bytes 393224 | tf_op jit(solution)/shard_map/ppermute | solution.py:290
  127.7 1.3 collective-permute-start.2
  129.0 3.5 %shard_map.114 = (f32[64,32,128]{2,1,0:T(8,128)S(1)}, f32[64,32,128]{2,1,0:T(8,128)S(1)}, f32[32,8,128]{2,1,0:T(8,128)S(1)}, f32[32,8,128]{2,1,0:T(8,128)S(1)}) custom-call(s32[5]{0:T(128)S(1)} %stack.52.spots, f32[1]{0:T(128)} %bitcast.23.amount, f32[64,32,128]{2,1,0:T(8,128)S(1)} %copy-done.9, f32[64,32,128]{2,1,0:T(8,128)S(1)} %copy-done.7, ...), custom_call_target="tpu_custom_call" | custom-call | flops 10485760 | bytes 6291456 | tf_op jit(solution)/shard_map/pallas_call | solution.py:328
  132.6 1.0 copy-done.16
  133.6 6.1 %collective-permute-start.9 = (f32[32,8,128]{2,1,0:T(8,128)S(1)}, f32[32,8,128]{2,1,0:T(8,128)S(1)}, u32[]{:S(2)}, u32[]{:S(2)}) collective-permute-start(f32[32,8,128]{2,1,0:T(8,128)S(1)} %get-tuple-element.55), channel_id=1, source_target_pairs={{0,1},{1,2},{2,3},{3,4},{4,5},{5,6},{6,7},{8,9},{9,10},{10,11},{11... | collective-permute-start | bytes 393224 | tf_op jit(solution)/shard_map/ppermute | solution.py:290
  139.7 1.3 collective-permute-start.10
  141.0 5.1 %shard_map.110 = (f32[64,32,128]{2,1,0:T(8,128)S(1)}, f32[64,32,128]{2,1,0:T(8,128)S(1)}, f32[64,32,128]{2,1,0:T(8,128)S(1)}, f32[64,32,128]{2,1,0:T(8,128)S(1)}, f32[64,32,128]{2,1,0:T(8,128)S(1)}) custom-call(s32[256]{0:T(256)S(1)} %bitcast.65, s32[256]{0:T(256)S(1)} %compare_convert_fusion.mine, f32[4,256]{1,0:T(4,128)S(1)} %bitcast.63), custom_call_target="tpu_custom_call" | custom-call | bytes 6291456 | tf_op jit(solution)/shard_map/pallas_call | solution.py:319
  146.2 1.0 copy-done.15
  147.1 1.0 copy-done.17
  148.2 4.0 %shard_map.115 = (f32[64,32,128]{2,1,0:T(8,128)S(1)}, f32[64,32,128]{2,1,0:T(8,128)S(1)}, f32[32,8,128]{2,1,0:T(8,128)}, f32[32,8,128]{2,1,0:T(8,128)}) custom-call(s32[5]{0:T(128)S(1)} %stack.52.spots, f32[1]{0:T(128)} %bitcast.22.amount, f32[64,32,128]{2,1,0:T(8,128)S(1)} %get-tuple-element.54.now.wave, f32[64,32,128]{2,1,0:T(8,128)S(1)} %copy-done.9, ...), custom_call_target="tpu_custom_call" | custom-call | flops 10485760 | bytes 6291456 | tf_op jit(solution)/shard_map/pallas_call | solution.py:328
  152.2 1.0 copy-done.21
  153.2 1.0 copy-done.22
  154.2 6.0 %shard_map.116 = (f32[64,32,128]{2,1,0:T(8,128)S(1)}, f32[64,32,128]{2,1,0:T(8,128)S(1)}, f32[32,8,128]{2,1,0:T(8,128)S(1)}, f32[32,8,128]{2,1,0:T(8,128)S(1)}) custom-call(s32[5]{0:T(128)S(1)} %stack.52.spots, f32[8,2,8,32,128]{4,3,2,1,0:T(8,128)} %copy-done, f32[8,2,8,32,128]{4,3,2,1,0:T(8,128)} %copy-done, f32[8,8,32,128]{3,2,1,0:T(8,128)S(1)} %all-to-all-done.1.r2, ...), custom_call_target="tpu_custom_call" | custom-call | flops 10485760 | bytes 8388608 | tf_op jit(solution)/shard_map/pallas_call | solution.py:352
  160.2 4.0 %collective-permute-start.11 = (f32[32,8,128]{2,1,0:T(8,128)S(1)}, f32[32,8,128]{2,1,0:T(8,128)S(1)}, u32[]{:S(2)}, u32[]{:S(2)}) collective-permute-start(f32[32,8,128]{2,1,0:T(8,128)S(1)} %get-tuple-element.60), channel_id=1, source_target_pairs={{0,1},{1,2},{2,3},{3,4},{4,5},{5,6},{6,7},{8,9},{9,10},{10,11},{11... | collective-permute-start | bytes 393224 | tf_op jit(solution)/shard_map/ppermute | solution.py:290
  164.2 1.3 collective-permute-start.12
  166.1 4.5 %collective-permute-done.12.halo_hi = f32[32,8,128]{2,1,0:T(8,128)S(1)} collective-permute-done((f32[32,8,128]{2,1,0:T(8,128)S(1)}, f32[32,8,128]{2,1,0:T(8,128)S(1)}, u32[]{:S(2)}, u32[]{:S(2)}) %collective-permute-start.12) | collective-permute-done | bytes 131104 | tf_op jit(solution)/shard_map/ppermute | solution.py:290
  170.6 5.3 %shard_map.117 = (f32[64,32,128]{2,1,0:T(8,128)S(1)}, f32[64,32,128]{2,1,0:T(8,128)S(1)}, f32[32,8,128]{2,1,0:T(8,128)S(1)}, f32[32,8,128]{2,1,0:T(8,128)S(1)}) custom-call(s32[5]{0:T(128)S(1)} %stack.52.spots, f32[64,32,128]{2,1,0:T(8,128)S(1)} %get-tuple-element.59.late.later, f32[64,32,128]{2,1,0:T(8,128)S(1)} %bitcast.61, ...), custom_call_target="tpu_custom_call" | custom-call | flops 10485760 | bytes 8388608 | tf_op jit(solution)/shard_map/pallas_call | solution.py:352
  175.9 1.0 copy-done.19
  176.9 5.4 %collective-permute-start.13 = (f32[32,8,128]{2,1,0:T(8,128)S(1)}, f32[32,8,128]{2,1,0:T(8,128)S(1)}, u32[]{:S(2)}, u32[]{:S(2)}) collective-permute-start(f32[32,8,128]{2,1,0:T(8,128)S(1)} %get-tuple-element.66), channel_id=1, source_target_pairs={{0,1},{1,2},{2,3},{3,4},{4,5},{5,6},{6,7},{8,9},{9,10},{10,11},{11... | collective-permute-start | bytes 393224 | tf_op jit(solution)/shard_map/ppermute | solution.py:290
  182.4 1.3 collective-permute-start.14
  184.3 6.0 %collective-permute-done.14.halo_hi = f32[32,8,128]{2,1,0:T(8,128)S(1)} collective-permute-done((f32[32,8,128]{2,1,0:T(8,128)S(1)}, f32[32,8,128]{2,1,0:T(8,128)S(1)}, u32[]{:S(2)}, u32[]{:S(2)}) %collective-permute-start.14) | collective-permute-done | bytes 131104 | tf_op jit(solution)/shard_map/ppermute | solution.py:290
  190.3 5.4 %shard_map.118 = (f32[64,32,128]{2,1,0:T(8,128)S(1)}, f32[64,32,128]{2,1,0:T(8,128)S(1)}, f32[32,8,128]{2,1,0:T(8,128)S(1)}, f32[32,8,128]{2,1,0:T(8,128)S(1)}) custom-call(s32[5]{0:T(128)S(1)} %stack.52.spots, f32[64,32,128]{2,1,0:T(8,128)S(1)} %get-tuple-element.65.late.later, f32[64,32,128]{2,1,0:T(8,128)S(1)} %get-tuple-element.59.late.later, ...), custom_call_target="tpu_custom_call" | custom-call | flops 10485760 | bytes 8388608 | tf_op jit(solution)/shard_map/pallas_call | solution.py:352
  195.7 1.0 copy-done.18
  196.7 5.5 %collective-permute-start.15 = (f32[32,8,128]{2,1,0:T(8,128)S(1)}, f32[32,8,128]{2,1,0:T(8,128)S(1)}, u32[]{:S(2)}, u32[]{:S(2)}) collective-permute-start(f32[32,8,128]{2,1,0:T(8,128)S(1)} %get-tuple-element.72), channel_id=1, source_target_pairs={{0,1},{1,2},{2,3},{3,4},{4,5},{5,6},{6,7},{8,9},{9,10},{10,11},{11... | collective-permute-start | bytes 393224 | tf_op jit(solution)/shard_map/ppermute | solution.py:290
  202.2 1.3 collective-permute-start.16
  204.1 4.1 %collective-permute-done.16.halo_hi = f32[32,8,128]{2,1,0:T(8,128)S(1)} collective-permute-done((f32[32,8,128]{2,1,0:T(8,128)S(1)}, f32[32,8,128]{2,1,0:T(8,128)S(1)}, u32[]{:S(2)}, u32[]{:S(2)}) %collective-permute-start.16) | collective-permute-done | bytes 131104 | tf_op jit(solution)/shard_map/ppermute | solution.py:290
  208.2 5.6 %shard_map.119 = f32[8,8,32,128]{3,2,1,0:T(8,128)} custom-call(s32[5]{0:T(128)S(1)} %stack.52.spots, f32[64,32,128]{2,1,0:T(8,128)S(1)} %get-tuple-element.71.late, f32[64,32,128]{2,1,0:T(8,128)S(1)} %get-tuple-element.65.late.later, f32[8,8,32,128]{3,2,1,0:T(8,128)S(1)} %all-to-all-done.1.r2, f32[32,8,128]{2,1,0:T(8,128)S(1)} %collective-permute-done.15.halo_lo, ...), custom_call_target="tpu_custom_call" | custom-call | flops 10485760 | bytes 8388608 | tf_op jit(solution)/shard_map/pallas_call | solution.py:352
  213.8 11.5 %all-to-all-start.3 = ((f32[8,8,32,128]{3,2,1,0:T(8,128)}), f32[8,8,32,128]{3,2,1,0:T(8,128)S(1)}, u32[]{:S(2)}, u32[]{:S(2)}) async-start(f32[8,8,32,128]{3,2,1,0:T(8,128)} %shard_map.119), calls=%async_computation.3 | async-start | bytes 2097152 | tf_op jit(solution)/shard_map/all_to_all | solution.py:364
  225.4 15.0 %all-to-all-done.3.recv = f32[8,8,32,128]{3,2,1,0:T(8,128)S(1)} async-done(((f32[8,8,32,128]{3,2,1,0:T(8,128)}), f32[8,8,32,128]{3,2,1,0:T(8,128)S(1)}, u32[]{:S(2)}, u32[]{:S(2)}) %all-to-all-start.3) | async-done | bytes 1048608 | tf_op jit(solution)/shard_map/all_to_all | solution.py:364
  240.4 0.8 shard_map.120
  241.2 2.6 %collective-permute-start.17 = (f32[2,8,32,128]{3,2,1,0:T(8,128)S(1)}, f32[2,8,32,128]{3,2,1,0:T(8,128)S(1)}, u32[]{:S(2)}, u32[]{:S(2)}) collective-permute-start(f32[2,8,32,128]{3,2,1,0:T(8,128)S(1)} %get-tuple-element.78), channel_id=1, source_target_pairs={{0,64},{8,72},{16,80},{24,88},{32,96},{40,104},{48,112},{56,120},{... | collective-permute-start | bytes 786440 | tf_op jit(solution)/shard_map/ppermute | solution.py:367
  243.8 5.9 %collective-permute-done.17 = f32[2,8,32,128]{3,2,1,0:T(8,128)S(1)} collective-permute-done((f32[2,8,32,128]{3,2,1,0:T(8,128)S(1)}, f32[2,8,32,128]{3,2,1,0:T(8,128)S(1)}, u32[]{:S(2)}, u32[]{:S(2)}) %collective-permute-start.17) | collective-permute-done | bytes 262176 | tf_op jit(solution)/shard_map/ppermute | solution.py:367
  249.7 0.7 add_bitcast_fusion
  (67 shorter events, 5.0 us)
Async XLA Ops:
  0.0 9.3 %collective-permute-start = (f32[2,8,32,128]{3,2,1,0:T(8,128)}, f32[2,8,32,128]{3,2,1,0:T(8,128)S(1)}, u32[]{:S(2)}, u32[]{:S(2)}) collective-permute-start(f32[2,8,32,128]{3,2,1,0:T(8,128)} %bitcast.70), channel_id=1, source_target_pairs={{0,64},{8,72},{16,80},{24,88},{32,96},{40,104},{48,112},{56,120},{... | collective-permute-start | bytes 786440 | tf_op jit(solution)/shard_map/ppermute | solution.py:297
  11.0 7.8 %copy-start.25 = (f32[1,8,256,128]{3,2,1,0:T(8,128)S(1)}, f32[1,8,256,128]{3,2,1,0:T(8,128)}, u32[]{:S(2)}) copy-start(f32[1,8,256,128]{3,2,1,0:T(8,128)} %param.13) | copy-start | bytes 3145732
  12.3 6.5 %copy-start.26 = (f32[1,8,256,128]{3,2,1,0:T(8,128)S(1)}, f32[1,8,256,128]{3,2,1,0:T(8,128)}, u32[]{:S(2)}) copy-start(f32[1,8,256,128]{3,2,1,0:T(8,128)} %param.12) | copy-start | bytes 3145732
  12.3 21.6 %all-to-all-start.1 = ((f32[8,8,32,128]{3,2,1,0:T(8,128)}), f32[8,8,32,128]{3,2,1,0:T(8,128)S(1)}, u32[]{:S(2)}, u32[]{:S(2)}) async-start(f32[8,8,32,128]{3,2,1,0:T(8,128)} %broadcast_select_fusion), calls=%async_computation.1 | async-start | bytes 2097152 | tf_op jit(solution)/shard_map/all_to_all | solution.py:309
  33.9 32.1 %all-to-all-start.2 = ((f32[8,2,8,32,128]{4,3,2,1,0:T(8,128)}), f32[8,2,8,32,128]{4,3,2,1,0:T(8,128)S(1)}, u32[]{:S(2)}, u32[]{:S(2)}) async-start(f32[8,2,8,32,128]{4,3,2,1,0:T(8,128)} %pad_maximum_fusion.1), calls=%async_computation.2 | async-start | bytes 4194304 | tf_op jit(solution)/shard_map/all_to_all | solution.py:294
  66.0 1.3 copy-start.2
  67.3 54.2 %all-to-all-start = ((f32[8,2,8,32,128]{4,3,2,1,0:T(8,128)}), f32[8,2,8,32,128]{4,3,2,1,0:T(8,128)S(1)}, u32[]{:S(2)}, u32[]{:S(2)}) async-start(f32[8,2,8,32,128]{4,3,2,1,0:T(8,128)} %pad_maximum_fusion), calls=%async_computation | async-start | bytes 4194304 | tf_op jit(solution)/shard_map/all_to_all | solution.py:294
  71.0 10.6 %copy-start.27 = (f32[1,4]{1,0:T(1,128)S(1)}, f32[1,4]{1,0:T(1,128)}, u32[]{:S(2)}) copy-start(f32[1,4]{1,0:T(1,128)} %param.16) | copy-start | bytes 52
  71.0 27.2 %copy-start.10 = (bf16[256,256]{1,0:T(8,128)(2,1)S(1)}, bf16[256,256]{1,0:T(8,128)(2,1)}, u32[]{:S(2)}) copy-start(bf16[256,256]{1,0:T(8,128)(2,1)} %constant.161.clone.oper) | copy-start | bytes 393220
  74.4 1.6 copy-start.3
  77.0 19.2 %collective-permute-start.3 = (f32[32,8,128]{2,1,0:T(8,128)S(1)}, f32[32,8,128]{2,1,0:T(8,128)S(1)}, u32[]{:S(2)}, u32[]{:S(2)}) collective-permute-start(f32[32,8,128]{2,1,0:T(8,128)S(1)} %get-tuple-element.46), channel_id=1, source_target_pairs={{0,1},{1,2},{2,3},{3,4},{4,5},{5,6},{6,7},{8,9},{9,10},{10,11},{11... | collective-permute-start | bytes 393224 | tf_op jit(solution)/shard_map/ppermute | solution.py:290
  80.3 17.9 %collective-permute-start.4 = (f32[32,8,128]{2,1,0:T(8,128)S(1)}, f32[32,8,128]{2,1,0:T(8,128)S(1)}, u32[]{:S(2)}, u32[]{:S(2)}) collective-permute-start(f32[32,8,128]{2,1,0:T(8,128)S(1)} %get-tuple-element.47), channel_id=1, source_target_pairs={{1,0},{2,1},{3,2},{4,3},{5,4},{6,5},{7,6},{9,8},{10,9},{11,10},{12... | collective-permute-start | bytes 393224 | tf_op jit(solution)/shard_map/ppermute | solution.py:290
  101.6 1.0 copy-start.12
  102.6 12.9 %copy-start.6 = (f32[64,32,128]{2,1,0:T(8,128)}, f32[64,32,128]{2,1,0:T(8,128)S(1)}, u32[]{:S(2)}) copy-start(f32[64,32,128]{2,1,0:T(8,128)S(1)} %get-tuple-element.48.now.prev.wave) | copy-start | bytes 3145732
  102.6 5.0 %collective-permute-start.5 = (f32[32,8,128]{2,1,0:T(8,128)S(1)}, f32[32,8,128]{2,1,0:T(8,128)S(1)}, u32[]{:S(2)}, u32[]{:S(2)}) collective-permute-start(f32[32,8,128]{2,1,0:T(8,128)S(1)} %get-tuple-element.49), channel_id=1, source_target_pairs={{0,1},{1,2},{2,3},{3,4},{4,5},{5,6},{6,7},{8,9},{9,10},{10,11},{11... | collective-permute-start | bytes 393224 | tf_op jit(solution)/shard_map/ppermute | solution.py:290
  105.7 5.7 %collective-permute-start.6 = (f32[32,8,128]{2,1,0:T(8,128)S(1)}, f32[32,8,128]{2,1,0:T(8,128)S(1)}, u32[]{:S(2)}, u32[]{:S(2)}) collective-permute-start(f32[32,8,128]{2,1,0:T(8,128)S(1)} %get-tuple-element.50), channel_id=1, source_target_pairs={{1,0},{2,1},{3,2},{4,3},{5,4},{6,5},{7,6},{9,8},{10,9},{11,10},{12... | collective-permute-start | bytes 393224 | tf_op jit(solution)/shard_map/ppermute | solution.py:290
  115.4 1.0 copy-start.8
  116.4 1.0 copy-start.13
  117.4 11.6 %collective-permute-start.7 = (f32[32,8,128]{2,1,0:T(8,128)}, f32[32,8,128]{2,1,0:T(8,128)S(1)}, u32[]{:S(2)}, u32[]{:S(2)}) collective-permute-start(f32[32,8,128]{2,1,0:T(8,128)} %get-tuple-element.52), channel_id=1, source_target_pairs={{0,1},{1,2},{2,3},{3,4},{4,5},{5,6},{6,7},{8,9},{9,10},{10,11},{11... | collective-permute-start | bytes 393224 | tf_op jit(solution)/shard_map/ppermute | solution.py:290
  120.3 8.7 %collective-permute-start.8 = (f32[32,8,128]{2,1,0:T(8,128)}, f32[32,8,128]{2,1,0:T(8,128)S(1)}, u32[]{:S(2)}, u32[]{:S(2)}) collective-permute-start(f32[32,8,128]{2,1,0:T(8,128)} %get-tuple-element.53), channel_id=1, source_target_pairs={{1,0},{2,1},{3,2},{4,3},{5,4},{6,5},{7,6},{9,8},{10,9},{11,10},{12... | collective-permute-start | bytes 393224 | tf_op jit(solution)/shard_map/ppermute | solution.py:290
  121.6 11.0 %copy-start = (f32[8,2,8,32,128]{4,3,2,1,0:T(8,128)}, f32[8,2,8,32,128]{4,3,2,1,0:T(8,128)S(1)}, u32[]{:S(2)}) copy-start(f32[8,2,8,32,128]{4,3,2,1,0:T(8,128)S(1)} %all-to-all-done.now.late.later) | copy-start | bytes 6291460
  121.6 7.4 %copy-start.7 = (f32[64,32,128]{2,1,0:T(8,128)S(1)}, f32[64,32,128]{2,1,0:T(8,128)}, u32[]{:S(2)}) copy-start(f32[64,32,128]{2,1,0:T(8,128)} %copy-done.6) | copy-start | bytes 3145732
  121.6 7.4 %copy-start.9 = (f32[64,32,128]{2,1,0:T(8,128)S(1)}, f32[64,32,128]{2,1,0:T(8,128)}, u32[]{:S(2)}) copy-start(f32[64,32,128]{2,1,0:T(8,128)} %copy-done.8) | copy-start | bytes 3145732
  122.7 18.2 %copy-start.24 = (s32[1,256]{1,0:T(1,128)S(1)}, s32[1,256]{1,0:T(1,128)}, u32[]{:S(2)}) copy-start(s32[1,256]{1,0:T(1,128)} %param.18) | copy-start | bytes 3076
  122.7 18.3 %copy-start.23 = (f32[1,4,256]{2,1,0:T(4,128)S(1)}, f32[1,4,256]{2,1,0:T(4,128)}, u32[]{:S(2)}) copy-start(f32[1,4,256]{2,1,0:T(4,128)} %param.19) | copy-start | bytes 12292
  122.8 31.4 %collective-permute-start.1 = (f32[32,8,128]{2,1,0:T(8,128)S(1)}, f32[32,8,128]{2,1,0:T(8,128)S(1)}, u32[]{:S(2)}, u32[]{:S(2)}) collective-permute-start(f32[32,8,128]{2,1,0:T(8,128)S(1)} %get-tuple-element.42), channel_id=1, source_target_pairs={{0,1},{1,2},{2,3},{3,4},{4,5},{5,6},{6,7},{8,9},{9,10},{10,11},{11... | collective-permute-start | bytes 393224 | tf_op jit(solution)/shard_map/ppermute | solution.py:290
  127.7 26.4 %collective-permute-start.2 = (f32[32,8,128]{2,1,0:T(8,128)S(1)}, f32[32,8,128]{2,1,0:T(8,128)S(1)}, u32[]{:S(2)}, u32[]{:S(2)}) collective-permute-start(f32[32,8,128]{2,1,0:T(8,128)S(1)} %get-tuple-element.43), channel_id=1, source_target_pairs={{1,0},{2,1},{3,2},{4,3},{5,4},{6,5},{7,6},{9,8},{10,9},{11,10},{12... | collective-permute-start | bytes 393224 | tf_op jit(solution)/shard_map/ppermute | solution.py:290
  132.6 1.0 copy-start.16
  133.6 26.6 %copy-start.11 = (f32[64,32,128]{2,1,0:T(8,128)}, f32[64,32,128]{2,1,0:T(8,128)S(1)}, u32[]{:S(2)}) copy-start(f32[64,32,128]{2,1,0:T(8,128)S(1)} %get-tuple-element.54.now.wave) | copy-start | bytes 3145732
  133.6 14.6 %collective-permute-start.9 = (f32[32,8,128]{2,1,0:T(8,128)S(1)}, f32[32,8,128]{2,1,0:T(8,128)S(1)}, u32[]{:S(2)}, u32[]{:S(2)}) collective-permute-start(f32[32,8,128]{2,1,0:T(8,128)S(1)} %get-tuple-element.55), channel_id=1, source_target_pairs={{0,1},{1,2},{2,3},{3,4},{4,5},{5,6},{6,7},{8,9},{9,10},{10,11},{11... | collective-permute-start | bytes 393224 | tf_op jit(solution)/shard_map/ppermute | solution.py:290
  139.7 8.5 %collective-permute-start.10 = (f32[32,8,128]{2,1,0:T(8,128)S(1)}, f32[32,8,128]{2,1,0:T(8,128)S(1)}, u32[]{:S(2)}, u32[]{:S(2)}) collective-permute-start(f32[32,8,128]{2,1,0:T(8,128)S(1)} %get-tuple-element.56), channel_id=1, source_target_pairs={{1,0},{2,1},{3,2},{4,3},{5,4},{6,5},{7,6},{9,8},{10,9},{11,10},{12... | collective-permute-start | bytes 393224 | tf_op jit(solution)/shard_map/ppermute | solution.py:290
  146.2 1.0 copy-start.15
  147.1 1.0 copy-start.17
  148.1 6.0 %copy-start.14 = (f32[64,32,128]{2,1,0:T(8,128)}, f32[64,32,128]{2,1,0:T(8,128)S(1)}, u32[]{:S(2)}) copy-start(f32[64,32,128]{2,1,0:T(8,128)S(1)} %get-tuple-element.74.data) | copy-start | bytes 3145732
  148.1 12.0 %copy-start.4 = (f32[64,32,128]{2,1,0:T(8,128)}, f32[64,32,128]{2,1,0:T(8,128)S(1)}, u32[]{:S(2)}) copy-start(f32[64,32,128]{2,1,0:T(8,128)S(1)} %get-tuple-element.44.count) | copy-start | bytes 3145732
  152.2 1.0 copy-start.21
  153.2 1.0 copy-start.22
  154.2 11.3 %copy-start.1 = (f32[8,2,8,32,128]{4,3,2,1,0:T(8,128)S(1)}, f32[8,2,8,32,128]{4,3,2,1,0:T(8,128)}, u32[]{:S(2)}) copy-start(f32[8,2,8,32,128]{4,3,2,1,0:T(8,128)} %copy-done) | copy-start | bytes 6291460
  160.2 10.4 %copy-start.20 = (f32[64,32,128]{2,1,0:T(8,128)}, f32[64,32,128]{2,1,0:T(8,128)S(1)}, u32[]{:S(2)}) copy-start(f32[64,32,128]{2,1,0:T(8,128)S(1)} %get-tuple-element.64.rest_0_) | copy-start | bytes 3145732
  160.2 5.9 %collective-permute-start.11 = (f32[32,8,128]{2,1,0:T(8,128)S(1)}, f32[32,8,128]{2,1,0:T(8,128)S(1)}, u32[]{:S(2)}, u32[]{:S(2)}) collective-permute-start(f32[32,8,128]{2,1,0:T(8,128)S(1)} %get-tuple-element.60), channel_id=1, source_target_pairs={{0,1},{1,2},{2,3},{3,4},{4,5},{5,6},{6,7},{8,9},{9,10},{10,11},{11... | collective-permute-start | bytes 393224 | tf_op jit(solution)/shard_map/ppermute | solution.py:290
  164.2 6.4 %collective-permute-start.12 = (f32[32,8,128]{2,1,0:T(8,128)S(1)}, f32[32,8,128]{2,1,0:T(8,128)S(1)}, u32[]{:S(2)}, u32[]{:S(2)}) collective-permute-start(f32[32,8,128]{2,1,0:T(8,128)S(1)} %get-tuple-element.61), channel_id=1, source_target_pairs={{1,0},{2,1},{3,2},{4,3},{5,4},{6,5},{7,6},{9,8},{10,9},{11,10},{12... | collective-permute-start | bytes 393224 | tf_op jit(solution)/shard_map/ppermute | solution.py:290
  175.9 1.0 copy-start.19
  176.9 7.3 %collective-permute-start.13 = (f32[32,8,128]{2,1,0:T(8,128)S(1)}, f32[32,8,128]{2,1,0:T(8,128)S(1)}, u32[]{:S(2)}, u32[]{:S(2)}) collective-permute-start(f32[32,8,128]{2,1,0:T(8,128)S(1)} %get-tuple-element.66), channel_id=1, source_target_pairs={{0,1},{1,2},{2,3},{3,4},{4,5},{5,6},{6,7},{8,9},{9,10},{10,11},{11... | collective-permute-start | bytes 393224 | tf_op jit(solution)/shard_map/ppermute | solution.py:290
  182.4 7.9 %collective-permute-start.14 = (f32[32,8,128]{2,1,0:T(8,128)S(1)}, f32[32,8,128]{2,1,0:T(8,128)S(1)}, u32[]{:S(2)}, u32[]{:S(2)}) collective-permute-start(f32[32,8,128]{2,1,0:T(8,128)S(1)} %get-tuple-element.67), channel_id=1, source_target_pairs={{1,0},{2,1},{3,2},{4,3},{5,4},{6,5},{7,6},{9,8},{10,9},{11,10},{12... | collective-permute-start | bytes 393224 | tf_op jit(solution)/shard_map/ppermute | solution.py:290
  190.3 17.9 %copy-start.5 = (f32[64,32,128]{2,1,0:T(8,128)S(1)}, f32[64,32,128]{2,1,0:T(8,128)}, u32[]{:S(2)}) copy-start(f32[64,32,128]{2,1,0:T(8,128)} %copy-done.4) | copy-start | bytes 3145732
  195.7 1.0 copy-start.18
  196.7 7.4 %collective-permute-start.15 = (f32[32,8,128]{2,1,0:T(8,128)S(1)}, f32[32,8,128]{2,1,0:T(8,128)S(1)}, u32[]{:S(2)}, u32[]{:S(2)}) collective-permute-start(f32[32,8,128]{2,1,0:T(8,128)S(1)} %get-tuple-element.72), channel_id=1, source_target_pairs={{0,1},{1,2},{2,3},{3,4},{4,5},{5,6},{6,7},{8,9},{9,10},{10,11},{11... | collective-permute-start | bytes 393224 | tf_op jit(solution)/shard_map/ppermute | solution.py:290
  202.2 6.0 %collective-permute-start.16 = (f32[32,8,128]{2,1,0:T(8,128)S(1)}, f32[32,8,128]{2,1,0:T(8,128)S(1)}, u32[]{:S(2)}, u32[]{:S(2)}) collective-permute-start(f32[32,8,128]{2,1,0:T(8,128)S(1)} %get-tuple-element.73), channel_id=1, source_target_pairs={{1,0},{2,1},{3,2},{4,3},{5,4},{6,5},{7,6},{9,8},{10,9},{11,10},{12... | collective-permute-start | bytes 393224 | tf_op jit(solution)/shard_map/ppermute | solution.py:290
  213.8 26.6 %all-to-all-start.3 = ((f32[8,8,32,128]{3,2,1,0:T(8,128)}), f32[8,8,32,128]{3,2,1,0:T(8,128)S(1)}, u32[]{:S(2)}, u32[]{:S(2)}) async-start(f32[8,8,32,128]{3,2,1,0:T(8,128)} %shard_map.119), calls=%async_computation.3 | async-start | bytes 2097152 | tf_op jit(solution)/shard_map/all_to_all | solution.py:364
  241.2 8.5 %collective-permute-start.17 = (f32[2,8,32,128]{3,2,1,0:T(8,128)S(1)}, f32[2,8,32,128]{3,2,1,0:T(8,128)S(1)}, u32[]{:S(2)}, u32[]{:S(2)}) collective-permute-start(f32[2,8,32,128]{3,2,1,0:T(8,128)S(1)} %get-tuple-element.78), channel_id=1, source_target_pairs={{0,64},{8,72},{16,80},{24,88},{32,96},{40,104},{48,112},{56,120},{... | collective-permute-start | bytes 786440 | tf_op jit(solution)/shard_map/ppermute | solution.py:367

commit v2 on v1

v2 whole, which is shorter than its diff:
```python
import functools

import jax
import jax.numpy as jnp
import ml_dtypes
import numpy as np
from jax import lax
from jax.experimental import pallas as pl
from jax.experimental.pallas import tpu as pltpu
from jax.sharding import PartitionSpec as P

STEPS = 4
STENCIL = (-205.0 / 72.0, 8.0 / 5.0, -1.0 / 5.0, 8.0 / 315.0, -1.0 / 560.0)
F32 = jnp.float32
BF16 = jnp.bfloat16
SMEM = pl.BlockSpec(memory_space=pltpu.SMEM)
VMEM = pl.BlockSpec(memory_space=pltpu.VMEM)
NX, NYL, NZ = 64, 32, 128
GROUP = 8
PAD = 4
ROW0 = 8
ROWS = 48


def depth_operator():
    band = np.zeros((NZ, NZ), np.float32)
    for i in range(NZ):
        band[i, i] = np.float32(3.0 * STENCIL[0])
        for k in range(1, 5):
            for j in (i - k, i + k):
                if 0 <= j < NZ:
                    band[j, i] = np.float32(STENCIL[k])
    high = band.astype(ml_dtypes.bfloat16)
    low = (band - high.astype(np.float32)).astype(ml_dtypes.bfloat16)
    zero = np.zeros_like(high)
    return np.block([[high, low], [high, zero]])


def read_field(ref, off, g, xi, rows):
    if off is None:
        return ref[g * GROUP + xi, rows, :]
    return ref[g, xi, off + rows.start : off + rows.stop, :]


def clear_ends(ext):
    zeros = jnp.zeros((PAD, ROWS, NZ), F32)
    ext[0:PAD] = zeros
    ext[PAD + NX : 2 * PAD + NX] = zeros


def fill_edges(ext, spots, halo_lo, halo_hi):
    has_lo, has_hi = spots[5] == 1, spots[6] == 1

    def body(t, carry):
        lo = jnp.where(has_lo, halo_lo[t], 0.0)
        hi = jnp.where(has_hi, halo_hi[t], 0.0)
        for half in range(2):
            x = PAD + 2 * t + half
            ext[x, ROW0 - 4 : ROW0, :] = lo[4 * half : 4 * half + 4]
            ext[x, ROW0 + NYL : ROW0 + NYL + 4, :] = hi[4 * half : 4 * half + 4]
        return carry

    lax.fori_loop(0, NX // 2, body, 0, unroll=4)


def apply_depth(ext, oper, depth):
    own = ext[PAD : PAD + NX, ROW0 : ROW0 + NYL, :].reshape(NX * NYL, NZ)
    high = own.astype(BF16)
    low = (own - high.astype(F32)).astype(BF16)
    prod = jnp.dot(jnp.concatenate([high, low], axis=1), oper[...], preferred_element_type=F32)
    depth[...] = (prod[:, :NZ] + prod[:, NZ:]).reshape(NX, NYL, NZ)


def laplace_group(ext, depth, g, emit):
    base = PAD + g * GROUP
    for j in range(NYL // 8):
        r0 = ROW0 + 8 * j
        col = [ext[base - PAD + i, r0 : r0 + 8, :] for i in range(GROUP + 2 * PAD)]
        for xi in range(GROUP):
            acc = depth[g * GROUP + xi, 8 * j : 8 * j + 8, :]
            for k in range(1, 5):
                beside = (
                    col[xi + PAD + k]
                    + col[xi + PAD - k]
                    + (
                        ext[base + xi, r0 + k : r0 + k + 8, :]
                        + ext[base + xi, r0 - k : r0 - k + 8, :]
                    )
                )
                acc = acc + STENCIL[k] * beside
            emit(xi, j, acc)


def send_rows(send_lo, send_hi, read):
    def body(t, carry):
        for half in range(2):
            send_lo[t, 4 * half : 4 * half + 4, :] = read(2 * t + half, slice(0, 4))
            send_hi[t, 4 * half : 4 * half + 4, :] = read(2 * t + half, slice(NYL - 4, NYL))
        return carry

    lax.fori_loop(0, NX // 2, body, 0, unroll=4)


EVERY = slice(0, NYL)


def forward_kernel(off_now, off_prev, last, spots, amount, now, prev, r2, oper, *rest):
    rest = list(rest)
    halos = None if off_now is not None else (rest.pop(0), rest.pop(0))
    if last:
        lap, new, ext, depth = rest
    else:
        lap, new, send_lo, send_hi, ext, depth = rest

    clear_ends(ext)

    def copy(g, carry):
        for xi in range(GROUP):
            ext[PAD + g * GROUP + xi, ROW0 : ROW0 + NYL, :] = read_field(now, off_now, g, xi, EVERY)
            if halos is None:
                edge = now[g, xi, EDGES : EDGES + 8, :]
                ext[PAD + g * GROUP + xi, ROW0 - 4 : ROW0, :] = edge[0:4]
                ext[PAD + g * GROUP + xi, ROW0 + NYL : ROW0 + NYL + 4, :] = edge[4:8]
        return carry

    lax.fori_loop(0, NX // GROUP, copy, 0)
    if halos is not None:
        fill_edges(ext, spots, *halos)
    apply_depth(ext, oper, depth)

    def body(g, carry):
        def emit(xi, j, value):
            rows = slice(8 * j, 8 * j + 8)
            x = g * GROUP + xi
            lap[x, rows, :] = value
            here = ext[PAD + x, ROW0 + 8 * j : ROW0 + 8 * j + 8, :]
            new[x, rows, :] = 2.0 * here - read_field(prev, off_prev, g, xi, rows) + r2[g, xi, rows, :] * value

        laplace_group(ext, depth, g, emit)
        return carry

    lax.fori_loop(0, NX // GROUP, body, 0)

    @pl.when(spots[1] == 1)
    def _():
        x, y, z = spots[2], spots[3], spots[4]
        lanes = lax.broadcasted_iota(jnp.int32, (1, NZ), 1)
        row = new[x, pl.ds(y, 1), :]
        new[x, pl.ds(y, 1), :] = row + jnp.where(lanes == z, amount[0], 0.0)

    if not last:
        send_rows(send_lo, send_hi, lambda x, rows: new[x, rows, :])


def edge_kernel(turned, r2, send_lo, send_hi):
    def read(x, rows):
        g, xi = x // GROUP, lax.rem(x, GROUP)
        return read_field(turned, LATE, g, xi, rows) * r2[g, xi, rows, :]

    send_rows(send_lo, send_hi, read)


def adjoint_kernel(
    off_late, off_later, begin, last, spots, late, later, r2, halo_lo, halo_hi, oper, count, data, wave, lap, *rest
):
    rest = list(rest)
    total_in = None if begin else rest.pop(0)
    if last:
        total, ext, depth = rest
    else:
        total, new, send_lo, send_hi, ext, depth = rest
    first = spots[0]

    clear_ends(ext)

    def copy(g, carry):
        for xi in range(GROUP):
            ext[PAD + g * GROUP + xi, ROW0 : ROW0 + NYL, :] = (
                read_field(late, off_late, g, xi, EVERY) * r2[g, xi]
            )
        return carry

    lax.fori_loop(0, NX // GROUP, copy, 0)
    fill_edges(ext, spots, halo_lo, halo_hi)
    apply_depth(ext, oper, depth)

    def body(g, carry):
        slot = lax.rem(first + g, GROUP)

        def emit(xi, j, value):
            rows = slice(8 * j, 8 * j + 8)
            x = g * GROUP + xi
            mu = 2.0 * read_field(late, off_late, g, xi, rows) + value - read_field(later, off_later, g, xi, rows)
            mu = mu + (count[x, rows, :] * wave[x, rows, :] - data[x, rows, :])
            part = mu * lap[x, rows, :]
            if total_in is not None:
                part = part + total_in[x, rows, :]
            if last:
                total[slot, xi, rows, :] = part
            else:
                total[x, rows, :] = part
                new[x, rows, :] = mu

        laplace_group(ext, depth, g, emit)
        return carry

    lax.fori_loop(0, NX // GROUP, body, 0)
    if not last:

        def read(x, rows):
            return new[x, rows, :] * r2[x // GROUP, lax.rem(x, GROUP), rows, :]

        send_rows(send_lo, send_hi, read)


NOW, PREV, LATE, LATER, EDGES, TURNED = 0, 32, 64, 96, 128, 136


def pack_kernel(now, prev, late, later, out):
    none = jnp.zeros((4, NZ), F32)

    def body(xi, carry):
        for p in range(8):
            lo = NYL * p
            for off, field in ((NOW, now), (PREV, prev), (LATE, late), (LATER, later)):
                out[p, xi, off : off + NYL, :] = field[xi, lo : lo + NYL, :]
            out[p, xi, EDGES : EDGES + 4, :] = now[xi, lo - 4 : lo, :] if p > 0 else none
            out[p, xi, EDGES + 4 : EDGES + 8, :] = now[xi, lo + NYL : lo + NYL + 4, :] if p < 7 else none
        return carry

    lax.fori_loop(0, GROUP, body, 0)


def copy_block(dst, src):
    def body(x, carry):
        dst[x] = src[x]
        return carry

    lax.fori_loop(0, GROUP, body, 0, unroll=4)


def select_kernel(slots, here, piece, other, piece_c, other_c, *outs):
    half, core = here[0], here[1]
    for k in range(4):
        for j in range(2):
            m = slots[2 * k + j]
            row = m // 2
            own_half = lax.rem(m, 2) == half
            own_core = core == j
            for src, same_half, same_core in (
                (piece, True, True),
                (other, False, True),
                (piece_c, True, False),
                (other_c, False, False),
            ):

                @pl.when(jnp.logical_and(own_half == same_half, own_core == same_core))
                def _():
                    copy_block(outs[k].at[j], src.at[row])


def assemble_kernel(places, r0, r1, r2, r3, out):
    for k, src in enumerate((r0, r1, r2, r3)):
        for j in range(2):
            copy_block(out.at[places[2 * k + j]], src.at[j])


def receivers_kernel(cells, mine, observed, count, *datas):
    zeros = jnp.zeros((NYL, NZ), F32)

    def clear(x, carry):
        count[x] = zeros
        for d in datas:
            d[x] = zeros
        return carry

    lax.fori_loop(0, NX, clear, 0)
    lanes = lax.broadcasted_iota(jnp.int32, (1, NZ), 1)

    def body(r, carry):
        @pl.when(mine[r] == 1)
        def _():
            cell = cells[r]
            x = cell // (256 * NZ)
            y = lax.rem(cell // NZ, NYL)
            hit = lanes == lax.rem(cell, NZ)
            count[x, pl.ds(y, 1), :] = count[x, pl.ds(y, 1), :] + jnp.where(hit, 1.0, 0.0)
            for n, d in enumerate(datas):
                d[x, pl.ds(y, 1), :] = d[x, pl.ds(y, 1), :] + jnp.where(hit, observed[n, r], 0.0)

        return carry

    lax.fori_loop(0, cells.shape[0], body, 0)


def bins_kernel(slots, half, recv, keep, give):
    zeros = jnp.zeros((GROUP, NYL, NZ), F32)
    for i in range(2):
        keep[i] = zeros
        give[i] = zeros
    mine = half[0]
    for t in range(GROUP):
        m = slots[t]
        i = m // 2

        @pl.when(lax.rem(m, 2) == mine)
        def _():
            keep[i] = keep[i] + recv[t]

        @pl.when(lax.rem(m, 2) != mine)
        def _():
            give[i] = give[i] + recv[t]


FIELD = jax.ShapeDtypeStruct((NX, NYL, NZ), F32)
EDGE = jax.ShapeDtypeStruct((NX // 2, 8, NZ), F32)
BLOCKS = jax.ShapeDtypeStruct((8, GROUP, NYL, NZ), F32)
PAIR = jax.ShapeDtypeStruct((2, GROUP, NYL, NZ), F32)
SCRATCH = [pltpu.VMEM((NX + 2 * PAD, ROWS, NZ), F32), pltpu.VMEM((NX, NYL, NZ), F32)]
PARAMS = pltpu.CompilerParams(vmem_limit_bytes=14 * 1024 * 1024)


def call(kernel, specs, outs, scratch=(), flops=0, moved=0):
    return pl.pallas_call(
        kernel,
        in_specs=specs,
        out_specs=[VMEM] * len(outs),
        out_shape=outs,
        scratch_shapes=list(scratch),
        compiler_params=PARAMS,
        cost_estimate=pl.CostEstimate(flops=flops, bytes_accessed=moved, transcendentals=0),
    )


def per_device(
    courant_squared,
    wave_now,
    wave_prev,
    adj_late,
    adj_later,
    wavelet,
    sources,
    receivers,
    observed,
    apertures,
):
    me = lax.axis_index("shot")
    part = lax.axis_index("sub")
    half, clas = me // 8, me % 8
    row, core = clas // 2, clas % 2
    starts = apertures[:, 0]
    first = starts[me]
    oper = jnp.asarray(depth_operator())
    up = [(i, (i + 1) % 8) for i in range(8)]
    down = [((i + 1) % 8, i) for i in range(8)]
    across = [(i, (i + 8) % 16) for i in range(16)]
    chip = [(i, i ^ 1) for i in range(16)]
    halves = [list(range(8)), list(range(8, 16))]

    def along(k):
        return [(8 * h + 2 * y + c, 8 * h + 2 * ((y + k) % 4) + c) for h in range(2) for y in range(4) for c in range(2)]

    def edges(lo, hi):
        return lax.ppermute(hi, "sub", up), lax.ppermute(lo, "sub", down)

    piece = courant_squared[:, 0]
    other = lax.ppermute(piece, "shot", across)
    piece_c = lax.ppermute(piece, "shot", chip)
    other_c = lax.ppermute(other, "shot", chip)
    ahead = jnp.arange(4)
    two = jnp.arange(2)
    want = starts[half * 8 + (row + ahead) % 4 * 2 + core][:, None]
    have = (2 * row + two)[None, :]
    chosen = ((want + (have - want) % 8) // 8).reshape(8).astype(jnp.int32)
    here = jnp.stack([half, core]).astype(jnp.int32)
    blocks = call(select_kernel, [SMEM] * 2 + [VMEM] * 4, [PAIR] * 4, moved=2 << 20)(chosen, here, piece, other, piece_c, other_c)
    come = [blocks[0]] + [lax.ppermute(blocks[k], "shot", along(k)) for k in (1, 2, 3)]
    from_class = ((row - ahead) % 4 * 2)[:, None] + two[None, :]
    places = ((from_class - first) % 8).reshape(8).astype(jnp.int32)

    (packed,) = call(pack_kernel, [VMEM] * 4, [jax.ShapeDtypeStruct((8, GROUP, TURNED, NZ), F32)], moved=8 << 20)(
        wave_now[0], wave_prev[0], adj_late[0], adj_later[0]
    )
    packed, come[1] = lax.optimization_barrier((packed, come[1]))
    turned = lax.all_to_all(packed, "sub", 0, 0, tiled=True)
    (r2,) = call(assemble_kernel, [SMEM] + [VMEM] * 4, [BLOCKS], moved=2 << 20)(places, *come)

    cell = sources[0]
    line = (cell // NZ) % 256
    spots = jnp.stack(
        [
            first % 8,
            (line // NYL == part).astype(jnp.int32),
            cell // (256 * NZ),
            line % NYL,
            cell % NZ,
            (part > 0).astype(jnp.int32),
            (part < 7).astype(jnp.int32),
        ]
    )
    cells = receivers[0]
    mine = ((cells // NZ) % 256 // NYL == part).astype(jnp.int32)
    count, *datas = call(receivers_kernel, [SMEM] * 3, [FIELD] * 5, moved=6 << 20)(cells, mine, observed[0])

    laps, fields = [], []
    now, prev = turned, turned
    offs = (NOW, PREV)
    halo = ()
    for step in range(STEPS):
        last = step == STEPS - 1
        args = [spots, wavelet[0, step : step + 1], now, prev, r2, oper, *halo]
        lap, new, *send = call(
            functools.partial(forward_kernel, *offs, last),
            [SMEM, SMEM] + [VMEM] * (len(args) - 2),
            [FIELD, FIELD] + ([] if last else [EDGE, EDGE]),
            SCRATCH,
            flops=10 << 20,
            moved=6 << 20,
        )(*args)
        laps.append(lap)
        fields.append(new)
        now, prev = new, now
        offs = (None, offs[0])
        if not last:
            halo = edges(*send)

    send = call(edge_kernel, [VMEM, VMEM], [EDGE] * 2, moved=1 << 20)(turned, r2)
    late, later = turned, turned
    offs = (LATE, LATER)
    total = None
    for step in range(STEPS, 0, -1):
        halo = edges(*send)
        begin, last = step == STEPS, step == 1
        outs = [BLOCKS] if last else [FIELD, FIELD, EDGE, EDGE]
        args = [spots, late, later, r2, *halo, oper, count, datas[step - 1], fields[step - 1], laps[step - 1]]
        if not begin:
            args.append(total)
        total, *more = call(
            functools.partial(adjoint_kernel, *offs, begin, last),
            [SMEM] + [VMEM] * (len(args) - 1),
            outs,
            SCRATCH,
            flops=10 << 20,
            moved=8 << 20,
        )(*args)
        if not last:
            late, later = more[0], late
            offs = (None, offs[0])
            send = more[1:]

    recv = lax.all_to_all(total, "shot", 0, 0, axis_index_groups=halves, tiled=True)
    group = starts[half * 8 + jnp.arange(8)]
    slots = ((group + (clas - group) % 8) // 8).astype(jnp.int32)
    keep, give = call(bins_kernel, [SMEM, SMEM, VMEM], [PAIR, PAIR], moved=2 << 20)(slots, half[None], recv)
    result = keep + lax.ppermute(give, "shot", across)
    return result[:, None]


def solution(mesh):
    in_specs = (
        P(None, "shot", None, "sub", None),
        P("shot", "sub", None, None),
        P("shot", "sub", None, None),
        P("shot", "sub", None, None),
        P("shot", "sub", None, None),
        P("shot", None),
        P("shot"),
        P("shot", None),
        P("shot", None, None),
        P(),
    )
    out_specs = P(None, "shot", None, "sub", None)
    return jax.shard_map(
        per_device, mesh=mesh, in_specs=in_specs, out_specs=out_specs, check_vma=False
    )
```

time: 253 us -> 195 us (0.77)
  starting transfers between devices: 79.4 us -> 55 us
  waiting for transfers between devices: 98.6 us -> 78.9 us
  local copies, waits for them, and re-layouts: 17.7 us -> 11.6 us
  other arithmetic: 6.37 us -> 1.7 us
    ppermute x16 -> x14, waiting for transfers between devices: 36.6 us -> 9.62 us  [edges(): return (lax.ppermute(hi, 'sub', up), lax.ppermute(lo, 'sub', down))]
    ppermute x16 -> x14, starting transfers between devices: 45.5 us -> 25.7 us  [edges(): return (lax.ppermute(hi, 'sub', up), lax.ppermute(lo, 'sub', down))]
    all_to_all x3 -> x1, starting transfers between devices: 16.2 us -> 5.87 us  [per_device(): turned = lax.all_to_all(packed, 'sub', 0, 0, tiled=True)]
    ppermute x0 -> x5, starting transfers between devices: none -> 7.26 us  [the longest x3 5.06 us: per_device(): lax.ppermute(blocks[k], 'shot', along(k))]
    ppermute x0 -> x5, waiting for transfers between devices: none -> 6.63 us  [the longest x3 6.46 us: per_device(): lax.ppermute(blocks[k], 'shot', along(k))]
    unnamed x56 -> x20, local copies, waits for them, and re-layouts: 13 us -> 7.96 us
    another operation x3 -> x1, other arithmetic: 3.18 us -> 0.07 us  [per_device(): here = jnp.stack([half, core]).astype(jnp.int32)]
    pallas_call x11 -> x13, Pallas kernels: 40.1 us -> 38.6 us  [the longest x4 17.5 us: per_device(): call(functools.partial(adjoint_kernel, *offs, begin, last), [SMEM] + [VME...]
  transfers between devices with their start and end apart: 22 -> 23, of which waited for: 15 -> 12; matrix products, arithmetic and copies ran while one was open for 3% -> 2% of each run, Pallas kernels for 9% -> 7%
where the time goes in v2:
time: 195 us; the launch traced here: 194 us
  waiting for transfers between devices  78.9 us (40%)
  starting transfers between devices  55 us (28%)
  Pallas kernels  43.7 us (22%)
  local copies, waits for them, and re-layouts  11.6 us (6%)
  between operations  3.07 us (2%)
    all_to_all x1, waiting for transfers between devices, per_device(): turned = lax.all_to_all(packed, 'sub', 0, 0, tiled=True)  36.1 us
    ppermute x14, starting transfers between devices, edges(): return (lax.ppermute(hi, 'sub', up), lax.ppermute(lo, 'sub', down))  25.7 us
    pallas_call x4, Pallas kernels, per_device(): call(functools.partial(adjoint_kernel, *offs, begin, last), [SMEM] + [VME...  17.5 us
    pallas_call x4, Pallas kernels, per_device(): call(functools.partial(forward_kernel, *offs, last), [SMEM, SMEM] + [VMEM...  15.8 us
    all_to_all x1, waiting for transfers between devices, per_device(): lax.all_to_all(total, 'shot', 0, 0, axis_index_groups=halves, tiled=True)  14.4 us
    all_to_all x1, starting transfers between devices, per_device(): lax.all_to_all(total, 'shot', 0, 0, axis_index_groups=halves, tiled=True)  10.9 us
    ppermute x14, waiting for transfers between devices, edges(): return (lax.ppermute(hi, 'sub', up), lax.ppermute(lo, 'sub', down))  9.62 us
    unnamed x20, local copies, waits for them, and re-layouts  7.96 us
  transfers between devices with their start and end apart: 23, of which 12 were waited for; matrix products, arithmetic and copies ran while one was open for 2% of the time, Pallas kernels for 7%

profile of v2, /device:TPU:1, one launch (start us, length us, event | category | flops | bytes accessed | tf_op | source)
XLA Modules:
  0.0 194.0 jit_solution(2011963043025026756)
XLA Ops:
  0.0 1.4 collective-permute-start.1
  1.4 2.8 %collective-permute-start = (f32[2,8,32,128]{3,2,1,0:T(8,128)}, f32[2,8,32,128]{3,2,1,0:T(8,128)S(1)}, u32[]{:S(2)}, u32[]{:S(2)}) collective-permute-start(f32[2,8,32,128]{3,2,1,0:T(8,128)} %bitcast.41), channel_id=1, source_target_pairs={{0,64},{8,72},{16,80},{24,88},{32,96},{40,104},{48,112},{56,120},{... | collective-permute-start | bytes 786440 | tf_op jit(solution)/shard_map/ppermute | solution.py:367
  4.3 0.7 fusion.14
  5.0 6.1 %collective-permute-done.other = f32[2,8,32,128]{3,2,1,0:T(8,128)S(1)} collective-permute-done((f32[2,8,32,128]{3,2,1,0:T(8,128)}, f32[2,8,32,128]{3,2,1,0:T(8,128)S(1)}, u32[]{:S(2)}, u32[]{:S(2)}) %collective-permute-start) | collective-permute-done | bytes 262176 | tf_op jit(solution)/shard_map/ppermute | solution.py:367
  11.1 0.8 collective-permute-start.2
  11.9 0.1 sub.81
  12.0 0.6 gather_fusion.1
  12.7 0.1 add.214
  12.9 0.2 collective-permute-done.2.other_c
  13.0 0.9 copy-done.6
  14.0 0.9 shard_map.110
  14.8 1.4 collective-permute-start.3
  16.3 1.2 copy-done.2
  17.5 1.2 copy-done.3
  18.7 1.2 copy-done.4
  20.0 1.2 copy-done.5
  21.2 0.3 shard_map.109
  21.5 2.1 %copy-done = f32[8,8,136,128]{3,2,1,0:T(8,128)} copy-done((f32[8,8,136,128]{3,2,1,0:T(8,128)}, f32[8,8,136,128]{3,2,1,0:T(8,128)S(1)}, u32[]{:S(2)}) %copy-start) | copy-done | bytes 4456472
  23.6 0.3 collective-permute-done.3.r1
  23.9 5.9 %all-to-all-start = ((f32[8,8,136,128]{3,2,1,0:T(8,128)}), f32[8,8,136,128]{3,2,1,0:T(8,128)}, u32[]{:S(2)}, u32[]{:S(2)}) async-start(f32[8,8,136,128]{3,2,1,0:T(8,128)} %copy-done), calls=%async_computation | async-start | bytes 8912896 | tf_op jit(solution)/shard_map/all_to_all | solution.py:385
  29.8 0.7 constant_dynamic-slice_fusion
  30.5 0.8 add_subtract_fusion
  31.2 2.5 %collective-permute-start.4 = (f32[2,8,32,128]{3,2,1,0:T(8,128)S(1)}, f32[2,8,32,128]{3,2,1,0:T(8,128)S(1)}, u32[]{:S(2)}, u32[]{:S(2)}) collective-permute-start(f32[2,8,32,128]{3,2,1,0:T(8,128)S(1)} %get-tuple-element.50), channel_id=1, source_target_pairs={{0,32},{8,40},{16,48},{24,56},{32,0},{40,8},{48,16},{56,24},{64,96... | collective-permute-start | bytes 786440 | tf_op jit(solution)/shard_map/ppermute | solution.py:377
  33.8 1.1 collective-permute-start.5
  34.9 0.6 fusion.15
  38.3 0.1 sub.87
  38.4 0.1 stack.50.spots
  38.5 0.8 collective-permute-done.4.r2
  39.3 5.3 %collective-permute-done.5.r3 = f32[2,8,32,128]{3,2,1,0:T(8,128)S(1)} collective-permute-done((f32[2,8,32,128]{3,2,1,0:T(8,128)S(1)}, f32[2,8,32,128]{3,2,1,0:T(8,128)S(1)}, u32[]{:S(2)}, u32[]{:S(2)}) %collective-permute-start.5) | collective-permute-done | bytes 262176 | tf_op jit(solution)/shard_map/ppermute | solution.py:377
  44.6 0.7 shard_map.111.r2
  45.3 36.1 %all-to-all-done.turned.now.prev.late.later = f32[8,8,136,128]{3,2,1,0:T(8,128)} async-done(((f32[8,8,136,128]{3,2,1,0:T(8,128)}), f32[8,8,136,128]{3,2,1,0:T(8,128)}, u32[]{:S(2)}, u32[]{:S(2)}) %all-to-all-start) | async-done | bytes 4456480 | tf_op jit(solution)/shard_map/all_to_all | solution.py:385
  81.3 5.9 %shard_map.114 = (f32[64,32,128]{2,1,0:T(8,128)S(1)}, f32[64,32,128]{2,1,0:T(8,128)S(1)}, f32[32,8,128]{2,1,0:T(8,128)S(1)}, f32[32,8,128]{2,1,0:T(8,128)S(1)}) custom-call(s32[7]{0:T(128)S(1)} %stack.50.spots, f32[1]{0:T(128)} %bitcast.24.amount, f32[8,8,136,128]{3,2,1,0:T(8,128)} %all-to-all-done.turned.now.prev.late.later, ...), custom_call_target="tpu_custom_call" | custom-call | flops 10485760 | bytes 6291456 | tf_op jit(solution)/shard_map/pallas_call | solution.py:412
  87.2 0.1 collective-permute-start.8
  87.3 3.6 %collective-permute-start.9 = (f32[32,8,128]{2,1,0:T(8,128)S(1)}, f32[32,8,128]{2,1,0:T(8,128)S(1)}, u32[]{:S(2)}, u32[]{:S(2)}) collective-permute-start(f32[32,8,128]{2,1,0:T(8,128)S(1)} %get-tuple-element.58), channel_id=1, source_target_pairs={{1,0},{2,1},{3,2},{4,3},{5,4},{6,5},{7,6},{0,7},{9,8},{10,9},{11,1... | collective-permute-start | bytes 393224 | tf_op jit(solution)/shard_map/ppermute | solution.py:364
  90.9 2.7 %collective-permute-done.8.rest_0_ = f32[32,8,128]{2,1,0:T(8,128)S(1)} collective-permute-done((f32[32,8,128]{2,1,0:T(8,128)S(1)}, f32[32,8,128]{2,1,0:T(8,128)S(1)}, u32[]{:S(2)}, u32[]{:S(2)}) %collective-permute-start.8) | collective-permute-done | bytes 131104 | tf_op jit(solution)/shard_map/ppermute | solution.py:364
  93.6 4.5 %shard_map.115 = (f32[64,32,128]{2,1,0:T(8,128)S(1)}, f32[64,32,128]{2,1,0:T(8,128)S(1)}, f32[32,8,128]{2,1,0:T(8,128)S(1)}, f32[32,8,128]{2,1,0:T(8,128)S(1)}) custom-call(s32[7]{0:T(128)S(1)} %stack.50.spots, f32[1]{0:T(128)} %bitcast.23.amount, f32[64,32,128]{2,1,0:T(8,128)S(1)} %get-tuple-element.56.now.prev.wave, ...), custom_call_target="tpu_custom_call" | custom-call | flops 10485760 | bytes 6291456 | tf_op jit(solution)/shard_map/pallas_call | solution.py:412
  98.0 0.1 collective-permute-start.10
  98.2 3.5 %collective-permute-start.11 = (f32[32,8,128]{2,1,0:T(8,128)S(1)}, f32[32,8,128]{2,1,0:T(8,128)S(1)}, u32[]{:S(2)}, u32[]{:S(2)}) collective-permute-start(f32[32,8,128]{2,1,0:T(8,128)S(1)} %get-tuple-element.61), channel_id=1, source_target_pairs={{1,0},{2,1},{3,2},{4,3},{5,4},{6,5},{7,6},{0,7},{9,8},{10,9},{11,1... | collective-permute-start | bytes 393224 | tf_op jit(solution)/shard_map/ppermute | solution.py:364
  101.7 2.7 %shard_map.112 = (f32[32,8,128]{2,1,0:T(8,128)S(1)}, f32[32,8,128]{2,1,0:T(8,128)S(1)}) custom-call(f32[8,8,136,128]{3,2,1,0:T(8,128)} %all-to-all-done.turned.now.prev.late.later, f32[8,8,32,128]{3,2,1,0:T(8,128)S(1)} %shard_map.111.r2), custom_call_target="tpu_custom_call" | custom-call | bytes 1048576 | tf_op jit(solution)/shard_map/pallas_call | solution.py:427
  104.4 0.1 collective-permute-start.6
  104.5 3.6 %collective-permute-start.7 = (f32[32,8,128]{2,1,0:T(8,128)S(1)}, f32[32,8,128]{2,1,0:T(8,128)S(1)}, u32[]{:S(2)}, u32[]{:S(2)}) collective-permute-start(f32[32,8,128]{2,1,0:T(8,128)S(1)} %get-tuple-element.53), channel_id=1, source_target_pairs={{1,0},{2,1},{3,2},{4,3},{5,4},{6,5},{7,6},{0,7},{9,8},{10,9},{11,1... | collective-permute-start | bytes 393224 | tf_op jit(solution)/shard_map/ppermute | solution.py:364
  108.0 2.8 %shard_map.116 = (f32[64,32,128]{2,1,0:T(8,128)S(1)}, f32[64,32,128]{2,1,0:T(8,128)S(1)}, f32[32,8,128]{2,1,0:T(8,128)S(1)}, f32[32,8,128]{2,1,0:T(8,128)S(1)}) custom-call(s32[7]{0:T(128)S(1)} %stack.50.spots, f32[1]{0:T(128)} %bitcast.22.amount, f32[64,32,128]{2,1,0:T(8,128)S(1)} %get-tuple-element.59.now.prev.wave, ...), custom_call_target="tpu_custom_call" | custom-call | flops 10485760 | bytes 6291456 | tf_op jit(solution)/shard_map/pallas_call | solution.py:412
  110.9 0.1 collective-permute-start.12
  110.9 3.6 %collective-permute-start.13 = (f32[32,8,128]{2,1,0:T(8,128)S(1)}, f32[32,8,128]{2,1,0:T(8,128)S(1)}, u32[]{:S(2)}, u32[]{:S(2)}) collective-permute-start(f32[32,8,128]{2,1,0:T(8,128)S(1)} %get-tuple-element.64), channel_id=1, source_target_pairs={{1,0},{2,1},{3,2},{4,3},{5,4},{6,5},{7,6},{0,7},{9,8},{10,9},{11,1... | collective-permute-start | bytes 393224 | tf_op jit(solution)/shard_map/ppermute | solution.py:364
  114.5 5.1 %shard_map.113 = (f32[64,32,128]{2,1,0:T(8,128)S(1)}, f32[64,32,128]{2,1,0:T(8,128)S(1)}, f32[64,32,128]{2,1,0:T(8,128)S(1)}, f32[64,32,128]{2,1,0:T(8,128)S(1)}, f32[64,32,128]{2,1,0:T(8,128)S(1)}) custom-call(s32[256]{0:T(256)S(1)} %bitcast.45, s32[256]{0:T(256)S(1)} %compare_convert_fusion.mine, f32[4,256]{1,0:T(4,128)S(1)} %bitcast.43), custom_call_target="tpu_custom_call" | custom-call | bytes 6291456 | tf_op jit(solution)/shard_map/pallas_call | solution.py:403
  119.7 2.6 %shard_map.117 = (f32[64,32,128]{2,1,0:T(8,128)S(1)}, f32[64,32,128]{2,1,0:T(8,128)S(1)}) custom-call(s32[7]{0:T(128)S(1)} %stack.50.spots, f32[1]{0:T(128)} %bitcast.21.amount, f32[64,32,128]{2,1,0:T(8,128)S(1)} %get-tuple-element.62.now.wave, f32[64,32,128]{2,1,0:T(8,128)S(1)} %get-tuple-element.59.now.prev.wave, f32[8,8,32,128]{3,2,1,0:T(8,128)S(1)} %shard_map.111.r2, ...), custom_call_target="tpu_custom_call" | custom-call | flops 10485760 | bytes 6291456 | tf_op jit(solution)/shard_map/pallas_call | solution.py:412
  122.3 6.0 %shard_map.118 = (f32[64,32,128]{2,1,0:T(8,128)S(1)}, f32[64,32,128]{2,1,0:T(8,128)S(1)}, f32[32,8,128]{2,1,0:T(8,128)S(1)}, f32[32,8,128]{2,1,0:T(8,128)S(1)}) custom-call(s32[7]{0:T(128)S(1)} %stack.50.spots, f32[8,8,136,128]{3,2,1,0:T(8,128)} %all-to-all-done.turned.now.prev.late.later, f32[8,8,136,128]{3,2,1,0:T(8,128)} %all-to-all-done.turned.now.prev.late.later, ...), custom_call_target="tpu_custom_call" | custom-call | flops 10485760 | bytes 8388608 | tf_op jit(solution)/shard_map/pallas_call | solution.py:438
  128.4 3.6 %collective-permute-start.15 = (f32[32,8,128]{2,1,0:T(8,128)S(1)}, f32[32,8,128]{2,1,0:T(8,128)S(1)}, u32[]{:S(2)}, u32[]{:S(2)}) collective-permute-start(f32[32,8,128]{2,1,0:T(8,128)S(1)} %get-tuple-element.69), channel_id=1, source_target_pairs={{1,0},{2,1},{3,2},{4,3},{5,4},{6,5},{7,6},{0,7},{9,8},{10,9},{11,1... | collective-permute-start | bytes 393224 | tf_op jit(solution)/shard_map/ppermute | solution.py:364
  132.0 2.4 %collective-permute-done.14.halo_lo = f32[32,8,128]{2,1,0:T(8,128)S(1)} collective-permute-done((f32[32,8,128]{2,1,0:T(8,128)S(1)}, f32[32,8,128]{2,1,0:T(8,128)S(1)}, u32[]{:S(2)}, u32[]{:S(2)}) %collective-permute-start.14) | collective-permute-done | bytes 131104 | tf_op jit(solution)/shard_map/ppermute | solution.py:364
  134.3 4.7 %shard_map.119 = (f32[64,32,128]{2,1,0:T(8,128)S(1)}, f32[64,32,128]{2,1,0:T(8,128)S(1)}, f32[32,8,128]{2,1,0:T(8,128)S(1)}, f32[32,8,128]{2,1,0:T(8,128)S(1)}) custom-call(s32[7]{0:T(128)S(1)} %stack.50.spots, f32[64,32,128]{2,1,0:T(8,128)S(1)} %get-tuple-element.67.late.later, f32[8,8,136,128]{3,2,1,0:T(8,128)} %all-to-all-done.turned.now.prev.late.later, ...), custom_call_target="tpu_custom_call" | custom-call | flops 10485760 | bytes 8388608 | tf_op jit(solution)/shard_map/pallas_call | solution.py:438
  139.1 3.6 %collective-permute-start.17 = (f32[32,8,128]{2,1,0:T(8,128)S(1)}, f32[32,8,128]{2,1,0:T(8,128)S(1)}, u32[]{:S(2)}, u32[]{:S(2)}) collective-permute-start(f32[32,8,128]{2,1,0:T(8,128)S(1)} %get-tuple-element.75), channel_id=1, source_target_pairs={{1,0},{2,1},{3,2},{4,3},{5,4},{6,5},{7,6},{0,7},{9,8},{10,9},{11,1... | collective-permute-start | bytes 393224 | tf_op jit(solution)/shard_map/ppermute | solution.py:364
  142.8 2.3 %collective-permute-done.16.halo_lo = f32[32,8,128]{2,1,0:T(8,128)S(1)} collective-permute-done((f32[32,8,128]{2,1,0:T(8,128)S(1)}, f32[32,8,128]{2,1,0:T(8,128)S(1)}, u32[]{:S(2)}, u32[]{:S(2)}) %collective-permute-start.16) | collective-permute-done | bytes 131104 | tf_op jit(solution)/shard_map/ppermute | solution.py:364
  145.1 3.1 %shard_map.120 = (f32[64,32,128]{2,1,0:T(8,128)S(1)}, f32[64,32,128]{2,1,0:T(8,128)S(1)}, f32[32,8,128]{2,1,0:T(8,128)S(1)}, f32[32,8,128]{2,1,0:T(8,128)S(1)}) custom-call(s32[7]{0:T(128)S(1)} %stack.50.spots, f32[64,32,128]{2,1,0:T(8,128)S(1)} %get-tuple-element.73.late.later, f32[64,32,128]{2,1,0:T(8,128)S(1)} %get-tuple-element.67.late.later, ...), custom_call_target="tpu_custom_call" | custom-call | flops 10485760 | bytes 8388608 | tf_op jit(solution)/shard_map/pallas_call | solution.py:438
  148.2 0.9 collective-permute-start.18
  149.1 2.9 %collective-permute-start.19 = (f32[32,8,128]{2,1,0:T(8,128)S(1)}, f32[32,8,128]{2,1,0:T(8,128)S(1)}, u32[]{:S(2)}, u32[]{:S(2)}) collective-permute-start(f32[32,8,128]{2,1,0:T(8,128)S(1)} %get-tuple-element.81), channel_id=1, source_target_pairs={{1,0},{2,1},{3,2},{4,3},{5,4},{6,5},{7,6},{0,7},{9,8},{10,9},{11,1... | collective-permute-start | bytes 393224 | tf_op jit(solution)/shard_map/ppermute | solution.py:364
  152.0 2.3 %collective-permute-done.18.halo_lo = f32[32,8,128]{2,1,0:T(8,128)S(1)} collective-permute-done((f32[32,8,128]{2,1,0:T(8,128)S(1)}, f32[32,8,128]{2,1,0:T(8,128)S(1)}, u32[]{:S(2)}, u32[]{:S(2)}) %collective-permute-start.18) | collective-permute-done | bytes 131104 | tf_op jit(solution)/shard_map/ppermute | solution.py:364
  154.2 3.7 %shard_map.121 = f32[8,8,32,128]{3,2,1,0:T(8,128)} custom-call(s32[7]{0:T(128)S(1)} %stack.50.spots, f32[64,32,128]{2,1,0:T(8,128)S(1)} %get-tuple-element.79.late, f32[64,32,128]{2,1,0:T(8,128)S(1)} %get-tuple-element.73.late.later, f32[8,8,32,128]{3,2,1,0:T(8,128)S(1)} %shard_map.111.r2, f32[32,8,128]{2,1,0:T(8,128)S(1)} %collective-permute-done.18.halo_lo, ...), custom_call_target="tpu_custom_call" | custom-call | flops 10485760 | bytes 8388608 | tf_op jit(solution)/shard_map/pallas_call | solution.py:438
  158.0 10.9 %all-to-all-start.1 = ((f32[8,8,32,128]{3,2,1,0:T(8,128)}), f32[8,8,32,128]{3,2,1,0:T(8,128)S(1)}, u32[]{:S(2)}, u32[]{:S(2)}) async-start(f32[8,8,32,128]{3,2,1,0:T(8,128)} %shard_map.121), calls=%async_computation.1 | async-start | bytes 2097152 | tf_op jit(solution)/shard_map/all_to_all | solution.py:451
  168.9 0.6 gather_fusion
  169.6 14.4 %all-to-all-done.1.recv = f32[8,8,32,128]{3,2,1,0:T(8,128)S(1)} async-done(((f32[8,8,32,128]{3,2,1,0:T(8,128)}), f32[8,8,32,128]{3,2,1,0:T(8,128)S(1)}, u32[]{:S(2)}, u32[]{:S(2)}) %all-to-all-start.1) | async-done | bytes 1048608 | tf_op jit(solution)/shard_map/all_to_all | solution.py:451
  184.0 0.8 shard_map.122
  184.8 2.5 %collective-permute-start.20 = (f32[2,8,32,128]{3,2,1,0:T(8,128)S(1)}, f32[2,8,32,128]{3,2,1,0:T(8,128)S(1)}, u32[]{:S(2)}, u32[]{:S(2)}) collective-permute-start(f32[2,8,32,128]{3,2,1,0:T(8,128)S(1)} %get-tuple-element.86), channel_id=1, source_target_pairs={{0,64},{8,72},{16,80},{24,88},{32,96},{40,104},{48,112},{56,120},{... | collective-permute-start | bytes 786440 | tf_op jit(solution)/shard_map/ppermute | solution.py:455
  187.2 6.1 %collective-permute-done.20 = f32[2,8,32,128]{3,2,1,0:T(8,128)S(1)} collective-permute-done((f32[2,8,32,128]{3,2,1,0:T(8,128)S(1)}, f32[2,8,32,128]{3,2,1,0:T(8,128)S(1)}, u32[]{:S(2)}, u32[]{:S(2)}) %collective-permute-start.20) | collective-permute-done | bytes 262176 | tf_op jit(solution)/shard_map/ppermute | solution.py:455
  193.3 0.7 add_bitcast_fusion
  (40 shorter events, 0.5 us)
Async XLA Ops:
  0.0 12.8 %collective-permute-start.1 = (f32[2,8,32,128]{3,2,1,0:T(8,128)}, f32[2,8,32,128]{3,2,1,0:T(8,128)S(1)}, u32[]{:S(2)}, u32[]{:S(2)}) collective-permute-start(f32[2,8,32,128]{3,2,1,0:T(8,128)} %bitcast.40), channel_id=1, source_target_pairs={{0,8},{8,0},{16,24},{24,16},{32,40},{40,32},{48,56},{56,48},{64,72... | collective-permute-start | bytes 786440 | tf_op jit(solution)/shard_map/ppermute | solution.py:368
  1.4 9.7 %collective-permute-start = (f32[2,8,32,128]{3,2,1,0:T(8,128)}, f32[2,8,32,128]{3,2,1,0:T(8,128)S(1)}, u32[]{:S(2)}, u32[]{:S(2)}) collective-permute-start(f32[2,8,32,128]{3,2,1,0:T(8,128)} %bitcast.41), channel_id=1, source_target_pairs={{0,64},{8,72},{16,80},{24,88},{32,96},{40,104},{48,112},{56,120},{... | collective-permute-start | bytes 786440 | tf_op jit(solution)/shard_map/ppermute | solution.py:367
  11.1 1.9 %collective-permute-start.2 = (f32[2,8,32,128]{3,2,1,0:T(8,128)S(1)}, f32[2,8,32,128]{3,2,1,0:T(8,128)S(1)}, u32[]{:S(2)}, u32[]{:S(2)}) collective-permute-start(f32[2,8,32,128]{3,2,1,0:T(8,128)S(1)} %collective-permute-done.other), channel_id=1, source_target_pairs={{0,8},{8,0},{16,24},{24,16},{32,40},{40,32},{48,56},{56,48},{64,72... | collective-permute-start | bytes 786440 | tf_op jit(solution)/shard_map/ppermute | solution.py:369
  13.0 0.9 copy-start.6
  14.8 9.1 %collective-permute-start.3 = (f32[2,8,32,128]{3,2,1,0:T(8,128)S(1)}, f32[2,8,32,128]{3,2,1,0:T(8,128)S(1)}, u32[]{:S(2)}, u32[]{:S(2)}) collective-permute-start(f32[2,8,32,128]{3,2,1,0:T(8,128)S(1)} %get-tuple-element.46), channel_id=1, source_target_pairs={{0,16},{8,24},{16,32},{24,40},{32,48},{40,56},{48,0},{56,8},{64,80... | collective-permute-start | bytes 786440 | tf_op jit(solution)/shard_map/ppermute | solution.py:377
  16.3 1.2 copy-start.2
  17.5 1.2 copy-start.3
  18.7 1.2 copy-start.4
  20.0 1.2 copy-start.5
  21.5 2.1 %copy-start = (f32[8,8,136,128]{3,2,1,0:T(8,128)}, f32[8,8,136,128]{3,2,1,0:T(8,128)S(1)}, u32[]{:S(2)}) copy-start(f32[8,8,136,128]{3,2,1,0:T(8,128)S(1)} %shard_map.109) | copy-start | bytes 13369348
  23.6 11.2 %copy-start.9 = (f32[1,4]{1,0:T(1,128)S(1)}, f32[1,4]{1,0:T(1,128)}, u32[]{:S(2)}) copy-start(f32[1,4]{1,0:T(1,128)} %param.16) | copy-start | bytes 52
  23.6 57.7 %copy-start.1 = (bf16[256,256]{1,0:T(8,128)(2,1)S(1)}, bf16[256,256]{1,0:T(8,128)(2,1)}, u32[]{:S(2)}) copy-start(bf16[256,256]{1,0:T(8,128)(2,1)} %constant.207.clone.oper) | copy-start | bytes 393220
  23.9 57.4 %all-to-all-start = ((f32[8,8,136,128]{3,2,1,0:T(8,128)}), f32[8,8,136,128]{3,2,1,0:T(8,128)}, u32[]{:S(2)}, u32[]{:S(2)}) async-start(f32[8,8,136,128]{3,2,1,0:T(8,128)} %copy-done), calls=%async_computation | async-start | bytes 8912896 | tf_op jit(solution)/shard_map/all_to_all | solution.py:385
  31.2 8.0 %collective-permute-start.4 = (f32[2,8,32,128]{3,2,1,0:T(8,128)S(1)}, f32[2,8,32,128]{3,2,1,0:T(8,128)S(1)}, u32[]{:S(2)}, u32[]{:S(2)}) collective-permute-start(f32[2,8,32,128]{3,2,1,0:T(8,128)S(1)} %get-tuple-element.50), channel_id=1, source_target_pairs={{0,32},{8,40},{16,48},{24,56},{32,0},{40,8},{48,16},{56,24},{64,96... | collective-permute-start | bytes 786440 | tf_op jit(solution)/shard_map/ppermute | solution.py:377
  33.8 10.8 %collective-permute-start.5 = (f32[2,8,32,128]{3,2,1,0:T(8,128)S(1)}, f32[2,8,32,128]{3,2,1,0:T(8,128)S(1)}, u32[]{:S(2)}, u32[]{:S(2)}) collective-permute-start(f32[2,8,32,128]{3,2,1,0:T(8,128)S(1)} %get-tuple-element.51), channel_id=1, source_target_pairs={{0,48},{8,56},{16,0},{24,8},{32,16},{40,24},{48,32},{56,40},{64,11... | collective-permute-start | bytes 786440 | tf_op jit(solution)/shard_map/ppermute | solution.py:377
  87.2 6.3 %collective-permute-start.8 = (f32[32,8,128]{2,1,0:T(8,128)S(1)}, f32[32,8,128]{2,1,0:T(8,128)S(1)}, u32[]{:S(2)}, u32[]{:S(2)}) collective-permute-start(f32[32,8,128]{2,1,0:T(8,128)S(1)} %get-tuple-element.57), channel_id=1, source_target_pairs={{0,1},{1,2},{2,3},{3,4},{4,5},{5,6},{6,7},{7,0},{8,9},{9,10},{10,1... | collective-permute-start | bytes 393224 | tf_op jit(solution)/shard_map/ppermute | solution.py:364
  87.3 6.3 %collective-permute-start.9 = (f32[32,8,128]{2,1,0:T(8,128)S(1)}, f32[32,8,128]{2,1,0:T(8,128)S(1)}, u32[]{:S(2)}, u32[]{:S(2)}) collective-permute-start(f32[32,8,128]{2,1,0:T(8,128)S(1)} %get-tuple-element.58), channel_id=1, source_target_pairs={{1,0},{2,1},{3,2},{4,3},{5,4},{6,5},{7,6},{0,7},{9,8},{10,9},{11,1... | collective-permute-start | bytes 393224 | tf_op jit(solution)/shard_map/ppermute | solution.py:364
  98.0 10.0 %collective-permute-start.10 = (f32[32,8,128]{2,1,0:T(8,128)S(1)}, f32[32,8,128]{2,1,0:T(8,128)S(1)}, u32[]{:S(2)}, u32[]{:S(2)}) collective-permute-start(f32[32,8,128]{2,1,0:T(8,128)S(1)} %get-tuple-element.60), channel_id=1, source_target_pairs={{0,1},{1,2},{2,3},{3,4},{4,5},{5,6},{6,7},{7,0},{8,9},{9,10},{10,1... | collective-permute-start | bytes 393224 | tf_op jit(solution)/shard_map/ppermute | solution.py:364
  98.1 16.4 %copy-start.8 = (s32[1,256]{1,0:T(1,128)S(1)}, s32[1,256]{1,0:T(1,128)}, u32[]{:S(2)}) copy-start(s32[1,256]{1,0:T(1,128)} %param.18) | copy-start | bytes 3076
  98.1 16.4 %copy-start.7 = (f32[1,4,256]{2,1,0:T(4,128)S(1)}, f32[1,4,256]{2,1,0:T(4,128)}, u32[]{:S(2)}) copy-start(f32[1,4,256]{2,1,0:T(4,128)} %param.19) | copy-start | bytes 12292
  98.2 9.9 %collective-permute-start.11 = (f32[32,8,128]{2,1,0:T(8,128)S(1)}, f32[32,8,128]{2,1,0:T(8,128)S(1)}, u32[]{:S(2)}, u32[]{:S(2)}) collective-permute-start(f32[32,8,128]{2,1,0:T(8,128)S(1)} %get-tuple-element.61), channel_id=1, source_target_pairs={{1,0},{2,1},{3,2},{4,3},{5,4},{6,5},{7,6},{0,7},{9,8},{10,9},{11,1... | collective-permute-start | bytes 393224 | tf_op jit(solution)/shard_map/ppermute | solution.py:364
  104.4 17.9 %collective-permute-start.6 = (f32[32,8,128]{2,1,0:T(8,128)S(1)}, f32[32,8,128]{2,1,0:T(8,128)S(1)}, u32[]{:S(2)}, u32[]{:S(2)}) collective-permute-start(f32[32,8,128]{2,1,0:T(8,128)S(1)} %get-tuple-element.52), channel_id=1, source_target_pairs={{0,1},{1,2},{2,3},{3,4},{4,5},{5,6},{6,7},{7,0},{8,9},{9,10},{10,1... | collective-permute-start | bytes 393224 | tf_op jit(solution)/shard_map/ppermute | solution.py:364
  104.5 17.8 %collective-permute-start.7 = (f32[32,8,128]{2,1,0:T(8,128)S(1)}, f32[32,8,128]{2,1,0:T(8,128)S(1)}, u32[]{:S(2)}, u32[]{:S(2)}) collective-permute-start(f32[32,8,128]{2,1,0:T(8,128)S(1)} %get-tuple-element.53), channel_id=1, source_target_pairs={{1,0},{2,1},{3,2},{4,3},{5,4},{6,5},{7,6},{0,7},{9,8},{10,9},{11,1... | collective-permute-start | bytes 393224 | tf_op jit(solution)/shard_map/ppermute | solution.py:364
  110.9 8.8 %collective-permute-start.12 = (f32[32,8,128]{2,1,0:T(8,128)S(1)}, f32[32,8,128]{2,1,0:T(8,128)S(1)}, u32[]{:S(2)}, u32[]{:S(2)}) collective-permute-start(f32[32,8,128]{2,1,0:T(8,128)S(1)} %get-tuple-element.63), channel_id=1, source_target_pairs={{0,1},{1,2},{2,3},{3,4},{4,5},{5,6},{6,7},{7,0},{8,9},{9,10},{10,1... | collective-permute-start | bytes 393224 | tf_op jit(solution)/shard_map/ppermute | solution.py:364
  110.9 8.7 %collective-permute-start.13 = (f32[32,8,128]{2,1,0:T(8,128)S(1)}, f32[32,8,128]{2,1,0:T(8,128)S(1)}, u32[]{:S(2)}, u32[]{:S(2)}) collective-permute-start(f32[32,8,128]{2,1,0:T(8,128)S(1)} %get-tuple-element.64), channel_id=1, source_target_pairs={{1,0},{2,1},{3,2},{4,3},{5,4},{6,5},{7,6},{0,7},{9,8},{10,9},{11,1... | collective-permute-start | bytes 393224 | tf_op jit(solution)/shard_map/ppermute | solution.py:364
  128.3 6.0 %collective-permute-start.14 = (f32[32,8,128]{2,1,0:T(8,128)S(1)}, f32[32,8,128]{2,1,0:T(8,128)S(1)}, u32[]{:S(2)}, u32[]{:S(2)}) collective-permute-start(f32[32,8,128]{2,1,0:T(8,128)S(1)} %get-tuple-element.68), channel_id=1, source_target_pairs={{0,1},{1,2},{2,3},{3,4},{4,5},{5,6},{6,7},{7,0},{8,9},{9,10},{10,1... | collective-permute-start | bytes 393224 | tf_op jit(solution)/shard_map/ppermute | solution.py:364
  128.4 5.9 %collective-permute-start.15 = (f32[32,8,128]{2,1,0:T(8,128)S(1)}, f32[32,8,128]{2,1,0:T(8,128)S(1)}, u32[]{:S(2)}, u32[]{:S(2)}) collective-permute-start(f32[32,8,128]{2,1,0:T(8,128)S(1)} %get-tuple-element.69), channel_id=1, source_target_pairs={{1,0},{2,1},{3,2},{4,3},{5,4},{6,5},{7,6},{0,7},{9,8},{10,9},{11,1... | collective-permute-start | bytes 393224 | tf_op jit(solution)/shard_map/ppermute | solution.py:364
  139.1 6.0 %collective-permute-start.16 = (f32[32,8,128]{2,1,0:T(8,128)S(1)}, f32[32,8,128]{2,1,0:T(8,128)S(1)}, u32[]{:S(2)}, u32[]{:S(2)}) collective-permute-start(f32[32,8,128]{2,1,0:T(8,128)S(1)} %get-tuple-element.74), channel_id=1, source_target_pairs={{0,1},{1,2},{2,3},{3,4},{4,5},{5,6},{6,7},{7,0},{8,9},{9,10},{10,1... | collective-permute-start | bytes 393224 | tf_op jit(solution)/shard_map/ppermute | solution.py:364
  139.1 5.9 %collective-permute-start.17 = (f32[32,8,128]{2,1,0:T(8,128)S(1)}, f32[32,8,128]{2,1,0:T(8,128)S(1)}, u32[]{:S(2)}, u32[]{:S(2)}) collective-permute-start(f32[32,8,128]{2,1,0:T(8,128)S(1)} %get-tuple-element.75), channel_id=1, source_target_pairs={{1,0},{2,1},{3,2},{4,3},{5,4},{6,5},{7,6},{0,7},{9,8},{10,9},{11,1... | collective-permute-start | bytes 393224 | tf_op jit(solution)/shard_map/ppermute | solution.py:364
  148.2 6.1 %collective-permute-start.18 = (f32[32,8,128]{2,1,0:T(8,128)S(1)}, f32[32,8,128]{2,1,0:T(8,128)S(1)}, u32[]{:S(2)}, u32[]{:S(2)}) collective-permute-start(f32[32,8,128]{2,1,0:T(8,128)S(1)} %get-tuple-element.80), channel_id=1, source_target_pairs={{0,1},{1,2},{2,3},{3,4},{4,5},{5,6},{6,7},{7,0},{8,9},{9,10},{10,1... | collective-permute-start | bytes 393224 | tf_op jit(solution)/shard_map/ppermute | solution.py:364
  149.1 5.2 %collective-permute-start.19 = (f32[32,8,128]{2,1,0:T(8,128)S(1)}, f32[32,8,128]{2,1,0:T(8,128)S(1)}, u32[]{:S(2)}, u32[]{:S(2)}) collective-permute-start(f32[32,8,128]{2,1,0:T(8,128)S(1)} %get-tuple-element.81), channel_id=1, source_target_pairs={{1,0},{2,1},{3,2},{4,3},{5,4},{6,5},{7,6},{0,7},{9,8},{10,9},{11,1... | collective-permute-start | bytes 393224 | tf_op jit(solution)/shard_map/ppermute | solution.py:364
  158.0 26.0 %all-to-all-start.1 = ((f32[8,8,32,128]{3,2,1,0:T(8,128)}), f32[8,8,32,128]{3,2,1,0:T(8,128)S(1)}, u32[]{:S(2)}, u32[]{:S(2)}) async-start(f32[8,8,32,128]{3,2,1,0:T(8,128)} %shard_map.121), calls=%async_computation.1 | async-start | bytes 2097152 | tf_op jit(solution)/shard_map/all_to_all | solution.py:451
  184.8 8.5 %collective-permute-start.20 = (f32[2,8,32,128]{3,2,1,0:T(8,128)S(1)}, f32[2,8,32,128]{3,2,1,0:T(8,128)S(1)}, u32[]{:S(2)}, u32[]{:S(2)}) collective-permute-start(f32[2,8,32,128]{3,2,1,0:T(8,128)S(1)} %get-tuple-element.86), channel_id=1, source_target_pairs={{0,64},{8,72},{16,80},{24,88},{32,96},{40,104},{48,112},{56,120},{... | collective-permute-start | bytes 786440 | tf_op jit(solution)/shard_map/ppermute | solution.py:455

commit v3 on v2

--- a/solution.py
+++ b/solution.py
@@ -15,6 +15,7 @@
 BF16 = jnp.bfloat16
 SMEM = pl.BlockSpec(memory_space=pltpu.SMEM)
 VMEM = pl.BlockSpec(memory_space=pltpu.VMEM)
+ANY = pl.BlockSpec(memory_space=pltpu.HBM)
 NX, NYL, NZ = 64, 32, 128
 GROUP = 8
 PAD = 4
@@ -34,12 +35,6 @@
     low = (band - high.astype(np.float32)).astype(ml_dtypes.bfloat16)
     zero = np.zeros_like(high)
     return np.block([[high, low], [high, zero]])
-
-
-def read_field(ref, off, g, xi, rows):
-    if off is None:
-        return ref[g * GROUP + xi, rows, :]
-    return ref[g, xi, off + rows.start : off + rows.stop, :]
 
 
 def clear_ends(ext):
@@ -101,31 +96,16 @@
     lax.fori_loop(0, NX // 2, body, 0, unroll=4)
 
 
-EVERY = slice(0, NYL)
-
-
-def forward_kernel(off_now, off_prev, last, spots, amount, now, prev, r2, oper, *rest):
-    rest = list(rest)
-    halos = None if off_now is not None else (rest.pop(0), rest.pop(0))
-    if last:
-        lap, new, ext, depth = rest
-    else:
-        lap, new, send_lo, send_hi, ext, depth = rest
-
-    clear_ends(ext)
-
-    def copy(g, carry):
-        for xi in range(GROUP):
-            ext[PAD + g * GROUP + xi, ROW0 : ROW0 + NYL, :] = read_field(now, off_now, g, xi, EVERY)
-            if halos is None:
-                edge = now[g, xi, EDGES : EDGES + 8, :]
-                ext[PAD + g * GROUP + xi, ROW0 - 4 : ROW0, :] = edge[0:4]
-                ext[PAD + g * GROUP + xi, ROW0 + NYL : ROW0 + NYL + 4, :] = edge[4:8]
-        return carry
-
-    lax.fori_loop(0, NX // GROUP, copy, 0)
-    if halos is not None:
-        fill_edges(ext, spots, *halos)
+def add_source(spots, amount, new):
+    @pl.when(spots[1] == 1)
+    def _():
+        x, y, z = spots[2], spots[3], spots[4]
+        lanes = lax.broadcasted_iota(jnp.int32, (1, NZ), 1)
+        row = new[x, pl.ds(y, 1), :]
+        new[x, pl.ds(y, 1), :] = row + jnp.where(lanes == z, amount[0], 0.0)
+
+
+def advance(ext, depth, oper, prev, r2, lap, new):
     apply_depth(ext, oper, depth)
 
     def body(g, carry):
@@ -134,34 +114,67 @@
             x = g * GROUP + xi
             lap[x, rows, :] = value
             here = ext[PAD + x, ROW0 + 8 * j : ROW0 + 8 * j + 8, :]
-            new[x, rows, :] = 2.0 * here - read_field(prev, off_prev, g, xi, rows) + r2[g, xi, rows, :] * value
+            new[x, rows, :] = 2.0 * here - prev[x, rows, :] + r2[x, rows, :] * value
 
         laplace_group(ext, depth, g, emit)
         return carry
 
     lax.fori_loop(0, NX // GROUP, body, 0)
 
-    @pl.when(spots[1] == 1)
-    def _():
-        x, y, z = spots[2], spots[3], spots[4]
-        lanes = lax.broadcasted_iota(jnp.int32, (1, NZ), 1)
-        row = new[x, pl.ds(y, 1), :]
-        new[x, pl.ds(y, 1), :] = row + jnp.where(lanes == z, amount[0], 0.0)
-
+
+OWN_X, OWN_Y = slice(PAD, PAD + NX), slice(ROW0, ROW0 + NYL)
+
+
+def first_kernel(
+    spots, amount, turned, r2, oper, lap, new, send_lo, send_hi, now, late, later, ext, depth, prev, edge, sems
+):
+    def take(n, off, rows, dst):
+        return pltpu.make_async_copy(turned.at[:, off : off + rows, :], dst, sems.at[n])
+
+    copies = [
+        take(0, NOW, NYL, ext.at[OWN_X, OWN_Y, :]),
+        take(1, EDGES, 8, edge),
+        take(2, PREV, NYL, prev),
+        take(3, LATE, NYL, late),
+        take(4, LATER, NYL, later),
+        take(5, NOW, NYL, now),
+    ]
+    for c in copies:
+        c.start()
+    clear_ends(ext)
+    for c in copies[:3]:
+        c.wait()
+
+    def fill(x, carry):
+        ext[PAD + x, ROW0 - 4 : ROW0, :] = edge[x, 0:4, :]
+        ext[PAD + x, ROW0 + NYL : ROW0 + NYL + 4, :] = edge[x, 4:8, :]
+        return carry
+
+    lax.fori_loop(0, NX, fill, 0, unroll=4)
+    advance(ext, depth, oper, prev, r2, lap, new)
+    add_source(spots, amount, new)
+    send_rows(send_lo.at[0], send_hi.at[0], lambda x, rows: new[x, rows, :])
+    for c in copies[3:]:
+        c.wait()
+    send_rows(send_lo.at[1], send_hi.at[1], lambda x, rows: late[x, rows, :] * r2[x, rows, :])
+
+
+def forward_kernel(last, spots, amount, now, prev, r2, oper, halo_lo, halo_hi, *rest):
+    if last:
+        lap, new, ext, depth = rest
+    else:
+        lap, new, send_lo, send_hi, ext, depth = rest
+    clear_ends(ext)
+    ext[OWN_X, OWN_Y, :] = now[...]
+    fill_edges(ext, spots, halo_lo.at[0], halo_hi.at[0])
+    advance(ext, depth, oper, prev, r2, lap, new)
+    add_source(spots, amount, new)
     if not last:
-        send_rows(send_lo, send_hi, lambda x, rows: new[x, rows, :])
-
-
-def edge_kernel(turned, r2, send_lo, send_hi):
-    def read(x, rows):
-        g, xi = x // GROUP, lax.rem(x, GROUP)
-        return read_field(turned, LATE, g, xi, rows) * r2[g, xi, rows, :]
-
-    send_rows(send_lo, send_hi, read)
+        send_rows(send_lo.at[0], send_hi.at[0], lambda x, rows: new[x, rows, :])
 
 
 def adjoint_kernel(
-    off_late, off_later, begin, last, spots, late, later, r2, halo_lo, halo_hi, oper, count, data, wave, lap, *rest
+    begin, last, spots, late, later, r2, halo_lo, halo_hi, oper, count, data, wave, lap, *rest
 ):
     rest = list(rest)
     total_in = None if begin else rest.pop(0)
@@ -173,15 +186,9 @@
 
     clear_ends(ext)
 
-    def copy(g, carry):
-        for xi in range(GROUP):
-            ext[PAD + g * GROUP + xi, ROW0 : ROW0 + NYL, :] = (
-                read_field(late, off_late, g, xi, EVERY) * r2[g, xi]
-            )
-        return carry
-
-    lax.fori_loop(0, NX // GROUP, copy, 0)
-    fill_edges(ext, spots, halo_lo, halo_hi)
+    ext[OWN_X, OWN_Y, :] = late[...] * r2[...]
+    which = 1 if begin else 0
+    fill_edges(ext, spots, halo_lo.at[which], halo_hi.at[which])
     apply_depth(ext, oper, depth)
 
     def body(g, carry):
@@ -190,7 +197,7 @@
         def emit(xi, j, value):
             rows = slice(8 * j, 8 * j + 8)
             x = g * GROUP + xi
-            mu = 2.0 * read_field(late, off_late, g, xi, rows) + value - read_field(later, off_later, g, xi, rows)
+            mu = 2.0 * late[x, rows, :] + value - later[x, rows, :]
             mu = mu + (count[x, rows, :] * wave[x, rows, :] - data[x, rows, :])
             part = mu * lap[x, rows, :]
             if total_in is not None:
@@ -206,29 +213,41 @@
 
     lax.fori_loop(0, NX // GROUP, body, 0)
     if not last:
-
-        def read(x, rows):
-            return new[x, rows, :] * r2[x // GROUP, lax.rem(x, GROUP), rows, :]
-
-        send_rows(send_lo, send_hi, read)
+        send_rows(send_lo.at[0], send_hi.at[0], lambda x, rows: new[x, rows, :] * r2[x, rows, :])
 
 
 NOW, PREV, LATE, LATER, EDGES, TURNED = 0, 32, 64, 96, 128, 136
 
 
-def pack_kernel(now, prev, late, later, out):
+def pack_kernel(now, prev, late, later, out, near, edge, sems):
+    bring = pltpu.make_async_copy(now, near, sems.at[32])
+    bring.start()
+    copies = []
+    for p in range(8):
+        for f, (off, field) in enumerate(((NOW, now), (PREV, prev), (LATE, late), (LATER, later))):
+            copies.append(
+                pltpu.make_async_copy(
+                    field.at[:, NYL * p : NYL * p + NYL, :], out.at[p, :, off : off + NYL, :], sems.at[4 * p + f]
+                )
+            )
+    for c in copies:
+        c.start()
     none = jnp.zeros((4, NZ), F32)
+    bring.wait()
 
     def body(xi, carry):
         for p in range(8):
             lo = NYL * p
-            for off, field in ((NOW, now), (PREV, prev), (LATE, late), (LATER, later)):
-                out[p, xi, off : off + NYL, :] = field[xi, lo : lo + NYL, :]
-            out[p, xi, EDGES : EDGES + 4, :] = now[xi, lo - 4 : lo, :] if p > 0 else none
-            out[p, xi, EDGES + 4 : EDGES + 8, :] = now[xi, lo + NYL : lo + NYL + 4, :] if p < 7 else none
+            edge[p, xi, 0:4, :] = near[xi, lo - 4 : lo, :] if p > 0 else none
+            edge[p, xi, 4:8, :] = near[xi, lo + NYL : lo + NYL + 4, :] if p < 7 else none
         return carry
 
     lax.fori_loop(0, GROUP, body, 0)
+    ends = pltpu.make_async_copy(edge, out.at[:, :, EDGES : EDGES + 8, :], sems.at[33])
+    ends.start()
+    for c in copies:
+        c.wait()
+    ends.wait()
 
 
 def copy_block(dst, src):
@@ -313,18 +332,19 @@
 
 
 FIELD = jax.ShapeDtypeStruct((NX, NYL, NZ), F32)
-EDGE = jax.ShapeDtypeStruct((NX // 2, 8, NZ), F32)
+EDGE = jax.ShapeDtypeStruct((1, NX // 2, 8, NZ), F32)
+EDGE2 = jax.ShapeDtypeStruct((2, NX // 2, 8, NZ), F32)
 BLOCKS = jax.ShapeDtypeStruct((8, GROUP, NYL, NZ), F32)
 PAIR = jax.ShapeDtypeStruct((2, GROUP, NYL, NZ), F32)
 SCRATCH = [pltpu.VMEM((NX + 2 * PAD, ROWS, NZ), F32), pltpu.VMEM((NX, NYL, NZ), F32)]
 PARAMS = pltpu.CompilerParams(vmem_limit_bytes=14 * 1024 * 1024)
 
 
-def call(kernel, specs, outs, scratch=(), flops=0, moved=0):
+def call(kernel, specs, outs, scratch=(), flops=0, moved=0, out_spec=VMEM):
     return pl.pallas_call(
         kernel,
         in_specs=specs,
-        out_specs=[VMEM] * len(outs),
+        out_specs=[out_spec] * len(outs),
         out_shape=outs,
         scratch_shapes=list(scratch),
         compiler_params=PARAMS,
@@ -378,12 +398,18 @@
     from_class = ((row - ahead) % 4 * 2)[:, None] + two[None, :]
     places = ((from_class - first) % 8).reshape(8).astype(jnp.int32)
 
-    (packed,) = call(pack_kernel, [VMEM] * 4, [jax.ShapeDtypeStruct((8, GROUP, TURNED, NZ), F32)], moved=8 << 20)(
-        wave_now[0], wave_prev[0], adj_late[0], adj_later[0]
-    )
-    packed, come[1] = lax.optimization_barrier((packed, come[1]))
-    turned = lax.all_to_all(packed, "sub", 0, 0, tiled=True)
+    (packed,) = call(
+        pack_kernel,
+        [ANY] * 4,
+        [jax.ShapeDtypeStruct((8, GROUP, TURNED, NZ), F32)],
+        [pltpu.VMEM((GROUP, 256, NZ), F32), pltpu.VMEM((8, GROUP, 8, NZ), F32), pltpu.SemaphoreType.DMA((34,))],
+        moved=8 << 20,
+        out_spec=ANY,
+    )(wave_now[0], wave_prev[0], adj_late[0], adj_later[0])
+    packed, other = lax.optimization_barrier((packed, other))
+    turned = lax.all_to_all(packed, "sub", 0, 0, tiled=True).reshape(NX, TURNED, NZ)
     (r2,) = call(assemble_kernel, [SMEM] + [VMEM] * 4, [BLOCKS], moved=2 << 20)(places, *come)
+    r2 = r2.reshape(NX, NYL, NZ)
 
     cell = sources[0]
     line = (cell // NZ) % 256
@@ -402,15 +428,25 @@
     mine = ((cells // NZ) % 256 // NYL == part).astype(jnp.int32)
     count, *datas = call(receivers_kernel, [SMEM] * 3, [FIELD] * 5, moved=6 << 20)(cells, mine, observed[0])
 
-    laps, fields = [], []
-    now, prev = turned, turned
-    offs = (NOW, PREV)
-    halo = ()
-    for step in range(STEPS):
+    r2, count = lax.optimization_barrier((r2, count))
+
+    lap, new, *more = call(
+        first_kernel,
+        [SMEM, SMEM, ANY, VMEM, VMEM],
+        [FIELD, FIELD, EDGE2, EDGE2, FIELD, FIELD, FIELD],
+        SCRATCH + [pltpu.VMEM((NX, NYL, NZ), F32), pltpu.VMEM((NX, 8, NZ), F32), pltpu.SemaphoreType.DMA((6,))],
+        flops=10 << 20,
+        moved=8 << 20,
+    )(spots, wavelet[0, 0:1], turned, r2, oper)
+    send, (prev, late, later) = more[:2], more[2:]
+    laps, fields = [lap], [new]
+    now = new
+    halo = held = edges(*send)
+    for step in range(1, STEPS):
         last = step == STEPS - 1
         args = [spots, wavelet[0, step : step + 1], now, prev, r2, oper, *halo]
         lap, new, *send = call(
-            functools.partial(forward_kernel, *offs, last),
+            functools.partial(forward_kernel, last),
             [SMEM, SMEM] + [VMEM] * (len(args) - 2),
             [FIELD, FIELD] + ([] if last else [EDGE, EDGE]),
             SCRATCH,
@@ -420,23 +456,19 @@
         laps.append(lap)
         fields.append(new)
         now, prev = new, now
-        offs = (None, offs[0])
         if not last:
             halo = edges(*send)
 
-    send = call(edge_kernel, [VMEM, VMEM], [EDGE] * 2, moved=1 << 20)(turned, r2)
-    late, later = turned, turned
-    offs = (LATE, LATER)
+    halo = held
     total = None
     for step in range(STEPS, 0, -1):
-        halo = edges(*send)
         begin, last = step == STEPS, step == 1
         outs = [BLOCKS] if last else [FIELD, FIELD, EDGE, EDGE]
         args = [spots, late, later, r2, *halo, oper, count, datas[step - 1], fields[step - 1], laps[step - 1]]
         if not begin:
             args.append(total)
         total, *more = call(
-            functools.partial(adjoint_kernel, *offs, begin, last),
+            functools.partial(adjoint_kernel, begin, last),
             [SMEM] + [VMEM] * (len(args) - 1),
             outs,
             SCRATCH,
@@ -445,8 +477,7 @@
         )(*args)
         if not last:
             late, later = more[0], late
-            offs = (None, offs[0])
-            send = more[1:]
+            halo = edges(*more[1:])
 
     recv = lax.all_to_all(total, "shot", 0, 0, axis_index_groups=halves, tiled=True)
     group = starts[half * 8 + jnp.arange(8)]

time: 195 us -> 171 us (0.88)
  waiting for transfers between devices: 78.9 us -> 63.2 us
  Pallas kernels: 43.7 us -> 33.9 us
  local copies, waits for them, and re-layouts: 11.6 us -> 18.6 us
  starting transfers between devices: 55 us -> 50.3 us
    all_to_all x1, waiting for transfers between devices: 36.1 us -> 23.8 us  [per_device(): lax.all_to_all(packed, 'sub', 0, 0, tiled=True).reshape(NX, TURNED, NZ)]
    pallas_call x10 -> x9, Pallas kernels: 36.3 us -> 25.8 us  [the longest x4 11.9 us: per_device(): call(functools.partial(adjoint_kernel, begin, last), [SMEM] + [VMEM] * (l...]
    ppermute x14 -> x12, waiting for transfers between devices: 9.62 us -> 17.4 us  [edges(): return (lax.ppermute(hi, 'sub', up), lax.ppermute(lo, 'sub', down))]
    unnamed x20 -> x44, local copies, waits for them, and re-layouts: 7.96 us -> 15 us
    ppermute x3, waiting for transfers between devices: 6.46 us -> 0.01 us  [per_device(): lax.ppermute(blocks[k], 'shot', along(k))]
    ppermute x1, waiting for transfers between devices: 6.09 us -> 0.01 us  [per_device(): other = lax.ppermute(piece, 'shot', across)]
    ppermute x14 -> x12, starting transfers between devices: 25.7 us -> 22.4 us  [edges(): return (lax.ppermute(hi, 'sub', up), lax.ppermute(lo, 'sub', down))]
  transfers between devices with their start and end apart: 23 -> 21, of which waited for: 12 -> 10; matrix products, arithmetic and copies ran while one was open for 2% -> 3% of each run, Pallas kernels for 7% -> 5%
where the time goes in v3:
time: 171 us; the launch traced here: 170 us
  waiting for transfers between devices  63.2 us (37%)
  starting transfers between devices  50.3 us (29%)
  Pallas kernels  33.9 us (20%)
  local copies, waits for them, and re-layouts  18.6 us (11%)
  between operations  2.91 us (2%)
    all_to_all x1, waiting for transfers between devices, per_device(): lax.all_to_all(packed, 'sub', 0, 0, tiled=True).reshape(NX, TURNED, NZ)  23.8 us
    ppermute x12, starting transfers between devices, edges(): return (lax.ppermute(hi, 'sub', up), lax.ppermute(lo, 'sub', down))  22.4 us
    ppermute x12, waiting for transfers between devices, edges(): return (lax.ppermute(hi, 'sub', up), lax.ppermute(lo, 'sub', down))  17.4 us
    unnamed x44, local copies, waits for them, and re-layouts  15 us
    all_to_all x1, waiting for transfers between devices, per_device(): lax.all_to_all(total, 'shot', 0, 0, axis_index_groups=halves, tiled=True)  14.4 us
    pallas_call x4, Pallas kernels, per_device(): call(functools.partial(adjoint_kernel, begin, last), [SMEM] + [VMEM] * (l...  11.9 us
    all_to_all x1, starting transfers between devices, per_device(): lax.all_to_all(total, 'shot', 0, 0, axis_index_groups=halves, tiled=True)  11.6 us
    pallas_call x3, Pallas kernels, per_device(): call(functools.partial(forward_kernel, last), [SMEM, SMEM] + [VMEM] * (le...  8.21 us
  transfers between devices with their start and end apart: 21, of which 10 were waited for; matrix products, arithmetic and copies ran while one was open for 3% of the time, Pallas kernels for 5%

profile of v3, /device:TPU:1, one launch (start us, length us, event | category | flops | bytes accessed | tf_op | source)
XLA Modules:
  0.0 170.4 jit_solution(6598468121785811723)
XLA Ops:
  0.0 3.6 %collective-permute-start = (f32[2,8,32,128]{3,2,1,0:T(8,128)}, f32[2,8,32,128]{3,2,1,0:T(8,128)S(1)}, u32[]{:S(2)}, u32[]{:S(2)}) collective-permute-start(f32[2,8,32,128]{3,2,1,0:T(8,128)} %bitcast.50), channel_id=1, source_target_pairs={{0,64},{8,72},{16,80},{24,88},{32,96},{40,104},{48,112},{56,120},{... | collective-permute-start | bytes 786440 | tf_op jit(solution)/shard_map/ppermute | solution.py:387
  3.6 1.2 copy-done.2
  4.8 1.2 copy-done.3
  6.0 1.2 copy-done.4
  7.3 1.2 copy-done.5
  8.5 1.2 shard_map.109
  9.7 2.1 %copy-done = f32[8,8,136,128]{3,2,1,0:T(8,128)} copy-done((f32[8,8,136,128]{3,2,1,0:T(8,128)}, f32[8,8,136,128]{3,2,1,0:T(8,128)S(1)}, u32[]{:S(2)}) %copy-start) | copy-done | bytes 4456472
  11.8 5.2 %all-to-all-start = ((f32[8,8,136,128]{3,2,1,0:T(8,128)}), f32[8,8,136,128]{3,2,1,0:T(8,128)}, u32[]{:S(2)}, u32[]{:S(2)}) async-start(f32[8,8,136,128]{3,2,1,0:T(8,128)} %copy-done), calls=%async_computation | async-start | bytes 8912896 | tf_op jit(solution)/shard_map/all_to_all | solution.py:410
  17.1 1.3 collective-permute-start.1
  18.4 0.1 sub.91
  18.5 0.7 fusion.14
  19.2 0.6 gather_fusion.1
  19.9 0.1 add.214
  20.1 0.2 collective-permute-start.2
  20.3 0.6 constant_dynamic-slice_fusion
  20.9 0.7 add_subtract_fusion
  21.7 1.7 %shard_map.110 = (f32[2,8,32,128]{3,2,1,0:T(8,128)S(1)}, f32[2,8,32,128]{3,2,1,0:T(8,128)}, f32[2,8,32,128]{3,2,1,0:T(8,128)}, f32[2,8,32,128]{3,2,1,0:T(8,128)}) custom-call(s32[8]{0:T(128)S(1)} %and_select_fusion.3.slots, s32[2]{0:T(128)S(1)} %pad_add_fusion.here, f32[2,8,32,128]{3,2,1,0:T(8,128)S(1)} %bitcast.52, ...), custom_call_target="tpu_custom_call" | custom-call | bytes 2097152 | tf_op jit(solution)/shard_map/pallas_call | solution.py:396
  23.4 1.3 collective-permute-start.3
  24.7 2.6 %collective-permute-start.4 = (f32[2,8,32,128]{3,2,1,0:T(8,128)}, f32[2,8,32,128]{3,2,1,0:T(8,128)S(1)}, u32[]{:S(2)}, u32[]{:S(2)}) collective-permute-start(f32[2,8,32,128]{3,2,1,0:T(8,128)} %get-tuple-element.51), channel_id=1, source_target_pairs={{0,32},{8,40},{16,48},{24,56},{32,0},{40,8},{48,16},{56,24},{64,96... | collective-permute-start | bytes 786440 | tf_op jit(solution)/shard_map/ppermute | solution.py:397
  27.3 1.1 collective-permute-start.5
  28.4 0.6 fusion.15
  31.7 0.1 sub.88
  31.7 4.9 %shard_map.112 = (f32[64,32,128]{2,1,0:T(8,128)S(1)}, f32[64,32,128]{2,1,0:T(8,128)S(1)}, f32[64,32,128]{2,1,0:T(8,128)S(1)}, f32[64,32,128]{2,1,0:T(8,128)S(1)}, f32[64,32,128]{2,1,0:T(8,128)S(1)}) custom-call(s32[256]{0:T(256)S(1)} %bitcast.55, s32[256]{0:T(256)S(1)} %compare_convert_fusion.mine, f32[4,256]{1,0:T(4,128)S(1)} %bitcast.53), custom_call_target="tpu_custom_call" | custom-call | bytes 6291456 | tf_op jit(solution)/shard_map/pallas_call | solution.py:429
  36.7 1.0 copy-done.6
  37.7 1.0 copy-done.8
  38.7 1.0 copy-done.10
  39.7 0.1 stack.50.spots
  39.8 0.7 copy-done.13
  40.5 0.7 copy-done.15
  41.2 0.7 copy-done.17
  41.9 0.9 copy-done.14
  42.9 0.9 copy-done.16
  43.8 0.9 copy-done.18
  44.8 0.7 shard_map.111
  45.4 23.8 %all-to-all-done = f32[8,8,136,128]{3,2,1,0:T(8,128)} async-done(((f32[8,8,136,128]{3,2,1,0:T(8,128)}), f32[8,8,136,128]{3,2,1,0:T(8,128)}, u32[]{:S(2)}, u32[]{:S(2)}) %all-to-all-start) | async-done | bytes 4456480 | tf_op jit(solution)/shard_map/all_to_all | solution.py:410
  69.3 4.4 %shard_map.113 = (f32[64,32,128]{2,1,0:T(8,128)S(1)}, f32[64,32,128]{2,1,0:T(8,128)S(1)}, f32[2,32,8,128]{3,2,1,0:T(8,128)S(1)}, f32[2,32,8,128]{3,2,1,0:T(8,128...) custom-call(s32[7]{0:T(128)S(1)} %stack.50.spots, f32[1]{0:T(128)} %bitcast.12.amount, ...), custom_call_target="tpu_custom_call" | custom-call | flops 10485760 | bytes 8388608 | tf_op jit(solution)/shard_map/pallas_call | solution.py:433
  73.7 0.4 collective-permute-start.6
  74.1 3.3 %collective-permute-start.7 = (f32[2,32,8,128]{3,2,1,0:T(8,128)S(1)}, f32[2,32,8,128]{3,2,1,0:T(8,128)S(1)}, u32[]{:S(2)}, u32[]{:S(2)}) collective-permute-start(f32[2,32,8,128]{3,2,1,0:T(8,128)S(1)} %get-tuple-element.58), channel_id=1, source_target_pairs={{1,0},{2,1},{3,2},{4,3},{5,4},{6,5},{7,6},{0,7},{9,8},{10,9},{11,1... | collective-permute-start | bytes 786440 | tf_op jit(solution)/shard_map/ppermute | solution.py:384
  77.3 5.9 %collective-permute-done.6.halo_lo = f32[2,32,8,128]{3,2,1,0:T(8,128)S(1)} collective-permute-done((f32[2,32,8,128]{3,2,1,0:T(8,128)S(1)}, f32[2,32,8,128]{3,2,1,0:T(8,128)S(1)}, u32[]{:S(2)}, u32[]{:S(2)}) %collective-permute-start.6) | collective-permute-done | bytes 262176 | tf_op jit(solution)/shard_map/ppermute | solution.py:384
  83.3 2.7 %shard_map.114 = (f32[64,32,128]{2,1,0:T(8,128)S(1)}, f32[64,32,128]{2,1,0:T(8,128)S(1)}, f32[1,32,8,128]{3,2,1,0:T(8,128)S(1)}, f32[1,32,8,128]{3,2,1,0:T(8,128)S(1)}) custom-call(s32[7]{0:T(128)S(1)} %stack.50.spots, f32[1]{0:T(128)} %bitcast.26.amount, f32[64,32,128]{2,1,0:T(8,128)S(1)} %get-tuple-element.61.now.prev.wave, ...), custom_call_target="tpu_custom_call" | custom-call | flops 10485760 | bytes 6291456 | tf_op jit(solution)/shard_map/pallas_call | solution.py:448
  86.1 3.6 %collective-permute-start.9 = (f32[1,32,8,128]{3,2,1,0:T(8,128)S(1)}, f32[1,32,8,128]{3,2,1,0:T(8,128)S(1)}, u32[]{:S(2)}, u32[]{:S(2)}) collective-permute-start(f32[1,32,8,128]{3,2,1,0:T(8,128)S(1)} %get-tuple-element.65), channel_id=1, source_target_pairs={{1,0},{2,1},{3,2},{4,3},{5,4},{6,5},{7,6},{0,7},{9,8},{10,9},{11,1... | collective-permute-start | bytes 393224 | tf_op jit(solution)/shard_map/ppermute | solution.py:384
  89.6 2.4 %collective-permute-done.8.halo_lo = f32[1,32,8,128]{3,2,1,0:T(8,128)S(1)} collective-permute-done((f32[1,32,8,128]{3,2,1,0:T(8,128)S(1)}, f32[1,32,8,128]{3,2,1,0:T(8,128)S(1)}, u32[]{:S(2)}, u32[]{:S(2)}) %collective-permute-start.8) | collective-permute-done | bytes 131104 | tf_op jit(solution)/shard_map/ppermute | solution.py:384
  92.0 2.8 %shard_map.115 = (f32[64,32,128]{2,1,0:T(8,128)S(1)}, f32[64,32,128]{2,1,0:T(8,128)S(1)}, f32[1,32,8,128]{3,2,1,0:T(8,128)S(1)}, f32[1,32,8,128]{3,2,1,0:T(8,128)S(1)}) custom-call(s32[7]{0:T(128)S(1)} %stack.50.spots, f32[1]{0:T(128)} %bitcast.25.amount, f32[64,32,128]{2,1,0:T(8,128)S(1)} %get-tuple-element.63.now.prev.wave, ...), custom_call_target="tpu_custom_call" | custom-call | flops 10485760 | bytes 6291456 | tf_op jit(solution)/shard_map/pallas_call | solution.py:448
  94.9 3.6 %collective-permute-start.11 = (f32[1,32,8,128]{3,2,1,0:T(8,128)S(1)}, f32[1,32,8,128]{3,2,1,0:T(8,128)S(1)}, u32[]{:S(2)}, u32[]{:S(2)}) collective-permute-start(f32[1,32,8,128]{3,2,1,0:T(8,128)S(1)} %get-tuple-element.68), channel_id=1, source_target_pairs={{1,0},{2,1},{3,2},{4,3},{5,4},{6,5},{7,6},{0,7},{9,8},{10,9},{11,1... | collective-permute-start | bytes 393224 | tf_op jit(solution)/shard_map/ppermute | solution.py:384
  98.6 2.3 %collective-permute-done.10.halo_lo = f32[1,32,8,128]{3,2,1,0:T(8,128)S(1)} collective-permute-done((f32[1,32,8,128]{3,2,1,0:T(8,128)S(1)}, f32[1,32,8,128]{3,2,1,0:T(8,128)S(1)}, u32[]{:S(2)}, u32[]{:S(2)}) %collective-permute-start.10) | collective-permute-done | bytes 131104 | tf_op jit(solution)/shard_map/ppermute | solution.py:384
  100.8 2.7 %shard_map.116 = (f32[64,32,128]{2,1,0:T(8,128)S(1)}, f32[64,32,128]{2,1,0:T(8,128)S(1)}) custom-call(s32[7]{0:T(128)S(1)} %stack.50.spots, f32[1]{0:T(128)} %bitcast.24.amount, f32[64,32,128]{2,1,0:T(8,128)S(1)} %get-tuple-element.66.now.wave, f32[64,32,128]{2,1,0:T(8,128)S(1)} %get-tuple-element.63.now.prev.wave, f32[64,32,128]{2,1,0:T(8,128)S(1)} %bitcast.41, ...), custom_call_target="tpu_custom_call" | custom-call | flops 10485760 | bytes 6291456 | tf_op jit(solution)/shard_map/pallas_call | solution.py:448
  103.5 2.7 %shard_map.117 = (f32[64,32,128]{2,1,0:T(8,128)S(1)}, f32[64,32,128]{2,1,0:T(8,128)S(1)}, f32[1,32,8,128]{3,2,1,0:T(8,128)S(1)}, f32[1,32,8,128]{3,2,1,0:T(8,128)S(1)}) custom-call(s32[7]{0:T(128)S(1)} %stack.50.spots, f32[64,32,128]{2,1,0:T(8,128)S(1)} %get-tuple-element.55.late.later, f32[64,32,128]{2,1,0:T(8,128)S(1)} %get-tuple-element.56.later, ...), custom_call_target="tpu_custom_call" | custom-call | flops 10485760 | bytes 8388608 | tf_op jit(solution)/shard_map/pallas_call | solution.py:470
  106.2 0.1 collective-permute-start.12
  106.3 3.7 %collective-permute-start.13 = (f32[1,32,8,128]{3,2,1,0:T(8,128)S(1)}, f32[1,32,8,128]{3,2,1,0:T(8,128)S(1)}, u32[]{:S(2)}, u32[]{:S(2)}) collective-permute-start(f32[1,32,8,128]{3,2,1,0:T(8,128)S(1)} %get-tuple-element.73), channel_id=1, source_target_pairs={{1,0},{2,1},{3,2},{4,3},{5,4},{6,5},{7,6},{0,7},{9,8},{10,9},{11,1... | collective-permute-start | bytes 393224 | tf_op jit(solution)/shard_map/ppermute | solution.py:384
  110.0 2.3 %collective-permute-done.12.halo_lo = f32[1,32,8,128]{3,2,1,0:T(8,128)S(1)} collective-permute-done((f32[1,32,8,128]{3,2,1,0:T(8,128)S(1)}, f32[1,32,8,128]{3,2,1,0:T(8,128)S(1)}, u32[]{:S(2)}, u32[]{:S(2)}) %collective-permute-start.12) | collective-permute-done | bytes 131104 | tf_op jit(solution)/shard_map/ppermute | solution.py:384
  112.3 2.7 %shard_map.118 = (f32[64,32,128]{2,1,0:T(8,128)S(1)}, f32[64,32,128]{2,1,0:T(8,128)S(1)}, f32[1,32,8,128]{3,2,1,0:T(8,128)S(1)}, f32[1,32,8,128]{3,2,1,0:T(8,128)S(1)}) custom-call(s32[7]{0:T(128)S(1)} %stack.50.spots, f32[64,32,128]{2,1,0:T(8,128)S(1)} %get-tuple-element.71.late.later, f32[64,32,128]{2,1,0:T(8,128)S(1)} %get-tuple-element.55.late.later, ...), custom_call_target="tpu_custom_call" | custom-call | flops 10485760 | bytes 8388608 | tf_op jit(solution)/shard_map/pallas_call | solution.py:470
  115.2 3.7 %collective-permute-start.15 = (f32[1,32,8,128]{3,2,1,0:T(8,128)S(1)}, f32[1,32,8,128]{3,2,1,0:T(8,128)S(1)}, u32[]{:S(2)}, u32[]{:S(2)}) collective-permute-start(f32[1,32,8,128]{3,2,1,0:T(8,128)S(1)} %get-tuple-element.79), channel_id=1, source_target_pairs={{1,0},{2,1},{3,2},{4,3},{5,4},{6,5},{7,6},{0,7},{9,8},{10,9},{11,1... | collective-permute-start | bytes 393224 | tf_op jit(solution)/shard_map/ppermute | solution.py:384
  118.9 2.3 %collective-permute-done.14.halo_lo = f32[1,32,8,128]{3,2,1,0:T(8,128)S(1)} collective-permute-done((f32[1,32,8,128]{3,2,1,0:T(8,128)S(1)}, f32[1,32,8,128]{3,2,1,0:T(8,128)S(1)}, u32[]{:S(2)}, u32[]{:S(2)}) %collective-permute-start.14) | collective-permute-done | bytes 131104 | tf_op jit(solution)/shard_map/ppermute | solution.py:384
  121.1 2.7 %shard_map.119 = (f32[64,32,128]{2,1,0:T(8,128)S(1)}, f32[64,32,128]{2,1,0:T(8,128)S(1)}, f32[1,32,8,128]{3,2,1,0:T(8,128)S(1)}, f32[1,32,8,128]{3,2,1,0:T(8,128)S(1)}) custom-call(s32[7]{0:T(128)S(1)} %stack.50.spots, f32[64,32,128]{2,1,0:T(8,128)S(1)} %get-tuple-element.77.late.later, f32[64,32,128]{2,1,0:T(8,128)S(1)} %get-tuple-element.71.late.later, ...), custom_call_target="tpu_custom_call" | custom-call | flops 10485760 | bytes 8388608 | tf_op jit(solution)/shard_map/pallas_call | solution.py:470
  124.0 3.7 %collective-permute-start.17 = (f32[1,32,8,128]{3,2,1,0:T(8,128)S(1)}, f32[1,32,8,128]{3,2,1,0:T(8,128)S(1)}, u32[]{:S(2)}, u32[]{:S(2)}) collective-permute-start(f32[1,32,8,128]{3,2,1,0:T(8,128)S(1)} %get-tuple-element.85), channel_id=1, source_target_pairs={{1,0},{2,1},{3,2},{4,3},{5,4},{6,5},{7,6},{0,7},{9,8},{10,9},{11,1... | collective-permute-start | bytes 393224 | tf_op jit(solution)/shard_map/ppermute | solution.py:384
  127.7 2.3 %collective-permute-done.16.halo_lo = f32[1,32,8,128]{3,2,1,0:T(8,128)S(1)} collective-permute-done((f32[1,32,8,128]{3,2,1,0:T(8,128)S(1)}, f32[1,32,8,128]{3,2,1,0:T(8,128)S(1)}, u32[]{:S(2)}, u32[]{:S(2)}) %collective-permute-start.16) | collective-permute-done | bytes 131104 | tf_op jit(solution)/shard_map/ppermute | solution.py:384
  130.0 3.7 %shard_map.120 = f32[8,8,32,128]{3,2,1,0:T(8,128)} custom-call(s32[7]{0:T(128)S(1)} %stack.50.spots, f32[64,32,128]{2,1,0:T(8,128)S(1)} %get-tuple-element.83.late, f32[64,32,128]{2,1,0:T(8,128)S(1)} %get-tuple-element.77.late.later, f32[64,32,128]{2,1,0:T(8,128)S(1)} %bitcast.45, f32[1,32,8,128]{3,2,1,0:T(8,128)S(1)} %collective-permute-done.16.halo_lo, ...), custom_call_target="tpu_custom_call" | custom-call | flops 10485760 | bytes 8388608 | tf_op jit(solution)/shard_map/pallas_call | solution.py:470
  133.7 11.6 %all-to-all-start.1 = ((f32[8,8,32,128]{3,2,1,0:T(8,128)}), f32[8,8,32,128]{3,2,1,0:T(8,128)S(1)}, u32[]{:S(2)}, u32[]{:S(2)}) async-start(f32[8,8,32,128]{3,2,1,0:T(8,128)} %shard_map.120), calls=%async_computation.1 | async-start | bytes 2097152 | tf_op jit(solution)/shard_map/all_to_all | solution.py:482
  145.3 0.6 gather_fusion
  145.9 14.4 %all-to-all-done.1.recv = f32[8,8,32,128]{3,2,1,0:T(8,128)S(1)} async-done(((f32[8,8,32,128]{3,2,1,0:T(8,128)}), f32[8,8,32,128]{3,2,1,0:T(8,128)S(1)}, u32[]{:S(2)}, u32[]{:S(2)}) %all-to-all-start.1) | async-done | bytes 1048608 | tf_op jit(solution)/shard_map/all_to_all | solution.py:482
  160.4 0.8 shard_map.121
  161.2 1.1 collective-permute-start.18
  162.3 7.4 %collective-permute-done.18 = f32[2,8,32,128]{3,2,1,0:T(8,128)S(1)} collective-permute-done((f32[2,8,32,128]{3,2,1,0:T(8,128)S(1)}, f32[2,8,32,128]{3,2,1,0:T(8,128)S(1)}, u32[]{:S(2)}, u32[]{:S(2)}) %collective-permute-start.18) | collective-permute-done | bytes 262176 | tf_op jit(solution)/shard_map/ppermute | solution.py:486
  169.7 0.7 add_bitcast_fusion
  (59 shorter events, 0.7 us)
Async XLA Ops:
  0.0 11.8 %collective-permute-start = (f32[2,8,32,128]{3,2,1,0:T(8,128)}, f32[2,8,32,128]{3,2,1,0:T(8,128)S(1)}, u32[]{:S(2)}, u32[]{:S(2)}) collective-permute-start(f32[2,8,32,128]{3,2,1,0:T(8,128)} %bitcast.50), channel_id=1, source_target_pairs={{0,64},{8,72},{16,80},{24,88},{32,96},{40,104},{48,112},{56,120},{... | collective-permute-start | bytes 786440 | tf_op jit(solution)/shard_map/ppermute | solution.py:387
  3.6 1.2 copy-start.2
  4.8 1.2 copy-start.3
  6.0 1.2 copy-start.4
  7.2 1.2 copy-start.5
  9.7 2.1 %copy-start = (f32[8,8,136,128]{3,2,1,0:T(8,128)}, f32[8,8,136,128]{3,2,1,0:T(8,128)S(1)}, u32[]{:S(2)}) copy-start(f32[8,8,136,128]{3,2,1,0:T(8,128)S(1)} %shard_map.109) | copy-start | bytes 13369348
  11.8 5.2 %copy-start.12 = (f32[2,1,8,32,128]{4,3,2,1,0:T(8,128)S(1)}, f32[2,1,8,32,128]{4,3,2,1,0:T(8,128)}, u32[]{:S(2)}) copy-start(f32[2,1,8,32,128]{4,3,2,1,0:T(8,128)} %param.11) | copy-start | bytes 786436
  11.8 8.2 %copy-start.20 = (s32[1,256]{1,0:T(1,128)S(1)}, s32[1,256]{1,0:T(1,128)}, u32[]{:S(2)}) copy-start(s32[1,256]{1,0:T(1,128)} %param.18) | copy-start | bytes 3076
  11.8 16.6 %copy-start.21 = (f32[1,4]{1,0:T(1,128)S(1)}, f32[1,4]{1,0:T(1,128)}, u32[]{:S(2)}) copy-start(f32[1,4]{1,0:T(1,128)} %param.16) | copy-start | bytes 52
  11.8 19.9 %copy-start.19 = (f32[1,4,256]{2,1,0:T(4,128)S(1)}, f32[1,4,256]{2,1,0:T(4,128)}, u32[]{:S(2)}) copy-start(f32[1,4,256]{2,1,0:T(4,128)} %param.19) | copy-start | bytes 12292
  11.8 57.5 %copy-start.1 = (bf16[256,256]{1,0:T(8,128)(2,1)S(1)}, bf16[256,256]{1,0:T(8,128)(2,1)}, u32[]{:S(2)}) copy-start(bf16[256,256]{1,0:T(8,128)(2,1)} %constant.207.clone.oper) | copy-start | bytes 393220
  11.8 57.4 %all-to-all-start = ((f32[8,8,136,128]{3,2,1,0:T(8,128)}), f32[8,8,136,128]{3,2,1,0:T(8,128)}, u32[]{:S(2)}, u32[]{:S(2)}) async-start(f32[8,8,136,128]{3,2,1,0:T(8,128)} %copy-done), calls=%async_computation | async-start | bytes 8912896 | tf_op jit(solution)/shard_map/all_to_all | solution.py:410
  17.1 4.5 %collective-permute-start.1 = (f32[2,8,32,128]{3,2,1,0:T(8,128)S(1)}, f32[2,8,32,128]{3,2,1,0:T(8,128)S(1)}, u32[]{:S(2)}, u32[]{:S(2)}) collective-permute-start(f32[2,8,32,128]{3,2,1,0:T(8,128)S(1)} %bitcast.51), channel_id=1, source_target_pairs={{0,8},{8,0},{16,24},{24,16},{32,40},{40,32},{48,56},{56,48},{64,72... | collective-permute-start | bytes 786440 | tf_op jit(solution)/shard_map/ppermute | solution.py:388
  20.1 1.6 collective-permute-start.2
  23.4 16.4 %collective-permute-start.3 = (f32[2,8,32,128]{3,2,1,0:T(8,128)}, f32[2,8,32,128]{3,2,1,0:T(8,128)S(1)}, u32[]{:S(2)}, u32[]{:S(2)}) collective-permute-start(f32[2,8,32,128]{3,2,1,0:T(8,128)} %get-tuple-element.50), channel_id=1, source_target_pairs={{0,16},{8,24},{16,32},{24,40},{32,48},{40,56},{48,0},{56,8},{64,80... | collective-permute-start | bytes 786440 | tf_op jit(solution)/shard_map/ppermute | solution.py:397
  24.7 15.8 %collective-permute-start.4 = (f32[2,8,32,128]{3,2,1,0:T(8,128)}, f32[2,8,32,128]{3,2,1,0:T(8,128)S(1)}, u32[]{:S(2)}, u32[]{:S(2)}) collective-permute-start(f32[2,8,32,128]{3,2,1,0:T(8,128)} %get-tuple-element.51), channel_id=1, source_target_pairs={{0,32},{8,40},{16,48},{24,56},{32,0},{40,8},{48,16},{56,24},{64,96... | collective-permute-start | bytes 786440 | tf_op jit(solution)/shard_map/ppermute | solution.py:397
  27.3 13.9 %collective-permute-start.5 = (f32[2,8,32,128]{3,2,1,0:T(8,128)}, f32[2,8,32,128]{3,2,1,0:T(8,128)S(1)}, u32[]{:S(2)}, u32[]{:S(2)}) collective-permute-start(f32[2,8,32,128]{3,2,1,0:T(8,128)} %get-tuple-element.52), channel_id=1, source_target_pairs={{0,48},{8,56},{16,0},{24,8},{32,16},{40,24},{48,32},{56,40},{64,11... | collective-permute-start | bytes 786440 | tf_op jit(solution)/shard_map/ppermute | solution.py:397
  36.7 1.0 copy-start.6
  37.7 1.0 copy-start.8
  38.7 1.0 copy-start.10
  39.8 0.7 copy-start.13
  40.5 0.7 copy-start.15
  41.2 0.7 copy-start.17
  41.9 0.9 copy-start.14
  42.9 0.9 copy-start.16
  43.8 0.9 copy-start.18
  73.7 9.6 %collective-permute-start.6 = (f32[2,32,8,128]{3,2,1,0:T(8,128)S(1)}, f32[2,32,8,128]{3,2,1,0:T(8,128)S(1)}, u32[]{:S(2)}, u32[]{:S(2)}) collective-permute-start(f32[2,32,8,128]{3,2,1,0:T(8,128)S(1)} %get-tuple-element.57), channel_id=1, source_target_pairs={{0,1},{1,2},{2,3},{3,4},{4,5},{5,6},{6,7},{7,0},{8,9},{9,10},{10,1... | collective-permute-start | bytes 786440 | tf_op jit(solution)/shard_map/ppermute | solution.py:384
  74.1 9.2 %collective-permute-start.7 = (f32[2,32,8,128]{3,2,1,0:T(8,128)S(1)}, f32[2,32,8,128]{3,2,1,0:T(8,128)S(1)}, u32[]{:S(2)}, u32[]{:S(2)}) collective-permute-start(f32[2,32,8,128]{3,2,1,0:T(8,128)S(1)} %get-tuple-element.58), channel_id=1, source_target_pairs={{1,0},{2,1},{3,2},{4,3},{5,4},{6,5},{7,6},{0,7},{9,8},{10,9},{11,1... | collective-permute-start | bytes 786440 | tf_op jit(solution)/shard_map/ppermute | solution.py:384
  86.0 17.5 %copy-start.11 = (f32[64,32,128]{2,1,0:T(8,128)S(1)}, f32[64,32,128]{2,1,0:T(8,128)}, u32[]{:S(2)}) copy-start(f32[64,32,128]{2,1,0:T(8,128)} %copy-done.10) | copy-start | bytes 3145732
  86.0 6.0 %collective-permute-start.8 = (f32[1,32,8,128]{3,2,1,0:T(8,128)S(1)}, f32[1,32,8,128]{3,2,1,0:T(8,128)S(1)}, u32[]{:S(2)}, u32[]{:S(2)}) collective-permute-start(f32[1,32,8,128]{3,2,1,0:T(8,128)S(1)} %get-tuple-element.64), channel_id=1, source_target_pairs={{0,1},{1,2},{2,3},{3,4},{4,5},{5,6},{6,7},{7,0},{8,9},{9,10},{10,1... | collective-permute-start | bytes 393224 | tf_op jit(solution)/shard_map/ppermute | solution.py:384
  86.1 5.9 %collective-permute-start.9 = (f32[1,32,8,128]{3,2,1,0:T(8,128)S(1)}, f32[1,32,8,128]{3,2,1,0:T(8,128)S(1)}, u32[]{:S(2)}, u32[]{:S(2)}) collective-permute-start(f32[1,32,8,128]{3,2,1,0:T(8,128)S(1)} %get-tuple-element.65), channel_id=1, source_target_pairs={{1,0},{2,1},{3,2},{4,3},{5,4},{6,5},{7,6},{0,7},{9,8},{10,9},{11,1... | collective-permute-start | bytes 393224 | tf_op jit(solution)/shard_map/ppermute | solution.py:384
  94.8 6.0 %collective-permute-start.10 = (f32[1,32,8,128]{3,2,1,0:T(8,128)S(1)}, f32[1,32,8,128]{3,2,1,0:T(8,128)S(1)}, u32[]{:S(2)}, u32[]{:S(2)}) collective-permute-start(f32[1,32,8,128]{3,2,1,0:T(8,128)S(1)} %get-tuple-element.67), channel_id=1, source_target_pairs={{0,1},{1,2},{2,3},{3,4},{4,5},{5,6},{6,7},{7,0},{8,9},{9,10},{10,1... | collective-permute-start | bytes 393224 | tf_op jit(solution)/shard_map/ppermute | solution.py:384
  94.9 5.9 %collective-permute-start.11 = (f32[1,32,8,128]{3,2,1,0:T(8,128)S(1)}, f32[1,32,8,128]{3,2,1,0:T(8,128)S(1)}, u32[]{:S(2)}, u32[]{:S(2)}) collective-permute-start(f32[1,32,8,128]{3,2,1,0:T(8,128)S(1)} %get-tuple-element.68), channel_id=1, source_target_pairs={{1,0},{2,1},{3,2},{4,3},{5,4},{6,5},{7,6},{0,7},{9,8},{10,9},{11,1... | collective-permute-start | bytes 393224 | tf_op jit(solution)/shard_map/ppermute | solution.py:384
  103.5 8.8 %copy-start.9 = (f32[64,32,128]{2,1,0:T(8,128)S(1)}, f32[64,32,128]{2,1,0:T(8,128)}, u32[]{:S(2)}) copy-start(f32[64,32,128]{2,1,0:T(8,128)} %copy-done.8) | copy-start | bytes 3145732
  106.2 14.9 %copy-start.7 = (f32[64,32,128]{2,1,0:T(8,128)S(1)}, f32[64,32,128]{2,1,0:T(8,128)}, u32[]{:S(2)}) copy-start(f32[64,32,128]{2,1,0:T(8,128)} %copy-done.6) | copy-start | bytes 3145732
  106.2 6.1 %collective-permute-start.12 = (f32[1,32,8,128]{3,2,1,0:T(8,128)S(1)}, f32[1,32,8,128]{3,2,1,0:T(8,128)S(1)}, u32[]{:S(2)}, u32[]{:S(2)}) collective-permute-start(f32[1,32,8,128]{3,2,1,0:T(8,128)S(1)} %get-tuple-element.72), channel_id=1, source_target_pairs={{0,1},{1,2},{2,3},{3,4},{4,5},{5,6},{6,7},{7,0},{8,9},{9,10},{10,1... | collective-permute-start | bytes 393224 | tf_op jit(solution)/shard_map/ppermute | solution.py:384
  106.3 6.0 %collective-permute-start.13 = (f32[1,32,8,128]{3,2,1,0:T(8,128)S(1)}, f32[1,32,8,128]{3,2,1,0:T(8,128)S(1)}, u32[]{:S(2)}, u32[]{:S(2)}) collective-permute-start(f32[1,32,8,128]{3,2,1,0:T(8,128)S(1)} %get-tuple-element.73), channel_id=1, source_target_pairs={{1,0},{2,1},{3,2},{4,3},{5,4},{6,5},{7,6},{0,7},{9,8},{10,9},{11,1... | collective-permute-start | bytes 393224 | tf_op jit(solution)/shard_map/ppermute | solution.py:384
  115.1 6.1 %collective-permute-start.14 = (f32[1,32,8,128]{3,2,1,0:T(8,128)S(1)}, f32[1,32,8,128]{3,2,1,0:T(8,128)S(1)}, u32[]{:S(2)}, u32[]{:S(2)}) collective-permute-start(f32[1,32,8,128]{3,2,1,0:T(8,128)S(1)} %get-tuple-element.78), channel_id=1, source_target_pairs={{0,1},{1,2},{2,3},{3,4},{4,5},{5,6},{6,7},{7,0},{8,9},{9,10},{10,1... | collective-permute-start | bytes 393224 | tf_op jit(solution)/shard_map/ppermute | solution.py:384
  115.2 6.0 %collective-permute-start.15 = (f32[1,32,8,128]{3,2,1,0:T(8,128)S(1)}, f32[1,32,8,128]{3,2,1,0:T(8,128)S(1)}, u32[]{:S(2)}, u32[]{:S(2)}) collective-permute-start(f32[1,32,8,128]{3,2,1,0:T(8,128)S(1)} %get-tuple-element.79), channel_id=1, source_target_pairs={{1,0},{2,1},{3,2},{4,3},{5,4},{6,5},{7,6},{0,7},{9,8},{10,9},{11,1... | collective-permute-start | bytes 393224 | tf_op jit(solution)/shard_map/ppermute | solution.py:384
  123.9 6.1 %collective-permute-start.16 = (f32[1,32,8,128]{3,2,1,0:T(8,128)S(1)}, f32[1,32,8,128]{3,2,1,0:T(8,128)S(1)}, u32[]{:S(2)}, u32[]{:S(2)}) collective-permute-start(f32[1,32,8,128]{3,2,1,0:T(8,128)S(1)} %get-tuple-element.84), channel_id=1, source_target_pairs={{0,1},{1,2},{2,3},{3,4},{4,5},{5,6},{6,7},{7,0},{8,9},{9,10},{10,1... | collective-permute-start | bytes 393224 | tf_op jit(solution)/shard_map/ppermute | solution.py:384
  124.0 6.0 %collective-permute-start.17 = (f32[1,32,8,128]{3,2,1,0:T(8,128)S(1)}, f32[1,32,8,128]{3,2,1,0:T(8,128)S(1)}, u32[]{:S(2)}, u32[]{:S(2)}) collective-permute-start(f32[1,32,8,128]{3,2,1,0:T(8,128)S(1)} %get-tuple-element.85), channel_id=1, source_target_pairs={{1,0},{2,1},{3,2},{4,3},{5,4},{6,5},{7,6},{0,7},{9,8},{10,9},{11,1... | collective-permute-start | bytes 393224 | tf_op jit(solution)/shard_map/ppermute | solution.py:384
  133.7 26.7 %all-to-all-start.1 = ((f32[8,8,32,128]{3,2,1,0:T(8,128)}), f32[8,8,32,128]{3,2,1,0:T(8,128)S(1)}, u32[]{:S(2)}, u32[]{:S(2)}) async-start(f32[8,8,32,128]{3,2,1,0:T(8,128)} %shard_map.120), calls=%async_computation.1 | async-start | bytes 2097152 | tf_op jit(solution)/shard_map/all_to_all | solution.py:482
  161.2 8.5 %collective-permute-start.18 = (f32[2,8,32,128]{3,2,1,0:T(8,128)S(1)}, f32[2,8,32,128]{3,2,1,0:T(8,128)S(1)}, u32[]{:S(2)}, u32[]{:S(2)}) collective-permute-start(f32[2,8,32,128]{3,2,1,0:T(8,128)S(1)} %get-tuple-element.90), channel_id=1, source_target_pairs={{0,64},{8,72},{16,80},{24,88},{32,96},{40,104},{48,112},{56,120},{... | collective-permute-start | bytes 786440 | tf_op jit(solution)/shard_map/ppermute | solution.py:486

commit v4 on v3

v4 whole, which is shorter than its diff:
```python
import functools

import jax
import jax.numpy as jnp
import ml_dtypes
import numpy as np
from jax import lax
from jax.experimental import pallas as pl
from jax.experimental.pallas import tpu as pltpu
from jax.sharding import PartitionSpec as P

STEPS = 4
STENCIL = (-205.0 / 72.0, 8.0 / 5.0, -1.0 / 5.0, 8.0 / 315.0, -1.0 / 560.0)
F32 = jnp.float32
BF16 = jnp.bfloat16
SMEM = pl.BlockSpec(memory_space=pltpu.SMEM)
VMEM = pl.BlockSpec(memory_space=pltpu.VMEM)
ANY = pl.BlockSpec(memory_space=pltpu.HBM)
NX, NYL, NZ = 64, 32, 128
GROUP = 8
PAD = 4
ROWS = 64
OWN0, OWN1 = 16, 48
WIDE0, WIDE1 = 8, 56
WIDE = WIDE1 - WIDE0
OWN_X, OWN_Y = slice(PAD, PAD + NX), slice(OWN0, OWN1)
CHUNK = 16
OWN, WITH_HALO = range(4), range(-1, 5)


def depth_operator():
    band = np.zeros((NZ, NZ), np.float32)
    for i in range(NZ):
        band[i, i] = np.float32(3.0 * STENCIL[0])
        for k in range(1, 5):
            for j in (i - k, i + k):
                if 0 <= j < NZ:
                    band[j, i] = np.float32(STENCIL[k])
    high = band.astype(ml_dtypes.bfloat16)
    low = (band - high.astype(np.float32)).astype(ml_dtypes.bfloat16)
    zero = np.zeros_like(high)
    return np.block([[high, low], [high, zero]])


def clear_ends(ext):
    zeros = jnp.zeros((PAD, ROWS, NZ), F32)
    ext[0:PAD] = zeros
    ext[PAD + NX : 2 * PAD + NX] = zeros


def planes(body):
    def step(x, carry):
        body(x)
        return carry

    lax.fori_loop(0, NX, step, 0, unroll=4)


def fill_edges(ext, spots, halo_lo, halo_hi):
    has_lo, has_hi = spots[5] == 1, spots[6] == 1

    def body(t, carry):
        lo = jnp.where(has_lo, halo_lo[t], 0.0)
        hi = jnp.where(has_hi, halo_hi[t], 0.0)
        for half in range(2):
            x = PAD + 2 * t + half
            ext[x, OWN0 - 4 : OWN0, :] = lo[4 * half : 4 * half + 4]
            ext[x, OWN1 : OWN1 + 4, :] = hi[4 * half : 4 * half + 4]
        return carry

    lax.fori_loop(0, NX // 2, body, 0, unroll=4)


def fill_tiles(ext, spots, lo, hi):
    has_lo, has_hi = spots[5] == 1, spots[6] == 1

    def body(x):
        ext[PAD + x, WIDE0:OWN0, :] = jnp.where(has_lo, lo(x), 0.0)
        ext[PAD + x, OWN1:WIDE1, :] = jnp.where(has_hi, hi(x), 0.0)

    planes(body)


def fill_ring(ext, edge):
    def body(x):
        ext[PAD + x, OWN0 - 4 : OWN0, :] = edge[x, 0:4, :]
        ext[PAD + x, OWN1 : OWN1 + 4, :] = edge[x, 4:8, :]

    planes(body)


def apply_depth(ext, oper, depth, wide=False):
    r0, r1 = (WIDE0, WIDE1) if wide else (OWN0, OWN1)
    n = CHUNK
    for at in range(0, NX, n):
        rows = ext[PAD + at : PAD + at + n, r0:r1, :].reshape(n * (r1 - r0), NZ)
        high = rows.astype(BF16)
        low = (rows - high.astype(F32)).astype(BF16)
        prod = jnp.dot(jnp.concatenate([high, low], axis=1), oper[...], preferred_element_type=F32)
        depth[at : at + n, r0 - WIDE0 : r1 - WIDE0, :] = (prod[:, :NZ] + prod[:, NZ:]).reshape(n, r1 - r0, NZ)


def laplace(ext, depth, tiles, emit):
    def body(g, carry):
        base = PAD + g * GROUP
        for j in tiles:
            r0 = OWN0 + 8 * j
            col = [ext[base - PAD + i, r0 : r0 + 8, :] for i in range(GROUP + 2 * PAD)]
            for xi in range(GROUP):
                acc = depth[g * GROUP + xi, r0 - WIDE0 : r0 - WIDE0 + 8, :]
                for k in range(1, 5):
                    beside = (
                        col[xi + PAD + k]
                        + col[xi + PAD - k]
                        + (
                            ext[base + xi, r0 + k : r0 + k + 8, :]
                            + ext[base + xi, r0 - k : r0 - k + 8, :]
                        )
                    )
                    acc = acc + STENCIL[k] * beside
                emit(g * GROUP + xi, g, xi, j, acc)
        return carry

    lax.fori_loop(0, NX // GROUP, body, 0)


def tile(j):
    return slice(8 * j, 8 * j + 8)


def ext_tile(j):
    return slice(OWN0 + 8 * j, OWN0 + 8 * j + 8)


def send_rows(send_lo, send_hi, read):
    def body(t, carry):
        for half in range(2):
            send_lo[t, 4 * half : 4 * half + 4, :] = read(2 * t + half, slice(0, 4))
            send_hi[t, 4 * half : 4 * half + 4, :] = read(2 * t + half, slice(NYL - 4, NYL))
        return carry

    lax.fori_loop(0, NX // 2, body, 0, unroll=4)


def send_tiles(send_lo, send_hi, field):
    def body(x):
        send_lo[x] = field[x, 0:8, :]
        send_hi[x] = field[x, NYL - 8 : NYL, :]

    planes(body)


def add_source(spots, amount, ref, x0, y0, wide=False):
    @pl.when(spots[7 if wide else 1] == 1)
    def _():
        x, y, z = x0 + spots[2], y0 + spots[3], spots[4]
        lanes = lax.broadcasted_iota(jnp.int32, (1, NZ), 1)
        row = ref[x, pl.ds(y, 1), :]
        ref[x, pl.ds(y, 1), :] = row + jnp.where(lanes == z, amount, 0.0)


NOW, PREV, EDGES, TURNED = 0, 32, 64, 72


def unpack(turned, sems, now, edge, prev, extra):
    copies = []
    for n, (off, rows, dst) in enumerate(
        ((NOW, NYL, now), (EDGES, 8, edge), (PREV, NYL, prev), (NOW, NYL, extra))
    ):
        copies.append(pltpu.make_async_copy(turned.at[:, off : off + rows, :], dst, sems.at[n]))
    for c in copies:
        c.start()
    return copies


def first_kernel(spots, wavelet, turned, r2, oper, lap, new, send_lo, send_hi, now, edge, ext, depth, prev, sems):
    copies = unpack(turned, sems, ext.at[OWN_X, OWN_Y, :], edge, prev, now)
    clear_ends(ext)
    for c in copies[:3]:
        c.wait()
    fill_ring(ext, edge)
    apply_depth(ext, oper, depth)

    def emit(x, g, xi, j, value):
        lap[x, tile(j), :] = value
        new[x, tile(j), :] = 2.0 * ext[PAD + x, ext_tile(j), :] - prev[x, tile(j), :] + r2[x, tile(j), :] * value

    laplace(ext, depth, OWN, emit)
    add_source(spots, wavelet[0], new, 0, 0)
    send_tiles(send_lo, send_hi, new)
    copies[3].wait()


def spread_edges(edge, lo, hi):
    def body(x):
        lo[x, 4:8, :] = edge[x, 0:4, :]
        hi[x, 0:4, :] = edge[x, 4:8, :]

    planes(body)


def spread_halos(halo_lo, halo_hi, lo, hi):
    def body(t, carry):
        for half in range(2):
            lo[2 * t + half, 4:8, :] = halo_lo[t, 4 * half : 4 * half + 4, :]
            hi[2 * t + half, 0:4, :] = halo_hi[t, 4 * half : 4 * half + 4, :]
        return carry

    lax.fori_loop(0, NX // 2, body, 0, unroll=4)


def middle_kernel(
    spots, wavelet, now, now_lo, now_hi, prev, edge, r2, r2_lo, r2_hi, oper,
    lap_a, new_a, lap_b, new_b, send_lo, send_hi, ext, ext2, depth, old_lo, old_hi,
):
    has = (spots[5] == 1, spots[6] == 1)
    clear_ends(ext)
    clear_ends(ext2)
    ext[OWN_X, OWN_Y, :] = now[...]
    fill_tiles(ext, spots, lambda x: now_lo[x], lambda x: now_hi[x])
    spread_edges(edge, old_lo, old_hi)
    apply_depth(ext, oper, depth, True)

    def emit(x, g, xi, j, value):
        twice = 2.0 * ext[PAD + x, ext_tile(j), :]
        if j in OWN:
            u = twice - prev[x, tile(j), :] + r2[x, tile(j), :] * value
            lap_a[x, tile(j), :] = value
            new_a[x, tile(j), :] = u
        else:
            old, weight, there = (old_lo, r2_lo, has[0]) if j < 0 else (old_hi, r2_hi, has[1])
            u = jnp.where(there, twice - old[x] + weight[x] * value, 0.0)
        ext2[PAD + x, ext_tile(j), :] = u

    laplace(ext, depth, WITH_HALO, emit)
    add_source(spots, wavelet[1], new_a, 0, 0)
    add_source(spots, wavelet[1], ext2, PAD, OWN0, True)
    apply_depth(ext2, oper, depth)

    def emit_b(x, g, xi, j, value):
        lap_b[x, tile(j), :] = value
        new_b[x, tile(j), :] = 2.0 * ext2[PAD + x, ext_tile(j), :] - now[x, tile(j), :] + r2[x, tile(j), :] * value

    laplace(ext2, depth, OWN, emit_b)
    add_source(spots, wavelet[2], new_b, 0, 0)
    send_rows(send_lo, send_hi, lambda x, rows: new_b[x, rows, :])


def late_kernel(spots, turned, r2, r2_lo, r2_hi, oper, mu, late, edge, ext, depth, later, sems):
    copies = unpack(turned, sems, late, edge, later, ext.at[OWN_X, OWN_Y, :])
    clear_ends(ext)
    for c in copies:
        c.wait()

    def weigh(x):
        ext[PAD + x, OWN_Y, :] = late[x] * r2[x]
        ext[PAD + x, OWN0 - 4 : OWN0, :] = edge[x, 0:4, :] * r2_lo[x, 4:8, :]
        ext[PAD + x, OWN1 : OWN1 + 4, :] = edge[x, 4:8, :] * r2_hi[x, 0:4, :]

    planes(weigh)
    apply_depth(ext, oper, depth)

    def emit(x, g, xi, j, value):
        mu[x, tile(j), :] = 2.0 * late[x, tile(j), :] + value - later[x, tile(j), :]

    laplace(ext, depth, OWN, emit)


def turn_kernel(
    spots, wavelet, now, halo_lo, halo_hi, prev, r2, oper, part, count, data, total, mu, send_lo, send_hi, ext, depth, new
):
    clear_ends(ext)
    ext[OWN_X, OWN_Y, :] = now[...]
    fill_edges(ext, spots, halo_lo, halo_hi)
    apply_depth(ext, oper, depth)

    def emit(x, g, xi, j, value):
        new[x, tile(j), :] = 2.0 * ext[PAD + x, ext_tile(j), :] - prev[x, tile(j), :] + r2[x, tile(j), :] * value
        total[x, tile(j), :] = value

    laplace(ext, depth, OWN, emit)
    add_source(spots, wavelet[3], new, 0, 0)

    def finish(x):
        m = part[x] + (count[x, 8 : 8 + NYL, :] * new[x] - data[x])
        mu[x] = m
        total[x] = m * total[x]

    planes(finish)
    send_tiles(send_lo, send_hi, mu)


def back_kernel(
    spots, late, late_lo, late_hi, later, edge, r2, r2_lo, r2_hi, oper, count, data_a, data_b,
    wave_a, wave_lo, wave_hi, wave_b, lap_a, lap_b, total_in,
    total, mu_a, mu_b, send_lo, send_hi, ext, ext2, depth, old_lo, old_hi, u_lo, u_hi,
):
    has = (spots[5] == 1, spots[6] == 1)
    clear_ends(ext)
    clear_ends(ext2)
    ext[OWN_X, OWN_Y, :] = late[...] * r2[...]
    fill_tiles(ext, spots, lambda x: late_lo[x] * r2_lo[x], lambda x: late_hi[x] * r2_hi[x])
    spread_edges(edge, old_lo, old_hi)
    spread_halos(wave_lo, wave_hi, u_lo, u_hi)
    apply_depth(ext, oper, depth, True)

    def emit(x, g, xi, j, value):
        wide = slice(8 + 8 * j, 16 + 8 * j)
        many, heard = count[x, wide, :], data_a[x, wide, :]
        if j in OWN:
            mu = 2.0 * late[x, tile(j), :] + value - later[x, tile(j), :]
            mu = mu + (many * wave_a[x, tile(j), :] - heard)
            mu_a[x, tile(j), :] = mu
            total[x, tile(j), :] = total_in[x, tile(j), :] + mu * lap_a[x, tile(j), :]
            w = mu * r2[x, tile(j), :]
        else:
            near, old, u, weight, there = (
                (late_lo, old_lo, u_lo, r2_lo, has[0]) if j < 0 else (late_hi, old_hi, u_hi, r2_hi, has[1])
            )
            mu = 2.0 * near[x] + value - old[x] + (many * u[x] - heard)
            w = jnp.where(there, mu * weight[x], 0.0)
        ext2[PAD + x, ext_tile(j), :] = w

    laplace(ext, depth, WITH_HALO, emit)
    apply_depth(ext2, oper, depth)

    def emit_b(x, g, xi, j, value):
        mu = 2.0 * mu_a[x, tile(j), :] + value - late[x, tile(j), :]
        mu = mu + (count[x, 8 + 8 * j : 16 + 8 * j, :] * wave_b[x, tile(j), :] - data_b[x, tile(j), :])
        mu_b[x, tile(j), :] = mu
        total[x, tile(j), :] = total[x, tile(j), :] + mu * lap_b[x, tile(j), :]

    laplace(ext2, depth, OWN, emit_b)
    send_rows(send_lo, send_hi, lambda x, rows: mu_b[x, rows, :] * r2[x, rows, :])


def last_kernel(
    spots, late, later, r2, halo_lo, halo_hi, oper, count, data, wave, lap, total_in, total, ext, depth
):
    first = spots[0]
    clear_ends(ext)
    ext[OWN_X, OWN_Y, :] = late[...] * r2[...]
    fill_edges(ext, spots, halo_lo, halo_hi)
    apply_depth(ext, oper, depth)

    def emit(x, g, xi, j, value):
        mu = 2.0 * late[x, tile(j), :] + value - later[x, tile(j), :]
        mu = mu + (count[x, 8 + 8 * j : 16 + 8 * j, :] * wave[x, tile(j), :] - data[x, tile(j), :])
        total[lax.rem(first + g, GROUP), xi, tile(j), :] = total_in[x, tile(j), :] + mu * lap[x, tile(j), :]

    laplace(ext, depth, OWN, emit)


def pack_kernel(now, prev, out, near, edge, sems):
    bring = pltpu.make_async_copy(now, near, sems.at[16])
    bring.start()
    copies = []
    for p in range(8):
        for f, (off, field) in enumerate(((NOW, now), (PREV, prev))):
            copies.append(
                pltpu.make_async_copy(
                    field.at[:, NYL * p : NYL * p + NYL, :], out.at[p, :, off : off + NYL, :], sems.at[2 * p + f]
                )
            )
    for c in copies:
        c.start()
    none = jnp.zeros((4, NZ), F32)
    bring.wait()

    def body(xi, carry):
        for p in range(8):
            lo = NYL * p
            edge[p, xi, 0:4, :] = near[xi, lo - 4 : lo, :] if p > 0 else none
            edge[p, xi, 4:8, :] = near[xi, lo + NYL : lo + NYL + 4, :] if p < 7 else none
        return carry

    lax.fori_loop(0, GROUP, body, 0)
    ends = pltpu.make_async_copy(edge, out.at[:, :, EDGES : EDGES + 8, :], sems.at[17])
    ends.start()
    for c in copies:
        c.wait()
    ends.wait()


def copy_block(dst, src):
    def body(x, carry):
        dst[x] = src[x]
        return carry

    lax.fori_loop(0, GROUP, body, 0, unroll=4)


def split_shot(me):
    return me // 8, lax.rem(me // 2, 4), lax.rem(me, 2)


def slot_of(start, which):
    return (start + lax.rem(which - start + 32, 8)) // 8


def select_kernel(ids, apertures, piece, other, piece_c, other_c, *outs):
    half, y, core = split_shot(ids[0])
    for k in range(4):
        start = apertures[8 * half + 2 * lax.rem(y + k, 4) + core, 0]
        for j in range(2):
            m = slot_of(start, 2 * y + j)
            row = m // 2
            own_half = lax.rem(m, 2) == half
            own_core = core == j
            for src, same_half, same_core in (
                (piece, True, True),
                (other, False, True),
                (piece_c, True, False),
                (other_c, False, False),
            ):

                @pl.when(jnp.logical_and(own_half == same_half, own_core == same_core))
                def _():
                    copy_block(outs[k].at[j], src.at[row])


def assemble_kernel(ids, apertures, r0, r1, r2, r3, out, send_lo, send_hi):
    _, y, _ = split_shot(ids[0])
    first = apertures[ids[0], 0]
    for k, src in enumerate((r0, r1, r2, r3)):
        for j in range(2):
            at = lax.rem(2 * lax.rem(y - k + 4, 4) + j - first + 32, 8)
            copy_block(out.at[pl.ds(at * GROUP, GROUP)], src.at[j])
    send_tiles(send_lo, send_hi, out)


def receivers_kernel(cells, lines, observed, count, data3, data1, data2, data4):
    zeros = jnp.zeros((NYL, NZ), F32)
    zeros_wide = jnp.zeros((WIDE, NZ), F32)

    def clear(x):
        for d in (count, data3):
            d[x] = zeros_wide
        for d in (data1, data2, data4):
            d[x] = zeros

    planes(clear)
    lanes = lax.broadcasted_iota(jnp.int32, (1, NZ), 1)

    def body(r, carry):
        y = lines[r]

        @pl.when(jnp.logical_and(y >= -8, y < NYL + 8))
        def _():
            cell = cells[r]
            x = cell // (256 * NZ)
            hit = lanes == lax.rem(cell, NZ)
            row = pl.ds(y + 8, 1)
            count[x, row, :] = count[x, row, :] + jnp.where(hit, 1.0, 0.0)
            data3[x, row, :] = data3[x, row, :] + jnp.where(hit, observed[2, r], 0.0)

            @pl.when(jnp.logical_and(y >= 0, y < NYL))
            def _():
                own = pl.ds(y, 1)
                for n, d in ((0, data1), (1, data2), (3, data4)):
                    d[x, own, :] = d[x, own, :] + jnp.where(hit, observed[n, r], 0.0)

        return carry

    lax.fori_loop(0, cells.shape[0], body, 0)


def bins_kernel(ids, apertures, recv, keep, give):
    mine, which = ids[0] // 8, lax.rem(ids[0], 8)
    zeros = jnp.zeros((GROUP, NYL, NZ), F32)
    for i in range(2):
        keep[i] = zeros
        give[i] = zeros
    for t in range(GROUP):
        m = slot_of(apertures[8 * mine + t, 0], which)
        i = m // 2

        @pl.when(lax.rem(m, 2) == mine)
        def _():
            keep[i] = keep[i] + recv[t]

        @pl.when(lax.rem(m, 2) != mine)
        def _():
            give[i] = give[i] + recv[t]


FIELD = jax.ShapeDtypeStruct((NX, NYL, NZ), F32)
WIDE_FIELD = jax.ShapeDtypeStruct((NX, WIDE, NZ), F32)
EDGE = jax.ShapeDtypeStruct((NX // 2, 8, NZ), F32)
TILE = jax.ShapeDtypeStruct((NX, 8, NZ), F32)
BLOCKS = jax.ShapeDtypeStruct((8, GROUP, NYL, NZ), F32)
PAIR = jax.ShapeDtypeStruct((2, GROUP, NYL, NZ), F32)
EXT = pltpu.VMEM((NX + 2 * PAD, ROWS, NZ), F32)
DEPTH = pltpu.VMEM((NX, WIDE, NZ), F32)
FIELD_VMEM = pltpu.VMEM((NX, NYL, NZ), F32)
TILE_VMEM = pltpu.VMEM((NX, 8, NZ), F32)
PARAMS = pltpu.CompilerParams(vmem_limit_bytes=12 * 1024 * 1024)


def call(kernel, specs, outs, scratch=(), flops=0, moved=0, out_spec=VMEM):
    return pl.pallas_call(
        kernel,
        in_specs=specs,
        out_specs=[out_spec] * len(outs),
        out_shape=outs,
        scratch_shapes=list(scratch),
        compiler_params=PARAMS,
        cost_estimate=pl.CostEstimate(flops=flops, bytes_accessed=moved, transcendentals=0),
    )


def per_device(
    courant_squared,
    wave_now,
    wave_prev,
    adj_late,
    adj_later,
    wavelet,
    sources,
    receivers,
    observed,
    apertures,
):
    me = lax.axis_index("shot")
    part = lax.axis_index("sub")
    ids = jnp.stack([me, part]).astype(jnp.int32)
    first = apertures[me, 0]
    oper = jnp.asarray(depth_operator())
    up = [(i, (i + 1) % 8) for i in range(8)]
    down = [((i + 1) % 8, i) for i in range(8)]
    across = [(i, (i + 8) % 16) for i in range(16)]
    chip = [(i, i ^ 1) for i in range(16)]
    halves = [list(range(8)), list(range(8, 16))]

    def along(k):
        return [(8 * h + 2 * y + c, 8 * h + 2 * ((y + k) % 4) + c) for h in range(2) for y in range(4) for c in range(2)]

    def edges(lo, hi):
        return lax.ppermute(hi, "sub", up), lax.ppermute(lo, "sub", down)

    piece = courant_squared[:, 0]
    other = lax.ppermute(piece, "shot", across)
    piece_c = lax.ppermute(piece, "shot", chip)
    other_c = lax.ppermute(other, "shot", chip)
    blocks = call(select_kernel, [SMEM] * 2 + [VMEM] * 4, [PAIR] * 4, moved=2 << 20)(
        ids, apertures, piece, other, piece_c, other_c
    )
    come = [blocks[0]] + [lax.ppermute(blocks[k], "shot", along(k)) for k in (1, 2, 3)]

    def turn(a, b):
        (packed,) = call(
            pack_kernel,
            [ANY] * 2,
            [jax.ShapeDtypeStruct((8, GROUP, TURNED, NZ), F32)],
            [pltpu.VMEM((GROUP, 256, NZ), F32), pltpu.VMEM((8, GROUP, 8, NZ), F32), pltpu.SemaphoreType.DMA((18,))],
            moved=5 << 20,
            out_spec=ANY,
        )(a, b)
        return packed

    def exchange(packed):
        return lax.all_to_all(packed, "sub", 0, 0, tiled=True).reshape(NX, TURNED, NZ)

    packed, other = lax.optimization_barrier((turn(wave_now[0], wave_prev[0]), other))
    waves = exchange(packed)
    r2, *r2_send = call(assemble_kernel, [SMEM] * 2 + [VMEM] * 4, [FIELD, TILE, TILE], moved=2 << 20)(
        ids, apertures, *come
    )
    r2_halo = edges(*r2_send)

    cell = sources[0]
    line = (cell // NZ) % 256 - NYL * part
    spots = jnp.stack(
        [
            first % 8,
            ((line >= 0) & (line < NYL)).astype(jnp.int32),
            cell // (256 * NZ),
            line,
            cell % NZ,
            (part > 0).astype(jnp.int32),
            (part < 7).astype(jnp.int32),
            ((line >= -8) & (line < NYL + 8)).astype(jnp.int32),
        ]
    )
    amounts = wavelet[0]
    cells = receivers[0]
    lines = (cells // NZ) % 256 - NYL * part

    lap0, u1, lo, hi, u0, u0_edge = call(
        first_kernel,
        [SMEM, SMEM, ANY, VMEM, VMEM],
        [FIELD, FIELD, TILE, TILE, FIELD, TILE],
        [EXT, DEPTH, FIELD_VMEM, pltpu.SemaphoreType.DMA((4,))],
        flops=10 << 20,
        moved=8 << 20,
    )(spots, amounts, waves, r2, oper)
    u1_halo = edges(lo, hi)
    adjs = exchange(turn(adj_late[0], adj_later[0]))
    count, data3, data1, data2, data4 = call(
        receivers_kernel, [SMEM] * 3, [WIDE_FIELD, WIDE_FIELD] + [FIELD] * 3, moved=6 << 20
    )(cells, lines, observed[0])
    lap1, u2, lap2, u3, lo, hi = call(
        middle_kernel,
        [SMEM, SMEM] + [VMEM] * 9,
        [FIELD] * 4 + [EDGE] * 2,
        [EXT, EXT, DEPTH, TILE_VMEM, TILE_VMEM],
        flops=20 << 20,
        moved=12 << 20,
    )(spots, amounts, u1, *u1_halo, u0, u0_edge, r2, *r2_halo, oper)
    u3_halo = edges(lo, hi)
    part4, mu5, mu5_edge = call(
        late_kernel,
        [SMEM, ANY] + [VMEM] * 4,
        [FIELD, FIELD, TILE],
        [EXT, DEPTH, FIELD_VMEM, pltpu.SemaphoreType.DMA((4,))],
        flops=10 << 20,
        moved=6 << 20,
    )(spots, adjs, r2, *r2_halo, oper)

    total, mu4, lo, hi = call(
        turn_kernel,
        [SMEM, SMEM] + [VMEM] * 9,
        [FIELD, FIELD, TILE, TILE],
        [EXT, DEPTH, FIELD_VMEM],
        flops=10 << 20,
        moved=8 << 20,
    )(spots, amounts, u3, *u3_halo, u2, r2, oper, part4, count, data4)
    mu4_halo = edges(lo, hi)
    total, mu3, mu2, lo, hi = call(
        back_kernel,
        [SMEM] + [VMEM] * 19,
        [FIELD] * 3 + [EDGE] * 2,
        [EXT, EXT, DEPTH] + [TILE_VMEM] * 4,
        flops=20 << 20,
        moved=16 << 20,
    )(
        spots, mu4, *mu4_halo, mu5, mu5_edge, r2, *r2_halo, oper, count, data3, data2,
        u3, *u3_halo, u2, lap2, lap1, total,
    )
    mu2_halo = edges(lo, hi)
    (total,) = call(last_kernel, [SMEM] + [VMEM] * 11, [BLOCKS], [EXT, DEPTH], flops=10 << 20, moved=8 << 20)(
        spots, mu2, mu3, r2, *mu2_halo, oper, count, data1, u1, lap0, total
    )

    recv = lax.all_to_all(total, "shot", 0, 0, axis_index_groups=halves, tiled=True)
    keep, give = call(bins_kernel, [SMEM, SMEM, VMEM], [PAIR, PAIR], moved=2 << 20)(ids, apertures, recv)
    result = keep + lax.ppermute(give, "shot", across)
    return result[:, None]


def solution(mesh):
    in_specs = (
        P(None, "shot", None, "sub", None),
        P("shot", "sub", None, None),
        P("shot", "sub", None, None),
        P("shot", "sub", None, None),
        P("shot", "sub", None, None),
        P("shot", None),
        P("shot"),
        P("shot", None),
        P("shot", None, None),
        P(),
    )
    out_specs = P(None, "shot", None, "sub", None)
    return jax.shard_map(
        per_device, mesh=mesh, in_specs=in_specs, out_specs=out_specs, check_vma=False
    )
```

time: 171 us -> 184 us (1.076)
  blocking collectives: 0 us -> 23.7 us
  waiting for transfers between devices: 63.2 us -> 51.9 us
  starting transfers between devices: 50.3 us -> 41.2 us
  local copies, waits for them, and re-layouts: 18.6 us -> 25.1 us
  Pallas kernels: 33.9 us -> 37 us
    all_to_all x0 -> x1, blocking collectives: none -> 23.7 us  [per_device(): lax.all_to_all(total, 'shot', 0, 0, axis_index_groups=halves, tiled=True)]
    all_to_all x2, waiting for transfers between devices: 38.3 us -> 26 us  [exchange(): lax.all_to_all(packed, 'sub', 0, 0, tiled=True).reshape(NX, TURNED, NZ)]
    unnamed x44 -> x95, local copies, waits for them, and re-layouts: 15 us -> 24.3 us
    ppermute x3, waiting for transfers between devices: 0.01 us -> 6.62 us  [per_device(): lax.ppermute(blocks[k], 'shot', along(k))]
    ppermute x12 -> x10, waiting for transfers between devices: 17.4 us -> 10.8 us  [edges(): return (lax.ppermute(hi, 'sub', up), lax.ppermute(lo, 'sub', down))]
    all_to_all x2, starting transfers between devices: 16.8 us -> 10.7 us  [exchange(): lax.all_to_all(packed, 'sub', 0, 0, tiled=True).reshape(NX, TURNED, NZ)]
    ppermute x12 -> x10, starting transfers between devices: 22.4 us -> 18.2 us  [edges(): return (lax.ppermute(hi, 'sub', up), lax.ppermute(lo, 'sub', down))]
    pallas_call x11 -> x10, Pallas kernels: 31.3 us -> 33.8 us  [the longest x1 6.21 us: per_device(): call(back_kernel, [SMEM] + [VMEM] * 19, [FIELD] * 3 + [EDGE] * 2, [EXT, E...]
  transfers between devices with their start and end apart: 21 -> 19, of which waited for: 10 -> 10; matrix products, arithmetic and copies ran while one was open for 3% -> 1% of each run, Pallas kernels for 5% -> 13%
where the time goes in v4:
time: 184 us; the launch traced here: 183 us
  waiting for transfers between devices  51.9 us (28%)
  starting transfers between devices  41.2 us (22%)
  Pallas kernels  37 us (20%)
  local copies, waits for them, and re-layouts  25.1 us (14%)
  blocking collectives  23.7 us (13%)
  between operations  3.28 us (2%)
    all_to_all x2, waiting for transfers between devices, exchange(): lax.all_to_all(packed, 'sub', 0, 0, tiled=True).reshape(NX, TURNED, NZ)  26 us
    unnamed x95, local copies, waits for them, and re-layouts  24.3 us
    all_to_all x1, blocking collectives, per_device(): lax.all_to_all(total, 'shot', 0, 0, axis_index_groups=halves, tiled=True)  23.7 us
    ppermute x10, starting transfers between devices, edges(): return (lax.ppermute(hi, 'sub', up), lax.ppermute(lo, 'sub', down))  18.2 us
    ppermute x10, waiting for transfers between devices, edges(): return (lax.ppermute(hi, 'sub', up), lax.ppermute(lo, 'sub', down))  10.8 us
    all_to_all x2, starting transfers between devices, exchange(): lax.all_to_all(packed, 'sub', 0, 0, tiled=True).reshape(NX, TURNED, NZ)  10.7 us
    ppermute x3, waiting for transfers between devices, per_device(): lax.ppermute(blocks[k], 'shot', along(k))  6.62 us
    pallas_call x1, Pallas kernels, per_device(): call(back_kernel, [SMEM] + [VMEM] * 19, [FIELD] * 3 + [EDGE] * 2, [EXT, E...  6.21 us
  transfers between devices with their start and end apart: 19, of which 10 were waited for; matrix products, arithmetic and copies ran while one was open for 1% of the time, Pallas kernels for 13%

profile of v4, /device:TPU:1, one launch (start us, length us, event | category | flops | bytes accessed | tf_op | source)
XLA Modules:
  0.0 182.9 jit_solution(11248381038565088034)
XLA Ops:
  0.0 3.6 %collective-permute-start = (f32[2,8,32,128]{3,2,1,0:T(8,128)}, f32[2,8,32,128]{3,2,1,0:T(8,128)}, u32[]{:S(2)}, u32[]{:S(2)}) collective-permute-start(f32[2,8,32,128]{3,2,1,0:T(8,128)} %bitcast.35), channel_id=1, source_target_pairs={{0,64},{8,72},{16,80},{24,88},{32,96},{40,104},{48,112},{56,120},{... | collective-permute-start | bytes 786440 | tf_op jit(solution)/shard_map/ppermute | solution.py:542
  3.6 1.2 copy-done.16
  4.8 1.2 copy-done.17
  6.0 0.7 shard_map.109
  6.8 1.4 copy-done
  8.2 1.3 collective-permute-done.other
  9.4 6.3 %all-to-all-start = ((f32[8,8,72,128]{3,2,1,0:T(8,128)}), f32[8,8,72,128]{3,2,1,0:T(8,128)S(1)}, u32[]{:S(2)}, u32[]{:S(2)}) async-start(f32[8,8,72,128]{3,2,1,0:T(8,128)} %copy-done), calls=%async_computation | async-start | bytes 4718592 | tf_op jit(solution)/shard_map/all_to_all | solution.py:562
  15.8 1.2 copy-done.19
  17.0 1.6 shard_map.114
  18.7 26.0 %all-to-all-done = f32[8,8,72,128]{3,2,1,0:T(8,128)S(1)} async-done(((f32[8,8,72,128]{3,2,1,0:T(8,128)}), f32[8,8,72,128]{3,2,1,0:T(8,128)S(1)}, u32[]{:S(2)}, u32[]{:S(2)}) %all-to-all-start) | async-done | bytes 2359328 | tf_op jit(solution)/shard_map/all_to_all | solution.py:562
  44.7 4.4 %all-to-all-start.1 = ((f32[8,8,72,128]{3,2,1,0:T(8,128)}), f32[8,8,72,128]{3,2,1,0:T(8,128)}, u32[]{:S(2)}, u32[]{:S(2)}) async-start(f32[8,8,72,128]{3,2,1,0:T(8,128)} %shard_map.114), calls=%async_computation.1 | async-start | bytes 4718592 | tf_op jit(solution)/shard_map/all_to_all | solution.py:562
  49.1 0.9 collective-permute-start.1
  50.3 0.9 collective-permute-done.1.piece_c
  51.2 0.6 collective-permute-done.2.other_c
  51.8 2.2 %shard_map.110 = (f32[2,8,32,128]{3,2,1,0:T(8,128)S(1)}, f32[2,8,32,128]{3,2,1,0:T(8,128)}, f32[2,8,32,128]{3,2,1,0:T(8,128)}, f32[2,8,32,128]{3,2,1,0:T(8,128)S(1)}) custom-call(s32[2]{0:T(128)S(1)} %pad_add_fusion.ids, s32[16,8]{1,0:T(8,128)S(1)} %copy.14.apertures, f32[2,8,32,128]{3,2,1,0:T(8,128)S(1)} %bitcast.37, ...), custom_call_target="tpu_custom_call" | custom-call | bytes 2097152 | tf_op jit(solution)/shard_map/pallas_call | solution.py:545
  54.0 0.7 copy-done.33
  54.7 1.3 collective-permute-start.3
  56.0 2.6 %collective-permute-start.4 = (f32[2,8,32,128]{3,2,1,0:T(8,128)}, f32[2,8,32,128]{3,2,1,0:T(8,128)S(1)}, u32[]{:S(2)}, u32[]{:S(2)}) collective-permute-start(f32[2,8,32,128]{3,2,1,0:T(8,128)} %get-tuple-element.47), channel_id=1, source_target_pairs={{0,32},{8,40},{16,48},{24,56},{32,0},{40,8},{48,16},{56,24},{64,96... | collective-permute-start | bytes 786440 | tf_op jit(solution)/shard_map/ppermute | solution.py:548
  58.6 1.1 collective-permute-start.5
  60.3 0.7 constant_dynamic-slice_fusion
  63.2 0.6 collective-permute-done.3.r1
  63.8 0.7 copy-done.35
  64.5 6.0 %collective-permute-done.4.r2 = f32[2,8,32,128]{3,2,1,0:T(8,128)S(1)} collective-permute-done((f32[2,8,32,128]{3,2,1,0:T(8,128)}, f32[2,8,32,128]{3,2,1,0:T(8,128)S(1)}, u32[]{:S(2)}, u32[]{:S(2)}) %collective-permute-start.4) | collective-permute-done | bytes 262176 | tf_op jit(solution)/shard_map/ppermute | solution.py:548
  70.6 0.7 copy-done.37
  71.3 0.7 copy-done.39
  72.0 0.9 copy-done.34
  72.9 0.9 copy-done.36
  73.9 0.9 copy-done.38
  74.8 0.9 copy-done.40
  75.8 0.9 shard_map.111
  76.7 1.5 collective-permute-start.8
  78.2 2.2 %collective-permute-start.9 = (f32[64,8,128]{2,1,0:T(8,128)S(1)}, f32[64,8,128]{2,1,0:T(8,128)S(1)}, u32[]{:S(2)}, u32[]{:S(2)}) collective-permute-start(f32[64,8,128]{2,1,0:T(8,128)S(1)} %get-tuple-element.56), channel_id=1, source_target_pairs={{1,0},{2,1},{3,2},{4,3},{5,4},{6,5},{7,6},{0,7},{9,8},{10,9},{11,1... | collective-permute-start | bytes 786440 | tf_op jit(solution)/shard_map/ppermute | solution.py:539
  80.4 0.7 copy-done.41
  81.1 2.9 %shard_map.112 = (f32[64,32,128]{2,1,0:T(8,128)S(1)}, f32[64,32,128]{2,1,0:T(8,128)S(1)}, f32[64,8,128]{2,1,0:T(8,128)S(1)}, f32[64,8,128]{2,1,0:T(8,128)S(1)}, ...) custom-call(s32[8]{0:T(128)S(1)} %stack.63.spots, f32[4]{0:T(128)S(1)} %bitcast.38, f32[64,72,128]{2,1,0:T(8,128)S(1)} %bitcast.30, ...), custom_call_target="tpu_custom_call" | custom-call | flops 10485760 | bytes 8388608 | tf_op jit(solution)/shard_map/pallas_call | solution.py:589
  84.0 1.0 copy-done.20
  85.0 3.6 %collective-permute-start.7 = (f32[64,8,128]{2,1,0:T(8,128)S(1)}, f32[64,8,128]{2,1,0:T(8,128)S(1)}, u32[]{:S(2)}, u32[]{:S(2)}) collective-permute-start(f32[64,8,128]{2,1,0:T(8,128)S(1)} %get-tuple-element.52), channel_id=1, source_target_pairs={{1,0},{2,1},{3,2},{4,3},{5,4},{6,5},{7,6},{0,7},{9,8},{10,9},{11,1... | collective-permute-start | bytes 786440 | tf_op jit(solution)/shard_map/ppermute | solution.py:539
  88.6 4.7 %collective-permute-done.6.now_lo = f32[64,8,128]{2,1,0:T(8,128)S(1)} collective-permute-done((f32[64,8,128]{2,1,0:T(8,128)S(1)}, f32[64,8,128]{2,1,0:T(8,128)S(1)}, u32[]{:S(2)}, u32[]{:S(2)}) %collective-permute-start.6) | collective-permute-done | bytes 262176 | tf_op jit(solution)/shard_map/ppermute | solution.py:539
  93.3 0.7 copy-done.42
  94.0 5.8 %shard_map.113 = (f32[64,32,128]{2,1,0:T(8,128)S(1)}, f32[64,32,128]{2,1,0:T(8,128)S(1)}, f32[64,32,128]{2,1,0:T(8,128)S(1)}, f32[64,32,128]{2,1,0:T(8,128)S(1)}...) custom-call(s32[8]{0:T(128)S(1)} %stack.63.spots, f32[4]{0:T(128)S(1)} %bitcast.39, ...), custom_call_target="tpu_custom_call" | custom-call | flops 20971520 | bytes 12582912 | tf_op jit(solution)/shard_map/pallas_call | solution.py:602
  99.8 1.0 copy-done.4
  100.8 1.1 copy-done.6
  101.8 1.0 copy-done.24
  102.8 1.0 copy-done.26
  103.8 3.6 %collective-permute-start.11 = (f32[32,8,128]{2,1,0:T(8,128)}, f32[32,8,128]{2,1,0:T(8,128)}, u32[]{:S(2)}, u32[]{:S(2)}) collective-permute-start(f32[32,8,128]{2,1,0:T(8,128)} %get-tuple-element.59), channel_id=1, source_target_pairs={{1,0},{2,1},{3,2},{4,3},{5,4},{6,5},{7,6},{0,7},{9,8},{10,9},{11,1... | collective-permute-start | bytes 393224 | tf_op jit(solution)/shard_map/ppermute | solution.py:539
  107.5 5.2 %shard_map.116 = (f32[64,48,128]{2,1,0:T(8,128)S(1)}, f32[64,48,128]{2,1,0:T(8,128)S(1)}, f32[64,32,128]{2,1,0:T(8,128)S(1)}, f32[64,32,128]{2,1,0:T(8,128)S(1)}, f32[64,32,128]{2,1,0:T(8,128)S(1)}) custom-call(s32[256]{0:T(256)S(1)} %bitcast.43, s32[256]{0:T(256)S(1)} %fusion.lines, f32[4,256]{1,0:T(4,128)S(1)} %bitcast.41), custom_call_target="tpu_custom_call" | custom-call | bytes 6291456 | tf_op jit(solution)/shard_map/pallas_call | solution.py:599
  112.7 1.2 copy-done.14
  113.8 1.0 copy-done.22
  114.8 1.0 copy-done.28
  115.8 1.0 copy-done.30
  116.8 1.1 copy-done.9
  117.8 0.9 copy-done.12
  118.8 4.4 %shard_map.115 = (f32[64,32,128]{2,1,0:T(8,128)S(1)}, f32[64,32,128]{2,1,0:T(8,128)S(1)}, f32[64,8,128]{2,1,0:T(8,128)S(1)}) custom-call(s32[8]{0:T(128)S(1)} %stack.63.spots, f32[64,72,128]{2,1,0:T(8,128)} %bitcast.19.turned, f32[64,32,128]{2,1,0:T(8,128)S(1)} %get-tuple-element.49.r2, f32[64,8,128]{2,1,0:T(8,128)S(1)} %copy-done.9, ...), custom_call_target="tpu_custom_call" | custom-call | flops 10485760 | bytes 6291456 | tf_op jit(solution)/shard_map/pallas_call | solution.py:611
  123.3 3.4 %shard_map.117 = (f32[64,32,128]{2,1,0:T(8,128)S(1)}, f32[64,32,128]{2,1,0:T(8,128)S(1)}, f32[64,8,128]{2,1,0:T(8,128)S(1)}, f32[64,8,128]{2,1,0:T(8,128)S(1)}) custom-call(s32[8]{0:T(128)S(1)} %stack.63.spots, f32[4]{0:T(128)S(1)} %bitcast.40, f32[64,32,128]{2,1,0:T(8,128)S(1)} %copy-done.7, f32[32,8,128]{2,1,0:T(8,128)} %collective-permute-done.10.halo_lo.wave_lo, ...), custom_call_target="tpu_custom_call" | custom-call | flops 10485760 | bytes 8388608 | tf_op jit(solution)/shard_map/pallas_call | solution.py:620
  126.9 3.6 %collective-permute-start.13 = (f32[64,8,128]{2,1,0:T(8,128)S(1)}, f32[64,8,128]{2,1,0:T(8,128)S(1)}, u32[]{:S(2)}, u32[]{:S(2)}) collective-permute-start(f32[64,8,128]{2,1,0:T(8,128)S(1)} %get-tuple-element.66), channel_id=1, source_target_pairs={{1,0},{2,1},{3,2},{4,3},{5,4},{6,5},{7,6},{0,7},{9,8},{10,9},{11,1... | collective-permute-start | bytes 786440 | tf_op jit(solution)/shard_map/ppermute | solution.py:539
  130.4 3.8 %collective-permute-done.12.late_lo = f32[64,8,128]{2,1,0:T(8,128)S(1)} collective-permute-done((f32[64,8,128]{2,1,0:T(8,128)S(1)}, f32[64,8,128]{2,1,0:T(8,128)S(1)}, u32[]{:S(2)}, u32[]{:S(2)}) %collective-permute-start.12) | collective-permute-done | bytes 262176 | tf_op jit(solution)/shard_map/ppermute | solution.py:539
  134.3 6.2 %shard_map.118 = (f32[64,32,128]{2,1,0:T(8,128)S(1)}, f32[64,32,128]{2,1,0:T(8,128)S(1)}, f32[64,32,128]{2,1,0:T(8,128)S(1)}, f32[32,8,128]{2,1,0:T(8,128)S(1)}, f32[32,8,128]{2,1,0:T(8,128)S(1)}) custom-call(s32[8]{0:T(128)S(1)} %stack.63.spots, f32[64,32,128]{2,1,0:T(8,128)S(1)} %get-tuple-element.64.late, ...), custom_call_target="tpu_custom_call" | custom-call | flops 20971520 | bytes 16777216 | tf_op jit(solution)/shard_map/pallas_call | solution.py:629
  140.6 3.6 %collective-permute-start.15 = (f32[32,8,128]{2,1,0:T(8,128)S(1)}, f32[32,8,128]{2,1,0:T(8,128)S(1)}, u32[]{:S(2)}, u32[]{:S(2)}) collective-permute-start(f32[32,8,128]{2,1,0:T(8,128)S(1)} %get-tuple-element.77), channel_id=1, source_target_pairs={{1,0},{2,1},{3,2},{4,3},{5,4},{6,5},{7,6},{0,7},{9,8},{10,9},{11,1... | collective-permute-start | bytes 393224 | tf_op jit(solution)/shard_map/ppermute | solution.py:539
  144.2 2.3 %collective-permute-done.14.halo_lo = f32[32,8,128]{2,1,0:T(8,128)S(1)} collective-permute-done((f32[32,8,128]{2,1,0:T(8,128)S(1)}, f32[32,8,128]{2,1,0:T(8,128)S(1)}, u32[]{:S(2)}, u32[]{:S(2)}) %collective-permute-start.14) | collective-permute-done | bytes 131104 | tf_op jit(solution)/shard_map/ppermute | solution.py:539
  146.5 2.6 %shard_map.119 = f32[8,8,32,128]{3,2,1,0:T(8,128)S(1)} custom-call(s32[8]{0:T(128)S(1)} %stack.63.spots, f32[64,32,128]{2,1,0:T(8,128)S(1)} %get-tuple-element.74.late, f32[64,32,128]{2,1,0:T(8,128)S(1)} %get-tuple-element.75.later, f32[64,32,128]{2,1,0:T(8,128)S(1)} %get-tuple-element.49.r2, f32[32,8,128]{2,1,0:T(8,128)S(1)} %collective-permute-done.14.halo_lo, ...), custom_call_target="tpu_custom_call" | custom-call | flops 10485760 | bytes 8388608 | tf_op jit(solution)/shard_map/pallas_call | solution.py:641
  149.1 23.7 %all_to_all.15.recv = f32[8,8,32,128]{3,2,1,0:T(8,128)S(1)} all-to-all(f32[8,8,32,128]{3,2,1,0:T(8,128)S(1)} %shard_map.119), channel_id=1, replica_groups={{0,8,16,24,32,40,48,56},{64,72,80,88,96,104,112,120},{1,9,17,25,33,41,4..., dimensions={0} | all-to-all | bytes 2097152 | tf_op jit(solution)/shard_map/all_to_all | solution.py:645
  172.8 1.0 shard_map.120
  173.8 2.7 %collective-permute-start.16 = (f32[2,8,32,128]{3,2,1,0:T(8,128)S(1)}, f32[2,8,32,128]{3,2,1,0:T(8,128)S(1)}, u32[]{:S(2)}, u32[]{:S(2)}) collective-permute-start(f32[2,8,32,128]{3,2,1,0:T(8,128)S(1)} %get-tuple-element.82), channel_id=1, source_target_pairs={{0,64},{8,72},{16,80},{24,88},{32,96},{40,104},{48,112},{56,120},{... | collective-permute-start | bytes 786440 | tf_op jit(solution)/shard_map/ppermute | solution.py:647
  176.5 5.6 %collective-permute-done.16 = f32[2,8,32,128]{3,2,1,0:T(8,128)S(1)} collective-permute-done((f32[2,8,32,128]{3,2,1,0:T(8,128)S(1)}, f32[2,8,32,128]{3,2,1,0:T(8,128)S(1)}, u32[]{:S(2)}, u32[]{:S(2)}) %collective-permute-start.16) | collective-permute-done | bytes 262176 | tf_op jit(solution)/shard_map/ppermute | solution.py:647
  182.1 0.7 add_bitcast_fusion
  (87 shorter events, 0.7 us)
Async XLA Ops:
  0.0 9.4 %collective-permute-start = (f32[2,8,32,128]{3,2,1,0:T(8,128)}, f32[2,8,32,128]{3,2,1,0:T(8,128)}, u32[]{:S(2)}, u32[]{:S(2)}) collective-permute-start(f32[2,8,32,128]{3,2,1,0:T(8,128)} %bitcast.35), channel_id=1, source_target_pairs={{0,64},{8,72},{16,80},{24,88},{32,96},{40,104},{48,112},{56,120},{... | collective-permute-start | bytes 786440 | tf_op jit(solution)/shard_map/ppermute | solution.py:542
  3.6 1.2 copy-start.16
  4.8 1.2 copy-start.17
  6.7 1.4 copy-start
  8.2 7.6 %copy-start.18 = (f32[1,8,256,128]{3,2,1,0:T(8,128)S(1)}, f32[1,8,256,128]{3,2,1,0:T(8,128)}, u32[]{:S(2)}) copy-start(f32[1,8,256,128]{3,2,1,0:T(8,128)} %param.14) | copy-start | bytes 3145732
  9.4 35.3 %all-to-all-start = ((f32[8,8,72,128]{3,2,1,0:T(8,128)}), f32[8,8,72,128]{3,2,1,0:T(8,128)S(1)}, u32[]{:S(2)}, u32[]{:S(2)}) async-start(f32[8,8,72,128]{3,2,1,0:T(8,128)} %copy-done), calls=%async_computation | async-start | bytes 4718592 | tf_op jit(solution)/shard_map/all_to_all | solution.py:562
  15.8 1.2 copy-start.19
  18.7 30.4 %copy-start.32 = (f32[2,1,8,32,128]{4,3,2,1,0:T(8,128)S(1)}, f32[2,1,8,32,128]{4,3,2,1,0:T(8,128)}, u32[]{:S(2)}) copy-start(f32[2,1,8,32,128]{4,3,2,1,0:T(8,128)} %param.11) | copy-start | bytes 786436
  18.7 31.5 %copy-start.46 = (s32[16,8]{0,1:T(8,128)S(1)}, s32[16,8]{0,1:T(8,128)}, u32[]{:S(2)}) copy-start(s32[16,8]{0,1:T(8,128)} %param.20) | copy-start | bytes 1540
  18.7 61.7 %copy-start.1 = (bf16[256,256]{1,0:T(8,128)(2,1)S(1)}, bf16[256,256]{1,0:T(8,128)(2,1)}, u32[]{:S(2)}) copy-start(bf16[256,256]{1,0:T(8,128)(2,1)} %constant.94.clone.oper) | copy-start | bytes 393220
  44.7 72.0 %all-to-all-start.1 = ((f32[8,8,72,128]{3,2,1,0:T(8,128)}), f32[8,8,72,128]{3,2,1,0:T(8,128)}, u32[]{:S(2)}, u32[]{:S(2)}) async-start(f32[8,8,72,128]{3,2,1,0:T(8,128)} %shard_map.114), calls=%async_computation.1 | async-start | bytes 4718592 | tf_op jit(solution)/shard_map/all_to_all | solution.py:562
  49.1 2.1 %collective-permute-start.1 = (f32[2,8,32,128]{3,2,1,0:T(8,128)S(1)}, f32[2,8,32,128]{3,2,1,0:T(8,128)S(1)}, u32[]{:S(2)}, u32[]{:S(2)}) collective-permute-start(f32[2,8,32,128]{3,2,1,0:T(8,128)S(1)} %bitcast.36), channel_id=1, source_target_pairs={{0,8},{8,0},{16,24},{24,16},{32,40},{40,32},{48,56},{56,48},{64,72... | collective-permute-start | bytes 786440 | tf_op jit(solution)/shard_map/ppermute | solution.py:543
  50.0 1.7 collective-permute-start.2
  54.0 0.7 copy-start.33
  54.7 9.2 %collective-permute-start.3 = (f32[2,8,32,128]{3,2,1,0:T(8,128)}, f32[2,8,32,128]{3,2,1,0:T(8,128)S(1)}, u32[]{:S(2)}, u32[]{:S(2)}) collective-permute-start(f32[2,8,32,128]{3,2,1,0:T(8,128)} %get-tuple-element.46), channel_id=1, source_target_pairs={{0,16},{8,24},{16,32},{24,40},{32,48},{40,56},{48,0},{56,8},{64,80... | collective-permute-start | bytes 786440 | tf_op jit(solution)/shard_map/ppermute | solution.py:548
  56.0 14.6 %collective-permute-start.4 = (f32[2,8,32,128]{3,2,1,0:T(8,128)}, f32[2,8,32,128]{3,2,1,0:T(8,128)S(1)}, u32[]{:S(2)}, u32[]{:S(2)}) collective-permute-start(f32[2,8,32,128]{3,2,1,0:T(8,128)} %get-tuple-element.47), channel_id=1, source_target_pairs={{0,32},{8,40},{16,48},{24,56},{32,0},{40,8},{48,16},{56,24},{64,96... | collective-permute-start | bytes 786440 | tf_op jit(solution)/shard_map/ppermute | solution.py:548
  58.6 12.7 %collective-permute-start.5 = (f32[2,8,32,128]{3,2,1,0:T(8,128)S(1)}, f32[2,8,32,128]{3,2,1,0:T(8,128)S(1)}, u32[]{:S(2)}, u32[]{:S(2)}) collective-permute-start(f32[2,8,32,128]{3,2,1,0:T(8,128)S(1)} %get-tuple-element.48), channel_id=1, source_target_pairs={{0,48},{8,56},{16,0},{24,8},{32,16},{40,24},{48,32},{56,40},{64,11... | collective-permute-start | bytes 786440 | tf_op jit(solution)/shard_map/ppermute | solution.py:548
  63.8 0.7 copy-start.35
  70.6 0.7 copy-start.37
  71.3 0.7 copy-start.39
  72.0 0.9 copy-start.34
  72.9 0.9 copy-start.36
  73.9 0.9 copy-start.38
  74.8 0.9 copy-start.40
  76.7 11.9 %collective-permute-start.8 = (f32[64,8,128]{2,1,0:T(8,128)S(1)}, f32[64,8,128]{2,1,0:T(8,128)S(1)}, u32[]{:S(2)}, u32[]{:S(2)}) collective-permute-start(f32[64,8,128]{2,1,0:T(8,128)S(1)} %get-tuple-element.55), channel_id=1, source_target_pairs={{0,1},{1,2},{2,3},{3,4},{4,5},{5,6},{6,7},{7,0},{8,9},{9,10},{10,1... | collective-permute-start | bytes 786440 | tf_op jit(solution)/shard_map/ppermute | solution.py:539
  78.2 10.4 %collective-permute-start.9 = (f32[64,8,128]{2,1,0:T(8,128)S(1)}, f32[64,8,128]{2,1,0:T(8,128)S(1)}, u32[]{:S(2)}, u32[]{:S(2)}) collective-permute-start(f32[64,8,128]{2,1,0:T(8,128)S(1)} %get-tuple-element.56), channel_id=1, source_target_pairs={{1,0},{2,1},{3,2},{4,3},{5,4},{6,5},{7,6},{0,7},{9,8},{10,9},{11,1... | collective-permute-start | bytes 786440 | tf_op jit(solution)/shard_map/ppermute | solution.py:539
  84.0 1.0 copy-start.20
  85.0 22.5 %copy-start.2 = (f32[64,32,128]{2,1,0:T(8,128)}, f32[64,32,128]{2,1,0:T(8,128)S(1)}, u32[]{:S(2)}) copy-start(f32[64,32,128]{2,1,0:T(8,128)S(1)} %get-tuple-element.50.now.wave) | copy-start | bytes 3145732
  85.0 22.4 %copy-start.45 = (s32[1,256]{1,0:T(1,128)S(1)}, s32[1,256]{1,0:T(1,128)}, u32[]{:S(2)}) copy-start(s32[1,256]{1,0:T(1,128)} %param.18) | copy-start | bytes 3076
  85.0 22.5 %copy-start.44 = (f32[1,4,256]{2,1,0:T(4,128)S(1)}, f32[1,4,256]{2,1,0:T(4,128)}, u32[]{:S(2)}) copy-start(f32[1,4,256]{2,1,0:T(4,128)} %param.19) | copy-start | bytes 12292
  85.0 8.3 %collective-permute-start.6 = (f32[64,8,128]{2,1,0:T(8,128)S(1)}, f32[64,8,128]{2,1,0:T(8,128)S(1)}, u32[]{:S(2)}, u32[]{:S(2)}) collective-permute-start(f32[64,8,128]{2,1,0:T(8,128)S(1)} %get-tuple-element.51), channel_id=1, source_target_pairs={{0,1},{1,2},{2,3},{3,4},{4,5},{5,6},{6,7},{7,0},{8,9},{9,10},{10,1... | collective-permute-start | bytes 786440 | tf_op jit(solution)/shard_map/ppermute | solution.py:539
  85.0 8.3 %collective-permute-start.7 = (f32[64,8,128]{2,1,0:T(8,128)S(1)}, f32[64,8,128]{2,1,0:T(8,128)S(1)}, u32[]{:S(2)}, u32[]{:S(2)}) collective-permute-start(f32[64,8,128]{2,1,0:T(8,128)S(1)} %get-tuple-element.52), channel_id=1, source_target_pairs={{1,0},{2,1},{3,2},{4,3},{5,4},{6,5},{7,6},{0,7},{9,8},{10,9},{11,1... | collective-permute-start | bytes 786440 | tf_op jit(solution)/shard_map/ppermute | solution.py:539
  88.6 18.9 %copy-start.8 = (f32[64,8,128]{2,1,0:T(8,128)}, f32[64,8,128]{2,1,0:T(8,128)S(1)}, u32[]{:S(2)}) copy-start(f32[64,8,128]{2,1,0:T(8,128)S(1)} %collective-permute-done.8.r2_lo) | copy-start | bytes 786436
  88.6 18.9 %copy-start.11 = (f32[64,8,128]{2,1,0:T(8,128)}, f32[64,8,128]{2,1,0:T(8,128)S(1)}, u32[]{:S(2)}) copy-start(f32[64,8,128]{2,1,0:T(8,128)S(1)} %collective-permute-done.9.r2_hi) | copy-start | bytes 786436
  99.8 1.0 copy-start.4
  100.8 1.1 copy-start.6
  101.8 1.0 copy-start.24
  102.8 1.0 copy-start.26
  103.8 19.4 %copy-start.43 = (f32[1,4]{1,0:T(1,128)S(1)}, f32[1,4]{1,0:T(1,128)}, u32[]{:S(2)}) copy-start(f32[1,4]{1,0:T(1,128)} %param.16) | copy-start | bytes 52
  103.8 19.4 %collective-permute-start.10 = (f32[32,8,128]{2,1,0:T(8,128)}, f32[32,8,128]{2,1,0:T(8,128)}, u32[]{:S(2)}, u32[]{:S(2)}) collective-permute-start(f32[32,8,128]{2,1,0:T(8,128)} %get-tuple-element.58), channel_id=1, source_target_pairs={{0,1},{1,2},{2,3},{3,4},{4,5},{5,6},{6,7},{7,0},{8,9},{9,10},{10,1... | collective-permute-start | bytes 393224 | tf_op jit(solution)/shard_map/ppermute | solution.py:539
  103.8 19.4 %collective-permute-start.11 = (f32[32,8,128]{2,1,0:T(8,128)}, f32[32,8,128]{2,1,0:T(8,128)}, u32[]{:S(2)}, u32[]{:S(2)}) collective-permute-start(f32[32,8,128]{2,1,0:T(8,128)} %get-tuple-element.59), channel_id=1, source_target_pairs={{1,0},{2,1},{3,2},{4,3},{5,4},{6,5},{7,6},{0,7},{9,8},{10,9},{11,1... | collective-permute-start | bytes 393224 | tf_op jit(solution)/shard_map/ppermute | solution.py:539
  112.6 1.2 copy-start.14
  113.8 1.0 copy-start.22
  114.8 1.0 copy-start.28
  115.8 1.0 copy-start.30
  116.7 6.5 %copy-start.5 = (f32[64,32,128]{2,1,0:T(8,128)S(1)}, f32[64,32,128]{2,1,0:T(8,128)}, u32[]{:S(2)}) copy-start(f32[64,32,128]{2,1,0:T(8,128)} %copy-done.4) | copy-start | bytes 3145732
  116.7 6.5 %copy-start.7 = (f32[64,32,128]{2,1,0:T(8,128)S(1)}, f32[64,32,128]{2,1,0:T(8,128)}, u32[]{:S(2)}) copy-start(f32[64,32,128]{2,1,0:T(8,128)} %copy-done.6) | copy-start | bytes 3145732
  116.7 1.1 copy-start.9
  117.8 0.9 copy-start.12
  118.8 4.5 %copy-start.31 = (f32[64,32,128]{2,1,0:T(8,128)S(1)}, f32[64,32,128]{2,1,0:T(8,128)}, u32[]{:S(2)}) copy-start(f32[64,32,128]{2,1,0:T(8,128)} %copy-done.30) | copy-start | bytes 3145732
  123.3 10.9 %copy-start.10 = (f32[64,8,128]{2,1,0:T(8,128)S(1)}, f32[64,8,128]{2,1,0:T(8,128)}, u32[]{:S(2)}) copy-start(f32[64,8,128]{2,1,0:T(8,128)} %copy-done.8) | copy-start | bytes 786436
  123.3 10.9 %copy-start.13 = (f32[64,8,128]{2,1,0:T(8,128)S(1)}, f32[64,8,128]{2,1,0:T(8,128)}, u32[]{:S(2)}) copy-start(f32[64,8,128]{2,1,0:T(8,128)} %copy-done.11) | copy-start | bytes 786436
  123.3 10.9 %copy-start.15 = (f32[64,48,128]{2,1,0:T(8,128)S(1)}, f32[64,48,128]{2,1,0:T(8,128)}, u32[]{:S(2)}) copy-start(f32[64,48,128]{2,1,0:T(8,128)} %copy-done.14) | copy-start | bytes 4718596
  123.3 10.9 %copy-start.25 = (f32[64,32,128]{2,1,0:T(8,128)S(1)}, f32[64,32,128]{2,1,0:T(8,128)}, u32[]{:S(2)}) copy-start(f32[64,32,128]{2,1,0:T(8,128)} %copy-done.24) | copy-start | bytes 3145732
  123.3 10.9 %copy-start.27 = (f32[64,32,128]{2,1,0:T(8,128)S(1)}, f32[64,32,128]{2,1,0:T(8,128)}, u32[]{:S(2)}) copy-start(f32[64,32,128]{2,1,0:T(8,128)} %copy-done.26) | copy-start | bytes 3145732
  123.3 10.9 %copy-start.29 = (f32[64,32,128]{2,1,0:T(8,128)S(1)}, f32[64,32,128]{2,1,0:T(8,128)}, u32[]{:S(2)}) copy-start(f32[64,32,128]{2,1,0:T(8,128)} %copy-done.28) | copy-start | bytes 3145732
  126.8 7.4 %collective-permute-start.12 = (f32[64,8,128]{2,1,0:T(8,128)S(1)}, f32[64,8,128]{2,1,0:T(8,128)S(1)}, u32[]{:S(2)}, u32[]{:S(2)}) collective-permute-start(f32[64,8,128]{2,1,0:T(8,128)S(1)} %get-tuple-element.65), channel_id=1, source_target_pairs={{0,1},{1,2},{2,3},{3,4},{4,5},{5,6},{6,7},{7,0},{8,9},{9,10},{10,1... | collective-permute-start | bytes 786440 | tf_op jit(solution)/shard_map/ppermute | solution.py:539
  126.9 7.3 %collective-permute-start.13 = (f32[64,8,128]{2,1,0:T(8,128)S(1)}, f32[64,8,128]{2,1,0:T(8,128)S(1)}, u32[]{:S(2)}, u32[]{:S(2)}) collective-permute-start(f32[64,8,128]{2,1,0:T(8,128)S(1)} %get-tuple-element.66), channel_id=1, source_target_pairs={{1,0},{2,1},{3,2},{4,3},{5,4},{6,5},{7,6},{0,7},{9,8},{10,9},{11,1... | collective-permute-start | bytes 786440 | tf_op jit(solution)/shard_map/ppermute | solution.py:539
  134.2 12.3 %copy-start.3 = (f32[64,32,128]{2,1,0:T(8,128)S(1)}, f32[64,32,128]{2,1,0:T(8,128)}, u32[]{:S(2)}) copy-start(f32[64,32,128]{2,1,0:T(8,128)} %copy-done.2) | copy-start | bytes 3145732
  134.2 12.2 %copy-start.21 = (f32[64,32,128]{2,1,0:T(8,128)S(1)}, f32[64,32,128]{2,1,0:T(8,128)}, u32[]{:S(2)}) copy-start(f32[64,32,128]{2,1,0:T(8,128)} %copy-done.20) | copy-start | bytes 3145732
  134.3 12.2 %copy-start.23 = (f32[64,32,128]{2,1,0:T(8,128)S(1)}, f32[64,32,128]{2,1,0:T(8,128)}, u32[]{:S(2)}) copy-start(f32[64,32,128]{2,1,0:T(8,128)} %copy-done.22) | copy-start | bytes 3145732
  140.5 6.0 %collective-permute-start.14 = (f32[32,8,128]{2,1,0:T(8,128)S(1)}, f32[32,8,128]{2,1,0:T(8,128)S(1)}, u32[]{:S(2)}, u32[]{:S(2)}) collective-permute-start(f32[32,8,128]{2,1,0:T(8,128)S(1)} %get-tuple-element.76), channel_id=1, source_target_pairs={{0,1},{1,2},{2,3},{3,4},{4,5},{5,6},{6,7},{7,0},{8,9},{9,10},{10,1... | collective-permute-start | bytes 393224 | tf_op jit(solution)/shard_map/ppermute | solution.py:539
  140.6 5.9 %collective-permute-start.15 = (f32[32,8,128]{2,1,0:T(8,128)S(1)}, f32[32,8,128]{2,1,0:T(8,128)S(1)}, u32[]{:S(2)}, u32[]{:S(2)}) collective-permute-start(f32[32,8,128]{2,1,0:T(8,128)S(1)} %get-tuple-element.77), channel_id=1, source_target_pairs={{1,0},{2,1},{3,2},{4,3},{5,4},{6,5},{7,6},{0,7},{9,8},{10,9},{11,1... | collective-permute-start | bytes 393224 | tf_op jit(solution)/shard_map/ppermute | solution.py:539
  173.8 8.3 %collective-permute-start.16 = (f32[2,8,32,128]{3,2,1,0:T(8,128)S(1)}, f32[2,8,32,128]{3,2,1,0:T(8,128)S(1)}, u32[]{:S(2)}, u32[]{:S(2)}) collective-permute-start(f32[2,8,32,128]{3,2,1,0:T(8,128)S(1)} %get-tuple-element.82), channel_id=1, source_target_pairs={{0,64},{8,72},{16,80},{24,88},{32,96},{40,104},{48,112},{56,120},{... | collective-permute-start | bytes 786440 | tf_op jit(solution)/shard_map/ppermute | solution.py:647
  (2 other events, 1.3 us)

commit v5 on v4

--- a/solution.py
+++ b/solution.py
@@ -159,22 +159,22 @@
         ref[x, pl.ds(y, 1), :] = row + jnp.where(lanes == z, amount, 0.0)
 
 
-NOW, PREV, EDGES, TURNED = 0, 32, 64, 72
-
-
-def unpack(turned, sems, now, edge, prev, extra):
+NOW, PREV, EDGES, HALF, TURNED = 0, 32, 64, 72, 144
+
+
+def unpack(turned, base, sems, now, edge, prev, extra):
     copies = []
     for n, (off, rows, dst) in enumerate(
         ((NOW, NYL, now), (EDGES, 8, edge), (PREV, NYL, prev), (NOW, NYL, extra))
     ):
-        copies.append(pltpu.make_async_copy(turned.at[:, off : off + rows, :], dst, sems.at[n]))
+        copies.append(pltpu.make_async_copy(turned.at[:, base + off : base + off + rows, :], dst, sems.at[n]))
     for c in copies:
         c.start()
     return copies
 
 
 def first_kernel(spots, wavelet, turned, r2, oper, lap, new, send_lo, send_hi, now, edge, ext, depth, prev, sems):
-    copies = unpack(turned, sems, ext.at[OWN_X, OWN_Y, :], edge, prev, now)
+    copies = unpack(turned, 0, sems, ext.at[OWN_X, OWN_Y, :], edge, prev, now)
     clear_ends(ext)
     for c in copies[:3]:
         c.wait()
@@ -247,7 +247,7 @@
 
 
 def late_kernel(spots, turned, r2, r2_lo, r2_hi, oper, mu, late, edge, ext, depth, later, sems):
-    copies = unpack(turned, sems, late, edge, later, ext.at[OWN_X, OWN_Y, :])
+    copies = unpack(turned, HALF, sems, late, edge, later, ext.at[OWN_X, OWN_Y, :])
     clear_ends(ext)
     for c in copies:
         c.wait()
@@ -351,35 +351,37 @@
     laplace(ext, depth, OWN, emit)
 
 
-def pack_kernel(now, prev, out, near, edge, sems):
-    bring = pltpu.make_async_copy(now, near, sems.at[16])
-    bring.start()
-    copies = []
-    for p in range(8):
-        for f, (off, field) in enumerate(((NOW, now), (PREV, prev))):
-            copies.append(
+def pack_kernel(now, prev, late, later, out, near, edge, sems):
+    order = ((0, now, NOW), (2, late, HALF + NOW), (1, prev, PREV), (3, later, HALF + PREV))
+    bring = {f: pltpu.make_async_copy(field, near.at[f], sems.at[f]) for f, field, _ in order}
+    for f, _, _ in order:
+        bring[f].start()
+    none = jnp.zeros((4, NZ), F32)
+    sent = []
+    for f, _, off in order:
+        bring[f].wait()
+        for p in range(8):
+            sent.append(
                 pltpu.make_async_copy(
-                    field.at[:, NYL * p : NYL * p + NYL, :], out.at[p, :, off : off + NYL, :], sems.at[2 * p + f]
+                    near.at[f, :, NYL * p : NYL * p + NYL, :], out.at[p, :, off : off + NYL, :], sems.at[4 + 8 * f + p]
                 )
             )
-    for c in copies:
-        c.start()
-    none = jnp.zeros((4, NZ), F32)
-    bring.wait()
-
-    def body(xi, carry):
-        for p in range(8):
-            lo = NYL * p
-            edge[p, xi, 0:4, :] = near[xi, lo - 4 : lo, :] if p > 0 else none
-            edge[p, xi, 4:8, :] = near[xi, lo + NYL : lo + NYL + 4, :] if p < 7 else none
-        return carry
-
-    lax.fori_loop(0, GROUP, body, 0)
-    ends = pltpu.make_async_copy(edge, out.at[:, :, EDGES : EDGES + 8, :], sems.at[17])
-    ends.start()
-    for c in copies:
+            sent[-1].start()
+        if f % 2 == 0:
+
+            def body(xi, carry):
+                for p in range(8):
+                    lo = NYL * p
+                    edge[f // 2, p, xi, 0:4, :] = near[f, xi, lo - 4 : lo, :] if p > 0 else none
+                    edge[f // 2, p, xi, 4:8, :] = near[f, xi, lo + NYL : lo + NYL + 4, :] if p < 7 else none
+                return carry
+
+            lax.fori_loop(0, GROUP, body, 0)
+            at = f // 2 * HALF + EDGES
+            sent.append(pltpu.make_async_copy(edge.at[f // 2], out.at[:, :, at : at + 8, :], sems.at[36 + f // 2]))
+            sent[-1].start()
+    for c in sent:
         c.wait()
-    ends.wait()
 
 
 def copy_block(dst, src):
@@ -494,17 +496,16 @@
 DEPTH = pltpu.VMEM((NX, WIDE, NZ), F32)
 FIELD_VMEM = pltpu.VMEM((NX, NYL, NZ), F32)
 TILE_VMEM = pltpu.VMEM((NX, 8, NZ), F32)
-PARAMS = pltpu.CompilerParams(vmem_limit_bytes=12 * 1024 * 1024)
-
-
-def call(kernel, specs, outs, scratch=(), flops=0, moved=0, out_spec=VMEM):
+
+
+def call(kernel, specs, outs, scratch=(), flops=0, moved=0, out_spec=VMEM, limit=12):
     return pl.pallas_call(
         kernel,
         in_specs=specs,
         out_specs=[out_spec] * len(outs),
         out_shape=outs,
         scratch_shapes=list(scratch),
-        compiler_params=PARAMS,
+        compiler_params=pltpu.CompilerParams(vmem_limit_bytes=limit << 20),
         cost_estimate=pl.CostEstimate(flops=flops, bytes_accessed=moved, transcendentals=0),
     )
 
@@ -547,22 +548,21 @@
     )
     come = [blocks[0]] + [lax.ppermute(blocks[k], "shot", along(k)) for k in (1, 2, 3)]
 
-    def turn(a, b):
-        (packed,) = call(
-            pack_kernel,
-            [ANY] * 2,
-            [jax.ShapeDtypeStruct((8, GROUP, TURNED, NZ), F32)],
-            [pltpu.VMEM((GROUP, 256, NZ), F32), pltpu.VMEM((8, GROUP, 8, NZ), F32), pltpu.SemaphoreType.DMA((18,))],
-            moved=5 << 20,
-            out_spec=ANY,
-        )(a, b)
-        return packed
-
-    def exchange(packed):
-        return lax.all_to_all(packed, "sub", 0, 0, tiled=True).reshape(NX, TURNED, NZ)
-
-    packed, other = lax.optimization_barrier((turn(wave_now[0], wave_prev[0]), other))
-    waves = exchange(packed)
+    (packed,) = call(
+        pack_kernel,
+        [ANY] * 4,
+        [jax.ShapeDtypeStruct((8, GROUP, TURNED, NZ), F32)],
+        [
+            pltpu.VMEM((4, GROUP, 256, NZ), F32),
+            pltpu.VMEM((2, 8, GROUP, 8, NZ), F32),
+            pltpu.SemaphoreType.DMA((38,)),
+        ],
+        moved=9 << 20,
+        out_spec=ANY,
+        limit=58,
+    )(wave_now[0], wave_prev[0], adj_late[0], adj_later[0])
+    packed, other = lax.optimization_barrier((packed, other))
+    turned = lax.all_to_all(packed, "sub", 0, 0, tiled=True).reshape(NX, TURNED, NZ)
     r2, *r2_send = call(assemble_kernel, [SMEM] * 2 + [VMEM] * 4, [FIELD, TILE, TILE], moved=2 << 20)(
         ids, apertures, *come
     )
@@ -586,6 +586,11 @@
     cells = receivers[0]
     lines = (cells // NZ) % 256 - NYL * part
 
+    count, data3, data1, data2, data4 = call(
+        receivers_kernel, [SMEM] * 3, [WIDE_FIELD, WIDE_FIELD] + [FIELD] * 3, moved=6 << 20
+    )(cells, lines, observed[0])
+    r2, count = lax.optimization_barrier((r2, count))
+
     lap0, u1, lo, hi, u0, u0_edge = call(
         first_kernel,
         [SMEM, SMEM, ANY, VMEM, VMEM],
@@ -593,12 +598,17 @@
         [EXT, DEPTH, FIELD_VMEM, pltpu.SemaphoreType.DMA((4,))],
         flops=10 << 20,
         moved=8 << 20,
-    )(spots, amounts, waves, r2, oper)
+    )(spots, amounts, turned, r2, oper)
     u1_halo = edges(lo, hi)
-    adjs = exchange(turn(adj_late[0], adj_later[0]))
-    count, data3, data1, data2, data4 = call(
-        receivers_kernel, [SMEM] * 3, [WIDE_FIELD, WIDE_FIELD] + [FIELD] * 3, moved=6 << 20
-    )(cells, lines, observed[0])
+    part4, mu5, mu5_edge = call(
+        late_kernel,
+        [SMEM, ANY] + [VMEM] * 4,
+        [FIELD, FIELD, TILE],
+        [EXT, DEPTH, FIELD_VMEM, pltpu.SemaphoreType.DMA((4,))],
+        flops=10 << 20,
+        moved=6 << 20,
+    )(spots, turned, r2, *r2_halo, oper)
+    u1, part4 = lax.optimization_barrier((u1, part4))
     lap1, u2, lap2, u3, lo, hi = call(
         middle_kernel,
         [SMEM, SMEM] + [VMEM] * 9,
@@ -608,15 +618,6 @@
         moved=12 << 20,
     )(spots, amounts, u1, *u1_halo, u0, u0_edge, r2, *r2_halo, oper)
     u3_halo = edges(lo, hi)
-    part4, mu5, mu5_edge = call(
-        late_kernel,
-        [SMEM, ANY] + [VMEM] * 4,
-        [FIELD, FIELD, TILE],
-        [EXT, DEPTH, FIELD_VMEM, pltpu.SemaphoreType.DMA((4,))],
-        flops=10 << 20,
-        moved=6 << 20,
-    )(spots, adjs, r2, *r2_halo, oper)
-
     total, mu4, lo, hi = call(
         turn_kernel,
         [SMEM, SMEM] + [VMEM] * 9,

time: 184 us -> 157 us (0.85)
  local copies, waits for them, and re-layouts: 25.1 us -> 7.99 us
  waiting for transfers between devices: 51.9 us -> 41.6 us
  starting transfers between devices: 41.2 us -> 38.2 us
  Pallas kernels: 37 us -> 39.3 us
    unnamed x95 -> x35, local copies, waits for them, and re-layouts: 24.3 us -> 7.26 us
    ppermute x3, waiting for transfers between devices: 6.62 us -> 0.01 us  [per_device(): lax.ppermute(blocks[k], 'shot', along(k))]
    all_to_all x2 -> x1, starting transfers between devices: 10.7 us -> 6.35 us  [per_device(): lax.all_to_all(packed, 'sub', 0, 0, tiled=True).reshape(NX, TURNED, NZ)]
    all_to_all x2 -> x1, waiting for transfers between devices: 26 us -> 23.6 us  [per_device(): lax.all_to_all(packed, 'sub', 0, 0, tiled=True).reshape(NX, TURNED, NZ)]
    ppermute x10, waiting for transfers between devices: 10.8 us -> 8.95 us  [edges(): return (lax.ppermute(hi, 'sub', up), lax.ppermute(lo, 'sub', down))]
    pallas_call x2 -> x1, Pallas kernels: 2.35 us -> 3.84 us  [per_device(): call(pack_kernel, [ANY] * 4, [jax.ShapeDtypeStruct((8, GROUP, TURNED, NZ)...]
  transfers between devices with their start and end apart: 19 -> 18, of which waited for: 10 -> 9; matrix products, arithmetic and copies ran while one was open for 1% -> 1% of each run, Pallas kernels for 13% -> 14%
where the time goes in v5:
time: 157 us; the launch traced here: 156 us
  waiting for transfers between devices  41.6 us (26%)
  Pallas kernels  39.3 us (25%)
  starting transfers between devices  38.2 us (24%)
  blocking collectives  24.9 us (16%)
  local copies, waits for them, and re-layouts  7.99 us (5%)
  between operations  3.03 us (2%)
    all_to_all x1, blocking collectives, per_device(): lax.all_to_all(total, 'shot', 0, 0, axis_index_groups=halves, tiled=True)  24.9 us
    all_to_all x1, waiting for transfers between devices, per_device(): lax.all_to_all(packed, 'sub', 0, 0, tiled=True).reshape(NX, TURNED, NZ)  23.6 us
    ppermute x10, starting transfers between devices, edges(): return (lax.ppermute(hi, 'sub', up), lax.ppermute(lo, 'sub', down))  18.8 us
    ppermute x10, waiting for transfers between devices, edges(): return (lax.ppermute(hi, 'sub', up), lax.ppermute(lo, 'sub', down))  8.95 us
    unnamed x35, local copies, waits for them, and re-layouts  7.26 us
    pallas_call x1, Pallas kernels, per_device(): call(back_kernel, [SMEM] + [VMEM] * 19, [FIELD] * 3 + [EDGE] * 2, [EXT, E...  6.4 us
    all_to_all x1, starting transfers between devices, per_device(): lax.all_to_all(packed, 'sub', 0, 0, tiled=True).reshape(NX, TURNED, NZ)  6.35 us
    ppermute x1, waiting for transfers between devices, per_device(): result = keep + lax.ppermute(give, 'shot', across)  5.82 us
  transfers between devices with their start and end apart: 18, of which 9 were waited for; matrix products, arithmetic and copies ran while one was open for 1% of the time, Pallas kernels for 14%

profile of v5, /device:TPU:1, one launch (start us, length us, event | category | flops | bytes accessed | tf_op | source)
XLA Modules:
  0.0 155.8 jit_solution(6636898619770647260)
XLA Ops:
  0.0 3.6 %collective-permute-start = (f32[2,8,32,128]{3,2,1,0:T(8,128)}, f32[2,8,32,128]{3,2,1,0:T(8,128)S(1)}, u32[]{:S(2)}, u32[]{:S(2)}) collective-permute-start(f32[2,8,32,128]{3,2,1,0:T(8,128)} %bitcast.29), channel_id=1, source_target_pairs={{0,64},{8,72},{16,80},{24,88},{32,96},{40,104},{48,112},{56,120},{... | collective-permute-start | bytes 786440 | tf_op jit(solution)/shard_map/ppermute | solution.py:543
  3.6 3.8 %shard_map.109 = f32[8,8,144,128]{3,2,1,0:T(8,128)} custom-call(f32[8,256,128]{2,1,0:T(8,128)} %bitcast.38, f32[8,256,128]{2,1,0:T(8,128)} %bitcast.39, f32[8,256,128]{2,1,0:T(8,128)} %bitcast.40, f32[8,256,128]{2,1,0:T(8,128)} %bitcast.41), custom_call_target="tpu_custom_call" | custom-call | bytes 9437184 | tf_op jit(solution)/shard_map/pallas_call | solution.py:551
  7.4 0.0 copy-start.9
  7.4 0.0 copy-start.16
  7.4 0.0 copy-start.14
  7.5 0.0 copy-start.13
  7.5 0.0 copy-start
  7.5 1.8 %collective-permute-done.other = f32[2,8,32,128]{3,2,1,0:T(8,128)S(1)} collective-permute-done((f32[2,8,32,128]{3,2,1,0:T(8,128)}, f32[2,8,32,128]{3,2,1,0:T(8,128)S(1)}, u32[]{:S(2)}, u32[]{:S(2)}) %collective-permute-start) | collective-permute-done | bytes 262176 | tf_op jit(solution)/shard_map/ppermute | solution.py:543
  9.3 6.3 %all-to-all-start = ((f32[8,8,144,128]{3,2,1,0:T(8,128)}), f32[8,8,144,128]{3,2,1,0:T(8,128)}, u32[]{:S(2)}, u32[]{:S(2)}) async-start(f32[8,8,144,128]{3,2,1,0:T(8,128)} %shard_map.109), calls=%async_computation | async-start | bytes 9437184 | tf_op jit(solution)/shard_map/all_to_all | solution.py:565
  15.7 1.9 %collective-permute-start.1 = (f32[2,8,32,128]{3,2,1,0:T(8,128)S(1)}, f32[2,8,32,128]{3,2,1,0:T(8,128)S(1)}, u32[]{:S(2)}, u32[]{:S(2)}) collective-permute-start(f32[2,8,32,128]{3,2,1,0:T(8,128)S(1)} %bitcast.30), channel_id=1, source_target_pairs={{0,8},{8,0},{16,24},{24,16},{32,40},{40,32},{48,56},{56,48},{64,72... | collective-permute-start | bytes 786440 | tf_op jit(solution)/shard_map/ppermute | solution.py:544
  17.6 0.1 collective-permute-start.2
  17.7 0.1 copy.14.apertures
  17.8 0.1 pad_add_fusion.ids
  17.8 0.9 collective-permute-done.1.piece_c
  18.8 0.4 collective-permute-done.2.other_c
  19.1 2.0 %shard_map.110 = (f32[2,8,32,128]{3,2,1,0:T(8,128)S(1)}, f32[2,8,32,128]{3,2,1,0:T(8,128)}, f32[2,8,32,128]{3,2,1,0:T(8,128)}, f32[2,8,32,128]{3,2,1,0:T(8,128)}) custom-call(s32[2]{0:T(128)S(1)} %pad_add_fusion.ids, s32[16,8]{1,0:T(8,128)S(1)} %copy.14.apertures, f32[2,8,32,128]{3,2,1,0:T(8,128)S(1)} %bitcast.31, ...), custom_call_target="tpu_custom_call" | custom-call | bytes 2097152 | tf_op jit(solution)/shard_map/pallas_call | solution.py:546
  21.1 1.3 collective-permute-start.3
  22.4 2.6 %collective-permute-start.4 = (f32[2,8,32,128]{3,2,1,0:T(8,128)}, f32[2,8,32,128]{3,2,1,0:T(8,128)S(1)}, u32[]{:S(2)}, u32[]{:S(2)}) collective-permute-start(f32[2,8,32,128]{3,2,1,0:T(8,128)} %get-tuple-element.51), channel_id=1, source_target_pairs={{0,32},{8,40},{16,48},{24,56},{32,0},{40,8},{48,16},{56,24},{64,96... | collective-permute-start | bytes 786440 | tf_op jit(solution)/shard_map/ppermute | solution.py:549
  25.0 1.1 collective-permute-start.5
  26.8 0.6 constant_dynamic-slice_fusion
  29.5 0.0 copy-start.15
  29.6 0.7 copy-done.15
  30.2 5.4 %shard_map.112 = (f32[64,48,128]{2,1,0:T(8,128)S(1)}, f32[64,48,128]{2,1,0:T(8,128)S(1)}, f32[64,32,128]{2,1,0:T(8,128)S(1)}, f32[64,32,128]{2,1,0:T(8,128)S(1)}, f32[64,32,128]{2,1,0:T(8,128)S(1)}) custom-call(s32[256]{0:T(256)S(1)} %bitcast.37, s32[256]{0:T(256)S(1)} %fusion.lines, f32[4,256]{1,0:T(4,128)S(1)} %bitcast.35), custom_call_target="tpu_custom_call" | custom-call | bytes 6291456 | tf_op jit(solution)/shard_map/pallas_call | solution.py:589
  35.6 1.1 copy-done.1
  36.8 1.0 copy-done.3
  37.7 1.1 copy-done.5
  38.8 1.0 copy-done.7
  39.8 0.1 stack.63.spots
  39.9 0.0 collective-permute-done.3.r1
  39.9 0.0 collective-permute-done.4.r2
  39.9 0.0 collective-permute-done.5.r3
  39.9 0.0 copy-start.10
  39.9 0.7 copy-done.10
  40.6 0.9 copy-done.11
  41.5 1.7 %shard_map.111 = (f32[64,32,128]{2,1,0:T(8,128)S(1)}, f32[64,8,128]{2,1,0:T(8,128)}, f32[64,8,128]{2,1,0:T(8,128)}) custom-call(s32[2]{0:T(128)S(1)} %pad_add_fusion.ids, s32[16,8]{1,0:T(8,128)S(1)} %copy.14.apertures, f32[2,8,32,128]{3,2,1,0:T(8,128)S(1)} %get-tuple-element.49.r0, f32[2,8,32,128]{3,2,1,0:T(8,128)S(1)} %collective-permute-done.3.r1, ...), custom_call_target="tpu_custom_call" | custom-call | bytes 2097152 | tf_op jit(solution)/shard_map/pallas_call | solution.py:566
  43.3 1.7 %collective-permute-start.6 = (f32[64,8,128]{2,1,0:T(8,128)}, f32[64,8,128]{2,1,0:T(8,128)S(1)}, u32[]{:S(2)}, u32[]{:S(2)}) collective-permute-start(f32[64,8,128]{2,1,0:T(8,128)} %get-tuple-element.57), channel_id=1, source_target_pairs={{0,1},{1,2},{2,3},{3,4},{4,5},{5,6},{6,7},{7,0},{8,9},{9,10},{10,1... | collective-permute-start | bytes 786440 | tf_op jit(solution)/shard_map/ppermute | solution.py:540
  44.9 1.9 %collective-permute-start.7 = (f32[64,8,128]{2,1,0:T(8,128)}, f32[64,8,128]{2,1,0:T(8,128)S(1)}, u32[]{:S(2)}, u32[]{:S(2)}) collective-permute-start(f32[64,8,128]{2,1,0:T(8,128)} %get-tuple-element.58), channel_id=1, source_target_pairs={{1,0},{2,1},{3,2},{4,3},{5,4},{6,5},{7,6},{0,7},{9,8},{10,9},{11,1... | collective-permute-start | bytes 786440 | tf_op jit(solution)/shard_map/ppermute | solution.py:540
  46.9 23.6 %all-to-all-done = f32[8,8,144,128]{3,2,1,0:T(8,128)} async-done(((f32[8,8,144,128]{3,2,1,0:T(8,128)}), f32[8,8,144,128]{3,2,1,0:T(8,128)}, u32[]{:S(2)}, u32[]{:S(2)}) %all-to-all-start) | async-done | bytes 4718624 | tf_op jit(solution)/shard_map/all_to_all | solution.py:565
  70.5 0.7 copy-done.12
  71.2 4.0 %shard_map.113 = (f32[64,32,128]{2,1,0:T(8,128)S(1)}, f32[64,32,128]{2,1,0:T(8,128)S(1)}, f32[64,8,128]{2,1,0:T(8,128)S(1)}, f32[64,8,128]{2,1,0:T(8,128)S(1)}, ...) custom-call(s32[8]{0:T(128)S(1)} %stack.63.spots, f32[4]{0:T(128)S(1)} %bitcast.32, ...), custom_call_target="tpu_custom_call" | custom-call | flops 10485760 | bytes 8388608 | tf_op jit(solution)/shard_map/pallas_call | solution.py:594
  75.2 0.1 collective-permute-start.8
  75.3 3.9 %collective-permute-start.9 = (f32[64,8,128]{2,1,0:T(8,128)S(1)}, f32[64,8,128]{2,1,0:T(8,128)S(1)}, u32[]{:S(2)}, u32[]{:S(2)}) collective-permute-start(f32[64,8,128]{2,1,0:T(8,128)S(1)} %get-tuple-element.62), channel_id=1, source_target_pairs={{1,0},{2,1},{3,2},{4,3},{5,4},{6,5},{7,6},{0,7},{9,8},{10,9},{11,1... | collective-permute-start | bytes 786440 | tf_op jit(solution)/shard_map/ppermute | solution.py:540
  79.3 4.4 %shard_map.114 = (f32[64,32,128]{2,1,0:T(8,128)S(1)}, f32[64,32,128]{2,1,0:T(8,128)S(1)}, f32[64,8,128]{2,1,0:T(8,128)S(1)}) custom-call(s32[8]{0:T(128)S(1)} %stack.63.spots, f32[64,144,128]{2,1,0:T(8,128)} %bitcast.18.turned, f32[64,32,128]{2,1,0:T(8,128)S(1)} %get-tuple-element.55.r2, f32[64,8,128]{2,1,0:T(8,128)S(1)} %collective-permute-done.6.r2_lo, ...), custom_call_target="tpu_custom_call" | custom-call | flops 10485760 | bytes 6291456 | tf_op jit(solution)/shard_map/pallas_call | solution.py:603
  83.7 0.6 collective-permute-done.8.now_lo
  84.3 0.0 collective-permute-done.9.now_hi
  84.3 5.0 %shard_map.115 = (f32[64,32,128]{2,1,0:T(8,128)S(1)}, f32[64,32,128]{2,1,0:T(8,128)S(1)}, f32[64,32,128]{2,1,0:T(8,128)S(1)}, f32[64,32,128]{2,1,0:T(8,128)S(1)}...) custom-call(s32[8]{0:T(128)S(1)} %stack.63.spots, f32[4]{0:T(128)S(1)} %bitcast.33, ...), custom_call_target="tpu_custom_call" | custom-call | flops 20971520 | bytes 12582912 | tf_op jit(solution)/shard_map/pallas_call | solution.py:612
  89.3 0.1 collective-permute-start.10
  89.4 3.6 %collective-permute-start.11 = (f32[32,8,128]{2,1,0:T(8,128)S(1)}, f32[32,8,128]{2,1,0:T(8,128)S(1)}, u32[]{:S(2)}, u32[]{:S(2)}) collective-permute-start(f32[32,8,128]{2,1,0:T(8,128)S(1)} %get-tuple-element.67), channel_id=1, source_target_pairs={{1,0},{2,1},{3,2},{4,3},{5,4},{6,5},{7,6},{0,7},{9,8},{10,9},{11,1... | collective-permute-start | bytes 393224 | tf_op jit(solution)/shard_map/ppermute | solution.py:540
  93.0 2.4 %collective-permute-done.10.halo_lo.wave_lo = f32[32,8,128]{2,1,0:T(8,128)S(1)} collective-permute-done((f32[32,8,128]{2,1,0:T(8,128)S(1)}, f32[32,8,128]{2,1,0:T(8,128)S(1)}, u32[]{:S(2)}, u32[]{:S(2)}) %collective-permute-start.10) | collective-permute-done | bytes 131104 | tf_op jit(solution)/shard_map/ppermute | solution.py:540
  95.3 0.0 collective-permute-done.11.halo_hi.wave_hi
  95.3 2.9 %shard_map.116 = (f32[64,32,128]{2,1,0:T(8,128)S(1)}, f32[64,32,128]{2,1,0:T(8,128)S(1)}, f32[64,8,128]{2,1,0:T(8,128)S(1)}, f32[64,8,128]{2,1,0:T(8,128)S(1)}) custom-call(s32[8]{0:T(128)S(1)} %stack.63.spots, f32[4]{0:T(128)S(1)} %bitcast.34, f32[64,32,128]{2,1,0:T(8,128)S(1)} %get-tuple-element.65.now.wave_a, ...), custom_call_target="tpu_custom_call" | custom-call | flops 10485760 | bytes 8388608 | tf_op jit(solution)/shard_map/pallas_call | solution.py:621
  98.2 1.1 collective-permute-start.12
  99.4 2.6 %collective-permute-start.13 = (f32[64,8,128]{2,1,0:T(8,128)S(1)}, f32[64,8,128]{2,1,0:T(8,128)S(1)}, u32[]{:S(2)}, u32[]{:S(2)}) collective-permute-start(f32[64,8,128]{2,1,0:T(8,128)S(1)} %get-tuple-element.74), channel_id=1, source_target_pairs={{1,0},{2,1},{3,2},{4,3},{5,4},{6,5},{7,6},{0,7},{9,8},{10,9},{11,1... | collective-permute-start | bytes 786440 | tf_op jit(solution)/shard_map/ppermute | solution.py:540
  101.9 3.7 %collective-permute-done.12.late_lo = f32[64,8,128]{2,1,0:T(8,128)S(1)} collective-permute-done((f32[64,8,128]{2,1,0:T(8,128)S(1)}, f32[64,8,128]{2,1,0:T(8,128)S(1)}, u32[]{:S(2)}, u32[]{:S(2)}) %collective-permute-start.12) | collective-permute-done | bytes 262176 | tf_op jit(solution)/shard_map/ppermute | solution.py:540
  105.6 6.4 %shard_map.117 = (f32[64,32,128]{2,1,0:T(8,128)S(1)}, f32[64,32,128]{2,1,0:T(8,128)S(1)}, f32[64,32,128]{2,1,0:T(8,128)S(1)}, f32[32,8,128]{2,1,0:T(8,128)S(1)}, f32[32,8,128]{2,1,0:T(8,128)S(1)}) custom-call(s32[8]{0:T(128)S(1)} %stack.63.spots, f32[64,32,128]{2,1,0:T(8,128)S(1)} %get-tuple-element.72.late, ...), custom_call_target="tpu_custom_call" | custom-call | flops 20971520 | bytes 16777216 | tf_op jit(solution)/shard_map/pallas_call | solution.py:630
  112.1 1.7 %collective-permute-start.14 = (f32[32,8,128]{2,1,0:T(8,128)S(1)}, f32[32,8,128]{2,1,0:T(8,128)S(1)}, u32[]{:S(2)}, u32[]{:S(2)}) collective-permute-start(f32[32,8,128]{2,1,0:T(8,128)S(1)} %get-tuple-element.84), channel_id=1, source_target_pairs={{0,1},{1,2},{2,3},{3,4},{4,5},{5,6},{6,7},{7,0},{8,9},{9,10},{10,1... | collective-permute-start | bytes 393224 | tf_op jit(solution)/shard_map/ppermute | solution.py:540
  113.7 2.1 %collective-permute-start.15 = (f32[32,8,128]{2,1,0:T(8,128)S(1)}, f32[32,8,128]{2,1,0:T(8,128)S(1)}, u32[]{:S(2)}, u32[]{:S(2)}) collective-permute-start(f32[32,8,128]{2,1,0:T(8,128)S(1)} %get-tuple-element.85), channel_id=1, source_target_pairs={{1,0},{2,1},{3,2},{4,3},{5,4},{6,5},{7,6},{0,7},{9,8},{10,9},{11,1... | collective-permute-start | bytes 393224 | tf_op jit(solution)/shard_map/ppermute | solution.py:540
  115.8 2.3 %collective-permute-done.14.halo_lo = f32[32,8,128]{2,1,0:T(8,128)S(1)} collective-permute-done((f32[32,8,128]{2,1,0:T(8,128)S(1)}, f32[32,8,128]{2,1,0:T(8,128)S(1)}, u32[]{:S(2)}, u32[]{:S(2)}) %collective-permute-start.14) | collective-permute-done | bytes 131104 | tf_op jit(solution)/shard_map/ppermute | solution.py:540
  118.1 2.7 %shard_map.118 = f32[8,8,32,128]{3,2,1,0:T(8,128)S(1)} custom-call(s32[8]{0:T(128)S(1)} %stack.63.spots, f32[64,32,128]{2,1,0:T(8,128)S(1)} %get-tuple-element.82.late, f32[64,32,128]{2,1,0:T(8,128)S(1)} %get-tuple-element.83.later, f32[64,32,128]{2,1,0:T(8,128)S(1)} %get-tuple-element.55.r2, f32[32,8,128]{2,1,0:T(8,128)S(1)} %collective-permute-done.14.halo_lo, ...), custom_call_target="tpu_custom_call" | custom-call | flops 10485760 | bytes 8388608 | tf_op jit(solution)/shard_map/pallas_call | solution.py:642
  120.8 24.9 %all_to_all.10.recv = f32[8,8,32,128]{3,2,1,0:T(8,128)S(1)} all-to-all(f32[8,8,32,128]{3,2,1,0:T(8,128)S(1)} %shard_map.118), channel_id=1, replica_groups={{0,8,16,24,32,40,48,56},{64,72,80,88,96,104,112,120},{1,9,17,25,33,41,4..., dimensions={0} | all-to-all | bytes 2097152 | tf_op jit(solution)/shard_map/all_to_all | solution.py:646
  145.7 1.0 shard_map.119
  146.7 2.5 %collective-permute-start.16 = (f32[2,8,32,128]{3,2,1,0:T(8,128)S(1)}, f32[2,8,32,128]{3,2,1,0:T(8,128)S(1)}, u32[]{:S(2)}, u32[]{:S(2)}) collective-permute-start(f32[2,8,32,128]{3,2,1,0:T(8,128)S(1)} %get-tuple-element.90), channel_id=1, source_target_pairs={{0,64},{8,72},{16,80},{24,88},{32,96},{40,104},{48,112},{56,120},{... | collective-permute-start | bytes 786440 | tf_op jit(solution)/shard_map/ppermute | solution.py:648
  149.3 5.8 %collective-permute-done.16 = f32[2,8,32,128]{3,2,1,0:T(8,128)S(1)} collective-permute-done((f32[2,8,32,128]{3,2,1,0:T(8,128)S(1)}, f32[2,8,32,128]{3,2,1,0:T(8,128)S(1)}, u32[]{:S(2)}, u32[]{:S(2)}) %collective-permute-start.16) | collective-permute-done | bytes 262176 | tf_op jit(solution)/shard_map/ppermute | solution.py:648
  155.1 0.7 add_bitcast_fusion
  (24 shorter events, 0.1 us)
Async XLA Ops:
  0.0 9.3 %collective-permute-start = (f32[2,8,32,128]{3,2,1,0:T(8,128)}, f32[2,8,32,128]{3,2,1,0:T(8,128)S(1)}, u32[]{:S(2)}, u32[]{:S(2)}) collective-permute-start(f32[2,8,32,128]{3,2,1,0:T(8,128)} %bitcast.29), channel_id=1, source_target_pairs={{0,64},{8,72},{16,80},{24,88},{32,96},{40,104},{48,112},{56,120},{... | collective-permute-start | bytes 786440 | tf_op jit(solution)/shard_map/ppermute | solution.py:543
  7.4 8.3 %copy-start.9 = (f32[2,1,8,32,128]{4,3,2,1,0:T(8,128)S(1)}, f32[2,1,8,32,128]{4,3,2,1,0:T(8,128)}, u32[]{:S(2)}) copy-start(f32[2,1,8,32,128]{4,3,2,1,0:T(8,128)} %param.11) | copy-start | bytes 786436
  7.4 10.3 %copy-start.16 = (s32[16,8]{0,1:T(8,128)S(1)}, s32[16,8]{0,1:T(8,128)}, u32[]{:S(2)}) copy-start(s32[16,8]{0,1:T(8,128)} %param.20) | copy-start | bytes 1540
  7.4 22.1 %copy-start.14 = (s32[1,256]{1,0:T(1,128)S(1)}, s32[1,256]{1,0:T(1,128)}, u32[]{:S(2)}) copy-start(s32[1,256]{1,0:T(1,128)} %param.18) | copy-start | bytes 3076
  7.5 22.1 %copy-start.13 = (f32[1,4,256]{2,1,0:T(4,128)S(1)}, f32[1,4,256]{2,1,0:T(4,128)}, u32[]{:S(2)}) copy-start(f32[1,4,256]{2,1,0:T(4,128)} %param.19) | copy-start | bytes 12292
  7.5 63.0 %copy-start = (bf16[256,256]{1,0:T(8,128)(2,1)S(1)}, bf16[256,256]{1,0:T(8,128)(2,1)}, u32[]{:S(2)}) copy-start(bf16[256,256]{1,0:T(8,128)(2,1)} %constant.94.clone.oper) | copy-start | bytes 393220
  9.3 61.2 %all-to-all-start = ((f32[8,8,144,128]{3,2,1,0:T(8,128)}), f32[8,8,144,128]{3,2,1,0:T(8,128)}, u32[]{:S(2)}, u32[]{:S(2)}) async-start(f32[8,8,144,128]{3,2,1,0:T(8,128)} %shard_map.109), calls=%async_computation | async-start | bytes 9437184 | tf_op jit(solution)/shard_map/all_to_all | solution.py:565
  15.7 3.1 %collective-permute-start.1 = (f32[2,8,32,128]{3,2,1,0:T(8,128)S(1)}, f32[2,8,32,128]{3,2,1,0:T(8,128)S(1)}, u32[]{:S(2)}, u32[]{:S(2)}) collective-permute-start(f32[2,8,32,128]{3,2,1,0:T(8,128)S(1)} %bitcast.30), channel_id=1, source_target_pairs={{0,8},{8,0},{16,24},{24,16},{32,40},{40,32},{48,56},{56,48},{64,72... | collective-permute-start | bytes 786440 | tf_op jit(solution)/shard_map/ppermute | solution.py:544
  17.6 1.5 collective-permute-start.2
  21.1 18.8 %collective-permute-start.3 = (f32[2,8,32,128]{3,2,1,0:T(8,128)}, f32[2,8,32,128]{3,2,1,0:T(8,128)S(1)}, u32[]{:S(2)}, u32[]{:S(2)}) collective-permute-start(f32[2,8,32,128]{3,2,1,0:T(8,128)} %get-tuple-element.50), channel_id=1, source_target_pairs={{0,16},{8,24},{16,32},{24,40},{32,48},{40,56},{48,0},{56,8},{64,80... | collective-permute-start | bytes 786440 | tf_op jit(solution)/shard_map/ppermute | solution.py:549
  22.4 17.5 %collective-permute-start.4 = (f32[2,8,32,128]{3,2,1,0:T(8,128)}, f32[2,8,32,128]{3,2,1,0:T(8,128)S(1)}, u32[]{:S(2)}, u32[]{:S(2)}) collective-permute-start(f32[2,8,32,128]{3,2,1,0:T(8,128)} %get-tuple-element.51), channel_id=1, source_target_pairs={{0,32},{8,40},{16,48},{24,56},{32,0},{40,8},{48,16},{56,24},{64,96... | collective-permute-start | bytes 786440 | tf_op jit(solution)/shard_map/ppermute | solution.py:549
  25.0 14.9 %collective-permute-start.5 = (f32[2,8,32,128]{3,2,1,0:T(8,128)}, f32[2,8,32,128]{3,2,1,0:T(8,128)S(1)}, u32[]{:S(2)}, u32[]{:S(2)}) collective-permute-start(f32[2,8,32,128]{3,2,1,0:T(8,128)} %get-tuple-element.52), channel_id=1, source_target_pairs={{0,48},{8,56},{16,0},{24,8},{32,16},{40,24},{48,32},{56,40},{64,11... | collective-permute-start | bytes 786440 | tf_op jit(solution)/shard_map/ppermute | solution.py:549
  29.5 0.7 copy-start.15
  35.6 1.2 copy-start.1
  36.8 1.0 copy-start.3
  37.7 1.1 copy-start.5
  38.8 1.0 copy-start.7
  39.9 0.7 copy-start.10
  40.6 0.9 copy-start.11
  43.3 36.0 %collective-permute-start.6 = (f32[64,8,128]{2,1,0:T(8,128)}, f32[64,8,128]{2,1,0:T(8,128)S(1)}, u32[]{:S(2)}, u32[]{:S(2)}) collective-permute-start(f32[64,8,128]{2,1,0:T(8,128)} %get-tuple-element.57), channel_id=1, source_target_pairs={{0,1},{1,2},{2,3},{3,4},{4,5},{5,6},{6,7},{7,0},{8,9},{9,10},{10,1... | collective-permute-start | bytes 786440 | tf_op jit(solution)/shard_map/ppermute | solution.py:540
  44.9 34.3 %collective-permute-start.7 = (f32[64,8,128]{2,1,0:T(8,128)}, f32[64,8,128]{2,1,0:T(8,128)S(1)}, u32[]{:S(2)}, u32[]{:S(2)}) collective-permute-start(f32[64,8,128]{2,1,0:T(8,128)} %get-tuple-element.58), channel_id=1, source_target_pairs={{1,0},{2,1},{3,2},{4,3},{5,4},{6,5},{7,6},{0,7},{9,8},{10,9},{11,1... | collective-permute-start | bytes 786440 | tf_op jit(solution)/shard_map/ppermute | solution.py:540
  70.5 0.7 copy-start.12
  75.2 9.1 %collective-permute-start.8 = (f32[64,8,128]{2,1,0:T(8,128)S(1)}, f32[64,8,128]{2,1,0:T(8,128)S(1)}, u32[]{:S(2)}, u32[]{:S(2)}) collective-permute-start(f32[64,8,128]{2,1,0:T(8,128)S(1)} %get-tuple-element.61), channel_id=1, source_target_pairs={{0,1},{1,2},{2,3},{3,4},{4,5},{5,6},{6,7},{7,0},{8,9},{9,10},{10,1... | collective-permute-start | bytes 786440 | tf_op jit(solution)/shard_map/ppermute | solution.py:540
  75.3 20.0 %copy-start.8 = (f32[64,32,128]{2,1,0:T(8,128)S(1)}, f32[64,32,128]{2,1,0:T(8,128)}, u32[]{:S(2)}) copy-start(f32[64,32,128]{2,1,0:T(8,128)} %copy-done.7) | copy-start | bytes 3145732
  75.3 9.0 %collective-permute-start.9 = (f32[64,8,128]{2,1,0:T(8,128)S(1)}, f32[64,8,128]{2,1,0:T(8,128)S(1)}, u32[]{:S(2)}, u32[]{:S(2)}) collective-permute-start(f32[64,8,128]{2,1,0:T(8,128)S(1)} %get-tuple-element.62), channel_id=1, source_target_pairs={{1,0},{2,1},{3,2},{4,3},{5,4},{6,5},{7,6},{0,7},{9,8},{10,9},{11,1... | collective-permute-start | bytes 786440 | tf_op jit(solution)/shard_map/ppermute | solution.py:540
  89.3 16.3 %copy-start.2 = (f32[64,48,128]{2,1,0:T(8,128)S(1)}, f32[64,48,128]{2,1,0:T(8,128)}, u32[]{:S(2)}) copy-start(f32[64,48,128]{2,1,0:T(8,128)} %copy-done.1) | copy-start | bytes 4718596
  89.3 16.3 %copy-start.6 = (f32[64,32,128]{2,1,0:T(8,128)S(1)}, f32[64,32,128]{2,1,0:T(8,128)}, u32[]{:S(2)}) copy-start(f32[64,32,128]{2,1,0:T(8,128)} %copy-done.5) | copy-start | bytes 3145732
  89.3 6.0 %collective-permute-start.10 = (f32[32,8,128]{2,1,0:T(8,128)S(1)}, f32[32,8,128]{2,1,0:T(8,128)S(1)}, u32[]{:S(2)}, u32[]{:S(2)}) collective-permute-start(f32[32,8,128]{2,1,0:T(8,128)S(1)} %get-tuple-element.66), channel_id=1, source_target_pairs={{0,1},{1,2},{2,3},{3,4},{4,5},{5,6},{6,7},{7,0},{8,9},{9,10},{10,1... | collective-permute-start | bytes 393224 | tf_op jit(solution)/shard_map/ppermute | solution.py:540
  89.4 5.9 %collective-permute-start.11 = (f32[32,8,128]{2,1,0:T(8,128)S(1)}, f32[32,8,128]{2,1,0:T(8,128)S(1)}, u32[]{:S(2)}, u32[]{:S(2)}) collective-permute-start(f32[32,8,128]{2,1,0:T(8,128)S(1)} %get-tuple-element.67), channel_id=1, source_target_pairs={{1,0},{2,1},{3,2},{4,3},{5,4},{6,5},{7,6},{0,7},{9,8},{10,9},{11,1... | collective-permute-start | bytes 393224 | tf_op jit(solution)/shard_map/ppermute | solution.py:540
  98.2 7.4 %collective-permute-start.12 = (f32[64,8,128]{2,1,0:T(8,128)S(1)}, f32[64,8,128]{2,1,0:T(8,128)S(1)}, u32[]{:S(2)}, u32[]{:S(2)}) collective-permute-start(f32[64,8,128]{2,1,0:T(8,128)S(1)} %get-tuple-element.73), channel_id=1, source_target_pairs={{0,1},{1,2},{2,3},{3,4},{4,5},{5,6},{6,7},{7,0},{8,9},{9,10},{10,1... | collective-permute-start | bytes 786440 | tf_op jit(solution)/shard_map/ppermute | solution.py:540
  99.4 6.3 %collective-permute-start.13 = (f32[64,8,128]{2,1,0:T(8,128)S(1)}, f32[64,8,128]{2,1,0:T(8,128)S(1)}, u32[]{:S(2)}, u32[]{:S(2)}) collective-permute-start(f32[64,8,128]{2,1,0:T(8,128)S(1)} %get-tuple-element.74), channel_id=1, source_target_pairs={{1,0},{2,1},{3,2},{4,3},{5,4},{6,5},{7,6},{0,7},{9,8},{10,9},{11,1... | collective-permute-start | bytes 786440 | tf_op jit(solution)/shard_map/ppermute | solution.py:540
  105.6 12.5 %copy-start.4 = (f32[64,32,128]{2,1,0:T(8,128)S(1)}, f32[64,32,128]{2,1,0:T(8,128)}, u32[]{:S(2)}) copy-start(f32[64,32,128]{2,1,0:T(8,128)} %copy-done.3) | copy-start | bytes 3145732
  112.1 6.1 %collective-permute-start.14 = (f32[32,8,128]{2,1,0:T(8,128)S(1)}, f32[32,8,128]{2,1,0:T(8,128)S(1)}, u32[]{:S(2)}, u32[]{:S(2)}) collective-permute-start(f32[32,8,128]{2,1,0:T(8,128)S(1)} %get-tuple-element.84), channel_id=1, source_target_pairs={{0,1},{1,2},{2,3},{3,4},{4,5},{5,6},{6,7},{7,0},{8,9},{9,10},{10,1... | collective-permute-start | bytes 393224 | tf_op jit(solution)/shard_map/ppermute | solution.py:540
  113.7 4.4 %collective-permute-start.15 = (f32[32,8,128]{2,1,0:T(8,128)S(1)}, f32[32,8,128]{2,1,0:T(8,128)S(1)}, u32[]{:S(2)}, u32[]{:S(2)}) collective-permute-start(f32[32,8,128]{2,1,0:T(8,128)S(1)} %get-tuple-element.85), channel_id=1, source_target_pairs={{1,0},{2,1},{3,2},{4,3},{5,4},{6,5},{7,6},{0,7},{9,8},{10,9},{11,1... | collective-permute-start | bytes 393224 | tf_op jit(solution)/shard_map/ppermute | solution.py:540
  146.7 8.3 %collective-permute-start.16 = (f32[2,8,32,128]{3,2,1,0:T(8,128)S(1)}, f32[2,8,32,128]{3,2,1,0:T(8,128)S(1)}, u32[]{:S(2)}, u32[]{:S(2)}) collective-permute-start(f32[2,8,32,128]{3,2,1,0:T(8,128)S(1)} %get-tuple-element.90), channel_id=1, source_target_pairs={{0,64},{8,72},{16,80},{24,88},{32,96},{40,104},{48,112},{56,120},{... | collective-permute-start | bytes 786440 | tf_op jit(solution)/shard_map/ppermute | solution.py:648

commit v6 on v5

--- a/solution.py
+++ b/solution.py
@@ -561,7 +561,6 @@
         out_spec=ANY,
         limit=58,
     )(wave_now[0], wave_prev[0], adj_late[0], adj_later[0])
-    packed, other = lax.optimization_barrier((packed, other))
     turned = lax.all_to_all(packed, "sub", 0, 0, tiled=True).reshape(NX, TURNED, NZ)
     r2, *r2_send = call(assemble_kernel, [SMEM] * 2 + [VMEM] * 4, [FIELD, TILE, TILE], moved=2 << 20)(
         ids, apertures, *come
@@ -587,7 +586,7 @@
     lines = (cells // NZ) % 256 - NYL * part
 
     count, data3, data1, data2, data4 = call(
-        receivers_kernel, [SMEM] * 3, [WIDE_FIELD, WIDE_FIELD] + [FIELD] * 3, moved=6 << 20
+        receivers_kernel, [SMEM] * 3, [WIDE_FIELD, WIDE_FIELD] + [FIELD] * 3, flops=1 << 40, moved=6 << 20
     )(cells, lines, observed[0])
     r2, count = lax.optimization_barrier((r2, count))
 

time: 157 us -> 153 us (0.975)
  waiting for transfers between devices: 41.6 us -> 45.4 us
  starting transfers between devices: 38.2 us -> 34.8 us
  local copies, waits for them, and re-layouts: 7.99 us -> 5.7 us
    all_to_all x1, waiting for transfers between devices: 23.6 us -> 27.2 us  [per_device(): lax.all_to_all(packed, 'sub', 0, 0, tiled=True).reshape(NX, TURNED, NZ)]
    unnamed x35 -> x37, local copies, waits for them, and re-layouts: 7.26 us -> 4.33 us
    ppermute x1, waiting for transfers between devices: 1.85 us -> 0.01 us  [per_device(): other = lax.ppermute(piece, 'shot', across)]
  transfers between devices with their start and end apart: 18 -> 18, of which waited for: 9 -> 7; matrix products, arithmetic and copies ran while one was open for 1% -> 1% of each run, Pallas kernels for 14% -> 14%
where the time goes in v6:
time: 153 us; the launch traced here: 152 us
  waiting for transfers between devices  45.4 us (30%)
  Pallas kernels  38.4 us (25%)
  starting transfers between devices  34.8 us (23%)
  blocking collectives  24 us (16%)
  local copies, waits for them, and re-layouts  5.7 us (4%)
  between operations  2.9 us (2%)
    all_to_all x1, waiting for transfers between devices, per_device(): lax.all_to_all(packed, 'sub', 0, 0, tiled=True).reshape(NX, TURNED, NZ)  27.2 us
    all_to_all x1, blocking collectives, per_device(): lax.all_to_all(total, 'shot', 0, 0, axis_index_groups=halves, tiled=True)  24 us
    ppermute x10, starting transfers between devices, edges(): return (lax.ppermute(hi, 'sub', up), lax.ppermute(lo, 'sub', down))  18.6 us
    ppermute x10, waiting for transfers between devices, edges(): return (lax.ppermute(hi, 'sub', up), lax.ppermute(lo, 'sub', down))  9.9 us
    ppermute x1, waiting for transfers between devices, per_device(): result = keep + lax.ppermute(give, 'shot', across)  7.24 us
    pallas_call x1, Pallas kernels, per_device(): call(back_kernel, [SMEM] + [VMEM] * 19, [FIELD] * 3 + [EDGE] * 2, [EXT, E...  5.61 us
    all_to_all x1, starting transfers between devices, per_device(): lax.all_to_all(packed, 'sub', 0, 0, tiled=True).reshape(NX, TURNED, NZ)  5.21 us
    pallas_call x1, Pallas kernels, per_device(): call(receivers_kernel, [SMEM] * 3, [WIDE_FIELD, WIDE_FIELD] + [FIELD] * 3...  5.11 us
  transfers between devices with their start and end apart: 18, of which 7 were waited for; matrix products, arithmetic and copies ran while one was open for 1% of the time, Pallas kernels for 14%

profile of v6, /device:TPU:1, one launch (start us, length us, event | category | flops | bytes accessed | tf_op | source)
XLA Modules:
  0.0 152.0 jit_solution(12726849439424745335)
XLA Ops:
  0.0 3.6 %collective-permute-start = (f32[2,8,32,128]{3,2,1,0:T(8,128)}, f32[2,8,32,128]{3,2,1,0:T(8,128)S(1)}, u32[]{:S(2)}, u32[]{:S(2)}) collective-permute-start(f32[2,8,32,128]{3,2,1,0:T(8,128)} %bitcast.29), channel_id=1, source_target_pairs={{0,64},{8,72},{16,80},{24,88},{32,96},{40,104},{48,112},{56,120},{... | collective-permute-start | bytes 786440 | tf_op jit(solution)/shard_map/ppermute | solution.py:543
  3.6 1.0 collective-permute-start.1
  4.5 3.8 %shard_map.109 = f32[8,8,144,128]{3,2,1,0:T(8,128)} custom-call(f32[8,256,128]{2,1,0:T(8,128)} %bitcast.38, f32[8,256,128]{2,1,0:T(8,128)} %bitcast.39, f32[8,256,128]{2,1,0:T(8,128)} %bitcast.40, f32[8,256,128]{2,1,0:T(8,128)} %bitcast.41), custom_call_target="tpu_custom_call" | custom-call | bytes 9437184 | tf_op jit(solution)/shard_map/pallas_call | solution.py:551
  8.3 0.0 copy-start.17
  8.3 0.0 copy-start.15
  8.3 0.0 copy-start.9
  8.3 0.0 copy-start.16
  8.3 5.2 %all-to-all-start = ((f32[8,8,144,128]{3,2,1,0:T(8,128)}), f32[8,8,144,128]{3,2,1,0:T(8,128)}, u32[]{:S(2)}, u32[]{:S(2)}) async-start(f32[8,8,144,128]{3,2,1,0:T(8,128)} %shard_map.109), calls=%async_computation | async-start | bytes 9437184 | tf_op jit(solution)/shard_map/all_to_all | solution.py:564
  13.6 0.0 collective-permute-done.other
  13.6 0.4 collective-permute-start.2
  13.9 0.1 pad_add_fusion.ids
  14.0 0.1 copy.14.apertures
  14.1 0.0 collective-permute-done.1.piece_c
  14.1 1.1 collective-permute-done.2.other_c
  15.2 2.0 %shard_map.110 = (f32[2,8,32,128]{3,2,1,0:T(8,128)S(1)}, f32[2,8,32,128]{3,2,1,0:T(8,128)}, f32[2,8,32,128]{3,2,1,0:T(8,128)}, f32[2,8,32,128]{3,2,1,0:T(8,128)}) custom-call(s32[2]{0:T(128)S(1)} %pad_add_fusion.ids, s32[16,8]{1,0:T(8,128)S(1)} %copy.14.apertures, f32[2,8,32,128]{3,2,1,0:T(8,128)S(1)} %bitcast.31, ...), custom_call_target="tpu_custom_call" | custom-call | bytes 2097152 | tf_op jit(solution)/shard_map/pallas_call | solution.py:546
  17.1 1.3 collective-permute-start.3
  18.4 2.6 %collective-permute-start.4 = (f32[2,8,32,128]{3,2,1,0:T(8,128)}, f32[2,8,32,128]{3,2,1,0:T(8,128)}, u32[]{:S(2)}, u32[]{:S(2)}) collective-permute-start(f32[2,8,32,128]{3,2,1,0:T(8,128)} %get-tuple-element.49), channel_id=1, source_target_pairs={{0,32},{8,40},{16,48},{24,56},{32,0},{40,8},{48,16},{56,24},{64,96... | collective-permute-start | bytes 786440 | tf_op jit(solution)/shard_map/ppermute | solution.py:549
  21.1 1.1 collective-permute-start.5
  22.1 0.0 copy-done.12
  22.1 0.0 copy-start
  22.2 0.0 copy-start.14
  22.2 5.1 %shard_map.112 = (f32[64,48,128]{2,1,0:T(8,128)S(1)}, f32[64,48,128]{2,1,0:T(8,128)S(1)}, f32[64,32,128]{2,1,0:T(8,128)S(1)}, f32[64,32,128]{2,1,0:T(8,128)S(1)}, f32[64,32,128]{2,1,0:T(8,128)S(1)}) custom-call(s32[256]{0:T(256)S(1)} %bitcast.36, s32[256]{0:T(256)S(1)} %fusion.lines, f32[4,256]{1,0:T(4,128)S(1)} %bitcast.37), custom_call_target="tpu_custom_call" | custom-call | flops 1099511627776 | bytes 6291456 | tf_op jit(solution)/shard_map/pallas_call | solution.py:588
  27.3 1.1 copy-done.1
  28.4 1.0 copy-done.3
  29.4 1.1 copy-done.5
  30.5 1.0 copy-done.7
  32.2 1.3 constant_dynamic-slice_fusion
  35.4 0.1 stack.63.spots
  35.5 0.0 collective-permute-done.3.r1
  35.5 0.0 collective-permute-done.4.r2
  35.5 0.0 collective-permute-done.5.r3
  35.6 2.2 %shard_map.111 = (f32[64,32,128]{2,1,0:T(8,128)S(1)}, f32[64,8,128]{2,1,0:T(8,128)}, f32[64,8,128]{2,1,0:T(8,128)}) custom-call(s32[2]{0:T(128)S(1)} %copy-done.13, s32[16,8]{1,0:T(8,128)S(1)} %copy-done.11, f32[2,8,32,128]{3,2,1,0:T(8,128)S(1)} %get-tuple-element.47.r0, f32[2,8,32,128]{3,2,1,0:T(8,128)} %collective-permute-done.3.r1, ...), custom_call_target="tpu_custom_call" | custom-call | bytes 2097152 | tf_op jit(solution)/shard_map/pallas_call | solution.py:565
  37.7 1.8 %collective-permute-start.6 = (f32[64,8,128]{2,1,0:T(8,128)}, f32[64,8,128]{2,1,0:T(8,128)S(1)}, u32[]{:S(2)}, u32[]{:S(2)}) collective-permute-start(f32[64,8,128]{2,1,0:T(8,128)} %get-tuple-element.55), channel_id=1, source_target_pairs={{0,1},{1,2},{2,3},{3,4},{4,5},{5,6},{6,7},{7,0},{8,9},{9,10},{10,1... | collective-permute-start | bytes 786440 | tf_op jit(solution)/shard_map/ppermute | solution.py:540
  39.5 2.0 %collective-permute-start.7 = (f32[64,8,128]{2,1,0:T(8,128)}, f32[64,8,128]{2,1,0:T(8,128)S(1)}, u32[]{:S(2)}, u32[]{:S(2)}) collective-permute-start(f32[64,8,128]{2,1,0:T(8,128)} %get-tuple-element.56), channel_id=1, source_target_pairs={{1,0},{2,1},{3,2},{4,3},{5,4},{6,5},{7,6},{0,7},{9,8},{10,9},{11,1... | collective-permute-start | bytes 786440 | tf_op jit(solution)/shard_map/ppermute | solution.py:540
  41.5 27.2 %all-to-all-done = f32[8,8,144,128]{3,2,1,0:T(8,128)} async-done(((f32[8,8,144,128]{3,2,1,0:T(8,128)}), f32[8,8,144,128]{3,2,1,0:T(8,128)}, u32[]{:S(2)}, u32[]{:S(2)}) %all-to-all-start) | async-done | bytes 4718624 | tf_op jit(solution)/shard_map/all_to_all | solution.py:564
  68.7 4.1 %shard_map.113 = (f32[64,32,128]{2,1,0:T(8,128)S(1)}, f32[64,32,128]{2,1,0:T(8,128)S(1)}, f32[64,8,128]{2,1,0:T(8,128)S(1)}, f32[64,8,128]{2,1,0:T(8,128)S(1)}, ...) custom-call(s32[8]{0:T(128)S(1)} %stack.63.spots, f32[4]{0:T(128)S(1)} %bitcast.32, ...), custom_call_target="tpu_custom_call" | custom-call | flops 10485760 | bytes 8388608 | tf_op jit(solution)/shard_map/pallas_call | solution.py:593
  72.8 0.6 collective-permute-start.8
  73.4 3.0 %collective-permute-start.9 = (f32[64,8,128]{2,1,0:T(8,128)S(1)}, f32[64,8,128]{2,1,0:T(8,128)S(1)}, u32[]{:S(2)}, u32[]{:S(2)}) collective-permute-start(f32[64,8,128]{2,1,0:T(8,128)S(1)} %get-tuple-element.60), channel_id=1, source_target_pairs={{1,0},{2,1},{3,2},{4,3},{5,4},{6,5},{7,6},{0,7},{9,8},{10,9},{11,1... | collective-permute-start | bytes 786440 | tf_op jit(solution)/shard_map/ppermute | solution.py:540
  76.4 0.0 collective-permute-done.6.r2_lo
  76.4 0.0 collective-permute-done.7.r2_hi
  76.4 4.4 %shard_map.114 = (f32[64,32,128]{2,1,0:T(8,128)S(1)}, f32[64,32,128]{2,1,0:T(8,128)S(1)}, f32[64,8,128]{2,1,0:T(8,128)S(1)}) custom-call(s32[8]{0:T(128)S(1)} %stack.63.spots, f32[64,144,128]{2,1,0:T(8,128)} %bitcast.17.turned, f32[64,32,128]{2,1,0:T(8,128)S(1)} %get-tuple-element.53.r2, f32[64,8,128]{2,1,0:T(8,128)S(1)} %collective-permute-done.6.r2_lo, ...), custom_call_target="tpu_custom_call" | custom-call | flops 10485760 | bytes 6291456 | tf_op jit(solution)/shard_map/pallas_call | solution.py:602
  80.9 1.6 %collective-permute-done.8.now_lo = f32[64,8,128]{2,1,0:T(8,128)S(1)} collective-permute-done((f32[64,8,128]{2,1,0:T(8,128)S(1)}, f32[64,8,128]{2,1,0:T(8,128)S(1)}, u32[]{:S(2)}, u32[]{:S(2)}) %collective-permute-start.8) | collective-permute-done | bytes 262176 | tf_op jit(solution)/shard_map/ppermute | solution.py:540
  82.4 0.0 collective-permute-done.9.now_hi
  82.4 5.0 %shard_map.115 = (f32[64,32,128]{2,1,0:T(8,128)S(1)}, f32[64,32,128]{2,1,0:T(8,128)S(1)}, f32[64,32,128]{2,1,0:T(8,128)S(1)}, f32[64,32,128]{2,1,0:T(8,128)S(1)}...) custom-call(s32[8]{0:T(128)S(1)} %stack.63.spots, f32[4]{0:T(128)S(1)} %bitcast.33, ...), custom_call_target="tpu_custom_call" | custom-call | flops 20971520 | bytes 12582912 | tf_op jit(solution)/shard_map/pallas_call | solution.py:611
  87.4 0.1 collective-permute-start.10
  87.5 3.6 %collective-permute-start.11 = (f32[32,8,128]{2,1,0:T(8,128)S(1)}, f32[32,8,128]{2,1,0:T(8,128)S(1)}, u32[]{:S(2)}, u32[]{:S(2)}) collective-permute-start(f32[32,8,128]{2,1,0:T(8,128)S(1)} %get-tuple-element.65), channel_id=1, source_target_pairs={{1,0},{2,1},{3,2},{4,3},{5,4},{6,5},{7,6},{0,7},{9,8},{10,9},{11,1... | collective-permute-start | bytes 393224 | tf_op jit(solution)/shard_map/ppermute | solution.py:540
  91.1 2.4 %collective-permute-done.10.halo_lo.wave_lo = f32[32,8,128]{2,1,0:T(8,128)S(1)} collective-permute-done((f32[32,8,128]{2,1,0:T(8,128)S(1)}, f32[32,8,128]{2,1,0:T(8,128)S(1)}, u32[]{:S(2)}, u32[]{:S(2)}) %collective-permute-start.10) | collective-permute-done | bytes 131104 | tf_op jit(solution)/shard_map/ppermute | solution.py:540
  93.4 0.0 collective-permute-done.11.halo_hi.wave_hi
  93.4 2.8 %shard_map.116 = (f32[64,32,128]{2,1,0:T(8,128)S(1)}, f32[64,32,128]{2,1,0:T(8,128)S(1)}, f32[64,8,128]{2,1,0:T(8,128)S(1)}, f32[64,8,128]{2,1,0:T(8,128)S(1)}) custom-call(s32[8]{0:T(128)S(1)} %stack.63.spots, f32[4]{0:T(128)S(1)} %bitcast.34, f32[64,32,128]{2,1,0:T(8,128)S(1)} %get-tuple-element.63.now.wave_a, ...), custom_call_target="tpu_custom_call" | custom-call | flops 10485760 | bytes 8388608 | tf_op jit(solution)/shard_map/pallas_call | solution.py:620
  96.2 0.1 collective-permute-start.12
  96.3 3.6 %collective-permute-start.13 = (f32[64,8,128]{2,1,0:T(8,128)S(1)}, f32[64,8,128]{2,1,0:T(8,128)S(1)}, u32[]{:S(2)}, u32[]{:S(2)}) collective-permute-start(f32[64,8,128]{2,1,0:T(8,128)S(1)} %get-tuple-element.72), channel_id=1, source_target_pairs={{1,0},{2,1},{3,2},{4,3},{5,4},{6,5},{7,6},{0,7},{9,8},{10,9},{11,1... | collective-permute-start | bytes 786440 | tf_op jit(solution)/shard_map/ppermute | solution.py:540
  99.9 3.7 %collective-permute-done.12.late_lo = f32[64,8,128]{2,1,0:T(8,128)S(1)} collective-permute-done((f32[64,8,128]{2,1,0:T(8,128)S(1)}, f32[64,8,128]{2,1,0:T(8,128)S(1)}, u32[]{:S(2)}, u32[]{:S(2)}) %collective-permute-start.12) | collective-permute-done | bytes 262176 | tf_op jit(solution)/shard_map/ppermute | solution.py:540
  103.6 0.0 collective-permute-done.13.late_hi
  103.7 5.6 %shard_map.117 = (f32[64,32,128]{2,1,0:T(8,128)S(1)}, f32[64,32,128]{2,1,0:T(8,128)S(1)}, f32[64,32,128]{2,1,0:T(8,128)S(1)}, f32[32,8,128]{2,1,0:T(8,128)S(1)}, f32[32,8,128]{2,1,0:T(8,128)S(1)}) custom-call(s32[8]{0:T(128)S(1)} %stack.63.spots, f32[64,32,128]{2,1,0:T(8,128)S(1)} %get-tuple-element.70.late, ...), custom_call_target="tpu_custom_call" | custom-call | flops 20971520 | bytes 16777216 | tf_op jit(solution)/shard_map/pallas_call | solution.py:629
  109.3 0.1 collective-permute-start.14
  109.4 3.7 %collective-permute-start.15 = (f32[32,8,128]{2,1,0:T(8,128)S(1)}, f32[32,8,128]{2,1,0:T(8,128)S(1)}, u32[]{:S(2)}, u32[]{:S(2)}) collective-permute-start(f32[32,8,128]{2,1,0:T(8,128)S(1)} %get-tuple-element.83), channel_id=1, source_target_pairs={{1,0},{2,1},{3,2},{4,3},{5,4},{6,5},{7,6},{0,7},{9,8},{10,9},{11,1... | collective-permute-start | bytes 393224 | tf_op jit(solution)/shard_map/ppermute | solution.py:540
  113.1 2.3 %collective-permute-done.14.halo_lo = f32[32,8,128]{2,1,0:T(8,128)S(1)} collective-permute-done((f32[32,8,128]{2,1,0:T(8,128)S(1)}, f32[32,8,128]{2,1,0:T(8,128)S(1)}, u32[]{:S(2)}, u32[]{:S(2)}) %collective-permute-start.14) | collective-permute-done | bytes 131104 | tf_op jit(solution)/shard_map/ppermute | solution.py:540
  115.3 0.0 collective-permute-done.15.halo_hi
  115.3 2.5 %shard_map.118 = f32[8,8,32,128]{3,2,1,0:T(8,128)S(1)} custom-call(s32[8]{0:T(128)S(1)} %stack.63.spots, f32[64,32,128]{2,1,0:T(8,128)S(1)} %get-tuple-element.80.late, f32[64,32,128]{2,1,0:T(8,128)S(1)} %get-tuple-element.81.later, f32[64,32,128]{2,1,0:T(8,128)S(1)} %get-tuple-element.53.r2, f32[32,8,128]{2,1,0:T(8,128)S(1)} %collective-permute-done.14.halo_lo, ...), custom_call_target="tpu_custom_call" | custom-call | flops 10485760 | bytes 8388608 | tf_op jit(solution)/shard_map/pallas_call | solution.py:641
  117.9 24.0 %all_to_all.10.recv = f32[8,8,32,128]{3,2,1,0:T(8,128)S(1)} all-to-all(f32[8,8,32,128]{3,2,1,0:T(8,128)S(1)} %shard_map.118), channel_id=1, replica_groups={{0,8,16,24,32,40,48,56},{64,72,80,88,96,104,112,120},{1,9,17,25,33,41,4..., dimensions={0} | all-to-all | bytes 2097152 | tf_op jit(solution)/shard_map/all_to_all | solution.py:645
  141.9 1.0 shard_map.119
  142.9 1.1 collective-permute-start.16
  144.0 7.2 %collective-permute-done.16 = f32[2,8,32,128]{3,2,1,0:T(8,128)S(1)} collective-permute-done((f32[2,8,32,128]{3,2,1,0:T(8,128)S(1)}, f32[2,8,32,128]{3,2,1,0:T(8,128)S(1)}, u32[]{:S(2)}, u32[]{:S(2)}) %collective-permute-start.16) | collective-permute-done | bytes 262176 | tf_op jit(solution)/shard_map/ppermute | solution.py:647
  151.3 0.7 add_bitcast_fusion
  (26 shorter events, 0.1 us)
Async XLA Ops:
  0.0 13.6 %collective-permute-start = (f32[2,8,32,128]{3,2,1,0:T(8,128)}, f32[2,8,32,128]{3,2,1,0:T(8,128)S(1)}, u32[]{:S(2)}, u32[]{:S(2)}) collective-permute-start(f32[2,8,32,128]{3,2,1,0:T(8,128)} %bitcast.29), channel_id=1, source_target_pairs={{0,64},{8,72},{16,80},{24,88},{32,96},{40,104},{48,112},{56,120},{... | collective-permute-start | bytes 786440 | tf_op jit(solution)/shard_map/ppermute | solution.py:543
  3.6 10.5 %collective-permute-start.1 = (f32[2,8,32,128]{3,2,1,0:T(8,128)}, f32[2,8,32,128]{3,2,1,0:T(8,128)S(1)}, u32[]{:S(2)}, u32[]{:S(2)}) collective-permute-start(f32[2,8,32,128]{3,2,1,0:T(8,128)} %bitcast.30), channel_id=1, source_target_pairs={{0,8},{8,0},{16,24},{24,16},{32,40},{40,32},{48,56},{56,48},{64,72... | collective-permute-start | bytes 786440 | tf_op jit(solution)/shard_map/ppermute | solution.py:544
  8.3 5.7 %copy-start.17 = (s32[16,8]{0,1:T(8,128)S(1)}, s32[16,8]{0,1:T(8,128)}, u32[]{:S(2)}) copy-start(s32[16,8]{0,1:T(8,128)} %param.20) | copy-start | bytes 1540
  8.3 5.8 %copy-start.15 = (s32[1,256]{1,0:T(1,128)S(1)}, s32[1,256]{1,0:T(1,128)}, u32[]{:S(2)}) copy-start(s32[1,256]{1,0:T(1,128)} %param.18) | copy-start | bytes 3076
  8.3 6.9 %copy-start.9 = (f32[2,1,8,32,128]{4,3,2,1,0:T(8,128)S(1)}, f32[2,1,8,32,128]{4,3,2,1,0:T(8,128)}, u32[]{:S(2)}) copy-start(f32[2,1,8,32,128]{4,3,2,1,0:T(8,128)} %param.11) | copy-start | bytes 786436
  8.3 13.8 %copy-start.16 = (f32[1,4,256]{2,1,0:T(4,128)S(1)}, f32[1,4,256]{2,1,0:T(4,128)}, u32[]{:S(2)}) copy-start(f32[1,4,256]{2,1,0:T(4,128)} %param.19) | copy-start | bytes 12292
  8.3 60.3 %all-to-all-start = ((f32[8,8,144,128]{3,2,1,0:T(8,128)}), f32[8,8,144,128]{3,2,1,0:T(8,128)}, u32[]{:S(2)}, u32[]{:S(2)}) async-start(f32[8,8,144,128]{3,2,1,0:T(8,128)} %shard_map.109), calls=%async_computation | async-start | bytes 9437184 | tf_op jit(solution)/shard_map/all_to_all | solution.py:564
  13.6 1.6 %collective-permute-start.2 = (f32[2,8,32,128]{3,2,1,0:T(8,128)S(1)}, f32[2,8,32,128]{3,2,1,0:T(8,128)S(1)}, u32[]{:S(2)}, u32[]{:S(2)}) collective-permute-start(f32[2,8,32,128]{3,2,1,0:T(8,128)S(1)} %collective-permute-done.other), channel_id=1, source_target_pairs={{0,8},{8,0},{16,24},{24,16},{32,40},{40,32},{48,56},{56,48},{64,72... | collective-permute-start | bytes 786440 | tf_op jit(solution)/shard_map/ppermute | solution.py:545
  14.0 8.1 %copy-start.12 = (s32[2]{0:T(128)}, s32[2]{0:T(128)S(1)}, u32[]{:S(2)}) copy-start(s32[2]{0:T(128)S(1)} %pad_add_fusion.ids) | copy-start | bytes 28
  14.1 8.1 %copy-start.10 = (s32[16,8]{1,0:T(8,128)}, s32[16,8]{1,0:T(8,128)S(1)}, u32[]{:S(2)}) copy-start(s32[16,8]{1,0:T(8,128)S(1)} %copy.14.apertures) | copy-start | bytes 1540
  17.1 18.4 %collective-permute-start.3 = (f32[2,8,32,128]{3,2,1,0:T(8,128)}, f32[2,8,32,128]{3,2,1,0:T(8,128)}, u32[]{:S(2)}, u32[]{:S(2)}) collective-permute-start(f32[2,8,32,128]{3,2,1,0:T(8,128)} %get-tuple-element.48), channel_id=1, source_target_pairs={{0,16},{8,24},{16,32},{24,40},{32,48},{40,56},{48,0},{56,8},{64,80... | collective-permute-start | bytes 786440 | tf_op jit(solution)/shard_map/ppermute | solution.py:549
  18.4 17.1 %collective-permute-start.4 = (f32[2,8,32,128]{3,2,1,0:T(8,128)}, f32[2,8,32,128]{3,2,1,0:T(8,128)}, u32[]{:S(2)}, u32[]{:S(2)}) collective-permute-start(f32[2,8,32,128]{3,2,1,0:T(8,128)} %get-tuple-element.49), channel_id=1, source_target_pairs={{0,32},{8,40},{16,48},{24,56},{32,0},{40,8},{48,16},{56,24},{64,96... | collective-permute-start | bytes 786440 | tf_op jit(solution)/shard_map/ppermute | solution.py:549
  21.1 14.5 %collective-permute-start.5 = (f32[2,8,32,128]{3,2,1,0:T(8,128)}, f32[2,8,32,128]{3,2,1,0:T(8,128)}, u32[]{:S(2)}, u32[]{:S(2)}) collective-permute-start(f32[2,8,32,128]{3,2,1,0:T(8,128)} %get-tuple-element.50), channel_id=1, source_target_pairs={{0,48},{8,56},{16,0},{24,8},{32,16},{40,24},{48,32},{56,40},{64,11... | collective-permute-start | bytes 786440 | tf_op jit(solution)/shard_map/ppermute | solution.py:549
  22.1 13.4 %copy-start.11 = (s32[16,8]{1,0:T(8,128)S(1)}, s32[16,8]{1,0:T(8,128)}, u32[]{:S(2)}) copy-start(s32[16,8]{1,0:T(8,128)} %copy-done.10) | copy-start | bytes 1540
  22.1 13.4 %copy-start.13 = (s32[2]{0:T(128)S(1)}, s32[2]{0:T(128)}, u32[]{:S(2)}) copy-start(s32[2]{0:T(128)} %copy-done.12) | copy-start | bytes 28
  22.1 46.5 %copy-start = (bf16[256,256]{1,0:T(8,128)(2,1)S(1)}, bf16[256,256]{1,0:T(8,128)(2,1)}, u32[]{:S(2)}) copy-start(bf16[256,256]{1,0:T(8,128)(2,1)} %constant.94.clone.oper) | copy-start | bytes 393220
  22.2 46.5 %copy-start.14 = (f32[1,4]{1,0:T(1,128)S(1)}, f32[1,4]{1,0:T(1,128)}, u32[]{:S(2)}) copy-start(f32[1,4]{1,0:T(1,128)} %param.16) | copy-start | bytes 52
  27.3 1.1 copy-start.1
  28.4 1.0 copy-start.3
  29.4 1.1 copy-start.5
  30.5 1.0 copy-start.7
  37.7 38.7 %collective-permute-start.6 = (f32[64,8,128]{2,1,0:T(8,128)}, f32[64,8,128]{2,1,0:T(8,128)S(1)}, u32[]{:S(2)}, u32[]{:S(2)}) collective-permute-start(f32[64,8,128]{2,1,0:T(8,128)} %get-tuple-element.55), channel_id=1, source_target_pairs={{0,1},{1,2},{2,3},{3,4},{4,5},{5,6},{6,7},{7,0},{8,9},{9,10},{10,1... | collective-permute-start | bytes 786440 | tf_op jit(solution)/shard_map/ppermute | solution.py:540
  39.5 37.0 %collective-permute-start.7 = (f32[64,8,128]{2,1,0:T(8,128)}, f32[64,8,128]{2,1,0:T(8,128)S(1)}, u32[]{:S(2)}, u32[]{:S(2)}) collective-permute-start(f32[64,8,128]{2,1,0:T(8,128)} %get-tuple-element.56), channel_id=1, source_target_pairs={{1,0},{2,1},{3,2},{4,3},{5,4},{6,5},{7,6},{0,7},{9,8},{10,9},{11,1... | collective-permute-start | bytes 786440 | tf_op jit(solution)/shard_map/ppermute | solution.py:540
  72.8 9.7 %collective-permute-start.8 = (f32[64,8,128]{2,1,0:T(8,128)S(1)}, f32[64,8,128]{2,1,0:T(8,128)S(1)}, u32[]{:S(2)}, u32[]{:S(2)}) collective-permute-start(f32[64,8,128]{2,1,0:T(8,128)S(1)} %get-tuple-element.59), channel_id=1, source_target_pairs={{0,1},{1,2},{2,3},{3,4},{4,5},{5,6},{6,7},{7,0},{8,9},{9,10},{10,1... | collective-permute-start | bytes 786440 | tf_op jit(solution)/shard_map/ppermute | solution.py:540
  73.4 20.0 %copy-start.8 = (f32[64,32,128]{2,1,0:T(8,128)S(1)}, f32[64,32,128]{2,1,0:T(8,128)}, u32[]{:S(2)}) copy-start(f32[64,32,128]{2,1,0:T(8,128)} %copy-done.7) | copy-start | bytes 3145732
  73.4 9.0 %collective-permute-start.9 = (f32[64,8,128]{2,1,0:T(8,128)S(1)}, f32[64,8,128]{2,1,0:T(8,128)S(1)}, u32[]{:S(2)}, u32[]{:S(2)}) collective-permute-start(f32[64,8,128]{2,1,0:T(8,128)S(1)} %get-tuple-element.60), channel_id=1, source_target_pairs={{1,0},{2,1},{3,2},{4,3},{5,4},{6,5},{7,6},{0,7},{9,8},{10,9},{11,1... | collective-permute-start | bytes 786440 | tf_op jit(solution)/shard_map/ppermute | solution.py:540
  87.4 16.2 %copy-start.2 = (f32[64,48,128]{2,1,0:T(8,128)S(1)}, f32[64,48,128]{2,1,0:T(8,128)}, u32[]{:S(2)}) copy-start(f32[64,48,128]{2,1,0:T(8,128)} %copy-done.1) | copy-start | bytes 4718596
  87.4 16.2 %copy-start.6 = (f32[64,32,128]{2,1,0:T(8,128)S(1)}, f32[64,32,128]{2,1,0:T(8,128)}, u32[]{:S(2)}) copy-start(f32[64,32,128]{2,1,0:T(8,128)} %copy-done.5) | copy-start | bytes 3145732
  87.4 6.0 %collective-permute-start.10 = (f32[32,8,128]{2,1,0:T(8,128)S(1)}, f32[32,8,128]{2,1,0:T(8,128)S(1)}, u32[]{:S(2)}, u32[]{:S(2)}) collective-permute-start(f32[32,8,128]{2,1,0:T(8,128)S(1)} %get-tuple-element.64), channel_id=1, source_target_pairs={{0,1},{1,2},{2,3},{3,4},{4,5},{5,6},{6,7},{7,0},{8,9},{9,10},{10,1... | collective-permute-start | bytes 393224 | tf_op jit(solution)/shard_map/ppermute | solution.py:540
  87.5 5.9 %collective-permute-start.11 = (f32[32,8,128]{2,1,0:T(8,128)S(1)}, f32[32,8,128]{2,1,0:T(8,128)S(1)}, u32[]{:S(2)}, u32[]{:S(2)}) collective-permute-start(f32[32,8,128]{2,1,0:T(8,128)S(1)} %get-tuple-element.65), channel_id=1, source_target_pairs={{1,0},{2,1},{3,2},{4,3},{5,4},{6,5},{7,6},{0,7},{9,8},{10,9},{11,1... | collective-permute-start | bytes 393224 | tf_op jit(solution)/shard_map/ppermute | solution.py:540
  96.2 7.4 %collective-permute-start.12 = (f32[64,8,128]{2,1,0:T(8,128)S(1)}, f32[64,8,128]{2,1,0:T(8,128)S(1)}, u32[]{:S(2)}, u32[]{:S(2)}) collective-permute-start(f32[64,8,128]{2,1,0:T(8,128)S(1)} %get-tuple-element.71), channel_id=1, source_target_pairs={{0,1},{1,2},{2,3},{3,4},{4,5},{5,6},{6,7},{7,0},{8,9},{9,10},{10,1... | collective-permute-start | bytes 786440 | tf_op jit(solution)/shard_map/ppermute | solution.py:540
  96.3 7.3 %collective-permute-start.13 = (f32[64,8,128]{2,1,0:T(8,128)S(1)}, f32[64,8,128]{2,1,0:T(8,128)S(1)}, u32[]{:S(2)}, u32[]{:S(2)}) collective-permute-start(f32[64,8,128]{2,1,0:T(8,128)S(1)} %get-tuple-element.72), channel_id=1, source_target_pairs={{1,0},{2,1},{3,2},{4,3},{5,4},{6,5},{7,6},{0,7},{9,8},{10,9},{11,1... | collective-permute-start | bytes 786440 | tf_op jit(solution)/shard_map/ppermute | solution.py:540
  103.6 11.7 %copy-start.4 = (f32[64,32,128]{2,1,0:T(8,128)S(1)}, f32[64,32,128]{2,1,0:T(8,128)}, u32[]{:S(2)}) copy-start(f32[64,32,128]{2,1,0:T(8,128)} %copy-done.3) | copy-start | bytes 3145732
  109.3 6.1 %collective-permute-start.14 = (f32[32,8,128]{2,1,0:T(8,128)S(1)}, f32[32,8,128]{2,1,0:T(8,128)S(1)}, u32[]{:S(2)}, u32[]{:S(2)}) collective-permute-start(f32[32,8,128]{2,1,0:T(8,128)S(1)} %get-tuple-element.82), channel_id=1, source_target_pairs={{0,1},{1,2},{2,3},{3,4},{4,5},{5,6},{6,7},{7,0},{8,9},{9,10},{10,1... | collective-permute-start | bytes 393224 | tf_op jit(solution)/shard_map/ppermute | solution.py:540
  109.4 6.0 %collective-permute-start.15 = (f32[32,8,128]{2,1,0:T(8,128)S(1)}, f32[32,8,128]{2,1,0:T(8,128)S(1)}, u32[]{:S(2)}, u32[]{:S(2)}) collective-permute-start(f32[32,8,128]{2,1,0:T(8,128)S(1)} %get-tuple-element.83), channel_id=1, source_target_pairs={{1,0},{2,1},{3,2},{4,3},{5,4},{6,5},{7,6},{0,7},{9,8},{10,9},{11,1... | collective-permute-start | bytes 393224 | tf_op jit(solution)/shard_map/ppermute | solution.py:540
  142.9 8.3 %collective-permute-start.16 = (f32[2,8,32,128]{3,2,1,0:T(8,128)S(1)}, f32[2,8,32,128]{3,2,1,0:T(8,128)S(1)}, u32[]{:S(2)}, u32[]{:S(2)}) collective-permute-start(f32[2,8,32,128]{3,2,1,0:T(8,128)S(1)} %get-tuple-element.88), channel_id=1, source_target_pairs={{0,64},{8,72},{16,80},{24,88},{32,96},{40,104},{48,112},{56,120},{... | collective-permute-start | bytes 786440 | tf_op jit(solution)/shard_map/ppermute | solution.py:647

commit v7 on v6

--- a/solution.py
+++ b/solution.py
@@ -53,7 +53,7 @@
         body(x)
         return carry
 
-    lax.fori_loop(0, NX, step, 0, unroll=4)
+    lax.fori_loop(0, NX, step, 0, unroll=16)
 
 
 def fill_edges(ext, spots, halo_lo, halo_hi):
@@ -68,7 +68,7 @@
             ext[x, OWN1 : OWN1 + 4, :] = hi[4 * half : 4 * half + 4]
         return carry
 
-    lax.fori_loop(0, NX // 2, body, 0, unroll=4)
+    lax.fori_loop(0, NX // 2, body, 0, unroll=8)
 
 
 def fill_tiles(ext, spots, lo, hi):
@@ -89,8 +89,43 @@
     planes(body)
 
 
-def apply_depth(ext, oper, depth, wide=False):
-    r0, r1 = (WIDE0, WIDE1) if wide else (OWN0, OWN1)
+def no_edges(ext):
+    zeros = jnp.zeros((4, NZ), F32)
+
+    def body(x):
+        ext[PAD + x, OWN0 - 4 : OWN0, :] = zeros
+        ext[PAD + x, OWN1 : OWN1 + 4, :] = zeros
+
+    planes(body)
+
+
+def halo_taps(strip, x, j):
+    way = -1 if j == 0 else 1
+    acc = None
+    for k in range(1, 5):
+        term = STENCIL[k] * strip[x, 8 + way * k : 16 + way * k, :]
+        acc = term if acc is None else acc + term
+    return acc
+
+
+def fill_strip(strip, spots, halo_lo, halo_hi):
+    has_lo, has_hi = spots[5] == 1, spots[6] == 1
+    zeros = jnp.zeros((8, NZ), F32)
+
+    def body(t, carry):
+        lo = jnp.where(has_lo, halo_lo[t], 0.0)
+        hi = jnp.where(has_hi, halo_hi[t], 0.0)
+        for half in range(2):
+            strip[2 * t + half, 4:8, :] = lo[4 * half : 4 * half + 4]
+            strip[2 * t + half, 8:16, :] = zeros
+            strip[2 * t + half, 16:20, :] = hi[4 * half : 4 * half + 4]
+        return carry
+
+    lax.fori_loop(0, NX // 2, body, 0, unroll=8)
+
+
+def apply_depth(ext, oper, depth, wide=False, span=None):
+    r0, r1 = span or ((WIDE0, WIDE1) if wide else (OWN0, OWN1))
     n = CHUNK
     for at in range(0, NX, n):
         rows = ext[PAD + at : PAD + at + n, r0:r1, :].reshape(n * (r1 - r0), NZ)
@@ -139,7 +174,7 @@
             send_hi[t, 4 * half : 4 * half + 4, :] = read(2 * t + half, slice(NYL - 4, NYL))
         return carry
 
-    lax.fori_loop(0, NX // 2, body, 0, unroll=4)
+    lax.fori_loop(0, NX // 2, body, 0, unroll=8)
 
 
 def send_tiles(send_lo, send_hi, field):
@@ -206,7 +241,7 @@
             hi[2 * t + half, 0:4, :] = halo_hi[t, 4 * half : 4 * half + 4, :]
         return carry
 
-    lax.fori_loop(0, NX // 2, body, 0, unroll=4)
+    lax.fori_loop(0, NX // 2, body, 0, unroll=8)
 
 
 def middle_kernel(
@@ -266,34 +301,62 @@
     laplace(ext, depth, OWN, emit)
 
 
-def turn_kernel(
-    spots, wavelet, now, halo_lo, halo_hi, prev, r2, oper, part, count, data, total, mu, send_lo, send_hi, ext, depth, new
-):
+def turn_kernel(spots, wavelet, now, prev, r2, oper, part, count, data, lap, mu, ext, depth, new):
     clear_ends(ext)
+    no_edges(ext)
     ext[OWN_X, OWN_Y, :] = now[...]
-    fill_edges(ext, spots, halo_lo, halo_hi)
     apply_depth(ext, oper, depth)
 
     def emit(x, g, xi, j, value):
         new[x, tile(j), :] = 2.0 * ext[PAD + x, ext_tile(j), :] - prev[x, tile(j), :] + r2[x, tile(j), :] * value
-        total[x, tile(j), :] = value
+        lap[x, tile(j), :] = value
 
     laplace(ext, depth, OWN, emit)
     add_source(spots, wavelet[3], new, 0, 0)
 
     def finish(x):
-        m = part[x] + (count[x, 8 : 8 + NYL, :] * new[x] - data[x])
-        mu[x] = m
-        total[x] = m * total[x]
+        mu[x] = part[x] + (count[x, 8 : 8 + NYL, :] * new[x] - data[x])
 
     planes(finish)
-    send_tiles(send_lo, send_hi, mu)
-
-
-def back_kernel(
-    spots, late, late_lo, late_hi, later, edge, r2, r2_lo, r2_hi, oper, count, data_a, data_b,
-    wave_a, wave_lo, wave_hi, wave_b, lap_a, lap_b, total_in,
-    total, mu_a, mu_b, send_lo, send_hi, ext, ext2, depth, old_lo, old_hi, u_lo, u_hi,
+
+
+def turn_end_kernel(spots, halo_lo, halo_hi, r2, count, lap, mu_in, total, mu, send_lo, send_hi, strip):
+    fill_strip(strip, spots, halo_lo, halo_hi)
+
+    def body(x):
+        for j in OWN:
+            m, value = mu_in[x, tile(j), :], lap[x, tile(j), :]
+            if j in (0, 3):
+                more = halo_taps(strip, x, j)
+                value = value + more
+                m = m + count[x, 8 + 8 * j : 16 + 8 * j, :] * (r2[x, tile(j), :] * more)
+                (send_hi if j else send_lo)[x] = m
+            mu[x, tile(j), :] = m
+            total[x, tile(j), :] = m * value
+
+    planes(body)
+
+
+def back_kernel(spots, late, later, r2, oper, count, data, wave, lap, total_in, total, mu, ext, depth):
+    clear_ends(ext)
+    no_edges(ext)
+    ext[OWN_X, OWN_Y, :] = late[...] * r2[...]
+    apply_depth(ext, oper, depth)
+
+    def emit(x, g, xi, j, value):
+        wide = slice(8 + 8 * j, 16 + 8 * j)
+        m = 2.0 * late[x, tile(j), :] + value - later[x, tile(j), :]
+        m = m + (count[x, wide, :] * wave[x, tile(j), :] - data[x, wide, :])
+        mu[x, tile(j), :] = m
+        total[x, tile(j), :] = total_in[x, tile(j), :] + m * lap[x, tile(j), :]
+
+    laplace(ext, depth, OWN, emit)
+
+
+def back_end_kernel(
+    spots, late, late_lo, late_hi, edge, r2, r2_lo, r2_hi, oper, count, data_a, data_b,
+    wave_lo, wave_hi, wave_b, lap_a, lap_b, mu_in, total_in,
+    total, mu_a, mu_b, send_lo, send_hi, ext, ext2, depth, old_lo, old_hi, u_lo, u_hi, strip,
 ):
     has = (spots[5] == 1, spots[6] == 1)
     clear_ends(ext)
@@ -302,26 +365,39 @@
     fill_tiles(ext, spots, lambda x: late_lo[x] * r2_lo[x], lambda x: late_hi[x] * r2_hi[x])
     spread_edges(edge, old_lo, old_hi)
     spread_halos(wave_lo, wave_hi, u_lo, u_hi)
-    apply_depth(ext, oper, depth, True)
+    zeros = jnp.zeros((8, NZ), F32)
+
+    def near(x):
+        strip[x, 4:8, :] = ext[PAD + x, OWN0 - 4 : OWN0, :]
+        strip[x, 8:16, :] = zeros
+        strip[x, 16:20, :] = ext[PAD + x, OWN1 : OWN1 + 4, :]
+
+    planes(near)
+    apply_depth(ext, oper, depth, span=(WIDE0, OWN0))
+    apply_depth(ext, oper, depth, span=(OWN1, WIDE1))
+
+    def own(x):
+        for j in OWN:
+            mu, sofar = mu_in[x, tile(j), :], total_in[x, tile(j), :]
+            if j in (0, 3):
+                more = halo_taps(strip, x, j)
+                mu = mu + more
+                sofar = sofar + more * lap_a[x, tile(j), :]
+            mu_a[x, tile(j), :] = mu
+            total[x, tile(j), :] = sofar
+            ext2[PAD + x, ext_tile(j), :] = mu * r2[x, tile(j), :]
+
+    planes(own)
 
     def emit(x, g, xi, j, value):
         wide = slice(8 + 8 * j, 16 + 8 * j)
-        many, heard = count[x, wide, :], data_a[x, wide, :]
-        if j in OWN:
-            mu = 2.0 * late[x, tile(j), :] + value - later[x, tile(j), :]
-            mu = mu + (many * wave_a[x, tile(j), :] - heard)
-            mu_a[x, tile(j), :] = mu
-            total[x, tile(j), :] = total_in[x, tile(j), :] + mu * lap_a[x, tile(j), :]
-            w = mu * r2[x, tile(j), :]
-        else:
-            near, old, u, weight, there = (
-                (late_lo, old_lo, u_lo, r2_lo, has[0]) if j < 0 else (late_hi, old_hi, u_hi, r2_hi, has[1])
-            )
-            mu = 2.0 * near[x] + value - old[x] + (many * u[x] - heard)
-            w = jnp.where(there, mu * weight[x], 0.0)
-        ext2[PAD + x, ext_tile(j), :] = w
-
-    laplace(ext, depth, WITH_HALO, emit)
+        close, old, u, weight, there = (
+            (late_lo, old_lo, u_lo, r2_lo, has[0]) if j < 0 else (late_hi, old_hi, u_hi, r2_hi, has[1])
+        )
+        mu = 2.0 * close[x] + value - old[x] + (count[x, wide, :] * u[x] - data_a[x, wide, :])
+        ext2[PAD + x, ext_tile(j), :] = jnp.where(there, mu * weight[x], 0.0)
+
+    laplace(ext, depth, (-1, 4), emit)
     apply_depth(ext2, oper, depth)
 
     def emit_b(x, g, xi, j, value):
@@ -335,12 +411,12 @@
 
 
 def last_kernel(
-    spots, late, later, r2, halo_lo, halo_hi, oper, count, data, wave, lap, total_in, total, ext, depth
+    spots, late, later, r2, oper, count, data, wave, lap, total_in, total, ext, depth
 ):
     first = spots[0]
     clear_ends(ext)
     ext[OWN_X, OWN_Y, :] = late[...] * r2[...]
-    fill_edges(ext, spots, halo_lo, halo_hi)
+    no_edges(ext)
     apply_depth(ext, oper, depth)
 
     def emit(x, g, xi, j, value):
@@ -349,6 +425,21 @@
         total[lax.rem(first + g, GROUP), xi, tile(j), :] = total_in[x, tile(j), :] + mu * lap[x, tile(j), :]
 
     laplace(ext, depth, OWN, emit)
+
+
+def last_end_kernel(spots, halo_lo, halo_hi, lap, total_in, total, strip):
+    fill_strip(strip, spots, halo_lo, halo_hi)
+    first = spots[0]
+
+    def body(x):
+        slot, xi = lax.rem(first + x // GROUP, GROUP), lax.rem(x, GROUP)
+        for j in OWN:
+            value = total_in[slot, xi, tile(j), :]
+            if j in (0, 3):
+                value = value + lap[x, tile(j), :] * halo_taps(strip, x, j)
+            total[slot, xi, tile(j), :] = value
+
+    planes(body)
 
 
 def pack_kernel(now, prev, late, later, out, near, edge, sems):
@@ -495,6 +586,8 @@
 EXT = pltpu.VMEM((NX + 2 * PAD, ROWS, NZ), F32)
 DEPTH = pltpu.VMEM((NX, WIDE, NZ), F32)
 FIELD_VMEM = pltpu.VMEM((NX, NYL, NZ), F32)
+STRIP = pltpu.VMEM((NX, 24, NZ), F32)
+MAIN = 10 << 20
 TILE_VMEM = pltpu.VMEM((NX, 8, NZ), F32)
 
 
@@ -617,29 +710,38 @@
         moved=12 << 20,
     )(spots, amounts, u1, *u1_halo, u0, u0_edge, r2, *r2_halo, oper)
     u3_halo = edges(lo, hi)
+    lap3, mu4 = call(
+        turn_kernel,
+        [SMEM, SMEM] + [VMEM] * 7,
+        [FIELD, FIELD],
+        [EXT, DEPTH, FIELD_VMEM],
+        flops=MAIN,
+        moved=8 << 20,
+    )(spots, amounts, u3, u2, r2, oper, part4, count, data4)
     total, mu4, lo, hi = call(
-        turn_kernel,
-        [SMEM, SMEM] + [VMEM] * 9,
-        [FIELD, FIELD, TILE, TILE],
-        [EXT, DEPTH, FIELD_VMEM],
-        flops=10 << 20,
-        moved=8 << 20,
-    )(spots, amounts, u3, *u3_halo, u2, r2, oper, part4, count, data4)
+        turn_end_kernel, [SMEM] + [VMEM] * 6, [FIELD, FIELD, TILE, TILE], [STRIP], flops=1 << 20, moved=4 << 20
+    )(spots, *u3_halo, r2, count, lap3, mu4)
     mu4_halo = edges(lo, hi)
+    total, mu3 = call(
+        back_kernel, [SMEM] + [VMEM] * 9, [FIELD, FIELD], [EXT, DEPTH], flops=MAIN, moved=8 << 20
+    )(spots, mu4, mu5, r2, oper, count, data3, u3, lap2, total)
     total, mu3, mu2, lo, hi = call(
-        back_kernel,
-        [SMEM] + [VMEM] * 19,
+        back_end_kernel,
+        [SMEM] + [VMEM] * 18,
         [FIELD] * 3 + [EDGE] * 2,
-        [EXT, EXT, DEPTH] + [TILE_VMEM] * 4,
+        [EXT, EXT, DEPTH] + [TILE_VMEM] * 4 + [STRIP],
         flops=20 << 20,
         moved=16 << 20,
     )(
-        spots, mu4, *mu4_halo, mu5, mu5_edge, r2, *r2_halo, oper, count, data3, data2,
-        u3, *u3_halo, u2, lap2, lap1, total,
+        spots, mu4, *mu4_halo, mu5_edge, r2, *r2_halo, oper, count, data3, data2,
+        *u3_halo, u2, lap2, lap1, mu3, total,
     )
     mu2_halo = edges(lo, hi)
-    (total,) = call(last_kernel, [SMEM] + [VMEM] * 11, [BLOCKS], [EXT, DEPTH], flops=10 << 20, moved=8 << 20)(
-        spots, mu2, mu3, r2, *mu2_halo, oper, count, data1, u1, lap0, total
+    (total,) = call(last_kernel, [SMEM] + [VMEM] * 9, [BLOCKS], [EXT, DEPTH], flops=MAIN, moved=8 << 20)(
+        spots, mu2, mu3, r2, oper, count, data1, u1, lap0, total
+    )
+    (total,) = call(last_end_kernel, [SMEM] + [VMEM] * 4, [BLOCKS], [STRIP], flops=1 << 20, moved=3 << 20)(
+        spots, *mu2_halo, lap0, total
     )
 
     recv = lax.all_to_all(total, "shot", 0, 0, axis_index_groups=halves, tiled=True)

time: 153 us -> 148 us (0.967)
  waiting for transfers between devices: 45.4 us -> 38.9 us
  Pallas kernels: 38.4 us -> 41.3 us
    ppermute x10, waiting for transfers between devices: 9.9 us -> 3.35 us  [edges(): return (lax.ppermute(hi, 'sub', up), lax.ppermute(lo, 'sub', down))]
    pallas_call x3 -> x6, Pallas kernels: 10.9 us -> 13.9 us  [the longest x1 4.36 us: per_device(): call(back_end_kernel, [SMEM] + [VMEM] * 18, [FIELD] * 3 + [EDGE] * 2, [EX...]
  transfers between devices with their start and end apart: 18 -> 18, of which waited for: 7 -> 5; matrix products, arithmetic and copies ran while one was open for 1% -> 1% of each run, Pallas kernels for 14% -> 20%
where the time goes in v7:
time: 148 us; the launch traced here: 147 us
  Pallas kernels  41.3 us (28%)
  waiting for transfers between devices  38.9 us (26%)
  starting transfers between devices  34.3 us (23%)
  blocking collectives  23.4 us (16%)
  local copies, waits for them, and re-layouts  5.68 us (4%)
  between operations  2.94 us (2%)
    all_to_all x1, waiting for transfers between devices, per_device(): lax.all_to_all(packed, 'sub', 0, 0, tiled=True).reshape(NX, TURNED, NZ)  27.2 us
    all_to_all x1, blocking collectives, per_device(): lax.all_to_all(total, 'shot', 0, 0, axis_index_groups=halves, tiled=True)  23.4 us
    ppermute x10, starting transfers between devices, edges(): return (lax.ppermute(hi, 'sub', up), lax.ppermute(lo, 'sub', down))  18.2 us
    ppermute x1, waiting for transfers between devices, per_device(): result = keep + lax.ppermute(give, 'shot', across)  7.31 us
    pallas_call x1, Pallas kernels, per_device(): call(receivers_kernel, [SMEM] * 3, [WIDE_FIELD, WIDE_FIELD] + [FIELD] * 3...  5.32 us
    all_to_all x1, starting transfers between devices, per_device(): lax.all_to_all(packed, 'sub', 0, 0, tiled=True).reshape(NX, TURNED, NZ)  5.21 us
    ppermute x3, starting transfers between devices, per_device(): lax.ppermute(blocks[k], 'shot', along(k))  4.99 us
    pallas_call x1, Pallas kernels, per_device(): call(middle_kernel, [SMEM, SMEM] + [VMEM] * 9, [FIELD] * 4 + [EDGE] * 2,...  4.86 us
  transfers between devices with their start and end apart: 18, of which 5 were waited for; matrix products, arithmetic and copies ran while one was open for 1% of the time, Pallas kernels for 20%

profile of v7, /device:TPU:1, one launch (start us, length us, event | category | flops | bytes accessed | tf_op | source)
XLA Modules:
  0.0 147.4 jit_solution(12675060704608430375)
XLA Ops:
  0.0 3.6 %collective-permute-start = (f32[2,8,32,128]{3,2,1,0:T(8,128)}, f32[2,8,32,128]{3,2,1,0:T(8,128)S(1)}, u32[]{:S(2)}, u32[]{:S(2)}) collective-permute-start(f32[2,8,32,128]{3,2,1,0:T(8,128)} %bitcast.29), channel_id=1, source_target_pairs={{0,64},{8,72},{16,80},{24,88},{32,96},{40,104},{48,112},{56,120},{... | collective-permute-start | bytes 786440 | tf_op jit(solution)/shard_map/ppermute | solution.py:636
  3.6 1.0 collective-permute-start.1
  4.5 3.8 %shard_map.109 = f32[8,8,144,128]{3,2,1,0:T(8,128)} custom-call(f32[8,256,128]{2,1,0:T(8,128)} %bitcast.38, f32[8,256,128]{2,1,0:T(8,128)} %bitcast.39, f32[8,256,128]{2,1,0:T(8,128)} %bitcast.40, f32[8,256,128]{2,1,0:T(8,128)} %bitcast.41), custom_call_target="tpu_custom_call" | custom-call | bytes 9437184 | tf_op jit(solution)/shard_map/pallas_call | solution.py:644
  8.3 0.0 copy-start.17
  8.3 0.0 copy-start.15
  8.3 0.0 copy-start.9
  8.4 0.0 copy-start.16
  8.4 5.2 %all-to-all-start = ((f32[8,8,144,128]{3,2,1,0:T(8,128)}), f32[8,8,144,128]{3,2,1,0:T(8,128)}, u32[]{:S(2)}, u32[]{:S(2)}) async-start(f32[8,8,144,128]{3,2,1,0:T(8,128)} %shard_map.109), calls=%async_computation | async-start | bytes 9437184 | tf_op jit(solution)/shard_map/all_to_all | solution.py:657
  13.6 0.0 collective-permute-done.other
  13.6 0.4 collective-permute-start.2
  13.9 0.1 pad_add_fusion.ids
  14.0 0.1 copy.14.apertures
  14.1 0.0 collective-permute-done.1.piece_c
  14.1 1.1 collective-permute-done.2.other_c
  15.2 2.0 %shard_map.110 = (f32[2,8,32,128]{3,2,1,0:T(8,128)S(1)}, f32[2,8,32,128]{3,2,1,0:T(8,128)}, f32[2,8,32,128]{3,2,1,0:T(8,128)}, f32[2,8,32,128]{3,2,1,0:T(8,128)}) custom-call(s32[2]{0:T(128)S(1)} %pad_add_fusion.ids, s32[16,8]{1,0:T(8,128)S(1)} %copy.14.apertures, f32[2,8,32,128]{3,2,1,0:T(8,128)S(1)} %bitcast.31, ...), custom_call_target="tpu_custom_call" | custom-call | bytes 2097152 | tf_op jit(solution)/shard_map/pallas_call | solution.py:639
  17.2 1.3 collective-permute-start.3
  18.5 2.6 %collective-permute-start.4 = (f32[2,8,32,128]{3,2,1,0:T(8,128)}, f32[2,8,32,128]{3,2,1,0:T(8,128)}, u32[]{:S(2)}, u32[]{:S(2)}) collective-permute-start(f32[2,8,32,128]{3,2,1,0:T(8,128)} %get-tuple-element.53), channel_id=1, source_target_pairs={{0,32},{8,40},{16,48},{24,56},{32,0},{40,8},{48,16},{56,24},{64,96... | collective-permute-start | bytes 786440 | tf_op jit(solution)/shard_map/ppermute | solution.py:642
  21.1 1.1 collective-permute-start.5
  22.2 0.0 copy-start
  22.2 0.0 copy-start.12
  22.2 5.3 %shard_map.112 = (f32[64,48,128]{2,1,0:T(8,128)S(1)}, f32[64,48,128]{2,1,0:T(8,128)S(1)}, f32[64,32,128]{2,1,0:T(8,128)S(1)}, f32[64,32,128]{2,1,0:T(8,128)S(1)}, f32[64,32,128]{2,1,0:T(8,128)S(1)}) custom-call(s32[256]{0:T(256)S(1)} %bitcast.36, s32[256]{0:T(256)S(1)} %fusion.lines, f32[4,256]{1,0:T(4,128)S(1)} %bitcast.37), custom_call_target="tpu_custom_call" | custom-call | flops 1099511627776 | bytes 6291456 | tf_op jit(solution)/shard_map/pallas_call | solution.py:681
  27.5 1.1 copy-done.1
  28.7 1.0 copy-done.3
  29.7 1.0 copy-done.5
  30.7 1.0 copy-done.7
  32.4 1.3 constant_dynamic-slice_fusion
  35.7 0.1 stack.63.spots
  35.7 0.0 collective-permute-done.3.r1
  35.8 0.0 collective-permute-done.4.r2
  35.8 0.0 collective-permute-done.5.r3
  35.8 2.1 %shard_map.111 = (f32[64,32,128]{2,1,0:T(8,128)S(1)}, f32[64,8,128]{2,1,0:T(8,128)}, f32[64,8,128]{2,1,0:T(8,128)}) custom-call(s32[2]{0:T(128)S(1)} %copy-done.14, s32[16,8]{1,0:T(8,128)S(1)} %copy-done.11, f32[2,8,32,128]{3,2,1,0:T(8,128)S(1)} %get-tuple-element.51.r0, f32[2,8,32,128]{3,2,1,0:T(8,128)} %collective-permute-done.3.r1, ...), custom_call_target="tpu_custom_call" | custom-call | bytes 2097152 | tf_op jit(solution)/shard_map/pallas_call | solution.py:658
  37.9 1.5 collective-permute-start.6
  39.3 2.2 %collective-permute-start.7 = (f32[64,8,128]{2,1,0:T(8,128)}, f32[64,8,128]{2,1,0:T(8,128)S(1)}, u32[]{:S(2)}, u32[]{:S(2)}) collective-permute-start(f32[64,8,128]{2,1,0:T(8,128)} %get-tuple-element.60), channel_id=1, source_target_pairs={{1,0},{2,1},{3,2},{4,3},{5,4},{6,5},{7,6},{0,7},{9,8},{10,9},{11,1... | collective-permute-start | bytes 786440 | tf_op jit(solution)/shard_map/ppermute | solution.py:633
  41.5 27.2 %all-to-all-done = f32[8,8,144,128]{3,2,1,0:T(8,128)} async-done(((f32[8,8,144,128]{3,2,1,0:T(8,128)}), f32[8,8,144,128]{3,2,1,0:T(8,128)}, u32[]{:S(2)}, u32[]{:S(2)}) %all-to-all-start) | async-done | bytes 4718624 | tf_op jit(solution)/shard_map/all_to_all | solution.py:657
  68.7 4.0 %shard_map.113 = (f32[64,32,128]{2,1,0:T(8,128)S(1)}, f32[64,32,128]{2,1,0:T(8,128)S(1)}, f32[64,8,128]{2,1,0:T(8,128)S(1)}, f32[64,8,128]{2,1,0:T(8,128)S(1)}, ...) custom-call(s32[8]{0:T(128)S(1)} %stack.63.spots, f32[4]{0:T(128)S(1)} %bitcast.32, ...), custom_call_target="tpu_custom_call" | custom-call | flops 10485760 | bytes 8388608 | tf_op jit(solution)/shard_map/pallas_call | solution.py:686
  72.7 0.7 collective-permute-start.8
  73.3 3.0 %collective-permute-start.9 = (f32[64,8,128]{2,1,0:T(8,128)S(1)}, f32[64,8,128]{2,1,0:T(8,128)S(1)}, u32[]{:S(2)}, u32[]{:S(2)}) collective-permute-start(f32[64,8,128]{2,1,0:T(8,128)S(1)} %get-tuple-element.64), channel_id=1, source_target_pairs={{1,0},{2,1},{3,2},{4,3},{5,4},{6,5},{7,6},{0,7},{9,8},{10,9},{11,1... | collective-permute-start | bytes 786440 | tf_op jit(solution)/shard_map/ppermute | solution.py:633
  76.3 0.0 collective-permute-done.6.r2_lo
  76.3 0.0 collective-permute-done.7.r2_hi
  76.3 4.4 %shard_map.114 = (f32[64,32,128]{2,1,0:T(8,128)S(1)}, f32[64,32,128]{2,1,0:T(8,128)S(1)}, f32[64,8,128]{2,1,0:T(8,128)S(1)}) custom-call(s32[8]{0:T(128)S(1)} %stack.63.spots, f32[64,144,128]{2,1,0:T(8,128)} %bitcast.17.turned, f32[64,32,128]{2,1,0:T(8,128)S(1)} %get-tuple-element.57.r2, f32[64,8,128]{2,1,0:T(8,128)S(1)} %collective-permute-done.6.r2_lo, ...), custom_call_target="tpu_custom_call" | custom-call | flops 10485760 | bytes 6291456 | tf_op jit(solution)/shard_map/pallas_call | solution.py:695
  80.7 1.6 %collective-permute-done.8.now_lo = f32[64,8,128]{2,1,0:T(8,128)S(1)} collective-permute-done((f32[64,8,128]{2,1,0:T(8,128)S(1)}, f32[64,8,128]{2,1,0:T(8,128)S(1)}, u32[]{:S(2)}, u32[]{:S(2)}) %collective-permute-start.8) | collective-permute-done | bytes 262176 | tf_op jit(solution)/shard_map/ppermute | solution.py:633
  82.3 0.0 collective-permute-done.9.now_hi
  82.3 4.9 %shard_map.115 = (f32[64,32,128]{2,1,0:T(8,128)S(1)}, f32[64,32,128]{2,1,0:T(8,128)S(1)}, f32[64,32,128]{2,1,0:T(8,128)S(1)}, f32[64,32,128]{2,1,0:T(8,128)S(1)}...) custom-call(s32[8]{0:T(128)S(1)} %stack.63.spots, f32[4]{0:T(128)S(1)} %bitcast.33, ...), custom_call_target="tpu_custom_call" | custom-call | flops 20971520 | bytes 12582912 | tf_op jit(solution)/shard_map/pallas_call | solution.py:704
  87.2 0.1 collective-permute-start.10
  87.3 3.6 %collective-permute-start.11 = (f32[32,8,128]{2,1,0:T(8,128)S(1)}, f32[32,8,128]{2,1,0:T(8,128)S(1)}, u32[]{:S(2)}, u32[]{:S(2)}) collective-permute-start(f32[32,8,128]{2,1,0:T(8,128)S(1)} %get-tuple-element.68), channel_id=1, source_target_pairs={{1,0},{2,1},{3,2},{4,3},{5,4},{6,5},{7,6},{0,7},{9,8},{10,9},{11,1... | collective-permute-start | bytes 393224 | tf_op jit(solution)/shard_map/ppermute | solution.py:633
  90.8 2.5 %shard_map.116 = (f32[64,32,128]{2,1,0:T(8,128)S(1)}, f32[64,32,128]{2,1,0:T(8,128)S(1)}) custom-call(s32[8]{0:T(128)S(1)} %stack.63.spots, f32[4]{0:T(128)S(1)} %bitcast.34, f32[64,32,128]{2,1,0:T(8,128)S(1)} %get-tuple-element.70.now.wave, f32[64,32,128]{2,1,0:T(8,128)S(1)} %get-tuple-element.71.prev.wave_b, f32[64,32,128]{2,1,0:T(8,128)S(1)} %get-tuple-element.57.r2, ...), custom_call_target="tpu_custom_call" | custom-call | flops 10485760 | bytes 8388608 | tf_op jit(solution)/shard_map/pallas_call | solution.py:713
  93.4 0.0 collective-permute-done.10.halo_lo.wave_lo
  93.4 0.0 collective-permute-done.11.halo_hi.wave_hi
  93.4 1.0 shard_map.117
  94.4 0.1 collective-permute-start.12
  94.4 3.6 %collective-permute-start.13 = (f32[64,8,128]{2,1,0:T(8,128)S(1)}, f32[64,8,128]{2,1,0:T(8,128)S(1)}, u32[]{:S(2)}, u32[]{:S(2)}) collective-permute-start(f32[64,8,128]{2,1,0:T(8,128)S(1)} %get-tuple-element.78), channel_id=1, source_target_pairs={{1,0},{2,1},{3,2},{4,3},{5,4},{6,5},{7,6},{0,7},{9,8},{10,9},{11,1... | collective-permute-start | bytes 786440 | tf_op jit(solution)/shard_map/ppermute | solution.py:633
  98.0 2.4 %shard_map.118 = (f32[64,32,128]{2,1,0:T(8,128)S(1)}, f32[64,32,128]{2,1,0:T(8,128)S(1)}) custom-call(s32[8]{0:T(128)S(1)} %stack.63.spots, f32[64,32,128]{2,1,0:T(8,128)S(1)} %get-tuple-element.76.late, f32[64,32,128]{2,1,0:T(8,128)S(1)} %get-tuple-element.84.later, f32[64,32,128]{2,1,0:T(8,128)S(1)} %get-tuple-element.57.r2, bf16[256,256]{1,0:T(8,128)(2,1)S(1)} %copy-done, ...), custom_call_target="tpu_custom_call" | custom-call | flops 10485760 | bytes 8388608 | tf_op jit(solution)/shard_map/pallas_call | solution.py:725
  100.4 1.7 %collective-permute-done.12.late_lo = f32[64,8,128]{2,1,0:T(8,128)S(1)} collective-permute-done((f32[64,8,128]{2,1,0:T(8,128)S(1)}, f32[64,8,128]{2,1,0:T(8,128)S(1)}, u32[]{:S(2)}, u32[]{:S(2)}) %collective-permute-start.12) | collective-permute-done | bytes 262176 | tf_op jit(solution)/shard_map/ppermute | solution.py:633
  102.1 0.0 collective-permute-done.13.late_hi
  102.1 4.4 %shard_map.119 = (f32[64,32,128]{2,1,0:T(8,128)S(1)}, f32[64,32,128]{2,1,0:T(8,128)S(1)}, f32[64,32,128]{2,1,0:T(8,128)S(1)}, f32[32,8,128]{2,1,0:T(8,128)S(1)}, f32[32,8,128]{2,1,0:T(8,128)S(1)}) custom-call(s32[8]{0:T(128)S(1)} %stack.63.spots, f32[64,32,128]{2,1,0:T(8,128)S(1)} %get-tuple-element.76.late, ...), custom_call_target="tpu_custom_call" | custom-call | flops 20971520 | bytes 16777216 | tf_op jit(solution)/shard_map/pallas_call | solution.py:728
  106.5 0.1 collective-permute-start.14
  106.6 3.6 %collective-permute-start.15 = (f32[32,8,128]{2,1,0:T(8,128)S(1)}, f32[32,8,128]{2,1,0:T(8,128)S(1)}, u32[]{:S(2)}, u32[]{:S(2)}) collective-permute-start(f32[32,8,128]{2,1,0:T(8,128)S(1)} %get-tuple-element.89), channel_id=1, source_target_pairs={{1,0},{2,1},{3,2},{4,3},{5,4},{6,5},{7,6},{0,7},{9,8},{10,9},{11,1... | collective-permute-start | bytes 393224 | tf_op jit(solution)/shard_map/ppermute | solution.py:633
  110.2 2.5 %shard_map.120.total_in = f32[8,8,32,128]{3,2,1,0:T(8,128)S(1)} custom-call(s32[8]{0:T(128)S(1)} %stack.63.spots, f32[64,32,128]{2,1,0:T(8,128)S(1)} %get-tuple-element.91.late, f32[64,32,128]{2,1,0:T(8,128)S(1)} %get-tuple-element.92.later, f32[64,32,128]{2,1,0:T(8,128)S(1)} %get-tuple-element.57.r2, bf16[256,256]{1,0:T(8,128)(2,1)S(1)} %copy-done, ...), custom_call_target="tpu_custom_call" | custom-call | flops 10485760 | bytes 8388608 | tf_op jit(solution)/shard_map/pallas_call | solution.py:740
  112.7 1.2 shard_map.121
  113.9 23.4 %all_to_all.10.recv = f32[8,8,32,128]{3,2,1,0:T(8,128)S(1)} all-to-all(f32[8,8,32,128]{3,2,1,0:T(8,128)S(1)} %shard_map.121), channel_id=1, replica_groups={{0,8,16,24,32,40,48,56},{64,72,80,88,96,104,112,120},{1,9,17,25,33,41,4..., dimensions={0} | all-to-all | bytes 2097152 | tf_op jit(solution)/shard_map/all_to_all | solution.py:747
  137.3 1.0 shard_map.122
  138.3 1.0 collective-permute-start.16
  139.3 7.3 %collective-permute-done.16 = f32[2,8,32,128]{3,2,1,0:T(8,128)S(1)} collective-permute-done((f32[2,8,32,128]{3,2,1,0:T(8,128)S(1)}, f32[2,8,32,128]{3,2,1,0:T(8,128)S(1)}, u32[]{:S(2)}, u32[]{:S(2)}) %collective-permute-start.16) | collective-permute-done | bytes 262176 | tf_op jit(solution)/shard_map/ppermute | solution.py:749
  146.6 0.7 add_bitcast_fusion
  (29 shorter events, 0.1 us)
Async XLA Ops:
  0.0 13.6 %collective-permute-start = (f32[2,8,32,128]{3,2,1,0:T(8,128)}, f32[2,8,32,128]{3,2,1,0:T(8,128)S(1)}, u32[]{:S(2)}, u32[]{:S(2)}) collective-permute-start(f32[2,8,32,128]{3,2,1,0:T(8,128)} %bitcast.29), channel_id=1, source_target_pairs={{0,64},{8,72},{16,80},{24,88},{32,96},{40,104},{48,112},{56,120},{... | collective-permute-start | bytes 786440 | tf_op jit(solution)/shard_map/ppermute | solution.py:636
  3.6 10.6 %collective-permute-start.1 = (f32[2,8,32,128]{3,2,1,0:T(8,128)}, f32[2,8,32,128]{3,2,1,0:T(8,128)S(1)}, u32[]{:S(2)}, u32[]{:S(2)}) collective-permute-start(f32[2,8,32,128]{3,2,1,0:T(8,128)} %bitcast.30), channel_id=1, source_target_pairs={{0,8},{8,0},{16,24},{24,16},{32,40},{40,32},{48,56},{56,48},{64,72... | collective-permute-start | bytes 786440 | tf_op jit(solution)/shard_map/ppermute | solution.py:637
  8.3 5.7 %copy-start.17 = (s32[16,8]{0,1:T(8,128)S(1)}, s32[16,8]{0,1:T(8,128)}, u32[]{:S(2)}) copy-start(s32[16,8]{0,1:T(8,128)} %param.20) | copy-start | bytes 1540
  8.3 5.8 %copy-start.15 = (s32[1,256]{1,0:T(1,128)S(1)}, s32[1,256]{1,0:T(1,128)}, u32[]{:S(2)}) copy-start(s32[1,256]{1,0:T(1,128)} %param.18) | copy-start | bytes 3076
  8.3 6.9 %copy-start.9 = (f32[2,1,8,32,128]{4,3,2,1,0:T(8,128)S(1)}, f32[2,1,8,32,128]{4,3,2,1,0:T(8,128)}, u32[]{:S(2)}) copy-start(f32[2,1,8,32,128]{4,3,2,1,0:T(8,128)} %param.11) | copy-start | bytes 786436
  8.4 13.8 %copy-start.16 = (f32[1,4,256]{2,1,0:T(4,128)S(1)}, f32[1,4,256]{2,1,0:T(4,128)}, u32[]{:S(2)}) copy-start(f32[1,4,256]{2,1,0:T(4,128)} %param.19) | copy-start | bytes 12292
  8.4 60.3 %all-to-all-start = ((f32[8,8,144,128]{3,2,1,0:T(8,128)}), f32[8,8,144,128]{3,2,1,0:T(8,128)}, u32[]{:S(2)}, u32[]{:S(2)}) async-start(f32[8,8,144,128]{3,2,1,0:T(8,128)} %shard_map.109), calls=%async_computation | async-start | bytes 9437184 | tf_op jit(solution)/shard_map/all_to_all | solution.py:657
  13.6 1.6 %collective-permute-start.2 = (f32[2,8,32,128]{3,2,1,0:T(8,128)S(1)}, f32[2,8,32,128]{3,2,1,0:T(8,128)S(1)}, u32[]{:S(2)}, u32[]{:S(2)}) collective-permute-start(f32[2,8,32,128]{3,2,1,0:T(8,128)S(1)} %collective-permute-done.other), channel_id=1, source_target_pairs={{0,8},{8,0},{16,24},{24,16},{32,40},{40,32},{48,56},{56,48},{64,72... | collective-permute-start | bytes 786440 | tf_op jit(solution)/shard_map/ppermute | solution.py:638
  14.0 8.1 %copy-start.13 = (s32[2]{0:T(128)}, s32[2]{0:T(128)S(1)}, u32[]{:S(2)}) copy-start(s32[2]{0:T(128)S(1)} %pad_add_fusion.ids) | copy-start | bytes 28
  14.1 8.1 %copy-start.10 = (s32[16,8]{1,0:T(8,128)}, s32[16,8]{1,0:T(8,128)S(1)}, u32[]{:S(2)}) copy-start(s32[16,8]{1,0:T(8,128)S(1)} %copy.14.apertures) | copy-start | bytes 1540
  17.2 18.6 %collective-permute-start.3 = (f32[2,8,32,128]{3,2,1,0:T(8,128)}, f32[2,8,32,128]{3,2,1,0:T(8,128)}, u32[]{:S(2)}, u32[]{:S(2)}) collective-permute-start(f32[2,8,32,128]{3,2,1,0:T(8,128)} %get-tuple-element.52), channel_id=1, source_target_pairs={{0,16},{8,24},{16,32},{24,40},{32,48},{40,56},{48,0},{56,8},{64,80... | collective-permute-start | bytes 786440 | tf_op jit(solution)/shard_map/ppermute | solution.py:642
  18.5 17.3 %collective-permute-start.4 = (f32[2,8,32,128]{3,2,1,0:T(8,128)}, f32[2,8,32,128]{3,2,1,0:T(8,128)}, u32[]{:S(2)}, u32[]{:S(2)}) collective-permute-start(f32[2,8,32,128]{3,2,1,0:T(8,128)} %get-tuple-element.53), channel_id=1, source_target_pairs={{0,32},{8,40},{16,48},{24,56},{32,0},{40,8},{48,16},{56,24},{64,96... | collective-permute-start | bytes 786440 | tf_op jit(solution)/shard_map/ppermute | solution.py:642
  21.1 14.7 %collective-permute-start.5 = (f32[2,8,32,128]{3,2,1,0:T(8,128)}, f32[2,8,32,128]{3,2,1,0:T(8,128)}, u32[]{:S(2)}, u32[]{:S(2)}) collective-permute-start(f32[2,8,32,128]{3,2,1,0:T(8,128)} %get-tuple-element.54), channel_id=1, source_target_pairs={{0,48},{8,56},{16,0},{24,8},{32,16},{40,24},{48,32},{56,40},{64,11... | collective-permute-start | bytes 786440 | tf_op jit(solution)/shard_map/ppermute | solution.py:642
  22.2 13.6 %copy-start.11 = (s32[16,8]{1,0:T(8,128)S(1)}, s32[16,8]{1,0:T(8,128)}, u32[]{:S(2)}) copy-start(s32[16,8]{1,0:T(8,128)} %copy-done.10) | copy-start | bytes 1540
  22.2 13.6 %copy-start.14 = (s32[2]{0:T(128)S(1)}, s32[2]{0:T(128)}, u32[]{:S(2)}) copy-start(s32[2]{0:T(128)} %copy-done.13) | copy-start | bytes 28
  22.2 46.5 %copy-start = (bf16[256,256]{1,0:T(8,128)(2,1)S(1)}, bf16[256,256]{1,0:T(8,128)(2,1)}, u32[]{:S(2)}) copy-start(bf16[256,256]{1,0:T(8,128)(2,1)} %constant.94.clone.oper) | copy-start | bytes 393220
  22.2 46.5 %copy-start.12 = (f32[1,4]{1,0:T(1,128)S(1)}, f32[1,4]{1,0:T(1,128)}, u32[]{:S(2)}) copy-start(f32[1,4]{1,0:T(1,128)} %param.16) | copy-start | bytes 52
  27.5 1.2 copy-start.1
  28.7 1.0 copy-start.3
  29.7 1.0 copy-start.5
  30.7 1.0 copy-start.7
  37.9 38.4 %collective-permute-start.6 = (f32[64,8,128]{2,1,0:T(8,128)}, f32[64,8,128]{2,1,0:T(8,128)S(1)}, u32[]{:S(2)}, u32[]{:S(2)}) collective-permute-start(f32[64,8,128]{2,1,0:T(8,128)} %get-tuple-element.59), channel_id=1, source_target_pairs={{0,1},{1,2},{2,3},{3,4},{4,5},{5,6},{6,7},{7,0},{8,9},{9,10},{10,1... | collective-permute-start | bytes 786440 | tf_op jit(solution)/shard_map/ppermute | solution.py:633
  39.3 37.0 %collective-permute-start.7 = (f32[64,8,128]{2,1,0:T(8,128)}, f32[64,8,128]{2,1,0:T(8,128)S(1)}, u32[]{:S(2)}, u32[]{:S(2)}) collective-permute-start(f32[64,8,128]{2,1,0:T(8,128)} %get-tuple-element.60), channel_id=1, source_target_pairs={{1,0},{2,1},{3,2},{4,3},{5,4},{6,5},{7,6},{0,7},{9,8},{10,9},{11,1... | collective-permute-start | bytes 786440 | tf_op jit(solution)/shard_map/ppermute | solution.py:633
  72.7 9.7 %collective-permute-start.8 = (f32[64,8,128]{2,1,0:T(8,128)S(1)}, f32[64,8,128]{2,1,0:T(8,128)S(1)}, u32[]{:S(2)}, u32[]{:S(2)}) collective-permute-start(f32[64,8,128]{2,1,0:T(8,128)S(1)} %get-tuple-element.63), channel_id=1, source_target_pairs={{0,1},{1,2},{2,3},{3,4},{4,5},{5,6},{6,7},{7,0},{8,9},{9,10},{10,1... | collective-permute-start | bytes 786440 | tf_op jit(solution)/shard_map/ppermute | solution.py:633
  73.3 17.5 %copy-start.8 = (f32[64,32,128]{2,1,0:T(8,128)S(1)}, f32[64,32,128]{2,1,0:T(8,128)}, u32[]{:S(2)}) copy-start(f32[64,32,128]{2,1,0:T(8,128)} %copy-done.7) | copy-start | bytes 3145732
  73.3 9.0 %collective-permute-start.9 = (f32[64,8,128]{2,1,0:T(8,128)S(1)}, f32[64,8,128]{2,1,0:T(8,128)S(1)}, u32[]{:S(2)}, u32[]{:S(2)}) collective-permute-start(f32[64,8,128]{2,1,0:T(8,128)S(1)} %get-tuple-element.64), channel_id=1, source_target_pairs={{1,0},{2,1},{3,2},{4,3},{5,4},{6,5},{7,6},{0,7},{9,8},{10,9},{11,1... | collective-permute-start | bytes 786440 | tf_op jit(solution)/shard_map/ppermute | solution.py:633
  87.2 6.2 %collective-permute-start.10 = (f32[32,8,128]{2,1,0:T(8,128)S(1)}, f32[32,8,128]{2,1,0:T(8,128)S(1)}, u32[]{:S(2)}, u32[]{:S(2)}) collective-permute-start(f32[32,8,128]{2,1,0:T(8,128)S(1)} %get-tuple-element.67), channel_id=1, source_target_pairs={{0,1},{1,2},{2,3},{3,4},{4,5},{5,6},{6,7},{7,0},{8,9},{9,10},{10,1... | collective-permute-start | bytes 393224 | tf_op jit(solution)/shard_map/ppermute | solution.py:633
  87.3 6.1 %collective-permute-start.11 = (f32[32,8,128]{2,1,0:T(8,128)S(1)}, f32[32,8,128]{2,1,0:T(8,128)S(1)}, u32[]{:S(2)}, u32[]{:S(2)}) collective-permute-start(f32[32,8,128]{2,1,0:T(8,128)S(1)} %get-tuple-element.68), channel_id=1, source_target_pairs={{1,0},{2,1},{3,2},{4,3},{5,4},{6,5},{7,6},{0,7},{9,8},{10,9},{11,1... | collective-permute-start | bytes 393224 | tf_op jit(solution)/shard_map/ppermute | solution.py:633
  90.8 7.2 %copy-start.2 = (f32[64,48,128]{2,1,0:T(8,128)S(1)}, f32[64,48,128]{2,1,0:T(8,128)}, u32[]{:S(2)}) copy-start(f32[64,48,128]{2,1,0:T(8,128)} %copy-done.1) | copy-start | bytes 4718596
  94.4 7.8 %collective-permute-start.12 = (f32[64,8,128]{2,1,0:T(8,128)S(1)}, f32[64,8,128]{2,1,0:T(8,128)S(1)}, u32[]{:S(2)}, u32[]{:S(2)}) collective-permute-start(f32[64,8,128]{2,1,0:T(8,128)S(1)} %get-tuple-element.77), channel_id=1, source_target_pairs={{0,1},{1,2},{2,3},{3,4},{4,5},{5,6},{6,7},{7,0},{8,9},{9,10},{10,1... | collective-permute-start | bytes 786440 | tf_op jit(solution)/shard_map/ppermute | solution.py:633
  94.4 7.7 %collective-permute-start.13 = (f32[64,8,128]{2,1,0:T(8,128)S(1)}, f32[64,8,128]{2,1,0:T(8,128)S(1)}, u32[]{:S(2)}, u32[]{:S(2)}) collective-permute-start(f32[64,8,128]{2,1,0:T(8,128)S(1)} %get-tuple-element.78), channel_id=1, source_target_pairs={{1,0},{2,1},{3,2},{4,3},{5,4},{6,5},{7,6},{0,7},{9,8},{10,9},{11,1... | collective-permute-start | bytes 786440 | tf_op jit(solution)/shard_map/ppermute | solution.py:633
  98.0 4.1 %copy-start.6 = (f32[64,32,128]{2,1,0:T(8,128)S(1)}, f32[64,32,128]{2,1,0:T(8,128)}, u32[]{:S(2)}) copy-start(f32[64,32,128]{2,1,0:T(8,128)} %copy-done.5) | copy-start | bytes 3145732
  102.1 8.0 %copy-start.4 = (f32[64,32,128]{2,1,0:T(8,128)S(1)}, f32[64,32,128]{2,1,0:T(8,128)}, u32[]{:S(2)}) copy-start(f32[64,32,128]{2,1,0:T(8,128)} %copy-done.3) | copy-start | bytes 3145732
  106.5 6.2 %collective-permute-start.14 = (f32[32,8,128]{2,1,0:T(8,128)S(1)}, f32[32,8,128]{2,1,0:T(8,128)S(1)}, u32[]{:S(2)}, u32[]{:S(2)}) collective-permute-start(f32[32,8,128]{2,1,0:T(8,128)S(1)} %get-tuple-element.88), channel_id=1, source_target_pairs={{0,1},{1,2},{2,3},{3,4},{4,5},{5,6},{6,7},{7,0},{8,9},{9,10},{10,1... | collective-permute-start | bytes 393224 | tf_op jit(solution)/shard_map/ppermute | solution.py:633
  106.6 6.1 %collective-permute-start.15 = (f32[32,8,128]{2,1,0:T(8,128)S(1)}, f32[32,8,128]{2,1,0:T(8,128)S(1)}, u32[]{:S(2)}, u32[]{:S(2)}) collective-permute-start(f32[32,8,128]{2,1,0:T(8,128)S(1)} %get-tuple-element.89), channel_id=1, source_target_pairs={{1,0},{2,1},{3,2},{4,3},{5,4},{6,5},{7,6},{0,7},{9,8},{10,9},{11,1... | collective-permute-start | bytes 393224 | tf_op jit(solution)/shard_map/ppermute | solution.py:633
  138.3 8.3 %collective-permute-start.16 = (f32[2,8,32,128]{3,2,1,0:T(8,128)S(1)}, f32[2,8,32,128]{3,2,1,0:T(8,128)S(1)}, u32[]{:S(2)}, u32[]{:S(2)}) collective-permute-start(f32[2,8,32,128]{3,2,1,0:T(8,128)S(1)} %get-tuple-element.96), channel_id=1, source_target_pairs={{0,64},{8,72},{16,80},{24,88},{32,96},{40,104},{48,112},{56,120},{... | collective-permute-start | bytes 786440 | tf_op jit(solution)/shard_map/ppermute | solution.py:749

commit v8 on v7

--- a/solution.py
+++ b/solution.py
@@ -413,7 +413,6 @@
 def last_kernel(
     spots, late, later, r2, oper, count, data, wave, lap, total_in, total, ext, depth
 ):
-    first = spots[0]
     clear_ends(ext)
     ext[OWN_X, OWN_Y, :] = late[...] * r2[...]
     no_edges(ext)
@@ -422,24 +421,27 @@
     def emit(x, g, xi, j, value):
         mu = 2.0 * late[x, tile(j), :] + value - later[x, tile(j), :]
         mu = mu + (count[x, 8 + 8 * j : 16 + 8 * j, :] * wave[x, tile(j), :] - data[x, tile(j), :])
-        total[lax.rem(first + g, GROUP), xi, tile(j), :] = total_in[x, tile(j), :] + mu * lap[x, tile(j), :]
+        total[x, tile(j), :] = total_in[x, tile(j), :] + mu * lap[x, tile(j), :]
 
     laplace(ext, depth, OWN, emit)
 
 
-def last_end_kernel(spots, halo_lo, halo_hi, lap, total_in, total, strip):
+def last_end_kernel(ids, spots, halo_lo, halo_hi, lap, total, *rest):
+    outs, strip = rest[:8], rest[8]
     fill_strip(strip, spots, halo_lo, halo_hi)
-    first = spots[0]
-
-    def body(x):
-        slot, xi = lax.rem(first + x // GROUP, GROUP), lax.rem(x, GROUP)
-        for j in OWN:
-            value = total_in[slot, xi, tile(j), :]
-            if j in (0, 3):
-                value = value + lap[x, tile(j), :] * halo_taps(strip, x, j)
-            total[slot, xi, tile(j), :] = value
-
-    planes(body)
+    _, y, core = split_shot(ids[0])
+    for k in range(4):
+        for side in range(2):
+            cls = 2 * lax.rem(y + k, 4) + (core if side == 0 else 1 - core)
+            g = lax.rem(cls - spots[0] + GROUP, GROUP)
+            out = outs[2 * k + side]
+            for xi in range(GROUP):
+                x = g * GROUP + xi
+                for j in OWN:
+                    value = total[x, tile(j), :]
+                    if j in (0, 3):
+                        value = value + lap[x, tile(j), :] * halo_taps(strip, x, j)
+                    out[xi, tile(j), :] = value
 
 
 def pack_kernel(now, prev, late, later, out, near, edge, sems):
@@ -558,30 +560,33 @@
     lax.fori_loop(0, cells.shape[0], body, 0)
 
 
-def bins_kernel(ids, apertures, recv, keep, give):
-    mine, which = ids[0] // 8, lax.rem(ids[0], 8)
+def bins_kernel(ids, apertures, *rest):
+    recv, (keep, give) = rest[:8], rest[8:]
+    mine, y, core = split_shot(ids[0])
+    which = lax.rem(ids[0], 8)
     zeros = jnp.zeros((GROUP, NYL, NZ), F32)
     for i in range(2):
         keep[i] = zeros
         give[i] = zeros
     for t in range(GROUP):
-        m = slot_of(apertures[8 * mine + t, 0], which)
+        shot = 8 * mine + 2 * lax.rem(y - t // 2 + 4, 4) + (core if t % 2 == 0 else 1 - core)
+        m = slot_of(apertures[shot, 0], which)
         i = m // 2
 
         @pl.when(lax.rem(m, 2) == mine)
         def _():
-            keep[i] = keep[i] + recv[t]
+            keep[i] = keep[i] + recv[t][...]
 
         @pl.when(lax.rem(m, 2) != mine)
         def _():
-            give[i] = give[i] + recv[t]
+            give[i] = give[i] + recv[t][...]
 
 
 FIELD = jax.ShapeDtypeStruct((NX, NYL, NZ), F32)
 WIDE_FIELD = jax.ShapeDtypeStruct((NX, WIDE, NZ), F32)
 EDGE = jax.ShapeDtypeStruct((NX // 2, 8, NZ), F32)
 TILE = jax.ShapeDtypeStruct((NX, 8, NZ), F32)
-BLOCKS = jax.ShapeDtypeStruct((8, GROUP, NYL, NZ), F32)
+BLOCK = jax.ShapeDtypeStruct((GROUP, NYL, NZ), F32)
 PAIR = jax.ShapeDtypeStruct((2, GROUP, NYL, NZ), F32)
 EXT = pltpu.VMEM((NX + 2 * PAD, ROWS, NZ), F32)
 DEPTH = pltpu.VMEM((NX, WIDE, NZ), F32)
@@ -624,7 +629,6 @@
     down = [((i + 1) % 8, i) for i in range(8)]
     across = [(i, (i + 8) % 16) for i in range(16)]
     chip = [(i, i ^ 1) for i in range(16)]
-    halves = [list(range(8)), list(range(8, 16))]
 
     def along(k):
         return [(8 * h + 2 * y + c, 8 * h + 2 * ((y + k) % 4) + c) for h in range(2) for y in range(4) for c in range(2)]
@@ -737,15 +741,20 @@
         *u3_halo, u2, lap2, lap1, mu3, total,
     )
     mu2_halo = edges(lo, hi)
-    (total,) = call(last_kernel, [SMEM] + [VMEM] * 9, [BLOCKS], [EXT, DEPTH], flops=MAIN, moved=8 << 20)(
+    (total,) = call(last_kernel, [SMEM] + [VMEM] * 9, [FIELD], [EXT, DEPTH], flops=MAIN, moved=8 << 20)(
         spots, mu2, mu3, r2, oper, count, data1, u1, lap0, total
     )
-    (total,) = call(last_end_kernel, [SMEM] + [VMEM] * 4, [BLOCKS], [STRIP], flops=1 << 20, moved=3 << 20)(
-        spots, *mu2_halo, lap0, total
-    )
-
-    recv = lax.all_to_all(total, "shot", 0, 0, axis_index_groups=halves, tiled=True)
-    keep, give = call(bins_kernel, [SMEM, SMEM, VMEM], [PAIR, PAIR], moved=2 << 20)(ids, apertures, recv)
+    sent = call(last_end_kernel, [SMEM] * 2 + [VMEM] * 4, [BLOCK] * 8, [STRIP], flops=1 << 20, moved=3 << 20)(
+        ids, spots, *mu2_halo, lap0, total
+    )
+
+    recv = []
+    for k in range(4):
+        mine, others = sent[2 * k], lax.ppermute(sent[2 * k + 1], "shot", chip)
+        if k:
+            mine, others = lax.ppermute(mine, "shot", along(k)), lax.ppermute(others, "shot", along(k))
+        recv += [mine, others]
+    keep, give = call(bins_kernel, [SMEM] * 2 + [VMEM] * 8, [PAIR, PAIR], moved=2 << 20)(ids, apertures, *recv)
     result = keep + lax.ppermute(give, "shot", across)
     return result[:, None]
 

time: 148 us -> 146 us (0.986); the launches traced: 147 us -> 144 us
  blocking collectives: 23.4 us -> 0 us
  starting transfers between devices: 34.3 us -> 47.7 us
  waiting for transfers between devices: 38.9 us -> 46.1 us
    all_to_all x1 -> x0, blocking collectives: 23.4 us -> none  [per_device(): lax.all_to_all(total, 'shot', 0, 0, axis_index_groups=halves, tiled=True)]
    ppermute x0 -> x10, starting transfers between devices: none -> 13.2 us  [the longest x3 5.35 us: per_device(): lax.ppermute(mine, 'shot', along(k))]
    ppermute x0 -> x10, waiting for transfers between devices: none -> 7.43 us  [the longest x3 5.77 us: per_device(): lax.ppermute(others, 'shot', along(k))]
  transfers between devices with their start and end apart: 18 -> 28, of which waited for: 5 -> 10; matrix products, arithmetic and copies ran while one was open for 1% -> 1% of each run, Pallas kernels for 20% -> 20%
where the time goes in v8:
time: 146 us; the launch traced here: 144 us
  starting transfers between devices  47.7 us (33%)
  waiting for transfers between devices  46.1 us (32%)
  Pallas kernels  40.7 us (28%)
  local copies, waits for them, and re-layouts  5.62 us (4%)
  between operations  2.7 us (2%)
    all_to_all x1, waiting for transfers between devices, per_device(): lax.all_to_all(packed, 'sub', 0, 0, tiled=True).reshape(NX, TURNED, NZ)  27.6 us
    ppermute x10, starting transfers between devices, edges(): return (lax.ppermute(hi, 'sub', up), lax.ppermute(lo, 'sub', down))  18.4 us
    ppermute x1, waiting for transfers between devices, per_device(): result = keep + lax.ppermute(give, 'shot', across)  6.43 us
    ppermute x3, waiting for transfers between devices, per_device(): lax.ppermute(others, 'shot', along(k))  5.77 us
    ppermute x3, starting transfers between devices, per_device(): lax.ppermute(mine, 'shot', along(k))  5.35 us
    all_to_all x1, starting transfers between devices, per_device(): lax.all_to_all(packed, 'sub', 0, 0, tiled=True).reshape(NX, TURNED, NZ)  5.21 us
    pallas_call x1, Pallas kernels, per_device(): call(receivers_kernel, [SMEM] * 3, [WIDE_FIELD, WIDE_FIELD] + [FIELD] * 3...  5.2 us
    ppermute x4, starting transfers between devices, per_device(): mine, others = (sent[2 * k], lax.ppermute(sent[2 * k + 1], 'shot', chip))  5.12 us
  transfers between devices with their start and end apart: 28, of which 10 were waited for; matrix products, arithmetic and copies ran while one was open for 1% of the time, Pallas kernels for 20%

profile of v8, /device:TPU:1, one launch (start us, length us, event | category | flops | bytes accessed | tf_op | source)
XLA Modules:
  0.0 143.6 jit_solution(5459703778923117686)
XLA Ops:
  0.0 3.6 %collective-permute-start = (f32[2,8,32,128]{3,2,1,0:T(8,128)}, f32[2,8,32,128]{3,2,1,0:T(8,128)S(1)}, u32[]{:S(2)}, u32[]{:S(2)}) collective-permute-start(f32[2,8,32,128]{3,2,1,0:T(8,128)} %bitcast.29), channel_id=1, source_target_pairs={{0,64},{8,72},{16,80},{24,88},{32,96},{40,104},{48,112},{56,120},{... | collective-permute-start | bytes 786440 | tf_op jit(solution)/shard_map/ppermute | solution.py:640
  3.6 1.0 collective-permute-start.1
  4.5 3.8 %shard_map.109 = f32[8,8,144,128]{3,2,1,0:T(8,128)} custom-call(f32[8,256,128]{2,1,0:T(8,128)} %bitcast.38, f32[8,256,128]{2,1,0:T(8,128)} %bitcast.39, f32[8,256,128]{2,1,0:T(8,128)} %bitcast.40, f32[8,256,128]{2,1,0:T(8,128)} %bitcast.41), custom_call_target="tpu_custom_call" | custom-call | bytes 9437184 | tf_op jit(solution)/shard_map/pallas_call | solution.py:648
  8.3 0.0 copy-start.17
  8.3 0.0 copy-start.15
  8.4 5.2 %all-to-all-start = ((f32[8,8,144,128]{3,2,1,0:T(8,128)}), f32[8,8,144,128]{3,2,1,0:T(8,128)}, u32[]{:S(2)}, u32[]{:S(2)}) async-start(f32[8,8,144,128]{3,2,1,0:T(8,128)} %shard_map.109), calls=%async_computation | async-start | bytes 9437184 | tf_op jit(solution)/shard_map/all_to_all | solution.py:661
  13.6 0.4 collective-permute-start.2
  14.0 0.1 pad_add_fusion.ids
  14.0 0.1 copy.14.apertures
  14.1 1.1 collective-permute-done.2.other_c
  15.2 2.0 %shard_map.110 = (f32[2,8,32,128]{3,2,1,0:T(8,128)S(1)}, f32[2,8,32,128]{3,2,1,0:T(8,128)}, f32[2,8,32,128]{3,2,1,0:T(8,128)}, f32[2,8,32,128]{3,2,1,0:T(8,128)}) custom-call(s32[2]{0:T(128)S(1)} %pad_add_fusion.ids, s32[16,8]{1,0:T(8,128)S(1)} %copy.14.apertures, f32[2,8,32,128]{3,2,1,0:T(8,128)S(1)} %bitcast.31, ...), custom_call_target="tpu_custom_call" | custom-call | bytes 2097152 | tf_op jit(solution)/shard_map/pallas_call | solution.py:643
  17.2 1.3 collective-permute-start.3
  18.5 2.6 %collective-permute-start.4 = (f32[2,8,32,128]{3,2,1,0:T(8,128)}, f32[2,8,32,128]{3,2,1,0:T(8,128)}, u32[]{:S(2)}, u32[]{:S(2)}) collective-permute-start(f32[2,8,32,128]{3,2,1,0:T(8,128)} %get-tuple-element.61), channel_id=1, source_target_pairs={{0,32},{8,40},{16,48},{24,56},{32,0},{40,8},{48,16},{56,24},{64,96... | collective-permute-start | bytes 786440 | tf_op jit(solution)/shard_map/ppermute | solution.py:646
  21.1 1.1 collective-permute-start.5
  22.2 0.0 copy-start
  22.2 5.2 %shard_map.112 = (f32[64,48,128]{2,1,0:T(8,128)S(1)}, f32[64,48,128]{2,1,0:T(8,128)S(1)}, f32[64,32,128]{2,1,0:T(8,128)S(1)}, f32[64,32,128]{2,1,0:T(8,128)S(1)}, f32[64,32,128]{2,1,0:T(8,128)S(1)}) custom-call(s32[256]{0:T(256)S(1)} %bitcast.36, s32[256]{0:T(256)S(1)} %fusion.lines, f32[4,256]{1,0:T(4,128)S(1)} %bitcast.37), custom_call_target="tpu_custom_call" | custom-call | flops 1099511627776 | bytes 6291456 | tf_op jit(solution)/shard_map/pallas_call | solution.py:685
  27.4 1.1 copy-done.1
  28.6 1.0 copy-done.3
  29.6 1.0 copy-done.5
  30.6 1.0 copy-done.7
  32.3 1.2 constant_dynamic-slice_fusion
  35.2 0.1 stack.63.spots
  35.4 2.1 %shard_map.111 = (f32[64,32,128]{2,1,0:T(8,128)S(1)}, f32[64,8,128]{2,1,0:T(8,128)}, f32[64,8,128]{2,1,0:T(8,128)}) custom-call(s32[2]{0:T(128)S(1)} %copy-done.13, s32[16,8]{1,0:T(8,128)S(1)} %copy-done.11, f32[2,8,32,128]{3,2,1,0:T(8,128)S(1)} %get-tuple-element.59.r0, f32[2,8,32,128]{3,2,1,0:T(8,128)} %collective-permute-done.3.r1, ...), custom_call_target="tpu_custom_call" | custom-call | bytes 2097152 | tf_op jit(solution)/shard_map/pallas_call | solution.py:662
  37.5 1.5 %collective-permute-start.6 = (f32[64,8,128]{2,1,0:T(8,128)}, f32[64,8,128]{2,1,0:T(8,128)S(1)}, u32[]{:S(2)}, u32[]{:S(2)}) collective-permute-start(f32[64,8,128]{2,1,0:T(8,128)} %get-tuple-element.67), channel_id=1, source_target_pairs={{0,1},{1,2},{2,3},{3,4},{4,5},{5,6},{6,7},{7,0},{8,9},{9,10},{10,1... | collective-permute-start | bytes 786440 | tf_op jit(solution)/shard_map/ppermute | solution.py:637
  39.0 2.1 %collective-permute-start.7 = (f32[64,8,128]{2,1,0:T(8,128)}, f32[64,8,128]{2,1,0:T(8,128)S(1)}, u32[]{:S(2)}, u32[]{:S(2)}) collective-permute-start(f32[64,8,128]{2,1,0:T(8,128)} %get-tuple-element.68), channel_id=1, source_target_pairs={{1,0},{2,1},{3,2},{4,3},{5,4},{6,5},{7,6},{0,7},{9,8},{10,9},{11,1... | collective-permute-start | bytes 786440 | tf_op jit(solution)/shard_map/ppermute | solution.py:637
  41.1 27.6 %all-to-all-done = f32[8,8,144,128]{3,2,1,0:T(8,128)} async-done(((f32[8,8,144,128]{3,2,1,0:T(8,128)}), f32[8,8,144,128]{3,2,1,0:T(8,128)}, u32[]{:S(2)}, u32[]{:S(2)}) %all-to-all-start) | async-done | bytes 4718624 | tf_op jit(solution)/shard_map/all_to_all | solution.py:661
  68.7 4.0 %shard_map.113 = (f32[64,32,128]{2,1,0:T(8,128)S(1)}, f32[64,32,128]{2,1,0:T(8,128)S(1)}, f32[64,8,128]{2,1,0:T(8,128)S(1)}, f32[64,8,128]{2,1,0:T(8,128)S(1)}, ...) custom-call(s32[8]{0:T(128)S(1)} %stack.63.spots, f32[4]{0:T(128)S(1)} %bitcast.32, ...), custom_call_target="tpu_custom_call" | custom-call | flops 10485760 | bytes 8388608 | tf_op jit(solution)/shard_map/pallas_call | solution.py:690
  72.8 0.6 collective-permute-start.8
  73.4 3.0 %collective-permute-start.9 = (f32[64,8,128]{2,1,0:T(8,128)S(1)}, f32[64,8,128]{2,1,0:T(8,128)S(1)}, u32[]{:S(2)}, u32[]{:S(2)}) collective-permute-start(f32[64,8,128]{2,1,0:T(8,128)S(1)} %get-tuple-element.72), channel_id=1, source_target_pairs={{1,0},{2,1},{3,2},{4,3},{5,4},{6,5},{7,6},{0,7},{9,8},{10,9},{11,1... | collective-permute-start | bytes 786440 | tf_op jit(solution)/shard_map/ppermute | solution.py:637
  76.4 4.3 %shard_map.114 = (f32[64,32,128]{2,1,0:T(8,128)S(1)}, f32[64,32,128]{2,1,0:T(8,128)S(1)}, f32[64,8,128]{2,1,0:T(8,128)S(1)}) custom-call(s32[8]{0:T(128)S(1)} %stack.63.spots, f32[64,144,128]{2,1,0:T(8,128)} %bitcast.17.turned, f32[64,32,128]{2,1,0:T(8,128)S(1)} %get-tuple-element.65.r2, f32[64,8,128]{2,1,0:T(8,128)S(1)} %collective-permute-done.6.r2_lo, ...), custom_call_target="tpu_custom_call" | custom-call | flops 10485760 | bytes 6291456 | tf_op jit(solution)/shard_map/pallas_call | solution.py:699
  80.8 1.7 %collective-permute-done.8.now_lo = f32[64,8,128]{2,1,0:T(8,128)S(1)} collective-permute-done((f32[64,8,128]{2,1,0:T(8,128)S(1)}, f32[64,8,128]{2,1,0:T(8,128)S(1)}, u32[]{:S(2)}, u32[]{:S(2)}) %collective-permute-start.8) | collective-permute-done | bytes 262176 | tf_op jit(solution)/shard_map/ppermute | solution.py:637
  82.4 5.0 %shard_map.115 = (f32[64,32,128]{2,1,0:T(8,128)S(1)}, f32[64,32,128]{2,1,0:T(8,128)S(1)}, f32[64,32,128]{2,1,0:T(8,128)S(1)}, f32[64,32,128]{2,1,0:T(8,128)S(1)}...) custom-call(s32[8]{0:T(128)S(1)} %stack.63.spots, f32[4]{0:T(128)S(1)} %bitcast.33, ...), custom_call_target="tpu_custom_call" | custom-call | flops 20971520 | bytes 12582912 | tf_op jit(solution)/shard_map/pallas_call | solution.py:708
  87.5 0.1 collective-permute-start.10
  87.6 3.6 %collective-permute-start.11 = (f32[32,8,128]{2,1,0:T(8,128)S(1)}, f32[32,8,128]{2,1,0:T(8,128)S(1)}, u32[]{:S(2)}, u32[]{:S(2)}) collective-permute-start(f32[32,8,128]{2,1,0:T(8,128)S(1)} %get-tuple-element.76), channel_id=1, source_target_pairs={{1,0},{2,1},{3,2},{4,3},{5,4},{6,5},{7,6},{0,7},{9,8},{10,9},{11,1... | collective-permute-start | bytes 393224 | tf_op jit(solution)/shard_map/ppermute | solution.py:637
  91.1 2.6 %shard_map.116 = (f32[64,32,128]{2,1,0:T(8,128)S(1)}, f32[64,32,128]{2,1,0:T(8,128)S(1)}) custom-call(s32[8]{0:T(128)S(1)} %stack.63.spots, f32[4]{0:T(128)S(1)} %bitcast.34, f32[64,32,128]{2,1,0:T(8,128)S(1)} %get-tuple-element.78.now.wave, f32[64,32,128]{2,1,0:T(8,128)S(1)} %get-tuple-element.79.prev.wave_b, f32[64,32,128]{2,1,0:T(8,128)S(1)} %get-tuple-element.65.r2, ...), custom_call_target="tpu_custom_call" | custom-call | flops 10485760 | bytes 8388608 | tf_op jit(solution)/shard_map/pallas_call | solution.py:717
  93.7 1.0 shard_map.117
  94.7 0.1 collective-permute-start.12
  94.8 3.6 %collective-permute-start.13 = (f32[64,8,128]{2,1,0:T(8,128)S(1)}, f32[64,8,128]{2,1,0:T(8,128)S(1)}, u32[]{:S(2)}, u32[]{:S(2)}) collective-permute-start(f32[64,8,128]{2,1,0:T(8,128)S(1)} %get-tuple-element.86), channel_id=1, source_target_pairs={{1,0},{2,1},{3,2},{4,3},{5,4},{6,5},{7,6},{0,7},{9,8},{10,9},{11,1... | collective-permute-start | bytes 786440 | tf_op jit(solution)/shard_map/ppermute | solution.py:637
  98.3 2.3 %shard_map.118 = (f32[64,32,128]{2,1,0:T(8,128)S(1)}, f32[64,32,128]{2,1,0:T(8,128)S(1)}) custom-call(s32[8]{0:T(128)S(1)} %stack.63.spots, f32[64,32,128]{2,1,0:T(8,128)S(1)} %get-tuple-element.84.late, f32[64,32,128]{2,1,0:T(8,128)S(1)} %get-tuple-element.92.later, f32[64,32,128]{2,1,0:T(8,128)S(1)} %get-tuple-element.65.r2, bf16[256,256]{1,0:T(8,128)(2,1)S(1)} %copy-done, ...), custom_call_target="tpu_custom_call" | custom-call | flops 10485760 | bytes 8388608 | tf_op jit(solution)/shard_map/pallas_call | solution.py:729
  100.6 1.9 %collective-permute-done.12.late_lo = f32[64,8,128]{2,1,0:T(8,128)S(1)} collective-permute-done((f32[64,8,128]{2,1,0:T(8,128)S(1)}, f32[64,8,128]{2,1,0:T(8,128)S(1)}, u32[]{:S(2)}, u32[]{:S(2)}) %collective-permute-start.12) | collective-permute-done | bytes 262176 | tf_op jit(solution)/shard_map/ppermute | solution.py:637
  102.5 4.2 %shard_map.119 = (f32[64,32,128]{2,1,0:T(8,128)S(1)}, f32[64,32,128]{2,1,0:T(8,128)S(1)}, f32[64,32,128]{2,1,0:T(8,128)S(1)}, f32[32,8,128]{2,1,0:T(8,128)S(1)}, f32[32,8,128]{2,1,0:T(8,128)S(1)}) custom-call(s32[8]{0:T(128)S(1)} %stack.63.spots, f32[64,32,128]{2,1,0:T(8,128)S(1)} %get-tuple-element.84.late, ...), custom_call_target="tpu_custom_call" | custom-call | flops 20971520 | bytes 16777216 | tf_op jit(solution)/shard_map/pallas_call | solution.py:732
  106.7 0.3 collective-permute-start.14
  107.0 3.6 %collective-permute-start.15 = (f32[32,8,128]{2,1,0:T(8,128)S(1)}, f32[32,8,128]{2,1,0:T(8,128)S(1)}, u32[]{:S(2)}, u32[]{:S(2)}) collective-permute-start(f32[32,8,128]{2,1,0:T(8,128)S(1)} %get-tuple-element.97), channel_id=1, source_target_pairs={{1,0},{2,1},{3,2},{4,3},{5,4},{6,5},{7,6},{0,7},{9,8},{10,9},{11,1... | collective-permute-start | bytes 393224 | tf_op jit(solution)/shard_map/ppermute | solution.py:637
  110.6 2.4 %shard_map.120.total = f32[64,32,128]{2,1,0:T(8,128)S(1)} custom-call(s32[8]{0:T(128)S(1)} %stack.63.spots, f32[64,32,128]{2,1,0:T(8,128)S(1)} %get-tuple-element.99.late, f32[64,32,128]{2,1,0:T(8,128)S(1)} %get-tuple-element.100.later, f32[64,32,128]{2,1,0:T(8,128)S(1)} %get-tuple-element.65.r2, bf16[256,256]{1,0:T(8,128)(2,1)S(1)} %copy-done, ...), custom_call_target="tpu_custom_call" | custom-call | flops 10485760 | bytes 8388608 | tf_op jit(solution)/shard_map/pallas_call | solution.py:744
  113.0 0.8 shard_map.121
  113.8 4.3 %collective-permute-start.16 = (f32[8,32,128]{2,1,0:T(8,128)S(1)}, f32[8,32,128]{2,1,0:T(8,128)S(1)}, u32[]{:S(2)}, u32[]{:S(2)}) collective-permute-start(f32[8,32,128]{2,1,0:T(8,128)S(1)} %get-tuple-element.104), channel_id=1, source_target_pairs={{0,8},{8,0},{16,24},{24,16},{32,40},{40,32},{48,56},{56,48},{64,72... | collective-permute-start | bytes 393224 | tf_op jit(solution)/shard_map/ppermute | solution.py:753
  118.1 1.3 collective-permute-start.17
  119.4 0.3 collective-permute-start.18
  119.7 0.2 collective-permute-start.21
  119.9 0.3 collective-permute-start.24
  120.2 2.6 %collective-permute-start.20 = (f32[8,32,128]{2,1,0:T(8,128)S(1)}, f32[8,32,128]{2,1,0:T(8,128)S(1)}, u32[]{:S(2)}, u32[]{:S(2)}) collective-permute-start(f32[8,32,128]{2,1,0:T(8,128)S(1)} %get-tuple-element.107), channel_id=1, source_target_pairs={{0,32},{8,40},{16,48},{24,56},{32,0},{40,8},{48,16},{56,24},{64,96... | collective-permute-start | bytes 393224 | tf_op jit(solution)/shard_map/ppermute | solution.py:755
  122.9 1.6 %collective-permute-done.17.rest_2_ = f32[8,32,128]{2,1,0:T(8,128)S(1)} collective-permute-done((f32[8,32,128]{2,1,0:T(8,128)S(1)}, f32[8,32,128]{2,1,0:T(8,128)S(1)}, u32[]{:S(2)}, u32[]{:S(2)}) %collective-permute-start.17) | collective-permute-done | bytes 131104 | tf_op jit(solution)/shard_map/ppermute | solution.py:755
  124.4 1.4 collective-permute-start.23
  125.9 0.1 collective-permute-start.19
  125.9 1.6 %collective-permute-start.22 = (f32[8,32,128]{2,1,0:T(8,128)S(1)}, f32[8,32,128]{2,1,0:T(8,128)S(1)}, u32[]{:S(2)}, u32[]{:S(2)}) collective-permute-start(f32[8,32,128]{2,1,0:T(8,128)S(1)} %collective-permute-done.21), channel_id=1, source_target_pairs={{0,32},{8,40},{16,48},{24,56},{32,0},{40,8},{48,16},{56,24},{64,96... | collective-permute-start | bytes 393224 | tf_op jit(solution)/shard_map/ppermute | solution.py:755
  127.5 1.1 collective-permute-start.25
  128.6 0.1 collective-permute-done.23.rest_6_
  128.7 3.9 %collective-permute-done.19.rest_3_ = f32[8,32,128]{2,1,0:T(8,128)S(1)} collective-permute-done((f32[8,32,128]{2,1,0:T(8,128)S(1)}, f32[8,32,128]{2,1,0:T(8,128)S(1)}, u32[]{:S(2)}, u32[]{:S(2)}) %collective-permute-start.19) | collective-permute-done | bytes 131104 | tf_op jit(solution)/shard_map/ppermute | solution.py:755
  132.6 0.1 collective-permute-done.22.rest_5_
  132.6 1.8 %collective-permute-done.25.rest_7_ = f32[8,32,128]{2,1,0:T(8,128)S(1)} collective-permute-done((f32[8,32,128]{2,1,0:T(8,128)S(1)}, f32[8,32,128]{2,1,0:T(8,128)S(1)}, u32[]{:S(2)}, u32[]{:S(2)}) %collective-permute-start.25) | collective-permute-done | bytes 131104 | tf_op jit(solution)/shard_map/ppermute | solution.py:755
  134.4 1.0 shard_map.122
  135.5 1.0 collective-permute-start.26
  136.4 6.4 %collective-permute-done.26 = f32[2,8,32,128]{3,2,1,0:T(8,128)S(1)} collective-permute-done((f32[2,8,32,128]{3,2,1,0:T(8,128)S(1)}, f32[2,8,32,128]{3,2,1,0:T(8,128)S(1)}, u32[]{:S(2)}, u32[]{:S(2)}) %collective-permute-start.26) | collective-permute-done | bytes 262176 | tf_op jit(solution)/shard_map/ppermute | solution.py:758
  142.9 0.7 add_bitcast_fusion
  (48 shorter events, 0.1 us)
Async XLA Ops:
  0.0 13.6 %collective-permute-start = (f32[2,8,32,128]{3,2,1,0:T(8,128)}, f32[2,8,32,128]{3,2,1,0:T(8,128)S(1)}, u32[]{:S(2)}, u32[]{:S(2)}) collective-permute-start(f32[2,8,32,128]{3,2,1,0:T(8,128)} %bitcast.29), channel_id=1, source_target_pairs={{0,64},{8,72},{16,80},{24,88},{32,96},{40,104},{48,112},{56,120},{... | collective-permute-start | bytes 786440 | tf_op jit(solution)/shard_map/ppermute | solution.py:640
  3.6 10.6 %collective-permute-start.1 = (f32[2,8,32,128]{3,2,1,0:T(8,128)}, f32[2,8,32,128]{3,2,1,0:T(8,128)S(1)}, u32[]{:S(2)}, u32[]{:S(2)}) collective-permute-start(f32[2,8,32,128]{3,2,1,0:T(8,128)} %bitcast.30), channel_id=1, source_target_pairs={{0,8},{8,0},{16,24},{24,16},{32,40},{40,32},{48,56},{56,48},{64,72... | collective-permute-start | bytes 786440 | tf_op jit(solution)/shard_map/ppermute | solution.py:641
  8.3 5.7 %copy-start.17 = (s32[16,8]{0,1:T(8,128)S(1)}, s32[16,8]{0,1:T(8,128)}, u32[]{:S(2)}) copy-start(s32[16,8]{0,1:T(8,128)} %param.20) | copy-start | bytes 1540
  8.3 5.8 %copy-start.15 = (s32[1,256]{1,0:T(1,128)S(1)}, s32[1,256]{1,0:T(1,128)}, u32[]{:S(2)}) copy-start(s32[1,256]{1,0:T(1,128)} %param.18) | copy-start | bytes 3076
  8.4 6.9 %copy-start.9 = (f32[2,1,8,32,128]{4,3,2,1,0:T(8,128)S(1)}, f32[2,1,8,32,128]{4,3,2,1,0:T(8,128)}, u32[]{:S(2)}) copy-start(f32[2,1,8,32,128]{4,3,2,1,0:T(8,128)} %param.11) | copy-start | bytes 786436
  8.4 13.8 %copy-start.16 = (f32[1,4,256]{2,1,0:T(4,128)S(1)}, f32[1,4,256]{2,1,0:T(4,128)}, u32[]{:S(2)}) copy-start(f32[1,4,256]{2,1,0:T(4,128)} %param.19) | copy-start | bytes 12292
  8.4 60.3 %all-to-all-start = ((f32[8,8,144,128]{3,2,1,0:T(8,128)}), f32[8,8,144,128]{3,2,1,0:T(8,128)}, u32[]{:S(2)}, u32[]{:S(2)}) async-start(f32[8,8,144,128]{3,2,1,0:T(8,128)} %shard_map.109), calls=%async_computation | async-start | bytes 9437184 | tf_op jit(solution)/shard_map/all_to_all | solution.py:661
  13.6 1.6 %collective-permute-start.2 = (f32[2,8,32,128]{3,2,1,0:T(8,128)S(1)}, f32[2,8,32,128]{3,2,1,0:T(8,128)S(1)}, u32[]{:S(2)}, u32[]{:S(2)}) collective-permute-start(f32[2,8,32,128]{3,2,1,0:T(8,128)S(1)} %collective-permute-done.other), channel_id=1, source_target_pairs={{0,8},{8,0},{16,24},{24,16},{32,40},{40,32},{48,56},{56,48},{64,72... | collective-permute-start | bytes 786440 | tf_op jit(solution)/shard_map/ppermute | solution.py:642
  14.0 8.1 %copy-start.12 = (s32[2]{0:T(128)}, s32[2]{0:T(128)S(1)}, u32[]{:S(2)}) copy-start(s32[2]{0:T(128)S(1)} %pad_add_fusion.ids) | copy-start | bytes 28
  14.1 8.1 %copy-start.10 = (s32[16,8]{1,0:T(8,128)}, s32[16,8]{1,0:T(8,128)S(1)}, u32[]{:S(2)}) copy-start(s32[16,8]{1,0:T(8,128)S(1)} %copy.14.apertures) | copy-start | bytes 1540
  17.2 18.2 %collective-permute-start.3 = (f32[2,8,32,128]{3,2,1,0:T(8,128)}, f32[2,8,32,128]{3,2,1,0:T(8,128)}, u32[]{:S(2)}, u32[]{:S(2)}) collective-permute-start(f32[2,8,32,128]{3,2,1,0:T(8,128)} %get-tuple-element.60), channel_id=1, source_target_pairs={{0,16},{8,24},{16,32},{24,40},{32,48},{40,56},{48,0},{56,8},{64,80... | collective-permute-start | bytes 786440 | tf_op jit(solution)/shard_map/ppermute | solution.py:646
  18.5 16.9 %collective-permute-start.4 = (f32[2,8,32,128]{3,2,1,0:T(8,128)}, f32[2,8,32,128]{3,2,1,0:T(8,128)}, u32[]{:S(2)}, u32[]{:S(2)}) collective-permute-start(f32[2,8,32,128]{3,2,1,0:T(8,128)} %get-tuple-element.61), channel_id=1, source_target_pairs={{0,32},{8,40},{16,48},{24,56},{32,0},{40,8},{48,16},{56,24},{64,96... | collective-permute-start | bytes 786440 | tf_op jit(solution)/shard_map/ppermute | solution.py:646
  21.1 14.2 %collective-permute-start.5 = (f32[2,8,32,128]{3,2,1,0:T(8,128)}, f32[2,8,32,128]{3,2,1,0:T(8,128)}, u32[]{:S(2)}, u32[]{:S(2)}) collective-permute-start(f32[2,8,32,128]{3,2,1,0:T(8,128)} %get-tuple-element.62), channel_id=1, source_target_pairs={{0,48},{8,56},{16,0},{24,8},{32,16},{40,24},{48,32},{56,40},{64,11... | collective-permute-start | bytes 786440 | tf_op jit(solution)/shard_map/ppermute | solution.py:646
  22.2 13.2 %copy-start.11 = (s32[16,8]{1,0:T(8,128)S(1)}, s32[16,8]{1,0:T(8,128)}, u32[]{:S(2)}) copy-start(s32[16,8]{1,0:T(8,128)} %copy-done.10) | copy-start | bytes 1540
  22.2 13.2 %copy-start.13 = (s32[2]{0:T(128)S(1)}, s32[2]{0:T(128)}, u32[]{:S(2)}) copy-start(s32[2]{0:T(128)} %copy-done.12) | copy-start | bytes 28
  22.2 46.5 %copy-start = (bf16[256,256]{1,0:T(8,128)(2,1)S(1)}, bf16[256,256]{1,0:T(8,128)(2,1)}, u32[]{:S(2)}) copy-start(bf16[256,256]{1,0:T(8,128)(2,1)} %constant.94.clone.oper) | copy-start | bytes 393220
  22.2 46.5 %copy-start.14 = (f32[1,4]{1,0:T(1,128)S(1)}, f32[1,4]{1,0:T(1,128)}, u32[]{:S(2)}) copy-start(f32[1,4]{1,0:T(1,128)} %param.16) | copy-start | bytes 52
  27.4 1.2 copy-start.1
  28.6 1.0 copy-start.3
  29.6 1.0 copy-start.5
  30.6 1.0 copy-start.7
  37.5 38.9 %collective-permute-start.6 = (f32[64,8,128]{2,1,0:T(8,128)}, f32[64,8,128]{2,1,0:T(8,128)S(1)}, u32[]{:S(2)}, u32[]{:S(2)}) collective-permute-start(f32[64,8,128]{2,1,0:T(8,128)} %get-tuple-element.67), channel_id=1, source_target_pairs={{0,1},{1,2},{2,3},{3,4},{4,5},{5,6},{6,7},{7,0},{8,9},{9,10},{10,1... | collective-permute-start | bytes 786440 | tf_op jit(solution)/shard_map/ppermute | solution.py:637
  39.0 37.4 %collective-permute-start.7 = (f32[64,8,128]{2,1,0:T(8,128)}, f32[64,8,128]{2,1,0:T(8,128)S(1)}, u32[]{:S(2)}, u32[]{:S(2)}) collective-permute-start(f32[64,8,128]{2,1,0:T(8,128)} %get-tuple-element.68), channel_id=1, source_target_pairs={{1,0},{2,1},{3,2},{4,3},{5,4},{6,5},{7,6},{0,7},{9,8},{10,9},{11,1... | collective-permute-start | bytes 786440 | tf_op jit(solution)/shard_map/ppermute | solution.py:637
  72.8 9.6 %collective-permute-start.8 = (f32[64,8,128]{2,1,0:T(8,128)S(1)}, f32[64,8,128]{2,1,0:T(8,128)S(1)}, u32[]{:S(2)}, u32[]{:S(2)}) collective-permute-start(f32[64,8,128]{2,1,0:T(8,128)S(1)} %get-tuple-element.71), channel_id=1, source_target_pairs={{0,1},{1,2},{2,3},{3,4},{4,5},{5,6},{6,7},{7,0},{8,9},{9,10},{10,1... | collective-permute-start | bytes 786440 | tf_op jit(solution)/shard_map/ppermute | solution.py:637
  73.4 17.7 %copy-start.8 = (f32[64,32,128]{2,1,0:T(8,128)S(1)}, f32[64,32,128]{2,1,0:T(8,128)}, u32[]{:S(2)}) copy-start(f32[64,32,128]{2,1,0:T(8,128)} %copy-done.7) | copy-start | bytes 3145732
  73.4 9.0 %collective-permute-start.9 = (f32[64,8,128]{2,1,0:T(8,128)S(1)}, f32[64,8,128]{2,1,0:T(8,128)S(1)}, u32[]{:S(2)}, u32[]{:S(2)}) collective-permute-start(f32[64,8,128]{2,1,0:T(8,128)S(1)} %get-tuple-element.72), channel_id=1, source_target_pairs={{1,0},{2,1},{3,2},{4,3},{5,4},{6,5},{7,6},{0,7},{9,8},{10,9},{11,1... | collective-permute-start | bytes 786440 | tf_op jit(solution)/shard_map/ppermute | solution.py:637
  87.5 6.2 %collective-permute-start.10 = (f32[32,8,128]{2,1,0:T(8,128)S(1)}, f32[32,8,128]{2,1,0:T(8,128)S(1)}, u32[]{:S(2)}, u32[]{:S(2)}) collective-permute-start(f32[32,8,128]{2,1,0:T(8,128)S(1)} %get-tuple-element.75), channel_id=1, source_target_pairs={{0,1},{1,2},{2,3},{3,4},{4,5},{5,6},{6,7},{7,0},{8,9},{9,10},{10,1... | collective-permute-start | bytes 393224 | tf_op jit(solution)/shard_map/ppermute | solution.py:637
  87.6 6.1 %collective-permute-start.11 = (f32[32,8,128]{2,1,0:T(8,128)S(1)}, f32[32,8,128]{2,1,0:T(8,128)S(1)}, u32[]{:S(2)}, u32[]{:S(2)}) collective-permute-start(f32[32,8,128]{2,1,0:T(8,128)S(1)} %get-tuple-element.76), channel_id=1, source_target_pairs={{1,0},{2,1},{3,2},{4,3},{5,4},{6,5},{7,6},{0,7},{9,8},{10,9},{11,1... | collective-permute-start | bytes 393224 | tf_op jit(solution)/shard_map/ppermute | solution.py:637
  91.1 7.2 %copy-start.2 = (f32[64,48,128]{2,1,0:T(8,128)S(1)}, f32[64,48,128]{2,1,0:T(8,128)}, u32[]{:S(2)}) copy-start(f32[64,48,128]{2,1,0:T(8,128)} %copy-done.1) | copy-start | bytes 4718596
  94.7 7.8 %collective-permute-start.12 = (f32[64,8,128]{2,1,0:T(8,128)S(1)}, f32[64,8,128]{2,1,0:T(8,128)S(1)}, u32[]{:S(2)}, u32[]{:S(2)}) collective-permute-start(f32[64,8,128]{2,1,0:T(8,128)S(1)} %get-tuple-element.85), channel_id=1, source_target_pairs={{0,1},{1,2},{2,3},{3,4},{4,5},{5,6},{6,7},{7,0},{8,9},{9,10},{10,1... | collective-permute-start | bytes 786440 | tf_op jit(solution)/shard_map/ppermute | solution.py:637
  94.8 7.7 %collective-permute-start.13 = (f32[64,8,128]{2,1,0:T(8,128)S(1)}, f32[64,8,128]{2,1,0:T(8,128)S(1)}, u32[]{:S(2)}, u32[]{:S(2)}) collective-permute-start(f32[64,8,128]{2,1,0:T(8,128)S(1)} %get-tuple-element.86), channel_id=1, source_target_pairs={{1,0},{2,1},{3,2},{4,3},{5,4},{6,5},{7,6},{0,7},{9,8},{10,9},{11,1... | collective-permute-start | bytes 786440 | tf_op jit(solution)/shard_map/ppermute | solution.py:637
  98.3 4.2 %copy-start.6 = (f32[64,32,128]{2,1,0:T(8,128)S(1)}, f32[64,32,128]{2,1,0:T(8,128)}, u32[]{:S(2)}) copy-start(f32[64,32,128]{2,1,0:T(8,128)} %copy-done.5) | copy-start | bytes 3145732
  102.5 8.1 %copy-start.4 = (f32[64,32,128]{2,1,0:T(8,128)S(1)}, f32[64,32,128]{2,1,0:T(8,128)}, u32[]{:S(2)}) copy-start(f32[64,32,128]{2,1,0:T(8,128)} %copy-done.3) | copy-start | bytes 3145732
  106.7 6.2 %collective-permute-start.14 = (f32[32,8,128]{2,1,0:T(8,128)S(1)}, f32[32,8,128]{2,1,0:T(8,128)S(1)}, u32[]{:S(2)}, u32[]{:S(2)}) collective-permute-start(f32[32,8,128]{2,1,0:T(8,128)S(1)} %get-tuple-element.96), channel_id=1, source_target_pairs={{0,1},{1,2},{2,3},{3,4},{4,5},{5,6},{6,7},{7,0},{8,9},{9,10},{10,1... | collective-permute-start | bytes 393224 | tf_op jit(solution)/shard_map/ppermute | solution.py:637
  107.0 6.0 %collective-permute-start.15 = (f32[32,8,128]{2,1,0:T(8,128)S(1)}, f32[32,8,128]{2,1,0:T(8,128)S(1)}, u32[]{:S(2)}, u32[]{:S(2)}) collective-permute-start(f32[32,8,128]{2,1,0:T(8,128)S(1)} %get-tuple-element.97), channel_id=1, source_target_pairs={{1,0},{2,1},{3,2},{4,3},{5,4},{6,5},{7,6},{0,7},{9,8},{10,9},{11,1... | collective-permute-start | bytes 393224 | tf_op jit(solution)/shard_map/ppermute | solution.py:637
  113.8 6.4 %collective-permute-start.16 = (f32[8,32,128]{2,1,0:T(8,128)S(1)}, f32[8,32,128]{2,1,0:T(8,128)S(1)}, u32[]{:S(2)}, u32[]{:S(2)}) collective-permute-start(f32[8,32,128]{2,1,0:T(8,128)S(1)} %get-tuple-element.104), channel_id=1, source_target_pairs={{0,8},{8,0},{16,24},{24,16},{32,40},{40,32},{48,56},{56,48},{64,72... | collective-permute-start | bytes 393224 | tf_op jit(solution)/shard_map/ppermute | solution.py:753
  118.1 6.4 %collective-permute-start.17 = (f32[8,32,128]{2,1,0:T(8,128)S(1)}, f32[8,32,128]{2,1,0:T(8,128)S(1)}, u32[]{:S(2)}, u32[]{:S(2)}) collective-permute-start(f32[8,32,128]{2,1,0:T(8,128)S(1)} %get-tuple-element.105), channel_id=1, source_target_pairs={{0,16},{8,24},{16,32},{24,40},{32,48},{40,56},{48,0},{56,8},{64,80... | collective-permute-start | bytes 393224 | tf_op jit(solution)/shard_map/ppermute | solution.py:755
  119.4 6.5 %collective-permute-start.18 = (f32[8,32,128]{2,1,0:T(8,128)S(1)}, f32[8,32,128]{2,1,0:T(8,128)S(1)}, u32[]{:S(2)}, u32[]{:S(2)}) collective-permute-start(f32[8,32,128]{2,1,0:T(8,128)S(1)} %get-tuple-element.106), channel_id=1, source_target_pairs={{0,8},{8,0},{16,24},{24,16},{32,40},{40,32},{48,56},{56,48},{64,72... | collective-permute-start | bytes 393224 | tf_op jit(solution)/shard_map/ppermute | solution.py:753
  119.7 6.2 %collective-permute-start.21 = (f32[8,32,128]{2,1,0:T(8,128)S(1)}, f32[8,32,128]{2,1,0:T(8,128)S(1)}, u32[]{:S(2)}, u32[]{:S(2)}) collective-permute-start(f32[8,32,128]{2,1,0:T(8,128)S(1)} %get-tuple-element.108), channel_id=1, source_target_pairs={{0,8},{8,0},{16,24},{24,16},{32,40},{40,32},{48,56},{56,48},{64,72... | collective-permute-start | bytes 393224 | tf_op jit(solution)/shard_map/ppermute | solution.py:753
  119.9 7.6 %collective-permute-start.24 = (f32[8,32,128]{2,1,0:T(8,128)S(1)}, f32[8,32,128]{2,1,0:T(8,128)S(1)}, u32[]{:S(2)}, u32[]{:S(2)}) collective-permute-start(f32[8,32,128]{2,1,0:T(8,128)S(1)} %get-tuple-element.110), channel_id=1, source_target_pairs={{0,8},{8,0},{16,24},{24,16},{32,40},{40,32},{48,56},{56,48},{64,72... | collective-permute-start | bytes 393224 | tf_op jit(solution)/shard_map/ppermute | solution.py:753
  120.2 8.4 %collective-permute-start.20 = (f32[8,32,128]{2,1,0:T(8,128)S(1)}, f32[8,32,128]{2,1,0:T(8,128)S(1)}, u32[]{:S(2)}, u32[]{:S(2)}) collective-permute-start(f32[8,32,128]{2,1,0:T(8,128)S(1)} %get-tuple-element.107), channel_id=1, source_target_pairs={{0,32},{8,40},{16,48},{24,56},{32,0},{40,8},{48,16},{56,24},{64,96... | collective-permute-start | bytes 393224 | tf_op jit(solution)/shard_map/ppermute | solution.py:755
  124.4 4.2 %collective-permute-start.23 = (f32[8,32,128]{2,1,0:T(8,128)S(1)}, f32[8,32,128]{2,1,0:T(8,128)S(1)}, u32[]{:S(2)}, u32[]{:S(2)}) collective-permute-start(f32[8,32,128]{2,1,0:T(8,128)S(1)} %get-tuple-element.109), channel_id=1, source_target_pairs={{0,48},{8,56},{16,0},{24,8},{32,16},{40,24},{48,32},{56,40},{64,11... | collective-permute-start | bytes 393224 | tf_op jit(solution)/shard_map/ppermute | solution.py:755
  125.9 6.7 %collective-permute-start.19 = (f32[8,32,128]{2,1,0:T(8,128)S(1)}, f32[8,32,128]{2,1,0:T(8,128)S(1)}, u32[]{:S(2)}, u32[]{:S(2)}) collective-permute-start(f32[8,32,128]{2,1,0:T(8,128)S(1)} %collective-permute-done.18), channel_id=1, source_target_pairs={{0,16},{8,24},{16,32},{24,40},{32,48},{40,56},{48,0},{56,8},{64,80... | collective-permute-start | bytes 393224 | tf_op jit(solution)/shard_map/ppermute | solution.py:755
  125.9 6.7 %collective-permute-start.22 = (f32[8,32,128]{2,1,0:T(8,128)S(1)}, f32[8,32,128]{2,1,0:T(8,128)S(1)}, u32[]{:S(2)}, u32[]{:S(2)}) collective-permute-start(f32[8,32,128]{2,1,0:T(8,128)S(1)} %collective-permute-done.21), channel_id=1, source_target_pairs={{0,32},{8,40},{16,48},{24,56},{32,0},{40,8},{48,16},{56,24},{64,96... | collective-permute-start | bytes 393224 | tf_op jit(solution)/shard_map/ppermute | solution.py:755
  127.5 6.9 %collective-permute-start.25 = (f32[8,32,128]{2,1,0:T(8,128)S(1)}, f32[8,32,128]{2,1,0:T(8,128)S(1)}, u32[]{:S(2)}, u32[]{:S(2)}) collective-permute-start(f32[8,32,128]{2,1,0:T(8,128)S(1)} %collective-permute-done.24), channel_id=1, source_target_pairs={{0,48},{8,56},{16,0},{24,8},{32,16},{40,24},{48,32},{56,40},{64,11... | collective-permute-start | bytes 393224 | tf_op jit(solution)/shard_map/ppermute | solution.py:755
  135.5 7.4 %collective-permute-start.26 = (f32[2,8,32,128]{3,2,1,0:T(8,128)S(1)}, f32[2,8,32,128]{3,2,1,0:T(8,128)S(1)}, u32[]{:S(2)}, u32[]{:S(2)}) collective-permute-start(f32[2,8,32,128]{3,2,1,0:T(8,128)S(1)} %get-tuple-element.112), channel_id=1, source_target_pairs={{0,64},{8,72},{16,80},{24,88},{32,96},{40,104},{48,112},{56,120},{... | collective-permute-start | bytes 786440 | tf_op jit(solution)/shard_map/ppermute | solution.py:758

commit v9 on v8

--- a/solution.py
+++ b/solution.py
@@ -197,24 +197,23 @@
 NOW, PREV, EDGES, HALF, TURNED = 0, 32, 64, 72, 144
 
 
-def unpack(turned, base, sems, now, edge, prev, extra):
+def unpack(turned, base, sems, now, edge, prev):
     copies = []
-    for n, (off, rows, dst) in enumerate(
-        ((NOW, NYL, now), (EDGES, 8, edge), (PREV, NYL, prev), (NOW, NYL, extra))
-    ):
+    for n, (off, rows, dst) in enumerate(((NOW, NYL, now), (EDGES, 8, edge), (PREV, NYL, prev))):
         copies.append(pltpu.make_async_copy(turned.at[:, base + off : base + off + rows, :], dst, sems.at[n]))
-    for c in copies:
-        c.start()
+        copies[n].start()
     return copies
 
 
 def first_kernel(spots, wavelet, turned, r2, oper, lap, new, send_lo, send_hi, now, edge, ext, depth, prev, sems):
-    copies = unpack(turned, 0, sems, ext.at[OWN_X, OWN_Y, :], edge, prev, now)
+    copies = unpack(turned, 0, sems, now, edge, prev)
     clear_ends(ext)
-    for c in copies[:3]:
+    copies[0].wait()
+    ext[OWN_X, OWN_Y, :] = now[...]
+    apply_depth(ext, oper, depth)
+    for c in copies[1:]:
         c.wait()
     fill_ring(ext, edge)
-    apply_depth(ext, oper, depth)
 
     def emit(x, g, xi, j, value):
         lap[x, tile(j), :] = value
@@ -223,7 +222,6 @@
     laplace(ext, depth, OWN, emit)
     add_source(spots, wavelet[0], new, 0, 0)
     send_tiles(send_lo, send_hi, new)
-    copies[3].wait()
 
 
 def spread_edges(edge, lo, hi):
@@ -282,9 +280,9 @@
 
 
 def late_kernel(spots, turned, r2, r2_lo, r2_hi, oper, mu, late, edge, ext, depth, later, sems):
-    copies = unpack(turned, HALF, sems, late, edge, later, ext.at[OWN_X, OWN_Y, :])
+    copies = unpack(turned, HALF, sems, late, edge, later)
     clear_ends(ext)
-    for c in copies:
+    for c in copies[:2]:
         c.wait()
 
     def weigh(x):
@@ -294,6 +292,7 @@
 
     planes(weigh)
     apply_depth(ext, oper, depth)
+    copies[2].wait()
 
     def emit(x, g, xi, j, value):
         mu[x, tile(j), :] = 2.0 * late[x, tile(j), :] + value - later[x, tile(j), :]
@@ -427,14 +426,14 @@
 
 
 def last_end_kernel(ids, spots, halo_lo, halo_hi, lap, total, *rest):
-    outs, strip = rest[:8], rest[8]
+    outs, others, strip = rest[:4], rest[4], rest[5]
     fill_strip(strip, spots, halo_lo, halo_hi)
     _, y, core = split_shot(ids[0])
     for k in range(4):
         for side in range(2):
             cls = 2 * lax.rem(y + k, 4) + (core if side == 0 else 1 - core)
             g = lax.rem(cls - spots[0] + GROUP, GROUP)
-            out = outs[2 * k + side]
+            out = outs[k] if side == 0 else others.at[k]
             for xi in range(GROUP):
                 x = g * GROUP + xi
                 for j in OWN:
@@ -560,32 +559,27 @@
     lax.fori_loop(0, cells.shape[0], body, 0)
 
 
-def bins_kernel(ids, apertures, *rest):
-    recv, (keep, give) = rest[:8], rest[8:]
+def bins_kernel(give, ids, apertures, *rest):
+    recv, out = rest[:8], rest[8]
     mine, y, core = split_shot(ids[0])
     which = lax.rem(ids[0], 8)
-    zeros = jnp.zeros((GROUP, NYL, NZ), F32)
-    for i in range(2):
-        keep[i] = zeros
-        give[i] = zeros
-    for t in range(GROUP):
-        shot = 8 * mine + 2 * lax.rem(y - t // 2 + 4, 4) + (core if t % 2 == 0 else 1 - core)
+    out[...] = jnp.zeros((2, GROUP, NYL, NZ), F32)
+    for t in range(8):
+        shot = 8 * mine + 2 * lax.rem(y - t % 4 + 4, 4) + (core if t < 4 else 1 - core)
         m = slot_of(apertures[shot, 0], which)
         i = m // 2
-
-        @pl.when(lax.rem(m, 2) == mine)
+        block = recv[t].at[0] if t == 4 else recv[t]
+
+        @pl.when((lax.rem(m, 2) != mine) if give else (lax.rem(m, 2) == mine))
         def _():
-            keep[i] = keep[i] + recv[t][...]
-
-        @pl.when(lax.rem(m, 2) != mine)
-        def _():
-            give[i] = give[i] + recv[t][...]
+            out[i] = out[i] + block[...]
 
 
 FIELD = jax.ShapeDtypeStruct((NX, NYL, NZ), F32)
 WIDE_FIELD = jax.ShapeDtypeStruct((NX, WIDE, NZ), F32)
 EDGE = jax.ShapeDtypeStruct((NX // 2, 8, NZ), F32)
 TILE = jax.ShapeDtypeStruct((NX, 8, NZ), F32)
+BLOCKS = jax.ShapeDtypeStruct((4, GROUP, NYL, NZ), F32)
 BLOCK = jax.ShapeDtypeStruct((GROUP, NYL, NZ), F32)
 PAIR = jax.ShapeDtypeStruct((2, GROUP, NYL, NZ), F32)
 EXT = pltpu.VMEM((NX + 2 * PAD, ROWS, NZ), F32)
@@ -691,7 +685,7 @@
         first_kernel,
         [SMEM, SMEM, ANY, VMEM, VMEM],
         [FIELD, FIELD, TILE, TILE, FIELD, TILE],
-        [EXT, DEPTH, FIELD_VMEM, pltpu.SemaphoreType.DMA((4,))],
+        [EXT, DEPTH, FIELD_VMEM, pltpu.SemaphoreType.DMA((3,))],
         flops=10 << 20,
         moved=8 << 20,
     )(spots, amounts, turned, r2, oper)
@@ -700,7 +694,7 @@
         late_kernel,
         [SMEM, ANY] + [VMEM] * 4,
         [FIELD, FIELD, TILE],
-        [EXT, DEPTH, FIELD_VMEM, pltpu.SemaphoreType.DMA((4,))],
+        [EXT, DEPTH, FIELD_VMEM, pltpu.SemaphoreType.DMA((3,))],
         flops=10 << 20,
         moved=6 << 20,
     )(spots, turned, r2, *r2_halo, oper)
@@ -744,17 +738,17 @@
     (total,) = call(last_kernel, [SMEM] + [VMEM] * 9, [FIELD], [EXT, DEPTH], flops=MAIN, moved=8 << 20)(
         spots, mu2, mu3, r2, oper, count, data1, u1, lap0, total
     )
-    sent = call(last_end_kernel, [SMEM] * 2 + [VMEM] * 4, [BLOCK] * 8, [STRIP], flops=1 << 20, moved=3 << 20)(
-        ids, spots, *mu2_halo, lap0, total
-    )
-
-    recv = []
-    for k in range(4):
-        mine, others = sent[2 * k], lax.ppermute(sent[2 * k + 1], "shot", chip)
-        if k:
-            mine, others = lax.ppermute(mine, "shot", along(k)), lax.ppermute(others, "shot", along(k))
-        recv += [mine, others]
-    keep, give = call(bins_kernel, [SMEM] * 2 + [VMEM] * 8, [PAIR, PAIR], moved=2 << 20)(ids, apertures, *recv)
+    *sent, others = call(
+        last_end_kernel, [SMEM] * 2 + [VMEM] * 4, [BLOCK] * 4 + [BLOCKS], [STRIP], flops=1 << 20, moved=3 << 20
+    )(ids, spots, *mu2_halo, lap0, total)
+
+    own = [sent[0]] + [lax.ppermute(sent[k], "shot", along(k)) for k in (1, 2, 3)]
+    others = lax.ppermute(others, "shot", chip)
+    recv = own + [others] + [lax.ppermute(others[k], "shot", along(k)) for k in (1, 2, 3)]
+    give, keep = (
+        call(functools.partial(bins_kernel, side), [SMEM] * 2 + [VMEM] * 8, [PAIR], moved=1 << 20)(ids, apertures, *recv)[0]
+        for side in (True, False)
+    )
     result = keep + lax.ppermute(give, "shot", across)
     return result[:, None]
 

time: 146 us -> 145 us (level); the launches traced: 144 us -> 145 us
  waiting for transfers between devices: 46.1 us -> 49 us
  starting transfers between devices: 47.7 us -> 45.9 us
    ppermute x10 -> x7, starting transfers between devices: 13.2 us -> 11.5 us  [the longest x3 4.98 us: per_device(): lax.ppermute(sent[k], 'shot', along(k))]
    ppermute x10 -> x7, waiting for transfers between devices: 7.43 us -> 9.02 us  [the longest x3 5.98 us: per_device(): lax.ppermute(others[k], 'shot', along(k))]
  transfers between devices with their start and end apart: 28 -> 25, of which waited for: 10 -> 9; matrix products, arithmetic and copies ran while one was open for 1% -> 1% of each run, Pallas kernels for 20% -> 20%
where the time goes in v9:
time: 145 us
  waiting for transfers between devices  49 us (34%)
  starting transfers between devices  45.9 us (32%)
  Pallas kernels  40.3 us (28%)
  local copies, waits for them, and re-layouts  5.68 us (4%)
  between operations  2.78 us (2%)
    all_to_all x1, waiting for transfers between devices, per_device(): lax.all_to_all(packed, 'sub', 0, 0, tiled=True).reshape(NX, TURNED, NZ)  27.6 us
    ppermute x10, starting transfers between devices, edges(): return (lax.ppermute(hi, 'sub', up), lax.ppermute(lo, 'sub', down))  18.4 us
    ppermute x1, waiting for transfers between devices, per_device(): result = keep + lax.ppermute(give, 'shot', across)  7.06 us
    ppermute x3, waiting for transfers between devices, per_device(): lax.ppermute(others[k], 'shot', along(k))  5.98 us
    all_to_all x1, starting transfers between devices, per_device(): lax.all_to_all(packed, 'sub', 0, 0, tiled=True).reshape(NX, TURNED, NZ)  5.21 us
    pallas_call x1, Pallas kernels, per_device(): call(receivers_kernel, [SMEM] * 3, [WIDE_FIELD, WIDE_FIELD] + [FIELD] * 3...  5.17 us
    pallas_call x1, Pallas kernels, per_device(): call(middle_kernel, [SMEM, SMEM] + [VMEM] * 9, [FIELD] * 4 + [EDGE] * 2,...  5.04 us
    ppermute x3, starting transfers between devices, per_device(): lax.ppermute(blocks[k], 'shot', along(k))  4.99 us
  transfers between devices with their start and end apart: 25, of which 9 were waited for; matrix products, arithmetic and copies ran while one was open for 1% of the time, Pallas kernels for 20%

profile of v9, /device:TPU:1, one launch (start us, length us, event | category | flops | bytes accessed | tf_op | source)
XLA Modules:
  0.0 144.5 jit_solution(8606501657375637380)
XLA Ops:
  0.0 3.6 %collective-permute-start = (f32[2,8,32,128]{3,2,1,0:T(8,128)}, f32[2,8,32,128]{3,2,1,0:T(8,128)S(1)}, u32[]{:S(2)}, u32[]{:S(2)}) collective-permute-start(f32[2,8,32,128]{3,2,1,0:T(8,128)} %bitcast.35), channel_id=1, source_target_pairs={{0,64},{8,72},{16,80},{24,88},{32,96},{40,104},{48,112},{56,120},{... | collective-permute-start | bytes 786440 | tf_op jit(solution)/shard_map/ppermute | solution.py:634
  3.6 1.0 collective-permute-start.1
  4.5 3.7 %shard_map.109 = f32[8,8,144,128]{3,2,1,0:T(8,128)} custom-call(f32[8,256,128]{2,1,0:T(8,128)} %bitcast.44, f32[8,256,128]{2,1,0:T(8,128)} %bitcast.45, f32[8,256,128]{2,1,0:T(8,128)} %bitcast.46, f32[8,256,128]{2,1,0:T(8,128)} %bitcast.47), custom_call_target="tpu_custom_call" | custom-call | bytes 9437184 | tf_op jit(solution)/shard_map/pallas_call | solution.py:642
  8.3 0.0 copy-start.17
  8.3 0.0 copy-start.15
  8.3 0.0 copy-start.9
  8.3 0.0 copy-start.16
  8.3 5.2 %all-to-all-start = ((f32[8,8,144,128]{3,2,1,0:T(8,128)}), f32[8,8,144,128]{3,2,1,0:T(8,128)}, u32[]{:S(2)}, u32[]{:S(2)}) async-start(f32[8,8,144,128]{3,2,1,0:T(8,128)} %shard_map.109), calls=%async_computation | async-start | bytes 9437184 | tf_op jit(solution)/shard_map/all_to_all | solution.py:655
  13.5 0.0 collective-permute-done.other
  13.5 0.4 collective-permute-start.2
  13.9 0.1 pad_add_fusion.ids
  14.0 0.1 copy.14.apertures
  14.1 1.1 collective-permute-done.2.other_c
  15.1 1.9 %shard_map.110 = (f32[2,8,32,128]{3,2,1,0:T(8,128)S(1)}, f32[2,8,32,128]{3,2,1,0:T(8,128)}, f32[2,8,32,128]{3,2,1,0:T(8,128)}, f32[2,8,32,128]{3,2,1,0:T(8,128)}) custom-call(s32[2]{0:T(128)S(1)} %pad_add_fusion.ids, s32[16,8]{1,0:T(8,128)S(1)} %copy.14.apertures, f32[2,8,32,128]{3,2,1,0:T(8,128)S(1)} %bitcast.37, ...), custom_call_target="tpu_custom_call" | custom-call | bytes 2097152 | tf_op jit(solution)/shard_map/pallas_call | solution.py:637
  17.1 1.3 collective-permute-start.3
  18.4 2.6 %collective-permute-start.4 = (f32[2,8,32,128]{3,2,1,0:T(8,128)}, f32[2,8,32,128]{3,2,1,0:T(8,128)}, u32[]{:S(2)}, u32[]{:S(2)}) collective-permute-start(f32[2,8,32,128]{3,2,1,0:T(8,128)} %get-tuple-element.56), channel_id=1, source_target_pairs={{0,32},{8,40},{16,48},{24,56},{32,0},{40,8},{48,16},{56,24},{64,96... | collective-permute-start | bytes 786440 | tf_op jit(solution)/shard_map/ppermute | solution.py:640
  21.0 1.1 collective-permute-start.5
  22.1 0.0 copy-start
  22.1 0.0 copy-start.14
  22.1 5.2 %shard_map.112 = (f32[64,48,128]{2,1,0:T(8,128)S(1)}, f32[64,48,128]{2,1,0:T(8,128)S(1)}, f32[64,32,128]{2,1,0:T(8,128)S(1)}, f32[64,32,128]{2,1,0:T(8,128)S(1)}, f32[64,32,128]{2,1,0:T(8,128)S(1)}) custom-call(s32[256]{0:T(256)S(1)} %bitcast.42, s32[256]{0:T(256)S(1)} %fusion.lines, f32[4,256]{1,0:T(4,128)S(1)} %bitcast.43), custom_call_target="tpu_custom_call" | custom-call | flops 1099511627776 | bytes 6291456 | tf_op jit(solution)/shard_map/pallas_call | solution.py:679
  27.3 1.1 copy-done.1
  28.5 1.0 copy-done.3
  29.4 1.0 copy-done.5
  30.5 1.0 copy-done.7
  32.2 1.3 constant_dynamic-slice_fusion
  35.2 0.1 stack.63.spots
  35.3 2.1 %shard_map.111 = (f32[64,32,128]{2,1,0:T(8,128)S(1)}, f32[64,8,128]{2,1,0:T(8,128)}, f32[64,8,128]{2,1,0:T(8,128)}) custom-call(s32[2]{0:T(128)S(1)} %copy-done.13, s32[16,8]{1,0:T(8,128)S(1)} %copy-done.11, f32[2,8,32,128]{3,2,1,0:T(8,128)S(1)} %get-tuple-element.54.r0, f32[2,8,32,128]{3,2,1,0:T(8,128)} %collective-permute-done.3.r1, ...), custom_call_target="tpu_custom_call" | custom-call | bytes 2097152 | tf_op jit(solution)/shard_map/pallas_call | solution.py:656
  37.4 1.6 %collective-permute-start.6 = (f32[64,8,128]{2,1,0:T(8,128)}, f32[64,8,128]{2,1,0:T(8,128)S(1)}, u32[]{:S(2)}, u32[]{:S(2)}) collective-permute-start(f32[64,8,128]{2,1,0:T(8,128)} %get-tuple-element.62), channel_id=1, source_target_pairs={{0,1},{1,2},{2,3},{3,4},{4,5},{5,6},{6,7},{7,0},{8,9},{9,10},{10,1... | collective-permute-start | bytes 786440 | tf_op jit(solution)/shard_map/ppermute | solution.py:631
  39.1 2.0 %collective-permute-start.7 = (f32[64,8,128]{2,1,0:T(8,128)}, f32[64,8,128]{2,1,0:T(8,128)S(1)}, u32[]{:S(2)}, u32[]{:S(2)}) collective-permute-start(f32[64,8,128]{2,1,0:T(8,128)} %get-tuple-element.63), channel_id=1, source_target_pairs={{1,0},{2,1},{3,2},{4,3},{5,4},{6,5},{7,6},{0,7},{9,8},{10,9},{11,1... | collective-permute-start | bytes 786440 | tf_op jit(solution)/shard_map/ppermute | solution.py:631
  41.1 27.6 %all-to-all-done = f32[8,8,144,128]{3,2,1,0:T(8,128)} async-done(((f32[8,8,144,128]{3,2,1,0:T(8,128)}), f32[8,8,144,128]{3,2,1,0:T(8,128)}, u32[]{:S(2)}, u32[]{:S(2)}) %all-to-all-start) | async-done | bytes 4718624 | tf_op jit(solution)/shard_map/all_to_all | solution.py:655
  68.7 3.7 %shard_map.113 = (f32[64,32,128]{2,1,0:T(8,128)S(1)}, f32[64,32,128]{2,1,0:T(8,128)S(1)}, f32[64,8,128]{2,1,0:T(8,128)S(1)}, f32[64,8,128]{2,1,0:T(8,128)S(1)}, ...) custom-call(s32[8]{0:T(128)S(1)} %stack.63.spots, f32[4]{0:T(128)S(1)} %bitcast.38, ...), custom_call_target="tpu_custom_call" | custom-call | flops 10485760 | bytes 8388608 | tf_op jit(solution)/shard_map/pallas_call | solution.py:684
  72.3 0.6 collective-permute-start.8
  72.9 3.0 %collective-permute-start.9 = (f32[64,8,128]{2,1,0:T(8,128)S(1)}, f32[64,8,128]{2,1,0:T(8,128)S(1)}, u32[]{:S(2)}, u32[]{:S(2)}) collective-permute-start(f32[64,8,128]{2,1,0:T(8,128)S(1)} %get-tuple-element.67), channel_id=1, source_target_pairs={{1,0},{2,1},{3,2},{4,3},{5,4},{6,5},{7,6},{0,7},{9,8},{10,9},{11,1... | collective-permute-start | bytes 786440 | tf_op jit(solution)/shard_map/ppermute | solution.py:631
  76.0 3.6 %shard_map.114 = (f32[64,32,128]{2,1,0:T(8,128)S(1)}, f32[64,32,128]{2,1,0:T(8,128)S(1)}, f32[64,8,128]{2,1,0:T(8,128)S(1)}) custom-call(s32[8]{0:T(128)S(1)} %stack.63.spots, f32[64,144,128]{2,1,0:T(8,128)} %bitcast.17.turned, f32[64,32,128]{2,1,0:T(8,128)S(1)} %get-tuple-element.60.r2, f32[64,8,128]{2,1,0:T(8,128)S(1)} %collective-permute-done.6.r2_lo, ...), custom_call_target="tpu_custom_call" | custom-call | flops 10485760 | bytes 6291456 | tf_op jit(solution)/shard_map/pallas_call | solution.py:693
  79.6 2.3 %collective-permute-done.8.now_lo = f32[64,8,128]{2,1,0:T(8,128)S(1)} collective-permute-done((f32[64,8,128]{2,1,0:T(8,128)S(1)}, f32[64,8,128]{2,1,0:T(8,128)S(1)}, u32[]{:S(2)}, u32[]{:S(2)}) %collective-permute-start.8) | collective-permute-done | bytes 262176 | tf_op jit(solution)/shard_map/ppermute | solution.py:631
  82.0 5.0 %shard_map.115 = (f32[64,32,128]{2,1,0:T(8,128)S(1)}, f32[64,32,128]{2,1,0:T(8,128)S(1)}, f32[64,32,128]{2,1,0:T(8,128)S(1)}, f32[64,32,128]{2,1,0:T(8,128)S(1)}...) custom-call(s32[8]{0:T(128)S(1)} %stack.63.spots, f32[4]{0:T(128)S(1)} %bitcast.39, ...), custom_call_target="tpu_custom_call" | custom-call | flops 20971520 | bytes 12582912 | tf_op jit(solution)/shard_map/pallas_call | solution.py:702
  87.0 0.1 collective-permute-start.10
  87.1 3.6 %collective-permute-start.11 = (f32[32,8,128]{2,1,0:T(8,128)S(1)}, f32[32,8,128]{2,1,0:T(8,128)S(1)}, u32[]{:S(2)}, u32[]{:S(2)}) collective-permute-start(f32[32,8,128]{2,1,0:T(8,128)S(1)} %get-tuple-element.71), channel_id=1, source_target_pairs={{1,0},{2,1},{3,2},{4,3},{5,4},{6,5},{7,6},{0,7},{9,8},{10,9},{11,1... | collective-permute-start | bytes 393224 | tf_op jit(solution)/shard_map/ppermute | solution.py:631
  90.7 2.5 %shard_map.116 = (f32[64,32,128]{2,1,0:T(8,128)S(1)}, f32[64,32,128]{2,1,0:T(8,128)S(1)}) custom-call(s32[8]{0:T(128)S(1)} %stack.63.spots, f32[4]{0:T(128)S(1)} %bitcast.40, f32[64,32,128]{2,1,0:T(8,128)S(1)} %get-tuple-element.73.now.wave, f32[64,32,128]{2,1,0:T(8,128)S(1)} %get-tuple-element.74.prev.wave_b, f32[64,32,128]{2,1,0:T(8,128)S(1)} %get-tuple-element.60.r2, ...), custom_call_target="tpu_custom_call" | custom-call | flops 10485760 | bytes 8388608 | tf_op jit(solution)/shard_map/pallas_call | solution.py:711
  93.2 1.0 shard_map.117
  94.2 0.1 collective-permute-start.12
  94.3 3.6 %collective-permute-start.13 = (f32[64,8,128]{2,1,0:T(8,128)S(1)}, f32[64,8,128]{2,1,0:T(8,128)S(1)}, u32[]{:S(2)}, u32[]{:S(2)}) collective-permute-start(f32[64,8,128]{2,1,0:T(8,128)S(1)} %get-tuple-element.81), channel_id=1, source_target_pairs={{1,0},{2,1},{3,2},{4,3},{5,4},{6,5},{7,6},{0,7},{9,8},{10,9},{11,1... | collective-permute-start | bytes 786440 | tf_op jit(solution)/shard_map/ppermute | solution.py:631
  97.9 2.3 %shard_map.118 = (f32[64,32,128]{2,1,0:T(8,128)S(1)}, f32[64,32,128]{2,1,0:T(8,128)S(1)}) custom-call(s32[8]{0:T(128)S(1)} %stack.63.spots, f32[64,32,128]{2,1,0:T(8,128)S(1)} %get-tuple-element.79.late, f32[64,32,128]{2,1,0:T(8,128)S(1)} %get-tuple-element.87.later, f32[64,32,128]{2,1,0:T(8,128)S(1)} %get-tuple-element.60.r2, bf16[256,256]{1,0:T(8,128)(2,1)S(1)} %copy-done, ...), custom_call_target="tpu_custom_call" | custom-call | flops 10485760 | bytes 8388608 | tf_op jit(solution)/shard_map/pallas_call | solution.py:723
  100.2 1.9 %collective-permute-done.12.late_lo = f32[64,8,128]{2,1,0:T(8,128)S(1)} collective-permute-done((f32[64,8,128]{2,1,0:T(8,128)S(1)}, f32[64,8,128]{2,1,0:T(8,128)S(1)}, u32[]{:S(2)}, u32[]{:S(2)}) %collective-permute-start.12) | collective-permute-done | bytes 262176 | tf_op jit(solution)/shard_map/ppermute | solution.py:631
  102.0 4.2 %shard_map.119 = (f32[64,32,128]{2,1,0:T(8,128)S(1)}, f32[64,32,128]{2,1,0:T(8,128)S(1)}, f32[64,32,128]{2,1,0:T(8,128)S(1)}, f32[32,8,128]{2,1,0:T(8,128)S(1)}, f32[32,8,128]{2,1,0:T(8,128)S(1)}) custom-call(s32[8]{0:T(128)S(1)} %stack.63.spots, f32[64,32,128]{2,1,0:T(8,128)S(1)} %get-tuple-element.79.late, ...), custom_call_target="tpu_custom_call" | custom-call | flops 20971520 | bytes 16777216 | tf_op jit(solution)/shard_map/pallas_call | solution.py:726
  106.3 0.3 collective-permute-start.14
  106.5 3.6 %collective-permute-start.15 = (f32[32,8,128]{2,1,0:T(8,128)S(1)}, f32[32,8,128]{2,1,0:T(8,128)S(1)}, u32[]{:S(2)}, u32[]{:S(2)}) collective-permute-start(f32[32,8,128]{2,1,0:T(8,128)S(1)} %get-tuple-element.92), channel_id=1, source_target_pairs={{1,0},{2,1},{3,2},{4,3},{5,4},{6,5},{7,6},{0,7},{9,8},{10,9},{11,1... | collective-permute-start | bytes 393224 | tf_op jit(solution)/shard_map/ppermute | solution.py:631
  110.1 2.4 %shard_map.120.total = f32[64,32,128]{2,1,0:T(8,128)S(1)} custom-call(s32[8]{0:T(128)S(1)} %stack.63.spots, f32[64,32,128]{2,1,0:T(8,128)S(1)} %get-tuple-element.94.late, f32[64,32,128]{2,1,0:T(8,128)S(1)} %get-tuple-element.95.later, f32[64,32,128]{2,1,0:T(8,128)S(1)} %get-tuple-element.60.r2, bf16[256,256]{1,0:T(8,128)(2,1)S(1)} %copy-done, ...), custom_call_target="tpu_custom_call" | custom-call | flops 10485760 | bytes 8388608 | tf_op jit(solution)/shard_map/pallas_call | solution.py:738
  112.5 0.8 shard_map.121
  113.3 4.3 %collective-permute-start.19 = (f32[4,8,32,128]{3,2,1,0:T(8,128)S(1)}, f32[4,8,32,128]{3,2,1,0:T(8,128)S(1)}, u32[]{:S(2)}, u32[]{:S(2)}) collective-permute-start(f32[4,8,32,128]{3,2,1,0:T(8,128)S(1)} %get-tuple-element.102), channel_id=1, source_target_pairs={{0,8},{8,0},{16,24},{24,16},{32,40},{40,32},{48,56},{56,48},{64,72... | collective-permute-start | bytes 1572872 | tf_op jit(solution)/shard_map/ppermute | solution.py:746
  117.6 1.3 collective-permute-start.16
  118.9 2.6 %collective-permute-start.17 = (f32[8,32,128]{2,1,0:T(8,128)S(1)}, f32[8,32,128]{2,1,0:T(8,128)S(1)}, u32[]{:S(2)}, u32[]{:S(2)}) collective-permute-start(f32[8,32,128]{2,1,0:T(8,128)S(1)} %get-tuple-element.100), channel_id=1, source_target_pairs={{0,32},{8,40},{16,48},{24,56},{32,0},{40,8},{48,16},{56,24},{64,96... | collective-permute-start | bytes 393224 | tf_op jit(solution)/shard_map/ppermute | solution.py:745
  121.5 1.1 collective-permute-start.18
  122.6 0.1 collective-permute-start.22
  122.7 2.2 %collective-permute-start.21 = (f32[8,32,128]{2,1,0:T(8,128)S(1)}, f32[8,32,128]{2,1,0:T(8,128)S(1)}, u32[]{:S(2)}, u32[]{:S(2)}) collective-permute-start(f32[8,32,128]{2,1,0:T(8,128)S(1)} %get-tuple-element.104), channel_id=1, source_target_pairs={{0,32},{8,40},{16,48},{24,56},{32,0},{40,8},{48,16},{56,24},{64,96... | collective-permute-start | bytes 393224 | tf_op jit(solution)/shard_map/ppermute | solution.py:747
  124.9 3.0 %collective-permute-done.17.rest_2_ = f32[8,32,128]{2,1,0:T(8,128)S(1)} collective-permute-done((f32[8,32,128]{2,1,0:T(8,128)S(1)}, f32[8,32,128]{2,1,0:T(8,128)S(1)}, u32[]{:S(2)}, u32[]{:S(2)}) %collective-permute-start.17) | collective-permute-done | bytes 131104 | tf_op jit(solution)/shard_map/ppermute | solution.py:745
  127.9 2.0 %collective-permute-done.22.rest_7_ = f32[8,32,128]{2,1,0:T(8,128)S(1)} collective-permute-done((f32[8,32,128]{2,1,0:T(8,128)S(1)}, f32[8,32,128]{2,1,0:T(8,128)S(1)}, u32[]{:S(2)}, u32[]{:S(2)}) %collective-permute-start.22) | collective-permute-done | bytes 131104 | tf_op jit(solution)/shard_map/ppermute | solution.py:747
  129.9 0.9 collective-permute-done.21.rest_6_
  130.8 3.1 %collective-permute-done.20.rest_5_ = f32[8,32,128]{2,1,0:T(8,128)S(1)} collective-permute-done((f32[8,32,128]{2,1,0:T(8,128)S(1)}, f32[8,32,128]{2,1,0:T(8,128)S(1)}, u32[]{:S(2)}, u32[]{:S(2)}) %collective-permute-start.20) | collective-permute-done | bytes 131104 | tf_op jit(solution)/shard_map/ppermute | solution.py:747
  133.9 0.9 shard_map.123
  134.8 1.0 collective-permute-start.23
  135.8 0.9 shard_map.122
  136.7 7.1 %collective-permute-done.23 = f32[2,8,32,128]{3,2,1,0:T(8,128)S(1)} collective-permute-done((f32[2,8,32,128]{3,2,1,0:T(8,128)S(1)}, f32[2,8,32,128]{3,2,1,0:T(8,128)S(1)}, u32[]{:S(2)}, u32[]{:S(2)}) %collective-permute-start.23) | collective-permute-done | bytes 262176 | tf_op jit(solution)/shard_map/ppermute | solution.py:752
  143.8 0.7 add_bitcast_fusion
  (44 shorter events, 0.1 us)
Async XLA Ops:
  0.0 13.5 %collective-permute-start = (f32[2,8,32,128]{3,2,1,0:T(8,128)}, f32[2,8,32,128]{3,2,1,0:T(8,128)S(1)}, u32[]{:S(2)}, u32[]{:S(2)}) collective-permute-start(f32[2,8,32,128]{3,2,1,0:T(8,128)} %bitcast.35), channel_id=1, source_target_pairs={{0,64},{8,72},{16,80},{24,88},{32,96},{40,104},{48,112},{56,120},{... | collective-permute-start | bytes 786440 | tf_op jit(solution)/shard_map/ppermute | solution.py:634
  3.6 10.5 %collective-permute-start.1 = (f32[2,8,32,128]{3,2,1,0:T(8,128)}, f32[2,8,32,128]{3,2,1,0:T(8,128)S(1)}, u32[]{:S(2)}, u32[]{:S(2)}) collective-permute-start(f32[2,8,32,128]{3,2,1,0:T(8,128)} %bitcast.36), channel_id=1, source_target_pairs={{0,8},{8,0},{16,24},{24,16},{32,40},{40,32},{48,56},{56,48},{64,72... | collective-permute-start | bytes 786440 | tf_op jit(solution)/shard_map/ppermute | solution.py:635
  8.3 5.7 %copy-start.17 = (s32[16,8]{0,1:T(8,128)S(1)}, s32[16,8]{0,1:T(8,128)}, u32[]{:S(2)}) copy-start(s32[16,8]{0,1:T(8,128)} %param.20) | copy-start | bytes 1540
  8.3 5.8 %copy-start.15 = (s32[1,256]{1,0:T(1,128)S(1)}, s32[1,256]{1,0:T(1,128)}, u32[]{:S(2)}) copy-start(s32[1,256]{1,0:T(1,128)} %param.18) | copy-start | bytes 3076
  8.3 6.9 %copy-start.9 = (f32[2,1,8,32,128]{4,3,2,1,0:T(8,128)S(1)}, f32[2,1,8,32,128]{4,3,2,1,0:T(8,128)}, u32[]{:S(2)}) copy-start(f32[2,1,8,32,128]{4,3,2,1,0:T(8,128)} %param.11) | copy-start | bytes 786436
  8.3 13.8 %copy-start.16 = (f32[1,4,256]{2,1,0:T(4,128)S(1)}, f32[1,4,256]{2,1,0:T(4,128)}, u32[]{:S(2)}) copy-start(f32[1,4,256]{2,1,0:T(4,128)} %param.19) | copy-start | bytes 12292
  8.3 60.3 %all-to-all-start = ((f32[8,8,144,128]{3,2,1,0:T(8,128)}), f32[8,8,144,128]{3,2,1,0:T(8,128)}, u32[]{:S(2)}, u32[]{:S(2)}) async-start(f32[8,8,144,128]{3,2,1,0:T(8,128)} %shard_map.109), calls=%async_computation | async-start | bytes 9437184 | tf_op jit(solution)/shard_map/all_to_all | solution.py:655
  13.5 1.6 %collective-permute-start.2 = (f32[2,8,32,128]{3,2,1,0:T(8,128)S(1)}, f32[2,8,32,128]{3,2,1,0:T(8,128)S(1)}, u32[]{:S(2)}, u32[]{:S(2)}) collective-permute-start(f32[2,8,32,128]{3,2,1,0:T(8,128)S(1)} %collective-permute-done.other), channel_id=1, source_target_pairs={{0,8},{8,0},{16,24},{24,16},{32,40},{40,32},{48,56},{56,48},{64,72... | collective-permute-start | bytes 786440 | tf_op jit(solution)/shard_map/ppermute | solution.py:636
  14.0 8.1 %copy-start.12 = (s32[2]{0:T(128)}, s32[2]{0:T(128)S(1)}, u32[]{:S(2)}) copy-start(s32[2]{0:T(128)S(1)} %pad_add_fusion.ids) | copy-start | bytes 28
  14.0 8.0 %copy-start.10 = (s32[16,8]{1,0:T(8,128)}, s32[16,8]{1,0:T(8,128)S(1)}, u32[]{:S(2)}) copy-start(s32[16,8]{1,0:T(8,128)S(1)} %copy.14.apertures) | copy-start | bytes 1540
  17.1 18.2 %collective-permute-start.3 = (f32[2,8,32,128]{3,2,1,0:T(8,128)}, f32[2,8,32,128]{3,2,1,0:T(8,128)}, u32[]{:S(2)}, u32[]{:S(2)}) collective-permute-start(f32[2,8,32,128]{3,2,1,0:T(8,128)} %get-tuple-element.55), channel_id=1, source_target_pairs={{0,16},{8,24},{16,32},{24,40},{32,48},{40,56},{48,0},{56,8},{64,80... | collective-permute-start | bytes 786440 | tf_op jit(solution)/shard_map/ppermute | solution.py:640
  18.4 16.9 %collective-permute-start.4 = (f32[2,8,32,128]{3,2,1,0:T(8,128)}, f32[2,8,32,128]{3,2,1,0:T(8,128)}, u32[]{:S(2)}, u32[]{:S(2)}) collective-permute-start(f32[2,8,32,128]{3,2,1,0:T(8,128)} %get-tuple-element.56), channel_id=1, source_target_pairs={{0,32},{8,40},{16,48},{24,56},{32,0},{40,8},{48,16},{56,24},{64,96... | collective-permute-start | bytes 786440 | tf_op jit(solution)/shard_map/ppermute | solution.py:640
  21.0 14.3 %collective-permute-start.5 = (f32[2,8,32,128]{3,2,1,0:T(8,128)}, f32[2,8,32,128]{3,2,1,0:T(8,128)}, u32[]{:S(2)}, u32[]{:S(2)}) collective-permute-start(f32[2,8,32,128]{3,2,1,0:T(8,128)} %get-tuple-element.57), channel_id=1, source_target_pairs={{0,48},{8,56},{16,0},{24,8},{32,16},{40,24},{48,32},{56,40},{64,11... | collective-permute-start | bytes 786440 | tf_op jit(solution)/shard_map/ppermute | solution.py:640
  22.1 13.2 %copy-start.11 = (s32[16,8]{1,0:T(8,128)S(1)}, s32[16,8]{1,0:T(8,128)}, u32[]{:S(2)}) copy-start(s32[16,8]{1,0:T(8,128)} %copy-done.10) | copy-start | bytes 1540
  22.1 13.2 %copy-start.13 = (s32[2]{0:T(128)S(1)}, s32[2]{0:T(128)}, u32[]{:S(2)}) copy-start(s32[2]{0:T(128)} %copy-done.12) | copy-start | bytes 28
  22.1 46.6 %copy-start = (bf16[256,256]{1,0:T(8,128)(2,1)S(1)}, bf16[256,256]{1,0:T(8,128)(2,1)}, u32[]{:S(2)}) copy-start(bf16[256,256]{1,0:T(8,128)(2,1)} %constant.94.clone.oper) | copy-start | bytes 393220
  22.1 46.5 %copy-start.14 = (f32[1,4]{1,0:T(1,128)S(1)}, f32[1,4]{1,0:T(1,128)}, u32[]{:S(2)}) copy-start(f32[1,4]{1,0:T(1,128)} %param.16) | copy-start | bytes 52
  27.3 1.2 copy-start.1
  28.4 1.0 copy-start.3
  29.4 1.0 copy-start.5
  30.5 1.0 copy-start.7
  37.4 38.5 %collective-permute-start.6 = (f32[64,8,128]{2,1,0:T(8,128)}, f32[64,8,128]{2,1,0:T(8,128)S(1)}, u32[]{:S(2)}, u32[]{:S(2)}) collective-permute-start(f32[64,8,128]{2,1,0:T(8,128)} %get-tuple-element.62), channel_id=1, source_target_pairs={{0,1},{1,2},{2,3},{3,4},{4,5},{5,6},{6,7},{7,0},{8,9},{9,10},{10,1... | collective-permute-start | bytes 786440 | tf_op jit(solution)/shard_map/ppermute | solution.py:631
  39.1 36.9 %collective-permute-start.7 = (f32[64,8,128]{2,1,0:T(8,128)}, f32[64,8,128]{2,1,0:T(8,128)S(1)}, u32[]{:S(2)}, u32[]{:S(2)}) collective-permute-start(f32[64,8,128]{2,1,0:T(8,128)} %get-tuple-element.63), channel_id=1, source_target_pairs={{1,0},{2,1},{3,2},{4,3},{5,4},{6,5},{7,6},{0,7},{9,8},{10,9},{11,1... | collective-permute-start | bytes 786440 | tf_op jit(solution)/shard_map/ppermute | solution.py:631
  72.3 9.6 %collective-permute-start.8 = (f32[64,8,128]{2,1,0:T(8,128)S(1)}, f32[64,8,128]{2,1,0:T(8,128)S(1)}, u32[]{:S(2)}, u32[]{:S(2)}) collective-permute-start(f32[64,8,128]{2,1,0:T(8,128)S(1)} %get-tuple-element.66), channel_id=1, source_target_pairs={{0,1},{1,2},{2,3},{3,4},{4,5},{5,6},{6,7},{7,0},{8,9},{9,10},{10,1... | collective-permute-start | bytes 786440 | tf_op jit(solution)/shard_map/ppermute | solution.py:631
  72.9 17.7 %copy-start.8 = (f32[64,32,128]{2,1,0:T(8,128)S(1)}, f32[64,32,128]{2,1,0:T(8,128)}, u32[]{:S(2)}) copy-start(f32[64,32,128]{2,1,0:T(8,128)} %copy-done.7) | copy-start | bytes 3145732
  72.9 9.0 %collective-permute-start.9 = (f32[64,8,128]{2,1,0:T(8,128)S(1)}, f32[64,8,128]{2,1,0:T(8,128)S(1)}, u32[]{:S(2)}, u32[]{:S(2)}) collective-permute-start(f32[64,8,128]{2,1,0:T(8,128)S(1)} %get-tuple-element.67), channel_id=1, source_target_pairs={{1,0},{2,1},{3,2},{4,3},{5,4},{6,5},{7,6},{0,7},{9,8},{10,9},{11,1... | collective-permute-start | bytes 786440 | tf_op jit(solution)/shard_map/ppermute | solution.py:631
  87.0 6.2 %collective-permute-start.10 = (f32[32,8,128]{2,1,0:T(8,128)S(1)}, f32[32,8,128]{2,1,0:T(8,128)S(1)}, u32[]{:S(2)}, u32[]{:S(2)}) collective-permute-start(f32[32,8,128]{2,1,0:T(8,128)S(1)} %get-tuple-element.70), channel_id=1, source_target_pairs={{0,1},{1,2},{2,3},{3,4},{4,5},{5,6},{6,7},{7,0},{8,9},{9,10},{10,1... | collective-permute-start | bytes 393224 | tf_op jit(solution)/shard_map/ppermute | solution.py:631
  87.1 6.1 %collective-permute-start.11 = (f32[32,8,128]{2,1,0:T(8,128)S(1)}, f32[32,8,128]{2,1,0:T(8,128)S(1)}, u32[]{:S(2)}, u32[]{:S(2)}) collective-permute-start(f32[32,8,128]{2,1,0:T(8,128)S(1)} %get-tuple-element.71), channel_id=1, source_target_pairs={{1,0},{2,1},{3,2},{4,3},{5,4},{6,5},{7,6},{0,7},{9,8},{10,9},{11,1... | collective-permute-start | bytes 393224 | tf_op jit(solution)/shard_map/ppermute | solution.py:631
  90.7 7.2 %copy-start.2 = (f32[64,48,128]{2,1,0:T(8,128)S(1)}, f32[64,48,128]{2,1,0:T(8,128)}, u32[]{:S(2)}) copy-start(f32[64,48,128]{2,1,0:T(8,128)} %copy-done.1) | copy-start | bytes 4718596
  94.2 7.8 %collective-permute-start.12 = (f32[64,8,128]{2,1,0:T(8,128)S(1)}, f32[64,8,128]{2,1,0:T(8,128)S(1)}, u32[]{:S(2)}, u32[]{:S(2)}) collective-permute-start(f32[64,8,128]{2,1,0:T(8,128)S(1)} %get-tuple-element.80), channel_id=1, source_target_pairs={{0,1},{1,2},{2,3},{3,4},{4,5},{5,6},{6,7},{7,0},{8,9},{9,10},{10,1... | collective-permute-start | bytes 786440 | tf_op jit(solution)/shard_map/ppermute | solution.py:631
  94.3 7.7 %collective-permute-start.13 = (f32[64,8,128]{2,1,0:T(8,128)S(1)}, f32[64,8,128]{2,1,0:T(8,128)S(1)}, u32[]{:S(2)}, u32[]{:S(2)}) collective-permute-start(f32[64,8,128]{2,1,0:T(8,128)S(1)} %get-tuple-element.81), channel_id=1, source_target_pairs={{1,0},{2,1},{3,2},{4,3},{5,4},{6,5},{7,6},{0,7},{9,8},{10,9},{11,1... | collective-permute-start | bytes 786440 | tf_op jit(solution)/shard_map/ppermute | solution.py:631
  97.9 4.2 %copy-start.6 = (f32[64,32,128]{2,1,0:T(8,128)S(1)}, f32[64,32,128]{2,1,0:T(8,128)}, u32[]{:S(2)}) copy-start(f32[64,32,128]{2,1,0:T(8,128)} %copy-done.5) | copy-start | bytes 3145732
  102.0 8.1 %copy-start.4 = (f32[64,32,128]{2,1,0:T(8,128)S(1)}, f32[64,32,128]{2,1,0:T(8,128)}, u32[]{:S(2)}) copy-start(f32[64,32,128]{2,1,0:T(8,128)} %copy-done.3) | copy-start | bytes 3145732
  106.3 6.2 %collective-permute-start.14 = (f32[32,8,128]{2,1,0:T(8,128)S(1)}, f32[32,8,128]{2,1,0:T(8,128)S(1)}, u32[]{:S(2)}, u32[]{:S(2)}) collective-permute-start(f32[32,8,128]{2,1,0:T(8,128)S(1)} %get-tuple-element.91), channel_id=1, source_target_pairs={{0,1},{1,2},{2,3},{3,4},{4,5},{5,6},{6,7},{7,0},{8,9},{9,10},{10,1... | collective-permute-start | bytes 393224 | tf_op jit(solution)/shard_map/ppermute | solution.py:631
  106.5 6.0 %collective-permute-start.15 = (f32[32,8,128]{2,1,0:T(8,128)S(1)}, f32[32,8,128]{2,1,0:T(8,128)S(1)}, u32[]{:S(2)}, u32[]{:S(2)}) collective-permute-start(f32[32,8,128]{2,1,0:T(8,128)S(1)} %get-tuple-element.92), channel_id=1, source_target_pairs={{1,0},{2,1},{3,2},{4,3},{5,4},{6,5},{7,6},{0,7},{9,8},{10,9},{11,1... | collective-permute-start | bytes 393224 | tf_op jit(solution)/shard_map/ppermute | solution.py:631
  113.3 9.3 %collective-permute-start.19 = (f32[4,8,32,128]{3,2,1,0:T(8,128)S(1)}, f32[4,8,32,128]{3,2,1,0:T(8,128)S(1)}, u32[]{:S(2)}, u32[]{:S(2)}) collective-permute-start(f32[4,8,32,128]{3,2,1,0:T(8,128)S(1)} %get-tuple-element.102), channel_id=1, source_target_pairs={{0,8},{8,0},{16,24},{24,16},{32,40},{40,32},{48,56},{56,48},{64,72... | collective-permute-start | bytes 1572872 | tf_op jit(solution)/shard_map/ppermute | solution.py:746
  117.6 7.3 %collective-permute-start.16 = (f32[8,32,128]{2,1,0:T(8,128)S(1)}, f32[8,32,128]{2,1,0:T(8,128)S(1)}, u32[]{:S(2)}, u32[]{:S(2)}) collective-permute-start(f32[8,32,128]{2,1,0:T(8,128)S(1)} %get-tuple-element.99), channel_id=1, source_target_pairs={{0,16},{8,24},{16,32},{24,40},{32,48},{40,56},{48,0},{56,8},{64,80... | collective-permute-start | bytes 393224 | tf_op jit(solution)/shard_map/ppermute | solution.py:745
  118.9 9.0 %collective-permute-start.17 = (f32[8,32,128]{2,1,0:T(8,128)S(1)}, f32[8,32,128]{2,1,0:T(8,128)S(1)}, u32[]{:S(2)}, u32[]{:S(2)}) collective-permute-start(f32[8,32,128]{2,1,0:T(8,128)S(1)} %get-tuple-element.100), channel_id=1, source_target_pairs={{0,32},{8,40},{16,48},{24,56},{32,0},{40,8},{48,16},{56,24},{64,96... | collective-permute-start | bytes 393224 | tf_op jit(solution)/shard_map/ppermute | solution.py:745
  121.5 6.4 %collective-permute-start.18 = (f32[8,32,128]{2,1,0:T(8,128)S(1)}, f32[8,32,128]{2,1,0:T(8,128)S(1)}, u32[]{:S(2)}, u32[]{:S(2)}) collective-permute-start(f32[8,32,128]{2,1,0:T(8,128)S(1)} %get-tuple-element.101), channel_id=1, source_target_pairs={{0,48},{8,56},{16,0},{24,8},{32,16},{40,24},{48,32},{56,40},{64,11... | collective-permute-start | bytes 393224 | tf_op jit(solution)/shard_map/ppermute | solution.py:745
  122.6 7.3 %collective-permute-start.22 = (f32[8,32,128]{2,1,0:T(8,128)S(1)}, f32[8,32,128]{2,1,0:T(8,128)S(1)}, u32[]{:S(2)}, u32[]{:S(2)}) collective-permute-start(f32[8,32,128]{2,1,0:T(8,128)S(1)} %get-tuple-element.103), channel_id=1, source_target_pairs={{0,48},{8,56},{16,0},{24,8},{32,16},{40,24},{48,32},{56,40},{64,11... | collective-permute-start | bytes 393224 | tf_op jit(solution)/shard_map/ppermute | solution.py:747
  122.7 8.1 %collective-permute-start.21 = (f32[8,32,128]{2,1,0:T(8,128)S(1)}, f32[8,32,128]{2,1,0:T(8,128)S(1)}, u32[]{:S(2)}, u32[]{:S(2)}) collective-permute-start(f32[8,32,128]{2,1,0:T(8,128)S(1)} %get-tuple-element.104), channel_id=1, source_target_pairs={{0,32},{8,40},{16,48},{24,56},{32,0},{40,8},{48,16},{56,24},{64,96... | collective-permute-start | bytes 393224 | tf_op jit(solution)/shard_map/ppermute | solution.py:747
  124.9 9.0 %collective-permute-start.20 = (f32[8,32,128]{2,1,0:T(8,128)S(1)}, f32[8,32,128]{2,1,0:T(8,128)S(1)}, u32[]{:S(2)}, u32[]{:S(2)}) collective-permute-start(f32[8,32,128]{2,1,0:T(8,128)S(1)} %get-tuple-element.105), channel_id=1, source_target_pairs={{0,16},{8,24},{16,32},{24,40},{32,48},{40,56},{48,0},{56,8},{64,80... | collective-permute-start | bytes 393224 | tf_op jit(solution)/shard_map/ppermute | solution.py:747
  134.8 9.0 %collective-permute-start.23 = (f32[2,8,32,128]{3,2,1,0:T(8,128)S(1)}, f32[2,8,32,128]{3,2,1,0:T(8,128)S(1)}, u32[]{:S(2)}, u32[]{:S(2)}) collective-permute-start(f32[2,8,32,128]{3,2,1,0:T(8,128)S(1)} %shard_map.123), channel_id=1, source_target_pairs={{0,64},{8,72},{16,80},{24,88},{32,96},{40,104},{48,112},{56,120},{... | collective-permute-start | bytes 786440 | tf_op jit(solution)/shard_map/ppermute | solution.py:752

commit v10 on v9

--- a/solution.py
+++ b/solution.py
@@ -156,7 +156,7 @@
                 emit(g * GROUP + xi, g, xi, j, acc)
         return carry
 
-    lax.fori_loop(0, NX // GROUP, body, 0)
+    lax.fori_loop(0, NX // GROUP, body, 0, unroll=2)
 
 
 def tile(j):
@@ -242,9 +242,22 @@
     lax.fori_loop(0, NX // 2, body, 0, unroll=8)
 
 
-def middle_kernel(
-    spots, wavelet, now, now_lo, now_hi, prev, edge, r2, r2_lo, r2_hi, oper,
-    lap_a, new_a, lap_b, new_b, send_lo, send_hi, ext, ext2, depth, old_lo, old_hi,
+def middle_kernel(now, prev, r2, oper, lap, new, ext, depth):
+    clear_ends(ext)
+    no_edges(ext)
+    ext[OWN_X, OWN_Y, :] = now[...]
+    apply_depth(ext, oper, depth)
+
+    def emit(x, g, xi, j, value):
+        lap[x, tile(j), :] = value
+        new[x, tile(j), :] = 2.0 * ext[PAD + x, ext_tile(j), :] - prev[x, tile(j), :] + r2[x, tile(j), :] * value
+
+    laplace(ext, depth, OWN, emit)
+
+
+def middle_end_kernel(
+    spots, wavelet, now, now_lo, now_hi, edge, r2, r2_lo, r2_hi, oper, lap_in, new_in,
+    lap_a, new_a, lap_b, new_b, send_lo, send_hi, ext, ext2, depth, old_lo, old_hi, strip,
 ):
     has = (spots[5] == 1, spots[6] == 1)
     clear_ends(ext)
@@ -252,20 +265,36 @@
     ext[OWN_X, OWN_Y, :] = now[...]
     fill_tiles(ext, spots, lambda x: now_lo[x], lambda x: now_hi[x])
     spread_edges(edge, old_lo, old_hi)
-    apply_depth(ext, oper, depth, True)
-
-    def emit(x, g, xi, j, value):
-        twice = 2.0 * ext[PAD + x, ext_tile(j), :]
-        if j in OWN:
-            u = twice - prev[x, tile(j), :] + r2[x, tile(j), :] * value
+    zeros = jnp.zeros((8, NZ), F32)
+
+    def near(x):
+        strip[x, 4:8, :] = ext[PAD + x, OWN0 - 4 : OWN0, :]
+        strip[x, 8:16, :] = zeros
+        strip[x, 16:20, :] = ext[PAD + x, OWN1 : OWN1 + 4, :]
+
+    planes(near)
+    apply_depth(ext, oper, depth, span=(WIDE0, OWN0))
+    apply_depth(ext, oper, depth, span=(OWN1, WIDE1))
+
+    def own(x):
+        for j in OWN:
+            value, u = lap_in[x, tile(j), :], new_in[x, tile(j), :]
+            if j in (0, 3):
+                more = halo_taps(strip, x, j)
+                value = value + more
+                u = u + r2[x, tile(j), :] * more
             lap_a[x, tile(j), :] = value
             new_a[x, tile(j), :] = u
-        else:
-            old, weight, there = (old_lo, r2_lo, has[0]) if j < 0 else (old_hi, r2_hi, has[1])
-            u = jnp.where(there, twice - old[x] + weight[x] * value, 0.0)
-        ext2[PAD + x, ext_tile(j), :] = u
-
-    laplace(ext, depth, WITH_HALO, emit)
+            ext2[PAD + x, ext_tile(j), :] = u
+
+    planes(own)
+
+    def emit(x, g, xi, j, value):
+        old, weight, there = (old_lo, r2_lo, has[0]) if j < 0 else (old_hi, r2_hi, has[1])
+        u = 2.0 * ext[PAD + x, ext_tile(j), :] - old[x] + weight[x] * value
+        ext2[PAD + x, ext_tile(j), :] = jnp.where(there, u, 0.0)
+
+    laplace(ext, depth, (-1, 4), emit)
     add_source(spots, wavelet[1], new_a, 0, 0)
     add_source(spots, wavelet[1], ext2, PAD, OWN0, True)
     apply_depth(ext2, oper, depth)
@@ -698,15 +727,16 @@
         flops=10 << 20,
         moved=6 << 20,
     )(spots, turned, r2, *r2_halo, oper)
-    u1, part4 = lax.optimization_barrier((u1, part4))
+    lap1, u2 = call(middle_kernel, [VMEM] * 4, [FIELD, FIELD], [EXT, DEPTH], flops=MAIN, moved=6 << 20)(u1, u0, r2, oper)
+    u2, part4 = lax.optimization_barrier((u2, part4))
     lap1, u2, lap2, u3, lo, hi = call(
-        middle_kernel,
-        [SMEM, SMEM] + [VMEM] * 9,
+        middle_end_kernel,
+        [SMEM, SMEM] + [VMEM] * 10,
         [FIELD] * 4 + [EDGE] * 2,
-        [EXT, EXT, DEPTH, TILE_VMEM, TILE_VMEM],
+        [EXT, EXT, DEPTH, TILE_VMEM, TILE_VMEM, STRIP],
         flops=20 << 20,
         moved=12 << 20,
-    )(spots, amounts, u1, *u1_halo, u0, u0_edge, r2, *r2_halo, oper)
+    )(spots, amounts, u1, *u1_halo, u0_edge, r2, *r2_halo, oper, lap1, u2)
     u3_halo = edges(lo, hi)
     lap3, mu4 = call(
         turn_kernel,

time: 145 us -> 143 us (0.986)
  waiting for transfers between devices: 49 us -> 46.7 us
    ppermute x10, waiting for transfers between devices: 4.22 us -> 2.44 us  [edges(): return (lax.ppermute(hi, 'sub', up), lax.ppermute(lo, 'sub', down))]
    pallas_call x1 -> x2, Pallas kernels: 5.04 us -> 5.65 us  [the longest x1 3.91 us: per_device(): call(middle_end_kernel, [SMEM, SMEM] + [VMEM] * 10, [FIELD] * 4 + [EDGE]...]
  transfers between devices with their start and end apart: 25 -> 25, of which waited for: 9 -> 9; matrix products, arithmetic and copies ran while one was open for 1% -> 1% of each run, Pallas kernels for 20% -> 21%
where the time goes in v10:
time: 143 us
  waiting for transfers between devices  46.7 us (33%)
  starting transfers between devices  46.2 us (32%)
  Pallas kernels  40.7 us (28%)
  local copies, waits for them, and re-layouts  5.73 us (4%)
  between operations  2.99 us (2%)
    all_to_all x1, waiting for transfers between devices, per_device(): lax.all_to_all(packed, 'sub', 0, 0, tiled=True).reshape(NX, TURNED, NZ)  27.3 us
    ppermute x10, starting transfers between devices, edges(): return (lax.ppermute(hi, 'sub', up), lax.ppermute(lo, 'sub', down))  18.2 us
    ppermute x1, waiting for transfers between devices, per_device(): result = keep + lax.ppermute(give, 'shot', across)  6.92 us
    ppermute x3, waiting for transfers between devices, per_device(): lax.ppermute(others[k], 'shot', along(k))  5.98 us
    pallas_call x1, Pallas kernels, per_device(): call(receivers_kernel, [SMEM] * 3, [WIDE_FIELD, WIDE_FIELD] + [FIELD] * 3...  5.27 us
    all_to_all x1, starting transfers between devices, per_device(): lax.all_to_all(packed, 'sub', 0, 0, tiled=True).reshape(NX, TURNED, NZ)  5.21 us
    ppermute x3, starting transfers between devices, per_device(): lax.ppermute(sent[k], 'shot', along(k))  4.99 us
    ppermute x3, starting transfers between devices, per_device(): lax.ppermute(blocks[k], 'shot', along(k))  4.99 us
  transfers between devices with their start and end apart: 25, of which 9 were waited for; matrix products, arithmetic and copies ran while one was open for 1% of the time, Pallas kernels for 21%

profile of v10, /device:TPU:1, one launch (start us, length us, event | category | flops | bytes accessed | tf_op | source)
XLA Modules:
  0.0 143.2 jit_solution(7362727944140400965)
XLA Ops:
  0.0 3.6 %collective-permute-start = (f32[2,8,32,128]{3,2,1,0:T(8,128)}, f32[2,8,32,128]{3,2,1,0:T(8,128)S(1)}, u32[]{:S(2)}, u32[]{:S(2)}) collective-permute-start(f32[2,8,32,128]{3,2,1,0:T(8,128)} %bitcast.35), channel_id=1, source_target_pairs={{0,64},{8,72},{16,80},{24,88},{32,96},{40,104},{48,112},{56,120},{... | collective-permute-start | bytes 786440 | tf_op jit(solution)/shard_map/ppermute | solution.py:663
  3.6 1.0 collective-permute-start.1
  4.5 3.8 %shard_map.109 = f32[8,8,144,128]{3,2,1,0:T(8,128)} custom-call(f32[8,256,128]{2,1,0:T(8,128)} %bitcast.44, f32[8,256,128]{2,1,0:T(8,128)} %bitcast.45, f32[8,256,128]{2,1,0:T(8,128)} %bitcast.46, f32[8,256,128]{2,1,0:T(8,128)} %bitcast.47), custom_call_target="tpu_custom_call" | custom-call | bytes 9437184 | tf_op jit(solution)/shard_map/pallas_call | solution.py:671
  8.3 0.0 copy-start.17
  8.3 0.0 copy-start.9
  8.3 0.0 copy-start.16
  8.3 5.2 %all-to-all-start = ((f32[8,8,144,128]{3,2,1,0:T(8,128)}), f32[8,8,144,128]{3,2,1,0:T(8,128)}, u32[]{:S(2)}, u32[]{:S(2)}) async-start(f32[8,8,144,128]{3,2,1,0:T(8,128)} %shard_map.109), calls=%async_computation | async-start | bytes 9437184 | tf_op jit(solution)/shard_map/all_to_all | solution.py:684
  13.6 0.4 collective-permute-start.2
  13.9 0.1 pad_add_fusion.ids
  14.0 0.1 copy.14.apertures
  14.1 1.1 collective-permute-done.2.other_c
  15.2 2.0 %shard_map.110 = (f32[2,8,32,128]{3,2,1,0:T(8,128)S(1)}, f32[2,8,32,128]{3,2,1,0:T(8,128)}, f32[2,8,32,128]{3,2,1,0:T(8,128)}, f32[2,8,32,128]{3,2,1,0:T(8,128)}) custom-call(s32[2]{0:T(128)S(1)} %pad_add_fusion.ids, s32[16,8]{1,0:T(8,128)S(1)} %copy.14.apertures, f32[2,8,32,128]{3,2,1,0:T(8,128)S(1)} %bitcast.37, ...), custom_call_target="tpu_custom_call" | custom-call | bytes 2097152 | tf_op jit(solution)/shard_map/pallas_call | solution.py:666
  17.1 1.3 collective-permute-start.3
  18.4 2.6 %collective-permute-start.4 = (f32[2,8,32,128]{3,2,1,0:T(8,128)}, f32[2,8,32,128]{3,2,1,0:T(8,128)}, u32[]{:S(2)}, u32[]{:S(2)}) collective-permute-start(f32[2,8,32,128]{3,2,1,0:T(8,128)} %get-tuple-element.58), channel_id=1, source_target_pairs={{0,32},{8,40},{16,48},{24,56},{32,0},{40,8},{48,16},{56,24},{64,96... | collective-permute-start | bytes 786440 | tf_op jit(solution)/shard_map/ppermute | solution.py:669
  21.0 1.1 collective-permute-start.5
  22.1 0.0 copy-start
  22.1 0.0 copy-start.14
  22.2 5.3 %shard_map.112 = (f32[64,48,128]{2,1,0:T(8,128)S(1)}, f32[64,48,128]{2,1,0:T(8,128)S(1)}, f32[64,32,128]{2,1,0:T(8,128)S(1)}, f32[64,32,128]{2,1,0:T(8,128)S(1)}, f32[64,32,128]{2,1,0:T(8,128)S(1)}) custom-call(s32[256]{0:T(256)S(1)} %bitcast.42, s32[256]{0:T(256)S(1)} %fusion.lines, f32[4,256]{1,0:T(4,128)S(1)} %bitcast.43), custom_call_target="tpu_custom_call" | custom-call | flops 1099511627776 | bytes 6291456 | tf_op jit(solution)/shard_map/pallas_call | solution.py:708
  27.5 1.1 copy-done.1
  28.6 1.0 copy-done.3
  29.6 1.0 copy-done.5
  30.6 1.0 copy-done.7
  32.3 1.3 constant_dynamic-slice_fusion
  35.6 0.1 stack.63.spots
  35.7 2.1 %shard_map.111 = (f32[64,32,128]{2,1,0:T(8,128)S(1)}, f32[64,8,128]{2,1,0:T(8,128)}, f32[64,8,128]{2,1,0:T(8,128)}) custom-call(s32[2]{0:T(128)S(1)} %copy-done.13, s32[16,8]{1,0:T(8,128)S(1)} %copy-done.11, f32[2,8,32,128]{3,2,1,0:T(8,128)S(1)} %get-tuple-element.56.r0, f32[2,8,32,128]{3,2,1,0:T(8,128)} %collective-permute-done.3.r1, ...), custom_call_target="tpu_custom_call" | custom-call | bytes 2097152 | tf_op jit(solution)/shard_map/pallas_call | solution.py:685
  37.8 1.6 %collective-permute-start.8 = (f32[64,8,128]{2,1,0:T(8,128)}, f32[64,8,128]{2,1,0:T(8,128)S(1)}, u32[]{:S(2)}, u32[]{:S(2)}) collective-permute-start(f32[64,8,128]{2,1,0:T(8,128)} %get-tuple-element.67), channel_id=1, source_target_pairs={{0,1},{1,2},{2,3},{3,4},{4,5},{5,6},{6,7},{7,0},{8,9},{9,10},{10,1... | collective-permute-start | bytes 786440 | tf_op jit(solution)/shard_map/ppermute | solution.py:660
  39.4 2.0 %collective-permute-start.9 = (f32[64,8,128]{2,1,0:T(8,128)}, f32[64,8,128]{2,1,0:T(8,128)S(1)}, u32[]{:S(2)}, u32[]{:S(2)}) collective-permute-start(f32[64,8,128]{2,1,0:T(8,128)} %get-tuple-element.68), channel_id=1, source_target_pairs={{1,0},{2,1},{3,2},{4,3},{5,4},{6,5},{7,6},{0,7},{9,8},{10,9},{11,1... | collective-permute-start | bytes 786440 | tf_op jit(solution)/shard_map/ppermute | solution.py:660
  41.4 27.3 %all-to-all-done = f32[8,8,144,128]{3,2,1,0:T(8,128)} async-done(((f32[8,8,144,128]{3,2,1,0:T(8,128)}), f32[8,8,144,128]{3,2,1,0:T(8,128)}, u32[]{:S(2)}, u32[]{:S(2)}) %all-to-all-start) | async-done | bytes 4718624 | tf_op jit(solution)/shard_map/all_to_all | solution.py:684
  68.7 3.6 %shard_map.113 = (f32[64,32,128]{2,1,0:T(8,128)S(1)}, f32[64,32,128]{2,1,0:T(8,128)S(1)}, f32[64,8,128]{2,1,0:T(8,128)S(1)}, f32[64,8,128]{2,1,0:T(8,128)S(1)}, ...) custom-call(s32[8]{0:T(128)S(1)} %stack.63.spots, f32[4]{0:T(128)S(1)} %bitcast.38, ...), custom_call_target="tpu_custom_call" | custom-call | flops 10485760 | bytes 8388608 | tf_op jit(solution)/shard_map/pallas_call | solution.py:713
  72.3 0.6 collective-permute-start.6
  72.9 3.0 %collective-permute-start.7 = (f32[64,8,128]{2,1,0:T(8,128)S(1)}, f32[64,8,128]{2,1,0:T(8,128)S(1)}, u32[]{:S(2)}, u32[]{:S(2)}) collective-permute-start(f32[64,8,128]{2,1,0:T(8,128)S(1)} %get-tuple-element.65), channel_id=1, source_target_pairs={{1,0},{2,1},{3,2},{4,3},{5,4},{6,5},{7,6},{0,7},{9,8},{10,9},{11,1... | collective-permute-start | bytes 786440 | tf_op jit(solution)/shard_map/ppermute | solution.py:660
  76.0 1.7 %shard_map.114 = (f32[64,32,128]{2,1,0:T(8,128)S(1)}, f32[64,32,128]{2,1,0:T(8,128)S(1)}) custom-call(f32[64,32,128]{2,1,0:T(8,128)S(1)} %get-tuple-element.63.now.wave, f32[64,32,128]{2,1,0:T(8,128)S(1)} %get-tuple-element.69.prev, f32[64,32,128]{2,1,0:T(8,128)S(1)} %get-tuple-element.62.r2, bf16[256,256]{1,0:T(8,128)(2,1)S(1)} %copy-done), custom_call_target="tpu_custom_call" | custom-call | flops 10485760 | bytes 6291456 | tf_op jit(solution)/shard_map/pallas_call | solution.py:730
  77.7 3.6 %shard_map.115 = (f32[64,32,128]{2,1,0:T(8,128)S(1)}, f32[64,32,128]{2,1,0:T(8,128)S(1)}, f32[64,8,128]{2,1,0:T(8,128)S(1)}) custom-call(s32[8]{0:T(128)S(1)} %stack.63.spots, f32[64,144,128]{2,1,0:T(8,128)} %bitcast.17.turned, f32[64,32,128]{2,1,0:T(8,128)S(1)} %get-tuple-element.62.r2, f32[64,8,128]{2,1,0:T(8,128)S(1)} %collective-permute-done.8.r2_lo, ...), custom_call_target="tpu_custom_call" | custom-call | flops 10485760 | bytes 6291456 | tf_op jit(solution)/shard_map/pallas_call | solution.py:722
  81.3 0.6 collective-permute-done.6.now_lo
  82.0 3.9 %shard_map.116 = (f32[64,32,128]{2,1,0:T(8,128)S(1)}, f32[64,32,128]{2,1,0:T(8,128)S(1)}, f32[64,32,128]{2,1,0:T(8,128)S(1)}, f32[64,32,128]{2,1,0:T(8,128)S(1)}...) custom-call(s32[8]{0:T(128)S(1)} %stack.63.spots, f32[4]{0:T(128)S(1)} %bitcast.39, ...), custom_call_target="tpu_custom_call" | custom-call | flops 20971520 | bytes 12582912 | tf_op jit(solution)/shard_map/pallas_call | solution.py:732
  85.9 0.1 collective-permute-start.10
  86.0 3.6 %collective-permute-start.11 = (f32[32,8,128]{2,1,0:T(8,128)S(1)}, f32[32,8,128]{2,1,0:T(8,128)S(1)}, u32[]{:S(2)}, u32[]{:S(2)}) collective-permute-start(f32[32,8,128]{2,1,0:T(8,128)S(1)} %get-tuple-element.75), channel_id=1, source_target_pairs={{1,0},{2,1},{3,2},{4,3},{5,4},{6,5},{7,6},{0,7},{9,8},{10,9},{11,1... | collective-permute-start | bytes 393224 | tf_op jit(solution)/shard_map/ppermute | solution.py:660
  89.5 2.5 %shard_map.117 = (f32[64,32,128]{2,1,0:T(8,128)S(1)}, f32[64,32,128]{2,1,0:T(8,128)S(1)}) custom-call(s32[8]{0:T(128)S(1)} %stack.63.spots, f32[4]{0:T(128)S(1)} %bitcast.40, f32[64,32,128]{2,1,0:T(8,128)S(1)} %get-tuple-element.77.now.wave, f32[64,32,128]{2,1,0:T(8,128)S(1)} %get-tuple-element.78.prev.wave_b, f32[64,32,128]{2,1,0:T(8,128)S(1)} %get-tuple-element.62.r2, ...), custom_call_target="tpu_custom_call" | custom-call | flops 10485760 | bytes 8388608 | tf_op jit(solution)/shard_map/pallas_call | solution.py:741
  92.1 1.0 shard_map.118
  93.0 0.1 collective-permute-start.12
  93.1 3.7 %collective-permute-start.13 = (f32[64,8,128]{2,1,0:T(8,128)S(1)}, f32[64,8,128]{2,1,0:T(8,128)S(1)}, u32[]{:S(2)}, u32[]{:S(2)}) collective-permute-start(f32[64,8,128]{2,1,0:T(8,128)S(1)} %get-tuple-element.85), channel_id=1, source_target_pairs={{1,0},{2,1},{3,2},{4,3},{5,4},{6,5},{7,6},{0,7},{9,8},{10,9},{11,1... | collective-permute-start | bytes 786440 | tf_op jit(solution)/shard_map/ppermute | solution.py:660
  96.8 2.2 %shard_map.119 = (f32[64,32,128]{2,1,0:T(8,128)S(1)}, f32[64,32,128]{2,1,0:T(8,128)S(1)}) custom-call(s32[8]{0:T(128)S(1)} %stack.63.spots, f32[64,32,128]{2,1,0:T(8,128)S(1)} %get-tuple-element.83.late, f32[64,32,128]{2,1,0:T(8,128)S(1)} %get-tuple-element.91.later, f32[64,32,128]{2,1,0:T(8,128)S(1)} %get-tuple-element.62.r2, bf16[256,256]{1,0:T(8,128)(2,1)S(1)} %copy-done, ...), custom_call_target="tpu_custom_call" | custom-call | flops 10485760 | bytes 8388608 | tf_op jit(solution)/shard_map/pallas_call | solution.py:753
  99.0 1.8 %collective-permute-done.12.late_lo = f32[64,8,128]{2,1,0:T(8,128)S(1)} collective-permute-done((f32[64,8,128]{2,1,0:T(8,128)S(1)}, f32[64,8,128]{2,1,0:T(8,128)S(1)}, u32[]{:S(2)}, u32[]{:S(2)}) %collective-permute-start.12) | collective-permute-done | bytes 262176 | tf_op jit(solution)/shard_map/ppermute | solution.py:660
  100.8 4.1 %shard_map.120 = (f32[64,32,128]{2,1,0:T(8,128)S(1)}, f32[64,32,128]{2,1,0:T(8,128)S(1)}, f32[64,32,128]{2,1,0:T(8,128)S(1)}, f32[32,8,128]{2,1,0:T(8,128)S(1)}, f32[32,8,128]{2,1,0:T(8,128)S(1)}) custom-call(s32[8]{0:T(128)S(1)} %stack.63.spots, f32[64,32,128]{2,1,0:T(8,128)S(1)} %get-tuple-element.83.late, ...), custom_call_target="tpu_custom_call" | custom-call | flops 20971520 | bytes 16777216 | tf_op jit(solution)/shard_map/pallas_call | solution.py:756
  104.9 0.1 collective-permute-start.14
  105.0 3.6 %collective-permute-start.15 = (f32[32,8,128]{2,1,0:T(8,128)S(1)}, f32[32,8,128]{2,1,0:T(8,128)S(1)}, u32[]{:S(2)}, u32[]{:S(2)}) collective-permute-start(f32[32,8,128]{2,1,0:T(8,128)S(1)} %get-tuple-element.96), channel_id=1, source_target_pairs={{1,0},{2,1},{3,2},{4,3},{5,4},{6,5},{7,6},{0,7},{9,8},{10,9},{11,1... | collective-permute-start | bytes 393224 | tf_op jit(solution)/shard_map/ppermute | solution.py:660
  108.5 2.3 %shard_map.121.total = f32[64,32,128]{2,1,0:T(8,128)S(1)} custom-call(s32[8]{0:T(128)S(1)} %stack.63.spots, f32[64,32,128]{2,1,0:T(8,128)S(1)} %get-tuple-element.98.late, f32[64,32,128]{2,1,0:T(8,128)S(1)} %get-tuple-element.99.later, f32[64,32,128]{2,1,0:T(8,128)S(1)} %get-tuple-element.62.r2, bf16[256,256]{1,0:T(8,128)(2,1)S(1)} %copy-done, ...), custom_call_target="tpu_custom_call" | custom-call | flops 10485760 | bytes 8388608 | tf_op jit(solution)/shard_map/pallas_call | solution.py:768
  110.8 0.0 collective-permute-done.14.halo_lo
  110.9 0.8 shard_map.122
  111.7 4.5 %collective-permute-start.19 = (f32[4,8,32,128]{3,2,1,0:T(8,128)S(1)}, f32[4,8,32,128]{3,2,1,0:T(8,128)S(1)}, u32[]{:S(2)}, u32[]{:S(2)}) collective-permute-start(f32[4,8,32,128]{3,2,1,0:T(8,128)S(1)} %get-tuple-element.106), channel_id=1, source_target_pairs={{0,8},{8,0},{16,24},{24,16},{32,40},{40,32},{48,56},{56,48},{64,72... | collective-permute-start | bytes 1572872 | tf_op jit(solution)/shard_map/ppermute | solution.py:776
  116.2 1.3 collective-permute-start.16
  117.6 2.6 %collective-permute-start.17 = (f32[8,32,128]{2,1,0:T(8,128)S(1)}, f32[8,32,128]{2,1,0:T(8,128)S(1)}, u32[]{:S(2)}, u32[]{:S(2)}) collective-permute-start(f32[8,32,128]{2,1,0:T(8,128)S(1)} %get-tuple-element.104), channel_id=1, source_target_pairs={{0,32},{8,40},{16,48},{24,56},{32,0},{40,8},{48,16},{56,24},{64,96... | collective-permute-start | bytes 393224 | tf_op jit(solution)/shard_map/ppermute | solution.py:775
  120.2 1.1 collective-permute-start.18
  121.3 0.1 collective-permute-start.22
  121.3 2.2 %collective-permute-start.21 = (f32[8,32,128]{2,1,0:T(8,128)S(1)}, f32[8,32,128]{2,1,0:T(8,128)S(1)}, u32[]{:S(2)}, u32[]{:S(2)}) collective-permute-start(f32[8,32,128]{2,1,0:T(8,128)S(1)} %get-tuple-element.108), channel_id=1, source_target_pairs={{0,32},{8,40},{16,48},{24,56},{32,0},{40,8},{48,16},{56,24},{64,96... | collective-permute-start | bytes 393224 | tf_op jit(solution)/shard_map/ppermute | solution.py:777
  123.5 3.0 %collective-permute-done.17.rest_2_ = f32[8,32,128]{2,1,0:T(8,128)S(1)} collective-permute-done((f32[8,32,128]{2,1,0:T(8,128)S(1)}, f32[8,32,128]{2,1,0:T(8,128)S(1)}, u32[]{:S(2)}, u32[]{:S(2)}) %collective-permute-start.17) | collective-permute-done | bytes 131104 | tf_op jit(solution)/shard_map/ppermute | solution.py:775
  126.6 2.0 %collective-permute-done.22.rest_7_ = f32[8,32,128]{2,1,0:T(8,128)S(1)} collective-permute-done((f32[8,32,128]{2,1,0:T(8,128)S(1)}, f32[8,32,128]{2,1,0:T(8,128)S(1)}, u32[]{:S(2)}, u32[]{:S(2)}) %collective-permute-start.22) | collective-permute-done | bytes 131104 | tf_op jit(solution)/shard_map/ppermute | solution.py:777
  128.5 0.9 collective-permute-done.21.rest_6_
  129.4 3.1 %collective-permute-done.20.rest_5_ = f32[8,32,128]{2,1,0:T(8,128)S(1)} collective-permute-done((f32[8,32,128]{2,1,0:T(8,128)S(1)}, f32[8,32,128]{2,1,0:T(8,128)S(1)}, u32[]{:S(2)}, u32[]{:S(2)}) %collective-permute-start.20) | collective-permute-done | bytes 131104 | tf_op jit(solution)/shard_map/ppermute | solution.py:777
  132.5 0.9 shard_map.124
  133.5 1.1 collective-permute-start.23
  134.6 0.9 shard_map.123
  135.5 6.9 %collective-permute-done.23 = f32[2,8,32,128]{3,2,1,0:T(8,128)S(1)} collective-permute-done((f32[2,8,32,128]{3,2,1,0:T(8,128)S(1)}, f32[2,8,32,128]{3,2,1,0:T(8,128)S(1)}, u32[]{:S(2)}, u32[]{:S(2)}) %collective-permute-start.23) | collective-permute-done | bytes 262176 | tf_op jit(solution)/shard_map/ppermute | solution.py:782
  142.4 0.7 add_bitcast_fusion
  (45 shorter events, 0.1 us)
Async XLA Ops:
  0.0 13.6 %collective-permute-start = (f32[2,8,32,128]{3,2,1,0:T(8,128)}, f32[2,8,32,128]{3,2,1,0:T(8,128)S(1)}, u32[]{:S(2)}, u32[]{:S(2)}) collective-permute-start(f32[2,8,32,128]{3,2,1,0:T(8,128)} %bitcast.35), channel_id=1, source_target_pairs={{0,64},{8,72},{16,80},{24,88},{32,96},{40,104},{48,112},{56,120},{... | collective-permute-start | bytes 786440 | tf_op jit(solution)/shard_map/ppermute | solution.py:663
  3.6 10.5 %collective-permute-start.1 = (f32[2,8,32,128]{3,2,1,0:T(8,128)}, f32[2,8,32,128]{3,2,1,0:T(8,128)S(1)}, u32[]{:S(2)}, u32[]{:S(2)}) collective-permute-start(f32[2,8,32,128]{3,2,1,0:T(8,128)} %bitcast.36), channel_id=1, source_target_pairs={{0,8},{8,0},{16,24},{24,16},{32,40},{40,32},{48,56},{56,48},{64,72... | collective-permute-start | bytes 786440 | tf_op jit(solution)/shard_map/ppermute | solution.py:664
  8.3 5.7 %copy-start.17 = (s32[16,8]{0,1:T(8,128)S(1)}, s32[16,8]{0,1:T(8,128)}, u32[]{:S(2)}) copy-start(s32[16,8]{0,1:T(8,128)} %param.20) | copy-start | bytes 1540
  8.3 5.8 %copy-start.15 = (s32[1,256]{1,0:T(1,128)S(1)}, s32[1,256]{1,0:T(1,128)}, u32[]{:S(2)}) copy-start(s32[1,256]{1,0:T(1,128)} %param.18) | copy-start | bytes 3076
  8.3 6.9 %copy-start.9 = (f32[2,1,8,32,128]{4,3,2,1,0:T(8,128)S(1)}, f32[2,1,8,32,128]{4,3,2,1,0:T(8,128)}, u32[]{:S(2)}) copy-start(f32[2,1,8,32,128]{4,3,2,1,0:T(8,128)} %param.11) | copy-start | bytes 786436
  8.3 13.8 %copy-start.16 = (f32[1,4,256]{2,1,0:T(4,128)S(1)}, f32[1,4,256]{2,1,0:T(4,128)}, u32[]{:S(2)}) copy-start(f32[1,4,256]{2,1,0:T(4,128)} %param.19) | copy-start | bytes 12292
  8.3 60.3 %all-to-all-start = ((f32[8,8,144,128]{3,2,1,0:T(8,128)}), f32[8,8,144,128]{3,2,1,0:T(8,128)}, u32[]{:S(2)}, u32[]{:S(2)}) async-start(f32[8,8,144,128]{3,2,1,0:T(8,128)} %shard_map.109), calls=%async_computation | async-start | bytes 9437184 | tf_op jit(solution)/shard_map/all_to_all | solution.py:684
  13.6 1.6 %collective-permute-start.2 = (f32[2,8,32,128]{3,2,1,0:T(8,128)S(1)}, f32[2,8,32,128]{3,2,1,0:T(8,128)S(1)}, u32[]{:S(2)}, u32[]{:S(2)}) collective-permute-start(f32[2,8,32,128]{3,2,1,0:T(8,128)S(1)} %collective-permute-done.other), channel_id=1, source_target_pairs={{0,8},{8,0},{16,24},{24,16},{32,40},{40,32},{48,56},{56,48},{64,72... | collective-permute-start | bytes 786440 | tf_op jit(solution)/shard_map/ppermute | solution.py:665
  14.0 8.1 %copy-start.12 = (s32[2]{0:T(128)}, s32[2]{0:T(128)S(1)}, u32[]{:S(2)}) copy-start(s32[2]{0:T(128)S(1)} %pad_add_fusion.ids) | copy-start | bytes 28
  14.1 8.0 %copy-start.10 = (s32[16,8]{1,0:T(8,128)}, s32[16,8]{1,0:T(8,128)S(1)}, u32[]{:S(2)}) copy-start(s32[16,8]{1,0:T(8,128)S(1)} %copy.14.apertures) | copy-start | bytes 1540
  17.1 18.6 %collective-permute-start.3 = (f32[2,8,32,128]{3,2,1,0:T(8,128)}, f32[2,8,32,128]{3,2,1,0:T(8,128)}, u32[]{:S(2)}, u32[]{:S(2)}) collective-permute-start(f32[2,8,32,128]{3,2,1,0:T(8,128)} %get-tuple-element.57), channel_id=1, source_target_pairs={{0,16},{8,24},{16,32},{24,40},{32,48},{40,56},{48,0},{56,8},{64,80... | collective-permute-start | bytes 786440 | tf_op jit(solution)/shard_map/ppermute | solution.py:669
  18.4 17.3 %collective-permute-start.4 = (f32[2,8,32,128]{3,2,1,0:T(8,128)}, f32[2,8,32,128]{3,2,1,0:T(8,128)}, u32[]{:S(2)}, u32[]{:S(2)}) collective-permute-start(f32[2,8,32,128]{3,2,1,0:T(8,128)} %get-tuple-element.58), channel_id=1, source_target_pairs={{0,32},{8,40},{16,48},{24,56},{32,0},{40,8},{48,16},{56,24},{64,96... | collective-permute-start | bytes 786440 | tf_op jit(solution)/shard_map/ppermute | solution.py:669
  21.0 14.7 %collective-permute-start.5 = (f32[2,8,32,128]{3,2,1,0:T(8,128)}, f32[2,8,32,128]{3,2,1,0:T(8,128)}, u32[]{:S(2)}, u32[]{:S(2)}) collective-permute-start(f32[2,8,32,128]{3,2,1,0:T(8,128)} %get-tuple-element.59), channel_id=1, source_target_pairs={{0,48},{8,56},{16,0},{24,8},{32,16},{40,24},{48,32},{56,40},{64,11... | collective-permute-start | bytes 786440 | tf_op jit(solution)/shard_map/ppermute | solution.py:669
  22.1 13.6 %copy-start.11 = (s32[16,8]{1,0:T(8,128)S(1)}, s32[16,8]{1,0:T(8,128)}, u32[]{:S(2)}) copy-start(s32[16,8]{1,0:T(8,128)} %copy-done.10) | copy-start | bytes 1540
  22.1 13.6 %copy-start.13 = (s32[2]{0:T(128)S(1)}, s32[2]{0:T(128)}, u32[]{:S(2)}) copy-start(s32[2]{0:T(128)} %copy-done.12) | copy-start | bytes 28
  22.1 46.5 %copy-start = (bf16[256,256]{1,0:T(8,128)(2,1)S(1)}, bf16[256,256]{1,0:T(8,128)(2,1)}, u32[]{:S(2)}) copy-start(bf16[256,256]{1,0:T(8,128)(2,1)} %constant.94.clone.oper) | copy-start | bytes 393220
  22.1 46.5 %copy-start.14 = (f32[1,4]{1,0:T(1,128)S(1)}, f32[1,4]{1,0:T(1,128)}, u32[]{:S(2)}) copy-start(f32[1,4]{1,0:T(1,128)} %param.16) | copy-start | bytes 52
  27.4 1.1 copy-start.1
  28.6 1.0 copy-start.3
  29.6 1.0 copy-start.5
  30.6 1.0 copy-start.7
  37.8 39.9 %collective-permute-start.8 = (f32[64,8,128]{2,1,0:T(8,128)}, f32[64,8,128]{2,1,0:T(8,128)S(1)}, u32[]{:S(2)}, u32[]{:S(2)}) collective-permute-start(f32[64,8,128]{2,1,0:T(8,128)} %get-tuple-element.67), channel_id=1, source_target_pairs={{0,1},{1,2},{2,3},{3,4},{4,5},{5,6},{6,7},{7,0},{8,9},{9,10},{10,1... | collective-permute-start | bytes 786440 | tf_op jit(solution)/shard_map/ppermute | solution.py:660
  39.4 38.3 %collective-permute-start.9 = (f32[64,8,128]{2,1,0:T(8,128)}, f32[64,8,128]{2,1,0:T(8,128)S(1)}, u32[]{:S(2)}, u32[]{:S(2)}) collective-permute-start(f32[64,8,128]{2,1,0:T(8,128)} %get-tuple-element.68), channel_id=1, source_target_pairs={{1,0},{2,1},{3,2},{4,3},{5,4},{6,5},{7,6},{0,7},{9,8},{10,9},{11,1... | collective-permute-start | bytes 786440 | tf_op jit(solution)/shard_map/ppermute | solution.py:660
  72.3 9.7 %collective-permute-start.6 = (f32[64,8,128]{2,1,0:T(8,128)S(1)}, f32[64,8,128]{2,1,0:T(8,128)S(1)}, u32[]{:S(2)}, u32[]{:S(2)}) collective-permute-start(f32[64,8,128]{2,1,0:T(8,128)S(1)} %get-tuple-element.64), channel_id=1, source_target_pairs={{0,1},{1,2},{2,3},{3,4},{4,5},{5,6},{6,7},{7,0},{8,9},{9,10},{10,1... | collective-permute-start | bytes 786440 | tf_op jit(solution)/shard_map/ppermute | solution.py:660
  72.9 9.1 %collective-permute-start.7 = (f32[64,8,128]{2,1,0:T(8,128)S(1)}, f32[64,8,128]{2,1,0:T(8,128)S(1)}, u32[]{:S(2)}, u32[]{:S(2)}) collective-permute-start(f32[64,8,128]{2,1,0:T(8,128)S(1)} %get-tuple-element.65), channel_id=1, source_target_pairs={{1,0},{2,1},{3,2},{4,3},{5,4},{6,5},{7,6},{0,7},{9,8},{10,9},{11,1... | collective-permute-start | bytes 786440 | tf_op jit(solution)/shard_map/ppermute | solution.py:660
  77.7 11.8 %copy-start.8 = (f32[64,32,128]{2,1,0:T(8,128)S(1)}, f32[64,32,128]{2,1,0:T(8,128)}, u32[]{:S(2)}) copy-start(f32[64,32,128]{2,1,0:T(8,128)} %copy-done.7) | copy-start | bytes 3145732
  85.9 6.1 %collective-permute-start.10 = (f32[32,8,128]{2,1,0:T(8,128)S(1)}, f32[32,8,128]{2,1,0:T(8,128)S(1)}, u32[]{:S(2)}, u32[]{:S(2)}) collective-permute-start(f32[32,8,128]{2,1,0:T(8,128)S(1)} %get-tuple-element.74), channel_id=1, source_target_pairs={{0,1},{1,2},{2,3},{3,4},{4,5},{5,6},{6,7},{7,0},{8,9},{9,10},{10,1... | collective-permute-start | bytes 393224 | tf_op jit(solution)/shard_map/ppermute | solution.py:660
  86.0 6.1 %collective-permute-start.11 = (f32[32,8,128]{2,1,0:T(8,128)S(1)}, f32[32,8,128]{2,1,0:T(8,128)S(1)}, u32[]{:S(2)}, u32[]{:S(2)}) collective-permute-start(f32[32,8,128]{2,1,0:T(8,128)S(1)} %get-tuple-element.75), channel_id=1, source_target_pairs={{1,0},{2,1},{3,2},{4,3},{5,4},{6,5},{7,6},{0,7},{9,8},{10,9},{11,1... | collective-permute-start | bytes 393224 | tf_op jit(solution)/shard_map/ppermute | solution.py:660
  89.5 7.2 %copy-start.2 = (f32[64,48,128]{2,1,0:T(8,128)S(1)}, f32[64,48,128]{2,1,0:T(8,128)}, u32[]{:S(2)}) copy-start(f32[64,48,128]{2,1,0:T(8,128)} %copy-done.1) | copy-start | bytes 4718596
  93.0 7.7 %collective-permute-start.12 = (f32[64,8,128]{2,1,0:T(8,128)S(1)}, f32[64,8,128]{2,1,0:T(8,128)S(1)}, u32[]{:S(2)}, u32[]{:S(2)}) collective-permute-start(f32[64,8,128]{2,1,0:T(8,128)S(1)} %get-tuple-element.84), channel_id=1, source_target_pairs={{0,1},{1,2},{2,3},{3,4},{4,5},{5,6},{6,7},{7,0},{8,9},{9,10},{10,1... | collective-permute-start | bytes 786440 | tf_op jit(solution)/shard_map/ppermute | solution.py:660
  93.1 7.7 %collective-permute-start.13 = (f32[64,8,128]{2,1,0:T(8,128)S(1)}, f32[64,8,128]{2,1,0:T(8,128)S(1)}, u32[]{:S(2)}, u32[]{:S(2)}) collective-permute-start(f32[64,8,128]{2,1,0:T(8,128)S(1)} %get-tuple-element.85), channel_id=1, source_target_pairs={{1,0},{2,1},{3,2},{4,3},{5,4},{6,5},{7,6},{0,7},{9,8},{10,9},{11,1... | collective-permute-start | bytes 786440 | tf_op jit(solution)/shard_map/ppermute | solution.py:660
  96.8 4.0 %copy-start.6 = (f32[64,32,128]{2,1,0:T(8,128)S(1)}, f32[64,32,128]{2,1,0:T(8,128)}, u32[]{:S(2)}) copy-start(f32[64,32,128]{2,1,0:T(8,128)} %copy-done.5) | copy-start | bytes 3145732
  100.8 7.8 %copy-start.4 = (f32[64,32,128]{2,1,0:T(8,128)S(1)}, f32[64,32,128]{2,1,0:T(8,128)}, u32[]{:S(2)}) copy-start(f32[64,32,128]{2,1,0:T(8,128)} %copy-done.3) | copy-start | bytes 3145732
  104.9 6.0 %collective-permute-start.14 = (f32[32,8,128]{2,1,0:T(8,128)S(1)}, f32[32,8,128]{2,1,0:T(8,128)S(1)}, u32[]{:S(2)}, u32[]{:S(2)}) collective-permute-start(f32[32,8,128]{2,1,0:T(8,128)S(1)} %get-tuple-element.95), channel_id=1, source_target_pairs={{0,1},{1,2},{2,3},{3,4},{4,5},{5,6},{6,7},{7,0},{8,9},{9,10},{10,1... | collective-permute-start | bytes 393224 | tf_op jit(solution)/shard_map/ppermute | solution.py:660
  105.0 5.9 %collective-permute-start.15 = (f32[32,8,128]{2,1,0:T(8,128)S(1)}, f32[32,8,128]{2,1,0:T(8,128)S(1)}, u32[]{:S(2)}, u32[]{:S(2)}) collective-permute-start(f32[32,8,128]{2,1,0:T(8,128)S(1)} %get-tuple-element.96), channel_id=1, source_target_pairs={{1,0},{2,1},{3,2},{4,3},{5,4},{6,5},{7,6},{0,7},{9,8},{10,9},{11,1... | collective-permute-start | bytes 393224 | tf_op jit(solution)/shard_map/ppermute | solution.py:660
  111.7 9.5 %collective-permute-start.19 = (f32[4,8,32,128]{3,2,1,0:T(8,128)S(1)}, f32[4,8,32,128]{3,2,1,0:T(8,128)S(1)}, u32[]{:S(2)}, u32[]{:S(2)}) collective-permute-start(f32[4,8,32,128]{3,2,1,0:T(8,128)S(1)} %get-tuple-element.106), channel_id=1, source_target_pairs={{0,8},{8,0},{16,24},{24,16},{32,40},{40,32},{48,56},{56,48},{64,72... | collective-permute-start | bytes 1572872 | tf_op jit(solution)/shard_map/ppermute | solution.py:776
  116.2 7.3 %collective-permute-start.16 = (f32[8,32,128]{2,1,0:T(8,128)S(1)}, f32[8,32,128]{2,1,0:T(8,128)S(1)}, u32[]{:S(2)}, u32[]{:S(2)}) collective-permute-start(f32[8,32,128]{2,1,0:T(8,128)S(1)} %get-tuple-element.103), channel_id=1, source_target_pairs={{0,16},{8,24},{16,32},{24,40},{32,48},{40,56},{48,0},{56,8},{64,80... | collective-permute-start | bytes 393224 | tf_op jit(solution)/shard_map/ppermute | solution.py:775
  117.6 9.0 %collective-permute-start.17 = (f32[8,32,128]{2,1,0:T(8,128)S(1)}, f32[8,32,128]{2,1,0:T(8,128)S(1)}, u32[]{:S(2)}, u32[]{:S(2)}) collective-permute-start(f32[8,32,128]{2,1,0:T(8,128)S(1)} %get-tuple-element.104), channel_id=1, source_target_pairs={{0,32},{8,40},{16,48},{24,56},{32,0},{40,8},{48,16},{56,24},{64,96... | collective-permute-start | bytes 393224 | tf_op jit(solution)/shard_map/ppermute | solution.py:775
  120.2 6.4 %collective-permute-start.18 = (f32[8,32,128]{2,1,0:T(8,128)S(1)}, f32[8,32,128]{2,1,0:T(8,128)S(1)}, u32[]{:S(2)}, u32[]{:S(2)}) collective-permute-start(f32[8,32,128]{2,1,0:T(8,128)S(1)} %get-tuple-element.105), channel_id=1, source_target_pairs={{0,48},{8,56},{16,0},{24,8},{32,16},{40,24},{48,32},{56,40},{64,11... | collective-permute-start | bytes 393224 | tf_op jit(solution)/shard_map/ppermute | solution.py:775
  121.3 7.3 %collective-permute-start.22 = (f32[8,32,128]{2,1,0:T(8,128)S(1)}, f32[8,32,128]{2,1,0:T(8,128)S(1)}, u32[]{:S(2)}, u32[]{:S(2)}) collective-permute-start(f32[8,32,128]{2,1,0:T(8,128)S(1)} %get-tuple-element.107), channel_id=1, source_target_pairs={{0,48},{8,56},{16,0},{24,8},{32,16},{40,24},{48,32},{56,40},{64,11... | collective-permute-start | bytes 393224 | tf_op jit(solution)/shard_map/ppermute | solution.py:777
  121.3 8.1 %collective-permute-start.21 = (f32[8,32,128]{2,1,0:T(8,128)S(1)}, f32[8,32,128]{2,1,0:T(8,128)S(1)}, u32[]{:S(2)}, u32[]{:S(2)}) collective-permute-start(f32[8,32,128]{2,1,0:T(8,128)S(1)} %get-tuple-element.108), channel_id=1, source_target_pairs={{0,32},{8,40},{16,48},{24,56},{32,0},{40,8},{48,16},{56,24},{64,96... | collective-permute-start | bytes 393224 | tf_op jit(solution)/shard_map/ppermute | solution.py:777
  123.5 9.0 %collective-permute-start.20 = (f32[8,32,128]{2,1,0:T(8,128)S(1)}, f32[8,32,128]{2,1,0:T(8,128)S(1)}, u32[]{:S(2)}, u32[]{:S(2)}) collective-permute-start(f32[8,32,128]{2,1,0:T(8,128)S(1)} %get-tuple-element.109), channel_id=1, source_target_pairs={{0,16},{8,24},{16,32},{24,40},{32,48},{40,56},{48,0},{56,8},{64,80... | collective-permute-start | bytes 393224 | tf_op jit(solution)/shard_map/ppermute | solution.py:777
  133.5 8.9 %collective-permute-start.23 = (f32[2,8,32,128]{3,2,1,0:T(8,128)S(1)}, f32[2,8,32,128]{3,2,1,0:T(8,128)S(1)}, u32[]{:S(2)}, u32[]{:S(2)}) collective-permute-start(f32[2,8,32,128]{3,2,1,0:T(8,128)S(1)} %shard_map.124), channel_id=1, source_target_pairs={{0,64},{8,72},{16,80},{24,88},{32,96},{40,104},{48,112},{56,120},{... | collective-permute-start | bytes 786440 | tf_op jit(solution)/shard_map/ppermute | solution.py:782

commit v11 on v10

--- a/solution.py
+++ b/solution.py
@@ -24,7 +24,7 @@
 WIDE0, WIDE1 = 8, 56
 WIDE = WIDE1 - WIDE0
 OWN_X, OWN_Y = slice(PAD, PAD + NX), slice(OWN0, OWN1)
-CHUNK = 16
+CHUNK = 8
 OWN, WITH_HALO = range(4), range(-1, 5)
 
 

time: 143 us -> 144 us (level)
  no operation moved by 1% of the time
where the time goes in v11:
time: 144 us
  waiting for transfers between devices  46.7 us (32%)
  starting transfers between devices  46.1 us (32%)
  Pallas kernels  41.1 us (29%)
  local copies, waits for them, and re-layouts  5.73 us (4%)
  between operations  3 us (2%)
    all_to_all x1, waiting for transfers between devices, per_device(): lax.all_to_all(packed, 'sub', 0, 0, tiled=True).reshape(NX, TURNED, NZ)  27.3 us
    ppermute x10, starting transfers between devices, edges(): return (lax.ppermute(hi, 'sub', up), lax.ppermute(lo, 'sub', down))  18.2 us
    ppermute x1, waiting for transfers between devices, per_device(): result = keep + lax.ppermute(give, 'shot', across)  6.95 us
    ppermute x3, waiting for transfers between devices, per_device(): lax.ppermute(others[k], 'shot', along(k))  5.98 us
    pallas_call x1, Pallas kernels, per_device(): call(receivers_kernel, [SMEM] * 3, [WIDE_FIELD, WIDE_FIELD] + [FIELD] * 3...  5.27 us
    all_to_all x1, starting transfers between devices, per_device(): lax.all_to_all(packed, 'sub', 0, 0, tiled=True).reshape(NX, TURNED, NZ)  5.21 us
    ppermute x3, starting transfers between devices, per_device(): lax.ppermute(sent[k], 'shot', along(k))  5.03 us
    ppermute x3, starting transfers between devices, per_device(): lax.ppermute(blocks[k], 'shot', along(k))  4.99 us
  transfers between devices with their start and end apart: 25, of which 9 were waited for; matrix products, arithmetic and copies ran while one was open for 1% of the time, Pallas kernels for 21%

profile of v11, /device:TPU:1, one launch (start us, length us, event | category | flops | bytes accessed | tf_op | source)
XLA Modules:
  0.0 143.5 jit_solution(10711048101609865550)
XLA Ops:
  0.0 3.6 %collective-permute-start = (f32[2,8,32,128]{3,2,1,0:T(8,128)}, f32[2,8,32,128]{3,2,1,0:T(8,128)S(1)}, u32[]{:S(2)}, u32[]{:S(2)}) collective-permute-start(f32[2,8,32,128]{3,2,1,0:T(8,128)} %bitcast.35), channel_id=1, source_target_pairs={{0,64},{8,72},{16,80},{24,88},{32,96},{40,104},{48,112},{56,120},{... | collective-permute-start | bytes 786440 | tf_op jit(solution)/shard_map/ppermute | solution.py:663
  3.6 1.0 collective-permute-start.1
  4.5 3.8 %shard_map.109 = f32[8,8,144,128]{3,2,1,0:T(8,128)} custom-call(f32[8,256,128]{2,1,0:T(8,128)} %bitcast.44, f32[8,256,128]{2,1,0:T(8,128)} %bitcast.45, f32[8,256,128]{2,1,0:T(8,128)} %bitcast.46, f32[8,256,128]{2,1,0:T(8,128)} %bitcast.47), custom_call_target="tpu_custom_call" | custom-call | bytes 9437184 | tf_op jit(solution)/shard_map/pallas_call | solution.py:671
  8.3 0.0 copy-start.17
  8.3 0.0 copy-start.15
  8.3 0.0 copy-start.9
  8.3 5.2 %all-to-all-start = ((f32[8,8,144,128]{3,2,1,0:T(8,128)}), f32[8,8,144,128]{3,2,1,0:T(8,128)}, u32[]{:S(2)}, u32[]{:S(2)}) async-start(f32[8,8,144,128]{3,2,1,0:T(8,128)} %shard_map.109), calls=%async_computation | async-start | bytes 9437184 | tf_op jit(solution)/shard_map/all_to_all | solution.py:684
  13.6 0.4 collective-permute-start.2
  13.9 0.1 pad_add_fusion.ids
  14.0 0.1 copy.14.apertures
  14.1 1.1 collective-permute-done.2.other_c
  15.2 2.0 %shard_map.110 = (f32[2,8,32,128]{3,2,1,0:T(8,128)S(1)}, f32[2,8,32,128]{3,2,1,0:T(8,128)}, f32[2,8,32,128]{3,2,1,0:T(8,128)}, f32[2,8,32,128]{3,2,1,0:T(8,128)}) custom-call(s32[2]{0:T(128)S(1)} %pad_add_fusion.ids, s32[16,8]{1,0:T(8,128)S(1)} %copy.14.apertures, f32[2,8,32,128]{3,2,1,0:T(8,128)S(1)} %bitcast.37, ...), custom_call_target="tpu_custom_call" | custom-call | bytes 2097152 | tf_op jit(solution)/shard_map/pallas_call | solution.py:666
  17.1 1.3 collective-permute-start.3
  18.4 2.6 %collective-permute-start.4 = (f32[2,8,32,128]{3,2,1,0:T(8,128)}, f32[2,8,32,128]{3,2,1,0:T(8,128)}, u32[]{:S(2)}, u32[]{:S(2)}) collective-permute-start(f32[2,8,32,128]{3,2,1,0:T(8,128)} %get-tuple-element.58), channel_id=1, source_target_pairs={{0,32},{8,40},{16,48},{24,56},{32,0},{40,8},{48,16},{56,24},{64,96... | collective-permute-start | bytes 786440 | tf_op jit(solution)/shard_map/ppermute | solution.py:669
  21.0 1.1 collective-permute-start.5
  22.1 0.0 copy-start
  22.1 0.0 copy-start.14
  22.2 5.3 %shard_map.112 = (f32[64,48,128]{2,1,0:T(8,128)S(1)}, f32[64,48,128]{2,1,0:T(8,128)S(1)}, f32[64,32,128]{2,1,0:T(8,128)S(1)}, f32[64,32,128]{2,1,0:T(8,128)S(1)}, f32[64,32,128]{2,1,0:T(8,128)S(1)}) custom-call(s32[256]{0:T(256)S(1)} %bitcast.42, s32[256]{0:T(256)S(1)} %fusion.lines, f32[4,256]{1,0:T(4,128)S(1)} %bitcast.43), custom_call_target="tpu_custom_call" | custom-call | flops 1099511627776 | bytes 6291456 | tf_op jit(solution)/shard_map/pallas_call | solution.py:708
  27.4 1.1 copy-done.1
  28.6 1.0 copy-done.3
  29.6 1.0 copy-done.5
  30.6 1.0 copy-done.7
  32.3 1.3 constant_dynamic-slice_fusion
  35.6 0.1 stack.63.spots
  35.7 2.1 %shard_map.111 = (f32[64,32,128]{2,1,0:T(8,128)S(1)}, f32[64,8,128]{2,1,0:T(8,128)}, f32[64,8,128]{2,1,0:T(8,128)}) custom-call(s32[2]{0:T(128)S(1)} %copy-done.13, s32[16,8]{1,0:T(8,128)S(1)} %copy-done.11, f32[2,8,32,128]{3,2,1,0:T(8,128)S(1)} %get-tuple-element.56.r0, f32[2,8,32,128]{3,2,1,0:T(8,128)} %collective-permute-done.3.r1, ...), custom_call_target="tpu_custom_call" | custom-call | bytes 2097152 | tf_op jit(solution)/shard_map/pallas_call | solution.py:685
  37.8 1.7 %collective-permute-start.8 = (f32[64,8,128]{2,1,0:T(8,128)}, f32[64,8,128]{2,1,0:T(8,128)S(1)}, u32[]{:S(2)}, u32[]{:S(2)}) collective-permute-start(f32[64,8,128]{2,1,0:T(8,128)} %get-tuple-element.67), channel_id=1, source_target_pairs={{0,1},{1,2},{2,3},{3,4},{4,5},{5,6},{6,7},{7,0},{8,9},{9,10},{10,1... | collective-permute-start | bytes 786440 | tf_op jit(solution)/shard_map/ppermute | solution.py:660
  39.5 1.9 %collective-permute-start.9 = (f32[64,8,128]{2,1,0:T(8,128)}, f32[64,8,128]{2,1,0:T(8,128)S(1)}, u32[]{:S(2)}, u32[]{:S(2)}) collective-permute-start(f32[64,8,128]{2,1,0:T(8,128)} %get-tuple-element.68), channel_id=1, source_target_pairs={{1,0},{2,1},{3,2},{4,3},{5,4},{6,5},{7,6},{0,7},{9,8},{10,9},{11,1... | collective-permute-start | bytes 786440 | tf_op jit(solution)/shard_map/ppermute | solution.py:660
  41.4 27.3 %all-to-all-done = f32[8,8,144,128]{3,2,1,0:T(8,128)} async-done(((f32[8,8,144,128]{3,2,1,0:T(8,128)}), f32[8,8,144,128]{3,2,1,0:T(8,128)}, u32[]{:S(2)}, u32[]{:S(2)}) %all-to-all-start) | async-done | bytes 4718624 | tf_op jit(solution)/shard_map/all_to_all | solution.py:684
  68.7 3.6 %shard_map.113 = (f32[64,32,128]{2,1,0:T(8,128)S(1)}, f32[64,32,128]{2,1,0:T(8,128)S(1)}, f32[64,8,128]{2,1,0:T(8,128)S(1)}, f32[64,8,128]{2,1,0:T(8,128)S(1)}, ...) custom-call(s32[8]{0:T(128)S(1)} %stack.63.spots, f32[4]{0:T(128)S(1)} %bitcast.38, ...), custom_call_target="tpu_custom_call" | custom-call | flops 10485760 | bytes 8388608 | tf_op jit(solution)/shard_map/pallas_call | solution.py:713
  72.3 0.6 collective-permute-start.6
  72.9 3.0 %collective-permute-start.7 = (f32[64,8,128]{2,1,0:T(8,128)S(1)}, f32[64,8,128]{2,1,0:T(8,128)S(1)}, u32[]{:S(2)}, u32[]{:S(2)}) collective-permute-start(f32[64,8,128]{2,1,0:T(8,128)S(1)} %get-tuple-element.65), channel_id=1, source_target_pairs={{1,0},{2,1},{3,2},{4,3},{5,4},{6,5},{7,6},{0,7},{9,8},{10,9},{11,1... | collective-permute-start | bytes 786440 | tf_op jit(solution)/shard_map/ppermute | solution.py:660
  75.9 1.8 %shard_map.114 = (f32[64,32,128]{2,1,0:T(8,128)S(1)}, f32[64,32,128]{2,1,0:T(8,128)S(1)}) custom-call(f32[64,32,128]{2,1,0:T(8,128)S(1)} %get-tuple-element.63.now.wave, f32[64,32,128]{2,1,0:T(8,128)S(1)} %get-tuple-element.69.prev, f32[64,32,128]{2,1,0:T(8,128)S(1)} %get-tuple-element.62.r2, bf16[256,256]{1,0:T(8,128)(2,1)S(1)} %copy-done), custom_call_target="tpu_custom_call" | custom-call | flops 10485760 | bytes 6291456 | tf_op jit(solution)/shard_map/pallas_call | solution.py:730
  77.7 3.6 %shard_map.115 = (f32[64,32,128]{2,1,0:T(8,128)S(1)}, f32[64,32,128]{2,1,0:T(8,128)S(1)}, f32[64,8,128]{2,1,0:T(8,128)S(1)}) custom-call(s32[8]{0:T(128)S(1)} %stack.63.spots, f32[64,144,128]{2,1,0:T(8,128)} %bitcast.17.turned, f32[64,32,128]{2,1,0:T(8,128)S(1)} %get-tuple-element.62.r2, f32[64,8,128]{2,1,0:T(8,128)S(1)} %collective-permute-done.8.r2_lo, ...), custom_call_target="tpu_custom_call" | custom-call | flops 10485760 | bytes 6291456 | tf_op jit(solution)/shard_map/pallas_call | solution.py:722
  81.3 0.6 collective-permute-done.6.now_lo
  81.9 4.1 %shard_map.116 = (f32[64,32,128]{2,1,0:T(8,128)S(1)}, f32[64,32,128]{2,1,0:T(8,128)S(1)}, f32[64,32,128]{2,1,0:T(8,128)S(1)}, f32[64,32,128]{2,1,0:T(8,128)S(1)}...) custom-call(s32[8]{0:T(128)S(1)} %stack.63.spots, f32[4]{0:T(128)S(1)} %bitcast.39, ...), custom_call_target="tpu_custom_call" | custom-call | flops 20971520 | bytes 12582912 | tf_op jit(solution)/shard_map/pallas_call | solution.py:732
  86.0 0.1 collective-permute-start.10
  86.1 3.6 %collective-permute-start.11 = (f32[32,8,128]{2,1,0:T(8,128)S(1)}, f32[32,8,128]{2,1,0:T(8,128)S(1)}, u32[]{:S(2)}, u32[]{:S(2)}) collective-permute-start(f32[32,8,128]{2,1,0:T(8,128)S(1)} %get-tuple-element.75), channel_id=1, source_target_pairs={{1,0},{2,1},{3,2},{4,3},{5,4},{6,5},{7,6},{0,7},{9,8},{10,9},{11,1... | collective-permute-start | bytes 393224 | tf_op jit(solution)/shard_map/ppermute | solution.py:660
  89.7 2.5 %shard_map.117 = (f32[64,32,128]{2,1,0:T(8,128)S(1)}, f32[64,32,128]{2,1,0:T(8,128)S(1)}) custom-call(s32[8]{0:T(128)S(1)} %stack.63.spots, f32[4]{0:T(128)S(1)} %bitcast.40, f32[64,32,128]{2,1,0:T(8,128)S(1)} %get-tuple-element.77.now.wave, f32[64,32,128]{2,1,0:T(8,128)S(1)} %get-tuple-element.78.prev.wave_b, f32[64,32,128]{2,1,0:T(8,128)S(1)} %get-tuple-element.62.r2, ...), custom_call_target="tpu_custom_call" | custom-call | flops 10485760 | bytes 8388608 | tf_op jit(solution)/shard_map/pallas_call | solution.py:741
  92.2 1.0 shard_map.118
  93.2 0.1 collective-permute-start.12
  93.3 3.6 %collective-permute-start.13 = (f32[64,8,128]{2,1,0:T(8,128)S(1)}, f32[64,8,128]{2,1,0:T(8,128)S(1)}, u32[]{:S(2)}, u32[]{:S(2)}) collective-permute-start(f32[64,8,128]{2,1,0:T(8,128)S(1)} %get-tuple-element.85), channel_id=1, source_target_pairs={{1,0},{2,1},{3,2},{4,3},{5,4},{6,5},{7,6},{0,7},{9,8},{10,9},{11,1... | collective-permute-start | bytes 786440 | tf_op jit(solution)/shard_map/ppermute | solution.py:660
  96.9 2.3 %shard_map.119 = (f32[64,32,128]{2,1,0:T(8,128)S(1)}, f32[64,32,128]{2,1,0:T(8,128)S(1)}) custom-call(s32[8]{0:T(128)S(1)} %stack.63.spots, f32[64,32,128]{2,1,0:T(8,128)S(1)} %get-tuple-element.83.late, f32[64,32,128]{2,1,0:T(8,128)S(1)} %get-tuple-element.91.later, f32[64,32,128]{2,1,0:T(8,128)S(1)} %get-tuple-element.62.r2, bf16[256,256]{1,0:T(8,128)(2,1)S(1)} %copy-done, ...), custom_call_target="tpu_custom_call" | custom-call | flops 10485760 | bytes 8388608 | tf_op jit(solution)/shard_map/pallas_call | solution.py:753
  99.2 1.8 %collective-permute-done.12.late_lo = f32[64,8,128]{2,1,0:T(8,128)S(1)} collective-permute-done((f32[64,8,128]{2,1,0:T(8,128)S(1)}, f32[64,8,128]{2,1,0:T(8,128)S(1)}, u32[]{:S(2)}, u32[]{:S(2)}) %collective-permute-start.12) | collective-permute-done | bytes 262176 | tf_op jit(solution)/shard_map/ppermute | solution.py:660
  100.9 4.3 %shard_map.120 = (f32[64,32,128]{2,1,0:T(8,128)S(1)}, f32[64,32,128]{2,1,0:T(8,128)S(1)}, f32[64,32,128]{2,1,0:T(8,128)S(1)}, f32[32,8,128]{2,1,0:T(8,128)S(1)}, f32[32,8,128]{2,1,0:T(8,128)S(1)}) custom-call(s32[8]{0:T(128)S(1)} %stack.63.spots, f32[64,32,128]{2,1,0:T(8,128)S(1)} %get-tuple-element.83.late, ...), custom_call_target="tpu_custom_call" | custom-call | flops 20971520 | bytes 16777216 | tf_op jit(solution)/shard_map/pallas_call | solution.py:756
  105.2 0.1 collective-permute-start.14
  105.3 3.6 %collective-permute-start.15 = (f32[32,8,128]{2,1,0:T(8,128)S(1)}, f32[32,8,128]{2,1,0:T(8,128)S(1)}, u32[]{:S(2)}, u32[]{:S(2)}) collective-permute-start(f32[32,8,128]{2,1,0:T(8,128)S(1)} %get-tuple-element.96), channel_id=1, source_target_pairs={{1,0},{2,1},{3,2},{4,3},{5,4},{6,5},{7,6},{0,7},{9,8},{10,9},{11,1... | collective-permute-start | bytes 393224 | tf_op jit(solution)/shard_map/ppermute | solution.py:660
  108.9 2.3 %shard_map.121.total = f32[64,32,128]{2,1,0:T(8,128)S(1)} custom-call(s32[8]{0:T(128)S(1)} %stack.63.spots, f32[64,32,128]{2,1,0:T(8,128)S(1)} %get-tuple-element.98.late, f32[64,32,128]{2,1,0:T(8,128)S(1)} %get-tuple-element.99.later, f32[64,32,128]{2,1,0:T(8,128)S(1)} %get-tuple-element.62.r2, bf16[256,256]{1,0:T(8,128)(2,1)S(1)} %copy-done, ...), custom_call_target="tpu_custom_call" | custom-call | flops 10485760 | bytes 8388608 | tf_op jit(solution)/shard_map/pallas_call | solution.py:768
  111.2 0.0 collective-permute-done.14.halo_lo
  111.2 0.8 shard_map.122
  112.1 4.5 %collective-permute-start.19 = (f32[4,8,32,128]{3,2,1,0:T(8,128)S(1)}, f32[4,8,32,128]{3,2,1,0:T(8,128)S(1)}, u32[]{:S(2)}, u32[]{:S(2)}) collective-permute-start(f32[4,8,32,128]{3,2,1,0:T(8,128)S(1)} %get-tuple-element.106), channel_id=1, source_target_pairs={{0,8},{8,0},{16,24},{24,16},{32,40},{40,32},{48,56},{56,48},{64,72... | collective-permute-start | bytes 1572872 | tf_op jit(solution)/shard_map/ppermute | solution.py:776
  116.5 1.3 collective-permute-start.16
  117.9 2.6 %collective-permute-start.17 = (f32[8,32,128]{2,1,0:T(8,128)S(1)}, f32[8,32,128]{2,1,0:T(8,128)S(1)}, u32[]{:S(2)}, u32[]{:S(2)}) collective-permute-start(f32[8,32,128]{2,1,0:T(8,128)S(1)} %get-tuple-element.104), channel_id=1, source_target_pairs={{0,32},{8,40},{16,48},{24,56},{32,0},{40,8},{48,16},{56,24},{64,96... | collective-permute-start | bytes 393224 | tf_op jit(solution)/shard_map/ppermute | solution.py:775
  120.5 1.1 collective-permute-start.18
  121.6 0.1 collective-permute-start.22
  121.7 2.1 %collective-permute-start.21 = (f32[8,32,128]{2,1,0:T(8,128)S(1)}, f32[8,32,128]{2,1,0:T(8,128)S(1)}, u32[]{:S(2)}, u32[]{:S(2)}) collective-permute-start(f32[8,32,128]{2,1,0:T(8,128)S(1)} %get-tuple-element.108), channel_id=1, source_target_pairs={{0,32},{8,40},{16,48},{24,56},{32,0},{40,8},{48,16},{56,24},{64,96... | collective-permute-start | bytes 393224 | tf_op jit(solution)/shard_map/ppermute | solution.py:777
  123.9 3.0 %collective-permute-done.17.rest_2_ = f32[8,32,128]{2,1,0:T(8,128)S(1)} collective-permute-done((f32[8,32,128]{2,1,0:T(8,128)S(1)}, f32[8,32,128]{2,1,0:T(8,128)S(1)}, u32[]{:S(2)}, u32[]{:S(2)}) %collective-permute-start.17) | collective-permute-done | bytes 131104 | tf_op jit(solution)/shard_map/ppermute | solution.py:775
  126.9 1.9 %collective-permute-done.22.rest_7_ = f32[8,32,128]{2,1,0:T(8,128)S(1)} collective-permute-done((f32[8,32,128]{2,1,0:T(8,128)S(1)}, f32[8,32,128]{2,1,0:T(8,128)S(1)}, u32[]{:S(2)}, u32[]{:S(2)}) %collective-permute-start.22) | collective-permute-done | bytes 131104 | tf_op jit(solution)/shard_map/ppermute | solution.py:777
  128.8 0.9 collective-permute-done.21.rest_6_
  129.7 3.1 %collective-permute-done.20.rest_5_ = f32[8,32,128]{2,1,0:T(8,128)S(1)} collective-permute-done((f32[8,32,128]{2,1,0:T(8,128)S(1)}, f32[8,32,128]{2,1,0:T(8,128)S(1)}, u32[]{:S(2)}, u32[]{:S(2)}) %collective-permute-start.20) | collective-permute-done | bytes 131104 | tf_op jit(solution)/shard_map/ppermute | solution.py:777
  132.9 0.9 shard_map.124
  133.8 1.1 collective-permute-start.23
  134.9 0.9 shard_map.123
  135.8 7.0 %collective-permute-done.23 = f32[2,8,32,128]{3,2,1,0:T(8,128)S(1)} collective-permute-done((f32[2,8,32,128]{3,2,1,0:T(8,128)S(1)}, f32[2,8,32,128]{3,2,1,0:T(8,128)S(1)}, u32[]{:S(2)}, u32[]{:S(2)}) %collective-permute-start.23) | collective-permute-done | bytes 262176 | tf_op jit(solution)/shard_map/ppermute | solution.py:782
  142.8 0.7 add_bitcast_fusion
  (45 shorter events, 0.1 us)
Async XLA Ops:
  0.0 13.6 %collective-permute-start = (f32[2,8,32,128]{3,2,1,0:T(8,128)}, f32[2,8,32,128]{3,2,1,0:T(8,128)S(1)}, u32[]{:S(2)}, u32[]{:S(2)}) collective-permute-start(f32[2,8,32,128]{3,2,1,0:T(8,128)} %bitcast.35), channel_id=1, source_target_pairs={{0,64},{8,72},{16,80},{24,88},{32,96},{40,104},{48,112},{56,120},{... | collective-permute-start | bytes 786440 | tf_op jit(solution)/shard_map/ppermute | solution.py:663
  3.6 10.5 %collective-permute-start.1 = (f32[2,8,32,128]{3,2,1,0:T(8,128)}, f32[2,8,32,128]{3,2,1,0:T(8,128)S(1)}, u32[]{:S(2)}, u32[]{:S(2)}) collective-permute-start(f32[2,8,32,128]{3,2,1,0:T(8,128)} %bitcast.36), channel_id=1, source_target_pairs={{0,8},{8,0},{16,24},{24,16},{32,40},{40,32},{48,56},{56,48},{64,72... | collective-permute-start | bytes 786440 | tf_op jit(solution)/shard_map/ppermute | solution.py:664
  8.3 5.7 %copy-start.17 = (s32[16,8]{0,1:T(8,128)S(1)}, s32[16,8]{0,1:T(8,128)}, u32[]{:S(2)}) copy-start(s32[16,8]{0,1:T(8,128)} %param.20) | copy-start | bytes 1540
  8.3 5.8 %copy-start.15 = (s32[1,256]{1,0:T(1,128)S(1)}, s32[1,256]{1,0:T(1,128)}, u32[]{:S(2)}) copy-start(s32[1,256]{1,0:T(1,128)} %param.18) | copy-start | bytes 3076
  8.3 6.9 %copy-start.9 = (f32[2,1,8,32,128]{4,3,2,1,0:T(8,128)S(1)}, f32[2,1,8,32,128]{4,3,2,1,0:T(8,128)}, u32[]{:S(2)}) copy-start(f32[2,1,8,32,128]{4,3,2,1,0:T(8,128)} %param.11) | copy-start | bytes 786436
  8.3 13.8 %copy-start.16 = (f32[1,4,256]{2,1,0:T(4,128)S(1)}, f32[1,4,256]{2,1,0:T(4,128)}, u32[]{:S(2)}) copy-start(f32[1,4,256]{2,1,0:T(4,128)} %param.19) | copy-start | bytes 12292
  8.3 60.3 %all-to-all-start = ((f32[8,8,144,128]{3,2,1,0:T(8,128)}), f32[8,8,144,128]{3,2,1,0:T(8,128)}, u32[]{:S(2)}, u32[]{:S(2)}) async-start(f32[8,8,144,128]{3,2,1,0:T(8,128)} %shard_map.109), calls=%async_computation | async-start | bytes 9437184 | tf_op jit(solution)/shard_map/all_to_all | solution.py:684
  13.6 1.6 %collective-permute-start.2 = (f32[2,8,32,128]{3,2,1,0:T(8,128)S(1)}, f32[2,8,32,128]{3,2,1,0:T(8,128)S(1)}, u32[]{:S(2)}, u32[]{:S(2)}) collective-permute-start(f32[2,8,32,128]{3,2,1,0:T(8,128)S(1)} %collective-permute-done.other), channel_id=1, source_target_pairs={{0,8},{8,0},{16,24},{24,16},{32,40},{40,32},{48,56},{56,48},{64,72... | collective-permute-start | bytes 786440 | tf_op jit(solution)/shard_map/ppermute | solution.py:665
  14.0 8.1 %copy-start.12 = (s32[2]{0:T(128)}, s32[2]{0:T(128)S(1)}, u32[]{:S(2)}) copy-start(s32[2]{0:T(128)S(1)} %pad_add_fusion.ids) | copy-start | bytes 28
  14.1 8.0 %copy-start.10 = (s32[16,8]{1,0:T(8,128)}, s32[16,8]{1,0:T(8,128)S(1)}, u32[]{:S(2)}) copy-start(s32[16,8]{1,0:T(8,128)S(1)} %copy.14.apertures) | copy-start | bytes 1540
  17.1 18.6 %collective-permute-start.3 = (f32[2,8,32,128]{3,2,1,0:T(8,128)}, f32[2,8,32,128]{3,2,1,0:T(8,128)}, u32[]{:S(2)}, u32[]{:S(2)}) collective-permute-start(f32[2,8,32,128]{3,2,1,0:T(8,128)} %get-tuple-element.57), channel_id=1, source_target_pairs={{0,16},{8,24},{16,32},{24,40},{32,48},{40,56},{48,0},{56,8},{64,80... | collective-permute-start | bytes 786440 | tf_op jit(solution)/shard_map/ppermute | solution.py:669
  18.4 17.3 %collective-permute-start.4 = (f32[2,8,32,128]{3,2,1,0:T(8,128)}, f32[2,8,32,128]{3,2,1,0:T(8,128)}, u32[]{:S(2)}, u32[]{:S(2)}) collective-permute-start(f32[2,8,32,128]{3,2,1,0:T(8,128)} %get-tuple-element.58), channel_id=1, source_target_pairs={{0,32},{8,40},{16,48},{24,56},{32,0},{40,8},{48,16},{56,24},{64,96... | collective-permute-start | bytes 786440 | tf_op jit(solution)/shard_map/ppermute | solution.py:669
  21.0 14.7 %collective-permute-start.5 = (f32[2,8,32,128]{3,2,1,0:T(8,128)}, f32[2,8,32,128]{3,2,1,0:T(8,128)}, u32[]{:S(2)}, u32[]{:S(2)}) collective-permute-start(f32[2,8,32,128]{3,2,1,0:T(8,128)} %get-tuple-element.59), channel_id=1, source_target_pairs={{0,48},{8,56},{16,0},{24,8},{32,16},{40,24},{48,32},{56,40},{64,11... | collective-permute-start | bytes 786440 | tf_op jit(solution)/shard_map/ppermute | solution.py:669
  22.1 13.6 %copy-start.11 = (s32[16,8]{1,0:T(8,128)S(1)}, s32[16,8]{1,0:T(8,128)}, u32[]{:S(2)}) copy-start(s32[16,8]{1,0:T(8,128)} %copy-done.10) | copy-start | bytes 1540
  22.1 13.6 %copy-start.13 = (s32[2]{0:T(128)S(1)}, s32[2]{0:T(128)}, u32[]{:S(2)}) copy-start(s32[2]{0:T(128)} %copy-done.12) | copy-start | bytes 28
  22.1 46.5 %copy-start = (bf16[256,256]{1,0:T(8,128)(2,1)S(1)}, bf16[256,256]{1,0:T(8,128)(2,1)}, u32[]{:S(2)}) copy-start(bf16[256,256]{1,0:T(8,128)(2,1)} %constant.94.clone.oper) | copy-start | bytes 393220
  22.1 46.5 %copy-start.14 = (f32[1,4]{1,0:T(1,128)S(1)}, f32[1,4]{1,0:T(1,128)}, u32[]{:S(2)}) copy-start(f32[1,4]{1,0:T(1,128)} %param.16) | copy-start | bytes 52
  27.4 1.1 copy-start.1
  28.6 1.0 copy-start.3
  29.6 1.0 copy-start.5
  30.6 1.0 copy-start.7
  37.8 39.9 %collective-permute-start.8 = (f32[64,8,128]{2,1,0:T(8,128)}, f32[64,8,128]{2,1,0:T(8,128)S(1)}, u32[]{:S(2)}, u32[]{:S(2)}) collective-permute-start(f32[64,8,128]{2,1,0:T(8,128)} %get-tuple-element.67), channel_id=1, source_target_pairs={{0,1},{1,2},{2,3},{3,4},{4,5},{5,6},{6,7},{7,0},{8,9},{9,10},{10,1... | collective-permute-start | bytes 786440 | tf_op jit(solution)/shard_map/ppermute | solution.py:660
  39.5 38.2 %collective-permute-start.9 = (f32[64,8,128]{2,1,0:T(8,128)}, f32[64,8,128]{2,1,0:T(8,128)S(1)}, u32[]{:S(2)}, u32[]{:S(2)}) collective-permute-start(f32[64,8,128]{2,1,0:T(8,128)} %get-tuple-element.68), channel_id=1, source_target_pairs={{1,0},{2,1},{3,2},{4,3},{5,4},{6,5},{7,6},{0,7},{9,8},{10,9},{11,1... | collective-permute-start | bytes 786440 | tf_op jit(solution)/shard_map/ppermute | solution.py:660
  72.3 9.6 %collective-permute-start.6 = (f32[64,8,128]{2,1,0:T(8,128)S(1)}, f32[64,8,128]{2,1,0:T(8,128)S(1)}, u32[]{:S(2)}, u32[]{:S(2)}) collective-permute-start(f32[64,8,128]{2,1,0:T(8,128)S(1)} %get-tuple-element.64), channel_id=1, source_target_pairs={{0,1},{1,2},{2,3},{3,4},{4,5},{5,6},{6,7},{7,0},{8,9},{9,10},{10,1... | collective-permute-start | bytes 786440 | tf_op jit(solution)/shard_map/ppermute | solution.py:660
  72.9 9.0 %collective-permute-start.7 = (f32[64,8,128]{2,1,0:T(8,128)S(1)}, f32[64,8,128]{2,1,0:T(8,128)S(1)}, u32[]{:S(2)}, u32[]{:S(2)}) collective-permute-start(f32[64,8,128]{2,1,0:T(8,128)S(1)} %get-tuple-element.65), channel_id=1, source_target_pairs={{1,0},{2,1},{3,2},{4,3},{5,4},{6,5},{7,6},{0,7},{9,8},{10,9},{11,1... | collective-permute-start | bytes 786440 | tf_op jit(solution)/shard_map/ppermute | solution.py:660
  77.7 12.0 %copy-start.8 = (f32[64,32,128]{2,1,0:T(8,128)S(1)}, f32[64,32,128]{2,1,0:T(8,128)}, u32[]{:S(2)}) copy-start(f32[64,32,128]{2,1,0:T(8,128)} %copy-done.7) | copy-start | bytes 3145732
  86.0 6.2 %collective-permute-start.10 = (f32[32,8,128]{2,1,0:T(8,128)S(1)}, f32[32,8,128]{2,1,0:T(8,128)S(1)}, u32[]{:S(2)}, u32[]{:S(2)}) collective-permute-start(f32[32,8,128]{2,1,0:T(8,128)S(1)} %get-tuple-element.74), channel_id=1, source_target_pairs={{0,1},{1,2},{2,3},{3,4},{4,5},{5,6},{6,7},{7,0},{8,9},{9,10},{10,1... | collective-permute-start | bytes 393224 | tf_op jit(solution)/shard_map/ppermute | solution.py:660
  86.1 6.1 %collective-permute-start.11 = (f32[32,8,128]{2,1,0:T(8,128)S(1)}, f32[32,8,128]{2,1,0:T(8,128)S(1)}, u32[]{:S(2)}, u32[]{:S(2)}) collective-permute-start(f32[32,8,128]{2,1,0:T(8,128)S(1)} %get-tuple-element.75), channel_id=1, source_target_pairs={{1,0},{2,1},{3,2},{4,3},{5,4},{6,5},{7,6},{0,7},{9,8},{10,9},{11,1... | collective-permute-start | bytes 393224 | tf_op jit(solution)/shard_map/ppermute | solution.py:660
  89.7 7.2 %copy-start.2 = (f32[64,48,128]{2,1,0:T(8,128)S(1)}, f32[64,48,128]{2,1,0:T(8,128)}, u32[]{:S(2)}) copy-start(f32[64,48,128]{2,1,0:T(8,128)} %copy-done.1) | copy-start | bytes 4718596
  93.2 7.8 %collective-permute-start.12 = (f32[64,8,128]{2,1,0:T(8,128)S(1)}, f32[64,8,128]{2,1,0:T(8,128)S(1)}, u32[]{:S(2)}, u32[]{:S(2)}) collective-permute-start(f32[64,8,128]{2,1,0:T(8,128)S(1)} %get-tuple-element.84), channel_id=1, source_target_pairs={{0,1},{1,2},{2,3},{3,4},{4,5},{5,6},{6,7},{7,0},{8,9},{9,10},{10,1... | collective-permute-start | bytes 786440 | tf_op jit(solution)/shard_map/ppermute | solution.py:660
  93.3 7.7 %collective-permute-start.13 = (f32[64,8,128]{2,1,0:T(8,128)S(1)}, f32[64,8,128]{2,1,0:T(8,128)S(1)}, u32[]{:S(2)}, u32[]{:S(2)}) collective-permute-start(f32[64,8,128]{2,1,0:T(8,128)S(1)} %get-tuple-element.85), channel_id=1, source_target_pairs={{1,0},{2,1},{3,2},{4,3},{5,4},{6,5},{7,6},{0,7},{9,8},{10,9},{11,1... | collective-permute-start | bytes 786440 | tf_op jit(solution)/shard_map/ppermute | solution.py:660
  96.9 4.0 %copy-start.6 = (f32[64,32,128]{2,1,0:T(8,128)S(1)}, f32[64,32,128]{2,1,0:T(8,128)}, u32[]{:S(2)}) copy-start(f32[64,32,128]{2,1,0:T(8,128)} %copy-done.5) | copy-start | bytes 3145732
  100.9 7.9 %copy-start.4 = (f32[64,32,128]{2,1,0:T(8,128)S(1)}, f32[64,32,128]{2,1,0:T(8,128)}, u32[]{:S(2)}) copy-start(f32[64,32,128]{2,1,0:T(8,128)} %copy-done.3) | copy-start | bytes 3145732
  105.2 6.0 %collective-permute-start.14 = (f32[32,8,128]{2,1,0:T(8,128)S(1)}, f32[32,8,128]{2,1,0:T(8,128)S(1)}, u32[]{:S(2)}, u32[]{:S(2)}) collective-permute-start(f32[32,8,128]{2,1,0:T(8,128)S(1)} %get-tuple-element.95), channel_id=1, source_target_pairs={{0,1},{1,2},{2,3},{3,4},{4,5},{5,6},{6,7},{7,0},{8,9},{9,10},{10,1... | collective-permute-start | bytes 393224 | tf_op jit(solution)/shard_map/ppermute | solution.py:660
  105.3 5.9 %collective-permute-start.15 = (f32[32,8,128]{2,1,0:T(8,128)S(1)}, f32[32,8,128]{2,1,0:T(8,128)S(1)}, u32[]{:S(2)}, u32[]{:S(2)}) collective-permute-start(f32[32,8,128]{2,1,0:T(8,128)S(1)} %get-tuple-element.96), channel_id=1, source_target_pairs={{1,0},{2,1},{3,2},{4,3},{5,4},{6,5},{7,6},{0,7},{9,8},{10,9},{11,1... | collective-permute-start | bytes 393224 | tf_op jit(solution)/shard_map/ppermute | solution.py:660
  112.1 9.5 %collective-permute-start.19 = (f32[4,8,32,128]{3,2,1,0:T(8,128)S(1)}, f32[4,8,32,128]{3,2,1,0:T(8,128)S(1)}, u32[]{:S(2)}, u32[]{:S(2)}) collective-permute-start(f32[4,8,32,128]{3,2,1,0:T(8,128)S(1)} %get-tuple-element.106), channel_id=1, source_target_pairs={{0,8},{8,0},{16,24},{24,16},{32,40},{40,32},{48,56},{56,48},{64,72... | collective-permute-start | bytes 1572872 | tf_op jit(solution)/shard_map/ppermute | solution.py:776
  116.5 7.3 %collective-permute-start.16 = (f32[8,32,128]{2,1,0:T(8,128)S(1)}, f32[8,32,128]{2,1,0:T(8,128)S(1)}, u32[]{:S(2)}, u32[]{:S(2)}) collective-permute-start(f32[8,32,128]{2,1,0:T(8,128)S(1)} %get-tuple-element.103), channel_id=1, source_target_pairs={{0,16},{8,24},{16,32},{24,40},{32,48},{40,56},{48,0},{56,8},{64,80... | collective-permute-start | bytes 393224 | tf_op jit(solution)/shard_map/ppermute | solution.py:775
  117.9 9.0 %collective-permute-start.17 = (f32[8,32,128]{2,1,0:T(8,128)S(1)}, f32[8,32,128]{2,1,0:T(8,128)S(1)}, u32[]{:S(2)}, u32[]{:S(2)}) collective-permute-start(f32[8,32,128]{2,1,0:T(8,128)S(1)} %get-tuple-element.104), channel_id=1, source_target_pairs={{0,32},{8,40},{16,48},{24,56},{32,0},{40,8},{48,16},{56,24},{64,96... | collective-permute-start | bytes 393224 | tf_op jit(solution)/shard_map/ppermute | solution.py:775
  120.5 6.4 %collective-permute-start.18 = (f32[8,32,128]{2,1,0:T(8,128)S(1)}, f32[8,32,128]{2,1,0:T(8,128)S(1)}, u32[]{:S(2)}, u32[]{:S(2)}) collective-permute-start(f32[8,32,128]{2,1,0:T(8,128)S(1)} %get-tuple-element.105), channel_id=1, source_target_pairs={{0,48},{8,56},{16,0},{24,8},{32,16},{40,24},{48,32},{56,40},{64,11... | collective-permute-start | bytes 393224 | tf_op jit(solution)/shard_map/ppermute | solution.py:775
  121.6 7.2 %collective-permute-start.22 = (f32[8,32,128]{2,1,0:T(8,128)S(1)}, f32[8,32,128]{2,1,0:T(8,128)S(1)}, u32[]{:S(2)}, u32[]{:S(2)}) collective-permute-start(f32[8,32,128]{2,1,0:T(8,128)S(1)} %get-tuple-element.107), channel_id=1, source_target_pairs={{0,48},{8,56},{16,0},{24,8},{32,16},{40,24},{48,32},{56,40},{64,11... | collective-permute-start | bytes 393224 | tf_op jit(solution)/shard_map/ppermute | solution.py:777
  121.7 8.0 %collective-permute-start.21 = (f32[8,32,128]{2,1,0:T(8,128)S(1)}, f32[8,32,128]{2,1,0:T(8,128)S(1)}, u32[]{:S(2)}, u32[]{:S(2)}) collective-permute-start(f32[8,32,128]{2,1,0:T(8,128)S(1)} %get-tuple-element.108), channel_id=1, source_target_pairs={{0,32},{8,40},{16,48},{24,56},{32,0},{40,8},{48,16},{56,24},{64,96... | collective-permute-start | bytes 393224 | tf_op jit(solution)/shard_map/ppermute | solution.py:777
  123.8 9.0 %collective-permute-start.20 = (f32[8,32,128]{2,1,0:T(8,128)S(1)}, f32[8,32,128]{2,1,0:T(8,128)S(1)}, u32[]{:S(2)}, u32[]{:S(2)}) collective-permute-start(f32[8,32,128]{2,1,0:T(8,128)S(1)} %get-tuple-element.109), channel_id=1, source_target_pairs={{0,16},{8,24},{16,32},{24,40},{32,48},{40,56},{48,0},{56,8},{64,80... | collective-permute-start | bytes 393224 | tf_op jit(solution)/shard_map/ppermute | solution.py:777
  133.8 9.0 %collective-permute-start.23 = (f32[2,8,32,128]{3,2,1,0:T(8,128)S(1)}, f32[2,8,32,128]{3,2,1,0:T(8,128)S(1)}, u32[]{:S(2)}, u32[]{:S(2)}) collective-permute-start(f32[2,8,32,128]{3,2,1,0:T(8,128)S(1)} %shard_map.124), channel_id=1, source_target_pairs={{0,64},{8,72},{16,80},{24,88},{32,96},{40,104},{48,112},{56,120},{... | collective-permute-start | bytes 786440 | tf_op jit(solution)/shard_map/ppermute | solution.py:782
